TPU v7x, 32 devices: a whole 2x2x4 slice. The times are simulated.
32 devices in a mesh: grp: 2 (over x), gx: 4 (over z), gy: 4 (over y, core).
Axes of the slice: x: 2, y: 2, z: 4, core: 2. Of those that a mesh axis runs over, the one named last changes fastest.
Arguments:
- zonal_boundary_speed: float32 [32, 4, 4, 512], P(None, 'gy', 'grp', 'gx'), may hold values from -0.2 to 0.2
- meridional_boundary_speed: float32 [32, 4, 4, 512], P(None, 'gy', 'grp', 'gx'), may hold values from -0.2 to 0.2
- potential_warmth: float32 [32, 4, 4, 512], P(None, 'gy', 'grp', 'gx'), may hold values from 2 to 28
- saltiness_field: float32 [32, 4, 4, 512], P(None, 'gy', 'grp', 'gx'), may hold values from 33 to 37
- quiescent_mixing_profile: float32 [32, 4, 4, 512], P(None, 'gy', 'grp', 'gx'), may hold values from 0.005 to 0.05
- substance_amounts: float32 [19, 32, 16, 512], P(None, 'grp', 'gy', 'gx'), may hold values from 0.1 to 3
- submerged_layer_number: int32 [16, 512], P('gy', 'gx'), may hold values from 0 to 32
- solar_radiation: float32 [16, 512], P('gy', 'gx'), may hold values from 0.2 to 1
- interaction_rates: float32 [19, 19], replicated, may hold values from -1.25 to 1.25
- photosynthetic_rates: float32 [19], replicated, may hold values from 0.1 to 1
- saturation_irradiance: float32 [19], replicated, may hold values from 0.05 to 0.5
- pigment_per_tracer: float32 [19], replicated, may hold values from 0.01 to 0.1
Outputs:
- east_final: float32 [32, 4, 4, 512], P(None, 'gy', 'grp', 'gx')
- north_final: float32 [32, 4, 4, 512], P(None, 'gy', 'grp', 'gx')
- temperature_final: float32 [32, 4, 4, 512], P(None, 'gy', 'grp', 'gx')
- salinity_final: float32 [32, 4, 4, 512], P(None, 'gy', 'grp', 'gx')
- tracers_final: float32 [19, 32, 16, 512], P(None, 'grp', 'gy', 'gx')
All inputs are finite; a program needn't handle non-finite values.
Results may differ from a plain program's by a relative error of at most 0.0001.
Values sent between devices are 32-bit elements; how exact they have to be, the bound alone decides.
No kernel may reach another device: no remote copies, remote signals or barrier semaphores. Data moves between devices by JAX's collectives and lax.ppermute only.
A program may use at most 64 MiB of HBM per device.

v0:
```python
import jax
import jax.numpy as jnp
from jax import lax
from jax.sharding import PartitionSpec as P

STEPS = 2


WATER_ATTEN = 0.01
PIGMENT_ATTEN = 0.05
WARMING_UPTAKE = 5.0
WARM_EXPANSION = 0.2
SALT_EXPANSION = 0.8
CONVECT_MIX = 0.15
SIDE_DIFFUSE = 0.05
WARMING_FACTOR = 0.0633
TIME_STEP = 0.5


def with_halo(cells, sides, width):
    for axis, dim in sides:
        count = lax.axis_size(axis)
        ends = count - 1
        head = lax.slice_in_dim(cells, 0, width, axis=dim)
        tail = lax.slice_in_dim(cells, cells.shape[dim] - width, cells.shape[dim], axis=dim)
        cells = jnp.concatenate(
            [
                lax.ppermute(tail, axis, [(i, (i + 1) % count) for i in range(ends)]),
                cells,
                lax.ppermute(head, axis, [((i + 1) % count, i) for i in range(ends)]),
            ],
            axis=dim,
        )
    return cells


def trim_axis(values, dimension_slot, start, stop):
    leading = (slice(None),) * (values.ndim + dimension_slot)
    return values[leading + (slice(start, stop),)]


def face_divergence(tracer_amounts, velocity, submerged_mask, dimension_slot):
    lower_conc = trim_axis(tracer_amounts, dimension_slot, None, -1)
    upper_conc = trim_axis(tracer_amounts, dimension_slot, 1, None)
    face_speed = trim_axis(velocity, dimension_slot, None, -1)
    opening = trim_axis(submerged_mask, dimension_slot, None, -1) * trim_axis(
        submerged_mask, dimension_slot, 1, None
    )
    flux_face = opening * (
        jnp.maximum(face_speed, 0.0) * lower_conc
        + jnp.minimum(face_speed, 0.0) * upper_conc
        - SIDE_DIFFUSE * (upper_conc - lower_conc)
    )
    return trim_axis(flux_face, dimension_slot, 1, None) - trim_axis(
        flux_face, dimension_slot, None, -1
    )


def level_divergence(tracer_amounts, mixing_coefficient):
    flux_face = trim_axis(mixing_coefficient, -3, None, -1) * (
        trim_axis(tracer_amounts, -3, 1, None) - trim_axis(tracer_amounts, -3, None, -1)
    )
    return trim_axis(flux_face, -3, 1, None) - trim_axis(flux_face, -3, None, -1)


def light_columns(pigment, surface):
    attenuation = WATER_ATTEN + PIGMENT_ATTEN * pigment
    above = jnp.cumsum(attenuation, axis=0) - attenuation
    top_light = surface * jnp.exp(-above)
    return (top_light * (1.0 - jnp.exp(-attenuation)), top_light * jnp.exp(-0.5 * attenuation))


def marine_advance(
    zonal_transport,
    meridional_transport,
    thermal_mesh,
    brine_values,
    quiescent_mixing,
    radiative_warming,
    submerged_mask,
):
    thermal_mesh = thermal_mesh + WARMING_UPTAKE * radiative_warming * submerged_mask
    water_buoyancy = SALT_EXPANSION * brine_values - WARM_EXPANSION * thermal_mesh
    strat = water_buoyancy[1:] - water_buoyancy[:-1]
    face_mix = (
        0.5 * (quiescent_mixing[:-1] + quiescent_mixing[1:]) + CONVECT_MIX * jax.nn.sigmoid(-strat)
    ) * submerged_mask[1:]
    bottom = jnp.zeros_like(face_mix[:1])
    mixing_coefficient = jnp.concatenate([face_mix, bottom], axis=0)

    def turbulent_stirring(field):
        flux_face = face_mix * (field[1:] - field[:-1])
        return (
            field
            + jnp.concatenate([flux_face, bottom], axis=0)
            - jnp.concatenate([bottom, flux_face], axis=0)
        )

    return (
        turbulent_stirring(zonal_transport),
        turbulent_stirring(meridional_transport),
        turbulent_stirring(thermal_mesh),
        turbulent_stirring(brine_values),
        mixing_coefficient,
    )


def chemical_kinetics(
    tracer_amounts,
    thermal_mesh,
    photosynthetic_radiance,
    submerged_mask,
    interaction_rates,
    photosynthetic_rates,
    saturation_irradiance,
):
    thermal_multiplier = jnp.exp(WARMING_FACTOR * (thermal_mesh - 20.0))
    mixed_terms = jnp.einsum(
        "ij,jzyx->izyx", interaction_rates, tracer_amounts, precision=lax.Precision.HIGHEST
    )
    light_limit = photosynthetic_radiance / (
        photosynthetic_radiance + saturation_irradiance[:, None, None, None]
    )
    return (
        TIME_STEP
        * submerged_mask
        * (
            thermal_multiplier * mixed_terms
            + photosynthetic_rates[:, None, None, None] * light_limit * tracer_amounts
        )
    )


def per_device(
    zonal_boundary_speed,
    meridional_boundary_speed,
    potential_warmth,
    saltiness_field,
    quiescent_mixing_profile,
    substance_amounts,
    submerged_layer_number,
    solar_radiation,
    interaction_rates,
    photosynthetic_rates,
    saturation_irradiance,
    pigment_per_tracer,
):
    member = lax.axis_index("grp")
    result_dimensions = zonal_boundary_speed.shape
    vertical_span = (result_dimensions[0], result_dimensions[2], result_dimensions[3])
    strip_rows = result_dimensions[2]
    band_levels = substance_amounts.shape[1]
    tracer_count = substance_amounts.shape[0]
    zonal_transport = zonal_boundary_speed.reshape(vertical_span)
    meridional_transport = meridional_boundary_speed.reshape(vertical_span)
    thermal_mesh = potential_warmth.reshape(vertical_span)
    brine_values = saltiness_field.reshape(vertical_span)
    quiescent_mixing = quiescent_mixing_profile.reshape(vertical_span)
    depth_strip = lax.dynamic_slice_in_dim(
        submerged_layer_number, member * strip_rows, strip_rows, 0
    )
    light_strip = lax.dynamic_slice_in_dim(solar_radiation, member * strip_rows, strip_rows, 0)
    marine_profiles = (
        lax.broadcasted_iota(jnp.int32, vertical_span, 0) < depth_strip[None]
    ).astype(jnp.float32)
    band_index = member * band_levels + lax.broadcasted_iota(
        jnp.int32, substance_amounts.shape[1:], 0
    )
    wet_band = (band_index < submerged_layer_number[None]).astype(jnp.float32)
    tracer_amounts = substance_amounts
    for repeat in range(STEPS):
        pigment_band = jnp.einsum(
            "i,izyx->zyx", pigment_per_tracer, tracer_amounts, precision=lax.Precision.HIGHEST
        )
        pigment_cols = lax.all_to_all(pigment_band, "grp", split_axis=1, concat_axis=0, tiled=True)
        radiative_warming, irradiance_profiles = light_columns(pigment_cols, light_strip[None])
        zonal_transport, meridional_transport, thermal_mesh, brine_values, mixing_coefficient = (
            marine_advance(
                zonal_transport,
                meridional_transport,
                thermal_mesh,
                brine_values,
                quiescent_mixing,
                radiative_warming,
                marine_profiles,
            )
        )
        stacked = jnp.stack(
            [
                zonal_transport,
                meridional_transport,
                thermal_mesh,
                mixing_coefficient,
                irradiance_profiles,
            ],
            axis=0,
        )
        forcing = lax.all_to_all(stacked, "grp", split_axis=1, concat_axis=2, tiled=True)
        band_east = forcing[0]
        band_north = forcing[1]
        band_temp = forcing[2]
        band_diff = forcing[3]
        band_par = forcing[4]
        sideways = jnp.concatenate(
            [tracer_amounts, band_east[None], band_north[None], wet_band[None]], axis=0
        )
        side_padded = with_halo(sideways, (("gx", 3), ("gy", 2)), 1)
        across_east = side_padded[:, :, 1:-1, :]
        across_north = side_padded[:, :, :, 1:-1]
        upright = jnp.concatenate([tracer_amounts, band_diff[None]], axis=0)
        level_padded = with_halo(upright, (("grp", 1),), 1)
        level_conc = level_padded[:tracer_count]
        level_diff = level_padded[tracer_count]
        zonal_increment = face_divergence(
            across_east[:tracer_count], across_east[tracer_count], across_east[tracer_count + 2], -1
        )
        meridional_increment = face_divergence(
            across_north[:tracer_count],
            across_north[tracer_count + 1],
            across_north[tracer_count + 2],
            -2,
        )
        depthwise_transfer = level_divergence(level_conc, level_diff)
        tracer_amounts = (
            tracer_amounts
            - zonal_increment
            - meridional_increment
            + depthwise_transfer
            + chemical_kinetics(
                tracer_amounts,
                band_temp,
                band_par,
                wet_band,
                interaction_rates,
                photosynthetic_rates,
                saturation_irradiance,
            )
        )
    return (
        zonal_transport.reshape(result_dimensions),
        meridional_transport.reshape(result_dimensions),
        thermal_mesh.reshape(result_dimensions),
        brine_values.reshape(result_dimensions),
        tracer_amounts,
    )


def solution(mesh):
    placed = (
        P(None, "gy", "grp", "gx"),
        P(None, "gy", "grp", "gx"),
        P(None, "gy", "grp", "gx"),
        P(None, "gy", "grp", "gx"),
        P(None, "gy", "grp", "gx"),
        P(None, "grp", "gy", "gx"),
        P("gy", "gx"),
        P("gy", "gx"),
        P(),
        P(),
        P(),
        P(),
    )
    return jax.shard_map(
        per_device,
        mesh=mesh,
        in_specs=placed,
        out_specs=(
            P(None, "gy", "grp", "gx"),
            P(None, "gy", "grp", "gx"),
            P(None, "gy", "grp", "gx"),
            P(None, "gy", "grp", "gx"),
            P(None, "grp", "gy", "gx"),
        ),
        check_vma=False,
    )
```

profile of v0, /device:TPU:6, one launch (start us, length us, event | category | flops | bytes accessed | tf_op | source)
XLA Modules:
  0.0 108.6 jit_solution(5239790470282558192)
XLA Ops:
  0.7 2.0 %fusion.19 = f32[1,16,4,128]{3,0,2,1:T(1,128)S(1)} fusion(f32[19,16,4,128]{3,2,1,0:T(4,128)} %param.17, f32[19]{0:T(128)} %param.23), kind=kOutput, calls=%fused_computation.101 | convolution fusion | flops 1867776 | bytes 655436 | tf_op jit(solution)/shard_map/i,izyx->zyx/dot_general | solution.py:172
  3.3 3.8 %all-to-all-start = ((f32[16,4,128]{2,0,1:T(8,128)}), f32[16,4,128]{2,0,1:T(8,128)S(1)}, u32[]{:S(2)}, u32[]{:S(2)}) async-start(f32[16,4,128]{2,0,1:T(8,128)} %bitcast.204), calls=%async_computation | async-start | bytes 65536 | tf_op jit(solution)/shard_map/all_to_all | solution.py:175
  10.5 5.2 %all-to-all-start.1 = ((f32[5,32,2,128]{3,2,0,1:T(2,128)}), f32[5,32,2,128]{3,2,0,1:T(2,128)S(1)}, u32[]{:S(2)}, u32[]{:S(2)}) async-start(f32[5,32,2,128]{3,2,0,1:T(2,128)} %copy.84), calls=%async_computation.1 | async-start | bytes 327680 | tf_op jit(solution)/shard_map/all_to_all | solution.py:198
  16.8 1.6 %all-to-all-done.1 = f32[5,32,2,128]{3,2,0,1:T(2,128)S(1)} async-done(((f32[5,32,2,128]{3,2,0,1:T(2,128)}), f32[5,32,2,128]{3,2,0,1:T(2,128)S(1)}, u32[]{:S(2)}, u32[]{:S(2)}) %all-to-all-start.1) | async-done | bytes 163872 | tf_op jit(solution)/shard_map/all_to_all | solution.py:198
  21.6 5.1 %collective-permute-start = (f32[22,16,4,1]{0,1,3,2:T(8,128)S(1)}, f32[22,16,4,1]{0,1,3,2:T(8,128)}, u32[]{:S(2)}, u32[]{:S(2)}) collective-permute-start(f32[22,16,4,1]{0,1,3,2:T(8,128)S(1)} %copy.86), channel_id=1, source_target_pairs={{0,4},{4,8},{8,12},{1,5},{5,9},{9,13},{2,6},{6,10},{10,14},{3,7},{... | collective-permute-start | bytes 16904 | tf_op jit(solution)/shard_map/ppermute | solution.py:28
  28.0 4.5 %collective-permute-start.5 = (f32[20,1,4,128]{3,0,2,1:T(8,128)S(1)}, f32[20,1,4,128]{3,0,2,1:T(8,128)S(1)}, u32[]{:S(2)}, u32[]{:S(2)}) collective-permute-start(f32[20,1,4,128]{3,0,2,1:T(8,128)S(1)} %get-tuple-element.47), channel_id=1, source_target_pairs={{16,0},{17,1},{18,2},{19,3},{20,4},{21,5},{22,6},{23,7},{24,8},{25... | collective-permute-start | bytes 122888 | tf_op jit(solution)/shard_map/ppermute | solution.py:30
  33.5 1.6 %copy.88 = f32[22,16,4,1]{3,2,1,0:T(4,128)S(1)} copy(f32[22,16,4,1]{0,1,3,2:T(8,128)} %collective-permute-done) | data formatting | bytes 11264 | tf_op jit(solution)/shard_map/ppermute | solution.py:28
  35.2 4.9 %pad_maximum_fusion.63 = (f32[22,16,1,130]{3,2,1,0:T(1,128)S(1)}, f32[22,16,1,130]{3,2,1,0:T(1,128)S(1)}) fusion(f32[22,16,4,1]{3,2,1,0:T(4,128)S(1)} %copy.89, f32[22,16,4,1]{3,2,1,0:T(4,128)S(1)} %copy.88, f32[1,16,4,128]{3,2,1,0:T(4,128)S(1)} %compare_convert_fusion, f32[1,16,4,128]{3,2,1,0:T(4,128)S(1)} %bitcast.214, f32[1,16,4,128]{3,2,1,0:T(4,128)S(1)} %bitcast.222, ...), kind=kLoop, calls=%fused_computation.98 | loop fusion | flops 457600 | bytes 1098240 | tf_op jit(solution)/shard_map/slice | solution.py:25
  40.2 1.8 %fusion.69 = f32[19,16,4,129]{3,2,1,0:T(4,128)S(1)} fusion(f32[1,16,4,128]{3,2,1,0:T(4,128)S(1)} %compare_convert_fusion, f32[1,16,4,128]{3,2,1,0:T(4,128)S(1)} %bitcast.216, f32[1,16,4,128]{3,2,1,0:T(4,128)S(1)} %bitcast.224, f32[19,16,4,128]{3,2,1,0:T(4,128)S(1)} %copy-done.1, f32[22,16,4,1]{3,2,1,0:T(4,128)S(1)} %copy.88, f32[22,16,4,1]{3,2,1,0:T(4,128)S(1)} %copy.89), kind=kLoop, calls=%fused_computation.228 | loop fusion | flops 1411776 | bytes 1359616 | tf_op jit(solution)/shard_map/sub | solution.py:52
  42.0 1.9 %collective-permute-start.3 = (f32[22,16,1,130]{3,2,1,0:T(1,128)S(1)}, f32[22,16,1,130]{3,2,1,0:T(1,128)S(1)}, u32[]{:S(2)}, u32[]{:S(2)}) collective-permute-start(f32[22,16,1,130]{3,2,1,0:T(1,128)S(1)} %get-tuple-element.44), channel_id=1, source_target_pairs={{1,0},{2,1},{3,2},{5,4},{6,5},{7,6},{9,8},{10,9},{11,10},{13,12},{... | collective-permute-start | bytes 549128 | tf_op jit(solution)/shard_map/ppermute | solution.py:30
  43.9 2.6 %collective-permute-start.2 = (f32[22,16,1,130]{3,2,1,0:T(1,128)S(1)}, f32[22,16,1,130]{3,2,1,0:T(1,128)S(1)}, u32[]{:S(2)}, u32[]{:S(2)}) collective-permute-start(f32[22,16,1,130]{3,2,1,0:T(1,128)S(1)} %get-tuple-element.43), channel_id=1, source_target_pairs={{0,1},{1,2},{2,3},{4,5},{5,6},{6,7},{8,9},{9,10},{10,11},{12,13},{... | collective-permute-start | bytes 549128 | tf_op jit(solution)/shard_map/ppermute | solution.py:28
  46.7 1.8 %multiply_add_fusion.1 = f32[19,16,4,129]{3,2,1,0:T(4,128)S(1)} fusion(f32[16,4,129]{2,1,0:T(4,128)S(1)} %get-tuple-element.68, f32[16,4,129]{2,1,0:T(4,128)S(1)} %get-tuple-element.67, f32[1,16,4,128]{3,2,1,0:T(4,128)S(1)} %compare_convert_fusion, f32[1,16,4,128]{3,2,1,0:T(4,128)S(1)} %bitcast.217, f32[1,16,4,128]{3,2,1,0:T(4,128)S(1)} %bitcast.225, ...), kind=kLoop, calls=%fused_computation.44 | loop fusion | flops 1725504 | bytes 1425664 | tf_op jit(solution)/shard_map/add | solution.py:50
  50.2 2.4 %collective-permute-done.2 = f32[22,16,1,130]{3,2,1,0:T(1,128)S(1)} collective-permute-done((f32[22,16,1,130]{3,2,1,0:T(1,128)S(1)}, f32[22,16,1,130]{3,2,1,0:T(1,128)S(1)}, u32[]{:S(2)}, u32[]{:S(2)}) %collective-permute-start.2) | collective-permute-done | bytes 183072 | tf_op jit(solution)/shard_map/ppermute | solution.py:28
  52.7 2.6 %pad_maximum_fusion = f32[22,16,6,130]{3,2,1,0:T(8,128)S(1)} fusion(f32[22,16,1,130]{3,2,1,0:T(1,128)S(1)} %collective-permute-done.3, f32[22,16,4,1]{3,2,1,0:T(4,128)S(1)} %copy.89, f32[1,16,4,128]{3,2,1,0:T(4,128)S(1)} %compare_convert_fusion, f32[1,16,4,128]{3,2,1,0:T(4,128)S(1)} %bitcast.218, f32[1,16,4,128]{3,2,1,0:T(4,128)S(1)} %bitcast.226, ...), kind=kLoop, calls=%fused_computation | loop fusion | flops 1921920 | bytes 2196480 | tf_op jit(solution)/shard_map/concatenate | solution.py:26
  59.2 1.9 %fusion.4 = f32[19,16,4,128]{3,0,2,1:T(8,128)S(1)} fusion(f32[19,17,4,128]{3,0,2,1:T(8,128)S(1)} %fusion.12, f32[19,16,5,128]{3,0,2,1:T(8,128)S(1)} %fusion.8, f32[19,16,4,129]{3,0,2,1:T(8,128)S(1)} %fusion, f32[19]{0:T(128)S(1)} %copy-done.10, f32[16,4,128]{2,1,0:T(4,128)S(1)} %bitcast.270, f32[19]{0:T(128)S(1)} %copy-done.11, ...), kind=kOutput, calls=%fused_computation.19 | convolution fusion | flops 37666816 | bytes 6697984 | tf_op jit(solution)/shard_map/ij,jzyx->izyx/dot_general | solution.py:118
  61.7 5.0 %all_to_all.48 = f32[16,4,128]{2,0,1:T(8,128)S(1)} all-to-all(f32[16,4,128]{2,0,1:T(8,128)S(1)} %bitcast.265), channel_id=1, replica_groups=mesh['grp'=2,'gx'=4,'gy'=4] {'grp'}, dimensions={1} | all-to-all | bytes 65536 | tf_op jit(solution)/shard_map/all_to_all | solution.py:175
  68.5 5.4 %all-to-all-start.3 = ((f32[5,32,2,128]{3,2,0,1:T(2,128)}), f32[5,32,2,128]{3,2,0,1:T(2,128)S(1)}, u32[]{:S(2)}, u32[]{:S(2)}) async-start(f32[5,32,2,128]{3,2,0,1:T(2,128)} %copy.102), calls=%async_computation.3 | async-start | bytes 327680 | tf_op jit(solution)/shard_map/all_to_all | solution.py:198
  74.6 2.0 %all-to-all-done.3 = f32[5,32,2,128]{3,2,0,1:T(2,128)S(1)} async-done(((f32[5,32,2,128]{3,2,0,1:T(2,128)}), f32[5,32,2,128]{3,2,0,1:T(2,128)S(1)}, u32[]{:S(2)}, u32[]{:S(2)}) %all-to-all-start.3) | async-done | bytes 163872 | tf_op jit(solution)/shard_map/all_to_all | solution.py:198
  77.7 1.5 %collective-permute-start.7 = (f32[22,16,4,1]{0,1,3,2:T(8,128)S(1)}, f32[22,16,4,1]{0,1,3,2:T(8,128)S(1)}, u32[]{:S(2)}, u32[]{:S(2)}) collective-permute-start(f32[22,16,4,1]{0,1,3,2:T(8,128)S(1)} %copy.106), channel_id=1, source_target_pairs={{4,0},{8,4},{12,8},{5,1},{9,5},{13,9},{6,2},{10,6},{14,10},{7,3},{... | collective-permute-start | bytes 16904 | tf_op jit(solution)/shard_map/ppermute | solution.py:30
  79.7 4.5 %collective-permute-start.6 = (f32[22,16,4,1]{0,1,3,2:T(8,128)S(1)}, f32[22,16,4,1]{0,1,3,2:T(8,128)S(1)}, u32[]{:S(2)}, u32[]{:S(2)}) collective-permute-start(f32[22,16,4,1]{0,1,3,2:T(8,128)S(1)} %copy.105), channel_id=1, source_target_pairs={{0,4},{4,8},{8,12},{1,5},{5,9},{9,13},{2,6},{6,10},{10,14},{3,7},{... | collective-permute-start | bytes 16904 | tf_op jit(solution)/shard_map/ppermute | solution.py:28
  85.5 4.5 %collective-permute-start.11 = (f32[20,1,4,128]{3,0,2,1:T(8,128)S(1)}, f32[20,1,4,128]{3,0,2,1:T(8,128)S(1)}, u32[]{:S(2)}, u32[]{:S(2)}) collective-permute-start(f32[20,1,4,128]{3,0,2,1:T(8,128)S(1)} %get-tuple-element.45), channel_id=1, source_target_pairs={{16,0},{17,1},{18,2},{19,3},{20,4},{21,5},{22,6},{23,7},{24,8},{25... | collective-permute-start | bytes 122888 | tf_op jit(solution)/shard_map/ppermute | solution.py:30
  93.0 1.9 %collective-permute-start.9 = (f32[22,16,1,130]{3,0,2,1:T(8,128)S(1)}, f32[22,16,1,130]{3,0,2,1:T(8,128)S(1)}, u32[]{:S(2)}, u32[]{:S(2)}) collective-permute-start(f32[22,16,1,130]{3,0,2,1:T(8,128)S(1)} %get-tuple-element.38), channel_id=1, source_target_pairs={{1,0},{2,1},{3,2},{5,4},{6,5},{7,6},{9,8},{10,9},{11,10},{13,12},{... | collective-permute-start | bytes 549128 | tf_op jit(solution)/shard_map/ppermute | solution.py:30
  94.9 2.4 %collective-permute-start.8 = (f32[22,16,1,130]{3,0,2,1:T(8,128)S(1)}, f32[22,16,1,130]{3,0,2,1:T(8,128)S(1)}, u32[]{:S(2)}, u32[]{:S(2)}) collective-permute-start(f32[22,16,1,130]{3,0,2,1:T(8,128)S(1)} %get-tuple-element.37), channel_id=1, source_target_pairs={{0,1},{1,2},{2,3},{4,5},{5,6},{6,7},{8,9},{9,10},{10,11},{12,13},{... | collective-permute-start | bytes 549128 | tf_op jit(solution)/shard_map/ppermute | solution.py:28
  100.2 3.8 %collective-permute-done.8 = f32[22,16,1,130]{3,0,2,1:T(8,128)S(1)} collective-permute-done((f32[22,16,1,130]{3,0,2,1:T(8,128)S(1)}, f32[22,16,1,130]{3,0,2,1:T(8,128)S(1)}, u32[]{:S(2)}, u32[]{:S(2)}) %collective-permute-start.8) | collective-permute-done | bytes 183072 | tf_op jit(solution)/shard_map/ppermute | solution.py:28
  (121 shorter events, 32.3 us)
Async XLA Ops:
  0.6 58.5 %copy-start = (f32[19,19]{1,0:T(8,128)S(1)}, f32[19,19]{1,0:T(8,128)}, u32[]{:S(2)}) copy-start(f32[19,19]{1,0:T(8,128)} %param.20) | copy-start | bytes 4336
  0.6 8.7 %copy-start.2 = (f32[32,1,2,128]{3,2,1,0:T(2,128)S(1)}, f32[32,1,2,128]{3,2,1,0:T(2,128)}, u32[]{:S(2)}) copy-start(f32[32,1,2,128]{3,2,1,0:T(2,128)} %param.15) | copy-start | bytes 98308
  0.7 8.7 %copy-start.6 = (f32[32,1,2,128]{3,2,1,0:T(2,128)S(1)}, f32[32,1,2,128]{3,2,1,0:T(2,128)}, u32[]{:S(2)}) copy-start(f32[32,1,2,128]{3,2,1,0:T(2,128)} %param.14) | copy-start | bytes 98308
  0.7 8.8 %copy-start.3 = (f32[32,1,2,128]{3,2,1,0:T(2,128)S(1)}, f32[32,1,2,128]{3,2,1,0:T(2,128)}, u32[]{:S(2)}) copy-start(f32[32,1,2,128]{3,2,1,0:T(2,128)} %param.16) | copy-start | bytes 98308
  0.7 8.9 %copy-start.5 = (f32[32,1,2,128]{3,2,1,0:T(2,128)S(1)}, f32[32,1,2,128]{3,2,1,0:T(2,128)}, u32[]{:S(2)}) copy-start(f32[32,1,2,128]{3,2,1,0:T(2,128)} %param.13) | copy-start | bytes 98308
  0.7 8.9 %copy-start.4 = (f32[32,1,2,128]{3,2,1,0:T(2,128)S(1)}, f32[32,1,2,128]{3,2,1,0:T(2,128)}, u32[]{:S(2)}) copy-start(f32[32,1,2,128]{3,2,1,0:T(2,128)} %param.12) | copy-start | bytes 98308
  2.7 13.0 %copy-start.8 = (s32[4,128]{1,0:T(4,128)S(1)}, s32[4,128]{1,0:T(4,128)}, u32[]{:S(2)}) copy-start(s32[4,128]{1,0:T(4,128)} %param.18) | copy-start | bytes 6148
  2.7 13.7 %copy-start.1 = (f32[19,16,4,128]{3,2,1,0:T(4,128)S(1)}, f32[19,16,4,128]{3,2,1,0:T(4,128)}, u32[]{:S(2)}) copy-start(f32[19,16,4,128]{3,2,1,0:T(4,128)} %param.17) | copy-start | bytes 1867780
  3.3 6.0 %all-to-all-start = ((f32[16,4,128]{2,0,1:T(8,128)}), f32[16,4,128]{2,0,1:T(8,128)S(1)}, u32[]{:S(2)}, u32[]{:S(2)}) async-start(f32[16,4,128]{2,0,1:T(8,128)} %bitcast.204), calls=%async_computation | async-start | bytes 65536 | tf_op jit(solution)/shard_map/all_to_all | solution.py:175
  10.5 7.8 %all-to-all-start.1 = ((f32[5,32,2,128]{3,2,0,1:T(2,128)}), f32[5,32,2,128]{3,2,0,1:T(2,128)S(1)}, u32[]{:S(2)}, u32[]{:S(2)}) async-start(f32[5,32,2,128]{3,2,0,1:T(2,128)} %copy.84), calls=%async_computation.1 | async-start | bytes 327680 | tf_op jit(solution)/shard_map/all_to_all | solution.py:198
  19.7 12.9 %collective-permute-start.1 = (f32[22,16,4,1]{0,1,3,2:T(8,128)S(1)}, f32[22,16,4,1]{0,1,3,2:T(8,128)S(1)}, u32[]{:S(2)}, u32[]{:S(2)}) collective-permute-start(f32[22,16,4,1]{0,1,3,2:T(8,128)S(1)} %copy.87), channel_id=1, source_target_pairs={{4,0},{8,4},{12,8},{5,1},{9,5},{13,9},{6,2},{10,6},{14,10},{7,3},{... | collective-permute-start | bytes 16904 | tf_op jit(solution)/shard_map/ppermute | solution.py:30
  21.6 11.9 %collective-permute-start = (f32[22,16,4,1]{0,1,3,2:T(8,128)S(1)}, f32[22,16,4,1]{0,1,3,2:T(8,128)}, u32[]{:S(2)}, u32[]{:S(2)}) collective-permute-start(f32[22,16,4,1]{0,1,3,2:T(8,128)S(1)} %copy.86), channel_id=1, source_target_pairs={{0,4},{4,8},{8,12},{1,5},{5,9},{9,13},{2,6},{6,10},{10,14},{3,7},{... | collective-permute-start | bytes 16904 | tf_op jit(solution)/shard_map/ppermute | solution.py:28
  26.7 23.2 %collective-permute-start.4 = (f32[20,1,4,128]{3,0,2,1:T(8,128)S(1)}, f32[20,1,4,128]{3,0,2,1:T(8,128)S(1)}, u32[]{:S(2)}, u32[]{:S(2)}) collective-permute-start(f32[20,1,4,128]{3,0,2,1:T(8,128)S(1)} %get-tuple-element.48), channel_id=1, source_target_pairs={{0,16},{1,17},{2,18},{3,19},{4,20},{5,21},{6,22},{7,23},{8,24},{9,... | collective-permute-start | bytes 122888 | tf_op jit(solution)/shard_map/ppermute | solution.py:28
  28.0 22.0 %collective-permute-start.5 = (f32[20,1,4,128]{3,0,2,1:T(8,128)S(1)}, f32[20,1,4,128]{3,0,2,1:T(8,128)S(1)}, u32[]{:S(2)}, u32[]{:S(2)}) collective-permute-start(f32[20,1,4,128]{3,0,2,1:T(8,128)S(1)} %get-tuple-element.47), channel_id=1, source_target_pairs={{16,0},{17,1},{18,2},{19,3},{20,4},{21,5},{22,6},{23,7},{24,8},{25... | collective-permute-start | bytes 122888 | tf_op jit(solution)/shard_map/ppermute | solution.py:30
  42.0 8.2 %collective-permute-start.3 = (f32[22,16,1,130]{3,2,1,0:T(1,128)S(1)}, f32[22,16,1,130]{3,2,1,0:T(1,128)S(1)}, u32[]{:S(2)}, u32[]{:S(2)}) collective-permute-start(f32[22,16,1,130]{3,2,1,0:T(1,128)S(1)} %get-tuple-element.44), channel_id=1, source_target_pairs={{1,0},{2,1},{3,2},{5,4},{6,5},{7,6},{9,8},{10,9},{11,10},{13,12},{... | collective-permute-start | bytes 549128 | tf_op jit(solution)/shard_map/ppermute | solution.py:30
  43.9 8.7 %collective-permute-start.2 = (f32[22,16,1,130]{3,2,1,0:T(1,128)S(1)}, f32[22,16,1,130]{3,2,1,0:T(1,128)S(1)}, u32[]{:S(2)}, u32[]{:S(2)}) collective-permute-start(f32[22,16,1,130]{3,2,1,0:T(1,128)S(1)} %get-tuple-element.43), channel_id=1, source_target_pairs={{0,1},{1,2},{2,3},{4,5},{5,6},{6,7},{8,9},{9,10},{10,11},{12,13},{... | collective-permute-start | bytes 549128 | tf_op jit(solution)/shard_map/ppermute | solution.py:28
  59.2 1.9 %copy-start.9 = (f32[19]{0:T(128)S(1)}, f32[19]{0:T(128)}, u32[]{:S(2)}) copy-start(f32[19]{0:T(128)} %param.23) | copy-start | bytes 232
  68.5 8.1 %all-to-all-start.3 = ((f32[5,32,2,128]{3,2,0,1:T(2,128)}), f32[5,32,2,128]{3,2,0,1:T(2,128)S(1)}, u32[]{:S(2)}, u32[]{:S(2)}) async-start(f32[5,32,2,128]{3,2,0,1:T(2,128)} %copy.102), calls=%async_computation.3 | async-start | bytes 327680 | tf_op jit(solution)/shard_map/all_to_all | solution.py:198
  77.7 12.4 %collective-permute-start.7 = (f32[22,16,4,1]{0,1,3,2:T(8,128)S(1)}, f32[22,16,4,1]{0,1,3,2:T(8,128)S(1)}, u32[]{:S(2)}, u32[]{:S(2)}) collective-permute-start(f32[22,16,4,1]{0,1,3,2:T(8,128)S(1)} %copy.106), channel_id=1, source_target_pairs={{4,0},{8,4},{12,8},{5,1},{9,5},{13,9},{6,2},{10,6},{14,10},{7,3},{... | collective-permute-start | bytes 16904 | tf_op jit(solution)/shard_map/ppermute | solution.py:30
  79.7 10.9 %collective-permute-start.6 = (f32[22,16,4,1]{0,1,3,2:T(8,128)S(1)}, f32[22,16,4,1]{0,1,3,2:T(8,128)S(1)}, u32[]{:S(2)}, u32[]{:S(2)}) collective-permute-start(f32[22,16,4,1]{0,1,3,2:T(8,128)S(1)} %copy.105), channel_id=1, source_target_pairs={{0,4},{4,8},{8,12},{1,5},{5,9},{9,13},{2,6},{6,10},{10,14},{3,7},{... | collective-permute-start | bytes 16904 | tf_op jit(solution)/shard_map/ppermute | solution.py:28
  84.2 14.5 %collective-permute-start.10 = (f32[20,1,4,128]{3,0,2,1:T(8,128)S(1)}, f32[20,1,4,128]{3,0,2,1:T(8,128)S(1)}, u32[]{:S(2)}, u32[]{:S(2)}) collective-permute-start(f32[20,1,4,128]{3,0,2,1:T(8,128)S(1)} %get-tuple-element.46), channel_id=1, source_target_pairs={{0,16},{1,17},{2,18},{3,19},{4,20},{5,21},{6,22},{7,23},{8,24},{9,... | collective-permute-start | bytes 122888 | tf_op jit(solution)/shard_map/ppermute | solution.py:28
  85.5 13.3 %collective-permute-start.11 = (f32[20,1,4,128]{3,0,2,1:T(8,128)S(1)}, f32[20,1,4,128]{3,0,2,1:T(8,128)S(1)}, u32[]{:S(2)}, u32[]{:S(2)}) collective-permute-start(f32[20,1,4,128]{3,0,2,1:T(8,128)S(1)} %get-tuple-element.45), channel_id=1, source_target_pairs={{16,0},{17,1},{18,2},{19,3},{20,4},{21,5},{22,6},{23,7},{24,8},{25... | collective-permute-start | bytes 122888 | tf_op jit(solution)/shard_map/ppermute | solution.py:30
  93.0 7.2 %collective-permute-start.9 = (f32[22,16,1,130]{3,0,2,1:T(8,128)S(1)}, f32[22,16,1,130]{3,0,2,1:T(8,128)S(1)}, u32[]{:S(2)}, u32[]{:S(2)}) collective-permute-start(f32[22,16,1,130]{3,0,2,1:T(8,128)S(1)} %get-tuple-element.38), channel_id=1, source_target_pairs={{1,0},{2,1},{3,2},{5,4},{6,5},{7,6},{9,8},{10,9},{11,10},{13,12},{... | collective-permute-start | bytes 549128 | tf_op jit(solution)/shard_map/ppermute | solution.py:30
  94.9 9.1 %collective-permute-start.8 = (f32[22,16,1,130]{3,0,2,1:T(8,128)S(1)}, f32[22,16,1,130]{3,0,2,1:T(8,128)S(1)}, u32[]{:S(2)}, u32[]{:S(2)}) collective-permute-start(f32[22,16,1,130]{3,0,2,1:T(8,128)S(1)} %get-tuple-element.37), channel_id=1, source_target_pairs={{0,1},{1,2},{2,3},{4,5},{5,6},{6,7},{8,9},{9,10},{10,11},{12,13},{... | collective-permute-start | bytes 549128 | tf_op jit(solution)/shard_map/ppermute | solution.py:28
  (3 other events, 3.0 us)
where the time goes:
time: 109 us
  starting transfers between devices  47.4 us (43%)
  other arithmetic  26 us (24%)
  local copies, waits for them, and re-layouts  11.9 us (11%)
  waiting for transfers between devices  11 us (10%)
  matrix products  5.79 us (5%)
  blocking collectives  5.01 us (5%)
  between operations  1.39 us (1%)
    ppermute x6, starting transfers between devices, with_halo(): lax.ppermute(tail, axis, [(i, (i + 1) % count) for i in range(ends)])  17.3 us
    ppermute x6, starting transfers between devices, with_halo(): lax.ppermute(head, axis, [((i + 1) % count, i) for i in range(ends)])  15.7 us
    all_to_all x2, starting transfers between devices, per_device(): lax.all_to_all(stacked, 'grp', split_axis=1, concat_axis=2, tiled=True)  10.6 us
    ppermute x6, waiting for transfers between devices, with_halo(): lax.ppermute(tail, axis, [(i, (i + 1) % count) for i in range(ends)])  6.28 us
    slice x2, other arithmetic, with_halo(): lax.slice_in_dim(cells, cells.shape[dim] - width, cells.shape[dim], axis=...  5.46 us
    all_to_all x1, blocking collectives, per_device(): lax.all_to_all(pigment_band, 'grp', split_axis=1, concat_axis=0, tiled=True)  5.01 us
    mul x4, other arithmetic, face_divergence(): opening * (jnp.maximum(face_speed, 0.0) * lower_conc + jnp.minimum(face_s...  4.39 us
    all_to_all x1, starting transfers between devices, per_device(): lax.all_to_all(pigment_band, 'grp', split_axis=1, concat_axis=0, tiled=True)  3.78 us
  transfers between devices with their start and end apart: 15, of which 5 were waited for; matrix products, arithmetic and copies ran while one was open for 21% of the time, Pallas kernels for 0%

commit v1 on v0

v1 whole, which is shorter than its diff:
```python
import functools

import jax
import jax.numpy as jnp
from jax import lax
from jax.experimental import pallas as pl
from jax.experimental.pallas import tpu as pltpu
from jax.sharding import PartitionSpec as P

STEPS = 2

WATER_ATTEN = 0.01
PIGMENT_ATTEN = 0.05
WARMING_UPTAKE = 5.0
WARM_EXPANSION = 0.2
SALT_EXPANSION = 0.8
CONVECT_MIX = 0.15
SIDE_DIFFUSE = 0.05
WARMING_FACTOR = 0.0633
TIME_STEP = 0.5

SUB = 8
AXES = ("grp", "gx", "gy")
VMEM_LIMIT = 48 * 1024 * 1024

F32 = jnp.float32


def vmem():
    return pl.BlockSpec(memory_space=pltpu.VMEM)


def smem():
    return pl.BlockSpec(memory_space=pltpu.SMEM)


def shape(*dims):
    return jax.ShapeDtypeStruct(dims, F32)


def turn(x, shift, axis):
    shift = shift % x.shape[axis]
    return x if shift == 0 else pltpu.roll(x, shift, axis)


def iota(x, axis):
    return lax.broadcasted_iota(jnp.int32, x, axis)


def pairing(sizes, axis, odd):
    size_g, size_x, size_y = sizes

    def partner(g, x, y):
        i, n = (x, size_x) if axis == "gx" else (y, size_y)
        j = i + 1 if i % 2 == odd else i - 1
        if 0 <= j < n:
            return (g, j, y) if axis == "gx" else (g, x, j)
        if axis == "gx":
            return (g, x, y ^ 1) if (y ^ 1) < size_y else (g, x, y)
        return (g ^ 1, x, y) if (g ^ 1) < size_g else (g, x, y)

    def index(g, x, y):
        return (g * size_x + x) * size_y + y

    return [
        (index(g, x, y), index(*partner(g, x, y)))
        for g in range(size_g)
        for x in range(size_x)
        for y in range(size_y)
    ]


def from_others(value, count):
    return [
        lax.ppermute(value, "grp", [(i, (i + k) % count) for i in range(count)])
        for k in range(1, count)
    ]


def pick(mine, others, k):
    value = mine
    for at, other in enumerate(others):
        value = jnp.where(k == at + 1, other, value)
    return value


def pack_sides(c, t, left, right):
    lane = iota(c.shape, 1)
    left = jnp.where(lane == t, turn(c, t, 1), left)
    right = jnp.where(lane == t, turn(c, t + 1, 1), right)
    return left, right


def write_levels(c, t, lev_refs, g):
    if len(lev_refs) == 1:
        lev_refs[0][t] = jnp.where(g == 0, c[-SUB:], c[:SUB])
    else:
        lev_refs[0][t] = c[-SUB:]
        lev_refs[1][t] = c[:SUB]


def prep_kernel(rows, count, pig_ref, c_ref, p_ref, left_ref, right_ref, first_ref, last_ref, *lev_refs):
    g = lax.axis_index("grp")
    tracers, cells, _ = c_ref.shape
    levels = cells // rows
    pigment = left = right = jnp.zeros(c_ref.shape[1:], F32)
    for t in range(tracers):
        c = c_ref[t]
        pigment = pigment + pig_ref[t] * c
        left, right = pack_sides(c, t, left, right)
        first_ref[t] = c_ref[t, pl.ds(0, levels, stride=rows), :]
        last_ref[t] = c_ref[t, pl.ds(rows - 1, levels, stride=rows), :]
        write_levels(c, t, lev_refs, g)
    p_ref[...] = pigment
    left_ref[...] = left
    right_ref[...] = right


def ocean_kernel(rows, count, tracers, first_step, last_step, *refs):
    refs = list(refs)

    def take(n):
        out = refs[:n]
        del refs[:n]
        return out

    depth_ref, solar_ref, left_in, right_in, first_in, last_in, p_own = take(7)
    p_others = take(count - 1)
    if first_step:
        own_fields = take(5)
        other_fields = [take(5) for _ in range(count - 1)]
    else:
        full_in = take(5)
    band_ref, msg_xa, msg_xb, msg_ya, msg_yb = take(5)
    final_out = take(4) if last_step else []
    full_out = [] if last_step else take(5)
    (p_full, depth_s, solar_s, *scratch) = take(3 + 12)
    g = lax.axis_index("grp")
    x = lax.axis_index("gx")
    y = lax.axis_index("gy")
    cells, width = p_own.shape
    levels = cells // rows
    total = count * cells
    all_levels = total // rows
    strip = rows // count

    for b in range(count):
        k = lax.rem(g - b + count, count)
        p_full[pl.ds(b * cells, cells), :] = pick(p_own[...], [o[...] for o in p_others], k)
    fields = scratch[:5]
    if first_step:
        for at in range(5):
            for s in range(count):
                k = lax.rem(g - s + count, count)
                for r in range(strip):
                    here = pl.ds(r, all_levels, stride=strip)
                    fields[at][pl.ds(s * strip + r, all_levels, stride=rows), :] = pick(
                        own_fields[at][here, :], [o[at][here, :] for o in other_fields], k
                    )
    else:
        fields = full_in
    for r in range(0, SUB, rows):
        depth_s[pl.ds(r, rows), :] = depth_ref[...]
        solar_s[pl.ds(r, rows), :] = solar_ref[...]

    def spread(ref):
        v = ref[...]
        return jnp.broadcast_to(v[None], (total // SUB, SUB, width)).reshape(total, width)

    row = iota((total, width), 0)
    wet = jnp.where(row // rows < spread(depth_s), 1.0, 0.0)
    att = WATER_ATTEN + PIGMENT_ATTEN * p_full[...]
    summed = att
    step = rows
    while step < total:
        summed = summed + jnp.where(row >= step, turn(summed, step, 0), 0.0)
        step *= 2
    top = spread(solar_s) * jnp.exp(att - summed)
    par = top * jnp.exp(-0.5 * att)
    east, north, temp, sal, mixing = [f[...] for f in fields]
    temp = temp + WARMING_UPTAKE * (top * (1.0 - jnp.exp(-att))) * wet

    def below(v):
        return turn(v, -rows, 0)

    density = SALT_EXPANSION * sal - WARM_EXPANSION * temp
    face = 0.5 * (mixing + below(mixing)) + CONVECT_MIX / (1.0 + jnp.exp(below(density) - density))
    face = jnp.where(row < total - rows, face * below(wet), 0.0)

    def stir(v):
        flux = face * (below(v) - v)
        return v + flux - turn(flux, rows, 0)

    out = [stir(v) for v in (east, north, temp, sal)]
    for at, v in enumerate(out):
        if last_step:
            scratch[5 + at][...] = v
        else:
            full_out[at][...] = v
    if not last_step:
        full_out[4][...] = mixing
    stored = scratch[5:9] if last_step else full_out
    scratch[9][...] = face
    scratch[10][...] = par
    scratch[11][...] = wet

    if last_step:
        for at in range(4):
            for r in range(strip):
                value = stored[at][pl.ds(r, all_levels, stride=rows), :]
                for s in range(1, count):
                    value = jnp.where(
                        g == s, stored[at][pl.ds(s * strip + r, all_levels, stride=rows), :], value
                    )
                final_out[at][pl.ds(r, all_levels, stride=strip), :] = value

    band = pl.ds(pl.multiple_of(g * cells, SUB), cells)
    above = pl.ds(pl.multiple_of(lax.max(g * cells - SUB, 0), SUB), SUB)
    face_band = scratch[9][band, :]
    lifted = jnp.concatenate([scratch[9][above, :], face_band], axis=0)
    lifted = turn(lifted, rows, 0)[SUB:]
    lifted = jnp.where((iota((cells, width), 0) < rows) & (g == 0), 0.0, lifted)
    u = stored[0][band, :]
    wet_band = scratch[11][band, :]
    band_ref[0] = u
    band_ref[1] = stored[1][band, :]
    band_ref[2] = stored[2][band, :]
    band_ref[3] = face_band
    band_ref[4] = lifted
    band_ref[5] = scratch[10][band, :]
    band_ref[6] = wet_band

    left, right = pack_sides(wet_band, tracers + 1, left_in[...], right_in[...])
    _, right = pack_sides(u, tracers, left, right)
    even = lax.rem(x, 2) == 0
    msg_xa[...] = jnp.where(even, right, left)
    msg_xb[...] = jnp.where(even, left, right)
    even = lax.rem(y, 2) == 0
    for t in range(tracers):
        msg_ya[t] = jnp.where(even, last_in[t], first_in[t])
        msg_yb[t] = jnp.where(even, first_in[t], last_in[t])
    speed = band_ref[1, pl.ds(rows - 1, levels, stride=rows), :]
    wet_first = band_ref[6, pl.ds(0, levels, stride=rows), :]
    wet_last = band_ref[6, pl.ds(rows - 1, levels, stride=rows), :]
    msg_ya[tracers] = speed
    msg_yb[tracers] = speed
    msg_ya[tracers + 1] = jnp.where(even, wet_last, wet_first)
    msg_yb[tracers + 1] = jnp.where(even, wet_first, wet_last)


def tracer_kernel(rows, count, sizes, last_step, *refs):
    refs = list(refs)

    def take(n):
        out = refs[:n]
        del refs[:n]
        return out

    photo_ref, sat_ref, pig_ref, rates_ref, c_ref, band_ref = take(6)
    got_xa, got_xb, got_ya, got_yb = take(4)
    lev_in = take(1 if count == 2 else 2)
    (out_ref,) = take(1)
    if not last_step:
        p_ref, left_ref, right_ref, first_ref, last_ref = take(5)
        lev_out = take(1 if count == 2 else 2)
    south_s, north_s, mix_s = take(3)
    _, size_x, size_y = sizes
    g = lax.axis_index("grp")
    x = lax.axis_index("gx")
    y = lax.axis_index("gy")
    tracers, cells, width = c_ref.shape
    levels = cells // rows
    blocks = cells // SUB
    lane = iota((cells, width), 1)
    row = iota((cells, width), 0)
    at_row = lax.rem(row, rows)

    depth = tracers * SUB
    spread = jnp.where(iota((depth, tracers), 0) // SUB == iota((depth, tracers), 1), 1.0, 0.0)
    spread_t = jnp.where(iota((tracers, depth), 1) // SUB == iota((tracers, depth), 0), 1.0, 0.0)
    dot = functools.partial(jnp.dot, preferred_element_type=F32)
    exact = functools.partial(dot, precision=lax.Precision.HIGHEST)
    weights = exact(exact(spread, rates_ref[...]), spread_t)
    weights = jnp.where(
        lax.rem(iota((depth, depth), 0), SUB) == lax.rem(iota((depth, depth), 1), SUB), weights, 0.0
    )

    def halves(v):
        high = v.astype(jnp.bfloat16)
        return high, (v - high.astype(F32)).astype(jnp.bfloat16)

    w_high, w_low = halves(weights)
    for b in range(blocks):
        cut = c_ref[:, pl.ds(b * SUB, SUB), :].reshape(depth, width)
        c_high, c_low = halves(cut)
        mixed = dot(w_high, c_high) + (dot(w_high, c_low) + dot(w_low, c_high))
        mix_s[:, pl.ds(b * SUB, SUB), :] = mixed.reshape(tracers, SUB, width)

    even = lax.rem(x, 2) == 0
    west = jnp.where(even, got_xb[...], got_xa[...])
    east = jnp.where(even, got_xa[...], got_xb[...])
    even = lax.rem(y, 2) == 0
    for t in range(tracers + 2):
        south_s[t, pl.ds(0, levels, stride=rows), :] = jnp.where(even, got_yb[t], got_ya[t])
        north_s[t, pl.ds(rows - 1, levels, stride=rows), :] = jnp.where(even, got_ya[t], got_yb[t])

    def from_west(v, slot):
        return jnp.where(lane == 0, turn(west, -slot, 1), turn(v, 1, 1))

    def from_east(v, slot):
        return jnp.where(lane == width - 1, turn(east, -1 - slot, 1), turn(v, -1, 1))

    def from_south(v, slot):
        return jnp.where(at_row == 0, south_s[slot], turn(v, 1, 0))

    def from_north(v, slot):
        return jnp.where(at_row == rows - 1, north_s[slot], turn(v, -1, 0))

    u = band_ref[0]
    v = band_ref[1]
    wet = band_ref[6]
    open_w = wet * jnp.where((lane == 0) & (x == 0), 0.0, from_west(wet, tracers + 1))
    open_e = wet * jnp.where((lane == width - 1) & (x == size_x - 1), 0.0, from_east(wet, tracers + 1))
    open_s = wet * jnp.where((at_row == 0) & (y == 0), 0.0, from_south(wet, tracers + 1))
    open_n = wet * jnp.where((at_row == rows - 1) & (y == size_y - 1), 0.0, from_north(wet, tracers + 1))

    def lower(opening, speed):
        return opening * (jnp.maximum(speed, 0.0) + SIDE_DIFFUSE)

    def upper(opening, speed):
        return opening * (jnp.minimum(speed, 0.0) - SIDE_DIFFUSE)

    u_w = from_west(u, tracers)
    v_s = from_south(v, tracers)
    k_w = lower(open_w, u_w)
    k_e = -upper(open_e, u)
    k_s = lower(open_s, v_s)
    k_n = -upper(open_n, v)
    k_d = band_ref[3]
    k_u = band_ref[4]
    k_c = 1.0 - lower(open_e, u) + upper(open_w, u_w) - lower(open_n, v) + upper(open_s, v_s) - k_d - k_u
    par = band_ref[5]
    warm = TIME_STEP * wet * jnp.exp(WARMING_FACTOR * (band_ref[2] - 20.0))
    lit = TIME_STEP * wet * par

    if not last_step:
        pigment = left = right = jnp.zeros((cells, width), F32)
    for t in range(tracers):
        c = c_ref[t]
        up8, down8 = lev_in[0][t], lev_in[-1][t]
        c_u = turn(jnp.concatenate([up8, c], axis=0), rows, 0)[SUB:]
        c_d = turn(jnp.concatenate([c, down8], axis=0), -rows, 0)[:cells]
        new = (
            (k_c + photo_ref[t] * (lit / (par + sat_ref[t]))) * c
            + k_w * from_west(c, t)
            + k_e * from_east(c, t)
            + k_s * from_south(c, t)
            + k_n * from_north(c, t)
            + k_u * c_u
            + k_d * c_d
            + warm * mix_s[t]
        )
        out_ref[t] = new
        if not last_step:
            pigment = pigment + pig_ref[t] * new
            left, right = pack_sides(new, t, left, right)
            first_ref[t] = out_ref[t, pl.ds(0, levels, stride=rows), :]
            last_ref[t] = out_ref[t, pl.ds(rows - 1, levels, stride=rows), :]
            write_levels(new, t, lev_out, g)
    if not last_step:
        p_ref[...] = pigment
        left_ref[...] = left
        right_ref[...] = right


def call(kernel, ins, in_specs, outs, scratch=(), flops=0):
    return pl.pallas_call(
        kernel,
        in_specs=in_specs,
        out_specs=[vmem() for _ in outs],
        out_shape=outs,
        scratch_shapes=list(scratch),
        compiler_params=pltpu.CompilerParams(vmem_limit_bytes=VMEM_LIMIT),
        cost_estimate=pl.CostEstimate(flops=flops, bytes_accessed=1 << 20, transcendentals=0),
    )(*ins)


def per_device(
    sizes,
    zonal_boundary_speed,
    meridional_boundary_speed,
    potential_warmth,
    saltiness_field,
    quiescent_mixing_profile,
    substance_amounts,
    submerged_layer_number,
    solar_radiation,
    interaction_rates,
    photosynthetic_rates,
    saturation_irradiance,
    pigment_per_tracer,
):
    count = sizes[0]
    result_dimensions = zonal_boundary_speed.shape
    all_levels, _, strip, width = result_dimensions
    tracers, levels, rows, _ = substance_amounts.shape
    cells = levels * rows
    total = all_levels * rows
    lev_n = 1 if count == 2 else 2

    own = [
        f.reshape(all_levels * strip, width)
        for f in (
            zonal_boundary_speed,
            meridional_boundary_speed,
            potential_warmth,
            saltiness_field,
            quiescent_mixing_profile,
        )
    ]
    c = substance_amounts.reshape(tracers, cells, width)
    others = [from_others(f, count) for f in own]

    packs = [
        shape(cells, width),
        shape(cells, width),
        shape(cells, width),
        shape(tracers, levels, width),
        shape(tracers, levels, width),
    ] + [shape(tracers, SUB, width)] * lev_n
    prepared = call(
        functools.partial(prep_kernel, rows, count),
        (pigment_per_tracer, c),
        [smem(), vmem()],
        packs,
        flops=1 << 20,
    )
    full = None
    for step in range(STEPS):
        first_step, last_step = step == 0, step == STEPS - 1
        pigment, left, right, first, last, *lev = prepared
        p_others = from_others(pigment, count)
        if count == 2:
            lev = from_others(lev[0], count)
        else:
            lev = [
                lax.ppermute(lev[0], "grp", [(i, (i + 1) % count) for i in range(count)]),
                lax.ppermute(lev[1], "grp", [((i + 1) % count, i) for i in range(count)]),
            ]
        if first_step:
            fields = own + [others[at][k] for k in range(count - 1) for at in range(5)]
        else:
            fields = full
        ins = [submerged_layer_number, solar_radiation, left, right, first, last, pigment, *p_others, *fields]
        msg_rows = shape(tracers + 2, levels, width)
        msg_cols = shape(cells, width)
        outs = [shape(7, cells, width), msg_cols, msg_cols, msg_rows, msg_rows]
        if last_step:
            outs += [shape(all_levels * strip, width)] * 4
        else:
            outs += [shape(total, width)] * 5
        column = pltpu.VMEM((total, width), F32)
        band, xa, xb, ya, yb, *full = call(
            functools.partial(ocean_kernel, rows, count, tracers, first_step, last_step),
            ins,
            [vmem() for _ in ins],
            outs,
            [column, pltpu.VMEM((SUB, width), jnp.int32), pltpu.VMEM((SUB, width), F32)] + [column] * 12,
            flops=1 << 20,
        )
        xa = lax.ppermute(xa, AXES, pairing(sizes, "gx", 0))
        xb = lax.ppermute(xb, AXES, pairing(sizes, "gx", 1))
        ya = lax.ppermute(ya, AXES, pairing(sizes, "gy", 0))
        yb = lax.ppermute(yb, AXES, pairing(sizes, "gy", 1))
        ins = [
            photosynthetic_rates,
            saturation_irradiance,
            pigment_per_tracer,
            interaction_rates,
            c,
            band,
            xa,
            xb,
            ya,
            yb,
            *lev,
        ]
        c, *prepared = call(
            functools.partial(tracer_kernel, rows, count, sizes, last_step),
            ins,
            [smem(), smem(), smem()] + [vmem() for _ in ins[3:]],
            [shape(tracers, cells, width)] + ([] if last_step else packs),
            [pltpu.VMEM((tracers + 2, cells, width), F32)] * 2 + [pltpu.VMEM((tracers, cells, width), F32)],
            flops=1 << 22,
        )
    return tuple(f.reshape(result_dimensions) for f in full) + (c.reshape(substance_amounts.shape),)


def solution(mesh):
    ocean = P(None, "gy", "grp", "gx")
    tracer = P(None, "grp", "gy", "gx")
    surface = P("gy", "gx")
    sizes = tuple(mesh.shape[a] for a in AXES)
    return jax.shard_map(
        functools.partial(per_device, sizes),
        mesh=mesh,
        in_specs=(ocean,) * 5 + (tracer, surface, surface) + (P(),) * 4,
        out_specs=(ocean,) * 4 + (tracer,),
        check_vma=False,
    )
```

time: 109 us -> 42.9 us (0.39)
  the two profiles are of different devices: /device:TPU:6 before, /device:TPU:0 now
where the time goes in v1:
time: 42.9 us; the launch traced here: 42.4 us
  starting transfers between devices  15.9 us (37%)
  waiting for transfers between devices  13 us (30%)
  Pallas kernels  7.28 us (17%)
  local copies, waits for them, and re-layouts  5.58 us (13%)
  between operations  0.73 us (2%)
    ppermute x9, starting transfers between devices, from_others(): lax.ppermute(value, 'grp', [(i, (i + k) % count) for i in range(count)])  11.2 us
    ppermute x9, waiting for transfers between devices, from_others(): lax.ppermute(value, 'grp', [(i, (i + k) % count) for i in range(count)])  8.3 us
    pallas_call x5, Pallas kernels, call(): pl.pallas_call(kernel, in_specs=in_specs, out_specs=[vmem() for _ in outs...  7.28 us
    unnamed x26, local copies, waits for them, and re-layouts  5.58 us
    ppermute x2, waiting for transfers between devices, per_device(): xa = lax.ppermute(xa, AXES, pairing(sizes, 'gx', 0))  4.65 us
    ppermute x2, starting transfers between devices, per_device(): xa = lax.ppermute(xa, AXES, pairing(sizes, 'gx', 0))  3.17 us
    ppermute x2, starting transfers between devices, per_device(): yb = lax.ppermute(yb, AXES, pairing(sizes, 'gy', 1))  1.42 us
  transfers between devices with their start and end apart: 17, of which 6 were waited for; matrix products, arithmetic and copies ran while one was open for 0% of the time, Pallas kernels for 2%

profile of v1, /device:TPU:0, one launch (start us, length us, event | category | flops | bytes accessed | tf_op | source)
XLA Modules:
  0.0 42.4 jit_solution(7898327070864862071)
XLA Ops:
  0.6 3.0 %collective-permute-start.1 = (f32[64,128]{1,0:T(8,128)}, f32[64,128]{1,0:T(8,128)S(1)}, u32[]{:S(2)}, u32[]{:S(2)}) collective-permute-start(f32[64,128]{1,0:T(8,128)} %bitcast.21), channel_id=1, source_target_pairs={{0,16},{16,0},{1,17},{17,1},{2,18},{18,2},{3,19},{19,3},{4,20},{20... | collective-permute-start | bytes 98312 | tf_op jit(solution)/shard_map/ppermute | solution.py:75
  3.7 1.9 %collective-permute-start.3 = (f32[64,128]{1,0:T(8,128)}, f32[64,128]{1,0:T(8,128)S(1)}, u32[]{:S(2)}, u32[]{:S(2)}) collective-permute-start(f32[64,128]{1,0:T(8,128)} %bitcast.25), channel_id=1, source_target_pairs={{0,16},{16,0},{1,17},{17,1},{2,18},{18,2},{3,19},{19,3},{4,20},{20... | collective-permute-start | bytes 98312 | tf_op jit(solution)/shard_map/ppermute | solution.py:75
  5.7 1.9 %collective-permute-start.5 = (f32[64,128]{1,0:T(8,128)}, f32[64,128]{1,0:T(8,128)S(1)}, u32[]{:S(2)}, u32[]{:S(2)}) collective-permute-start(f32[64,128]{1,0:T(8,128)} %bitcast.29), channel_id=1, source_target_pairs={{0,16},{16,0},{1,17},{17,1},{2,18},{18,2},{3,19},{19,3},{4,20},{20... | collective-permute-start | bytes 98312 | tf_op jit(solution)/shard_map/ppermute | solution.py:75
  7.7 1.1 %copy-done = f32[19,16,4,128]{3,2,1,0:T(4,128)S(1)} copy-done((f32[19,16,4,128]{3,2,1,0:T(4,128)S(1)}, f32[19,16,4,128]{3,2,1,0:T(4,128)}, u32[]{:S(2)}) %copy-start) | copy-done | bytes 622616
  8.8 0.9 %shard_map.155 = (f32[64,128]{1,0:T(8,128)S(1)}, f32[64,128]{1,0:T(8,128)S(1)}, f32[64,128]{1,0:T(8,128)S(1)}, f32[19,16,128]{2,1,0:T(8,128)S(1)}, f32[19,16,128...) custom-call(f32[19]{0:T(128)S(1)} %copy-done.10, f32[19,64,128]{2,1,0:T(8,128)S(1)} %bitcast.19), custom_call_target="tpu_custom_call" | custom-call | flops 1048576 | bytes 1048576 | tf_op jit(solution)/shard_map/pallas_call | solution.py:377
  10.4 3.2 %collective-permute-done.refs_7_ = f32[64,128]{1,0:T(8,128)S(1)} collective-permute-done((f32[64,128]{1,0:T(8,128)S(1)}, f32[64,128]{1,0:T(8,128)S(1)}, u32[]{:S(2)}, u32[]{:S(2)}) %collective-permute-start) | collective-permute-done | bytes 32800 | tf_op jit(solution)/shard_map/ppermute | solution.py:75
  14.4 0.8 %copy-done.3 = f32[32,1,2,128]{3,2,1,0:T(2,128)S(1)} copy-done((f32[32,1,2,128]{3,2,1,0:T(2,128)S(1)}, f32[32,1,2,128]{3,2,1,0:T(2,128)}, u32[]{:S(2)}) %copy-start.3) | copy-done | bytes 32792
  15.1 0.8 %copy-done.4 = f32[32,1,2,128]{3,2,1,0:T(2,128)S(1)} copy-done((f32[32,1,2,128]{3,2,1,0:T(2,128)S(1)}, f32[32,1,2,128]{3,2,1,0:T(2,128)}, u32[]{:S(2)}) %copy-start.4) | copy-done | bytes 32792
  15.9 0.8 %copy-done.5 = f32[32,1,2,128]{3,2,1,0:T(2,128)S(1)} copy-done((f32[32,1,2,128]{3,2,1,0:T(2,128)S(1)}, f32[32,1,2,128]{3,2,1,0:T(2,128)}, u32[]{:S(2)}) %copy-start.5) | copy-done | bytes 32792
  16.7 0.8 %copy-done.6 = f32[32,1,2,128]{3,2,1,0:T(2,128)S(1)} copy-done((f32[32,1,2,128]{3,2,1,0:T(2,128)S(1)}, f32[32,1,2,128]{3,2,1,0:T(2,128)}, u32[]{:S(2)}) %copy-start.6) | copy-done | bytes 32792
  17.4 0.8 %copy-done.7 = f32[32,1,2,128]{3,2,1,0:T(2,128)S(1)} copy-done((f32[32,1,2,128]{3,2,1,0:T(2,128)S(1)}, f32[32,1,2,128]{3,2,1,0:T(2,128)}, u32[]{:S(2)}) %copy-start.7) | copy-done | bytes 32792
  18.6 0.7 %collective-permute-start.9 = (f32[21,16,128]{2,1,0:T(8,128)S(1)}, f32[21,16,128]{2,1,0:T(8,128)S(1)}, u32[]{:S(2)}, u32[]{:S(2)}) collective-permute-start(f32[21,16,128]{2,1,0:T(8,128)S(1)} %get-tuple-element.46), channel_id=1, source_target_pairs={{0,16},{1,2},{2,1},{3,19},{4,20},{5,6},{6,5},{7,23},{8,24},{9,10},... | collective-permute-start | bytes 516104 | tf_op jit(solution)/shard_map/ppermute | solution.py:474
  19.3 1.4 %collective-permute-start.10 = (f32[19,8,128]{2,1,0:T(8,128)S(1)}, f32[19,8,128]{2,1,0:T(8,128)S(1)}, u32[]{:S(2)}, u32[]{:S(2)}) collective-permute-start(f32[19,8,128]{2,1,0:T(8,128)S(1)} %get-tuple-element.47), channel_id=1, source_target_pairs={{0,16},{16,0},{1,17},{17,1},{2,18},{18,2},{3,19},{19,3},{4,20},{20... | collective-permute-start | bytes 233480 | tf_op jit(solution)/shard_map/ppermute | solution.py:75
  20.7 1.6 %collective-permute-start.6 = (f32[64,128]{1,0:T(8,128)S(1)}, f32[64,128]{1,0:T(8,128)S(1)}, u32[]{:S(2)}, u32[]{:S(2)}) collective-permute-start(f32[64,128]{1,0:T(8,128)S(1)} %get-tuple-element.43), channel_id=1, source_target_pairs={{0,4},{1,5},{2,6},{3,7},{4,0},{5,1},{6,2},{7,3},{8,12},{9,13},{10,... | collective-permute-start | bytes 98312 | tf_op jit(solution)/shard_map/ppermute | solution.py:471
  22.3 2.3 %collective-permute-done.6.refs_6_ = f32[64,128]{1,0:T(8,128)S(1)} collective-permute-done((f32[64,128]{1,0:T(8,128)S(1)}, f32[64,128]{1,0:T(8,128)S(1)}, u32[]{:S(2)}, u32[]{:S(2)}) %collective-permute-start.6) | collective-permute-done | bytes 32800 | tf_op jit(solution)/shard_map/ppermute | solution.py:471
  24.6 1.1 %collective-permute-done.10.refs_10_ = f32[19,8,128]{2,1,0:T(8,128)S(1)} collective-permute-done((f32[19,8,128]{2,1,0:T(8,128)S(1)}, f32[19,8,128]{2,1,0:T(8,128)S(1)}, u32[]{:S(2)}, u32[]{:S(2)}) %collective-permute-start.10) | collective-permute-done | bytes 77856 | tf_op jit(solution)/shard_map/ppermute | solution.py:75
  25.8 2.2 %shard_map.157 = (f32[19,64,128]{2,1,0:T(8,128)S(1)}, f32[64,128]{1,0:T(8,128)S(1)}, f32[64,128]{1,0:T(8,128)S(1)}, f32[64,128]{1,0:T(8,128)S(1)}, f32[19,16,128...) custom-call(f32[19]{0:T(128)S(1)} %copy-done.11, f32[19]{0:T(128)S(1)} %copy-done.12, ...), custom_call_target="tpu_custom_call" | custom-call | flops 4194304 | bytes 1048576 | tf_op jit(solution)/shard_map/pallas_call | solution.py:377
  28.0 0.7 %collective-permute-start.11 = (f32[64,128]{1,0:T(8,128)S(1)}, f32[64,128]{1,0:T(8,128)S(1)}, u32[]{:S(2)}, u32[]{:S(2)}) collective-permute-start(f32[64,128]{1,0:T(8,128)S(1)} %get-tuple-element.52.refs_6_), channel_id=1, source_target_pairs={{0,16},{16,0},{1,17},{17,1},{2,18},{18,2},{3,19},{19,3},{4,20},{20... | collective-permute-start | bytes 98312 | tf_op jit(solution)/shard_map/ppermute | solution.py:75
  28.8 3.2 %collective-permute-done.11.refs_7_ = f32[64,128]{1,0:T(8,128)S(1)} collective-permute-done((f32[64,128]{1,0:T(8,128)S(1)}, f32[64,128]{1,0:T(8,128)S(1)}, u32[]{:S(2)}, u32[]{:S(2)}) %collective-permute-start.11) | collective-permute-done | bytes 32800 | tf_op jit(solution)/shard_map/ppermute | solution.py:75
  32.0 0.9 %shard_map.158 = (f32[7,64,128]{2,1,0:T(8,128)S(1)}, f32[64,128]{1,0:T(8,128)S(1)}, f32[64,128]{1,0:T(8,128)S(1)}, f32[21,16,128]{2,1,0:T(8,128)S(1)}, f32[21,16...) custom-call(s32[4,128]{1,0:T(4,128)S(1)} %copy-done.8, ...), custom_call_target="tpu_custom_call" | custom-call | flops 1048576 | bytes 1048576 | tf_op jit(solution)/shard_map/pallas_call | solution.py:377
  33.6 1.3 %collective-permute-start.16 = (f32[19,8,128]{2,1,0:T(8,128)S(1)}, f32[19,8,128]{2,1,0:T(8,128)S(1)}, u32[]{:S(2)}, u32[]{:S(2)}) collective-permute-start(f32[19,8,128]{2,1,0:T(8,128)S(1)} %get-tuple-element.68), channel_id=1, source_target_pairs={{0,16},{16,0},{1,17},{17,1},{2,18},{18,2},{3,19},{19,3},{4,20},{20... | collective-permute-start | bytes 233480 | tf_op jit(solution)/shard_map/ppermute | solution.py:75
  35.0 1.6 %collective-permute-start.12 = (f32[64,128]{1,0:T(8,128)S(1)}, f32[64,128]{1,0:T(8,128)S(1)}, u32[]{:S(2)}, u32[]{:S(2)}) collective-permute-start(f32[64,128]{1,0:T(8,128)S(1)} %get-tuple-element.64), channel_id=1, source_target_pairs={{0,4},{1,5},{2,6},{3,7},{4,0},{5,1},{6,2},{7,3},{8,12},{9,13},{10,... | collective-permute-start | bytes 98312 | tf_op jit(solution)/shard_map/ppermute | solution.py:471
  36.6 2.3 %collective-permute-done.12.refs_6_ = f32[64,128]{1,0:T(8,128)S(1)} collective-permute-done((f32[64,128]{1,0:T(8,128)S(1)}, f32[64,128]{1,0:T(8,128)S(1)}, u32[]{:S(2)}, u32[]{:S(2)}) %collective-permute-start.12) | collective-permute-done | bytes 32800 | tf_op jit(solution)/shard_map/ppermute | solution.py:471
  39.6 2.9 %shard_map.159 = f32[19,64,128]{2,1,0:T(8,128)} custom-call(f32[19]{0:T(128)S(1)} %copy-done.11, f32[19]{0:T(128)S(1)} %copy-done.12, f32[19]{0:T(128)S(1)} %copy-done.10, f32[19,19]{1,0:T(8,128)S(1)} %copy-done.2, f32[19,64,128]{2,1,0:T(8,128)S(1)} %get-tuple-element.62.refs_4_, f32[7,64,128]{2,1,0:T(8,128)S(1)} %get-tuple-element.63.refs_5_, ...), custom_call_target="tpu_custom_call" | custom-call | flops 4194304 | bytes 1048576 | tf_op jit(solution)/shard_map/pallas_call | solution.py:377
  (41 shorter events, 3.4 us)
Async XLA Ops:
  0.6 9.1 %collective-permute-start.1 = (f32[64,128]{1,0:T(8,128)}, f32[64,128]{1,0:T(8,128)S(1)}, u32[]{:S(2)}, u32[]{:S(2)}) collective-permute-start(f32[64,128]{1,0:T(8,128)} %bitcast.21), channel_id=1, source_target_pairs={{0,16},{16,0},{1,17},{17,1},{2,18},{18,2},{3,19},{19,3},{4,20},{20... | collective-permute-start | bytes 98312 | tf_op jit(solution)/shard_map/ppermute | solution.py:75
  3.6 6.8 %collective-permute-start.2 = (f32[64,128]{1,0:T(8,128)}, f32[64,128]{1,0:T(8,128)S(1)}, u32[]{:S(2)}, u32[]{:S(2)}) collective-permute-start(f32[64,128]{1,0:T(8,128)} %bitcast.23), channel_id=1, source_target_pairs={{0,16},{16,0},{1,17},{17,1},{2,18},{18,2},{3,19},{19,3},{4,20},{20... | collective-permute-start | bytes 98312 | tf_op jit(solution)/shard_map/ppermute | solution.py:75
  3.7 6.7 %collective-permute-start.3 = (f32[64,128]{1,0:T(8,128)}, f32[64,128]{1,0:T(8,128)S(1)}, u32[]{:S(2)}, u32[]{:S(2)}) collective-permute-start(f32[64,128]{1,0:T(8,128)} %bitcast.25), channel_id=1, source_target_pairs={{0,16},{16,0},{1,17},{17,1},{2,18},{18,2},{3,19},{19,3},{4,20},{20... | collective-permute-start | bytes 98312 | tf_op jit(solution)/shard_map/ppermute | solution.py:75
  5.7 4.8 %collective-permute-start.4 = (f32[64,128]{1,0:T(8,128)}, f32[64,128]{1,0:T(8,128)S(1)}, u32[]{:S(2)}, u32[]{:S(2)}) collective-permute-start(f32[64,128]{1,0:T(8,128)} %bitcast.27), channel_id=1, source_target_pairs={{0,16},{16,0},{1,17},{17,1},{2,18},{18,2},{3,19},{19,3},{4,20},{20... | collective-permute-start | bytes 98312 | tf_op jit(solution)/shard_map/ppermute | solution.py:75
  5.7 1.9 %copy-start.10 = (f32[19]{0:T(128)S(1)}, f32[19]{0:T(128)}, u32[]{:S(2)}) copy-start(f32[19]{0:T(128)} %refs_2_.3) | copy-start | bytes 232
  5.7 4.7 %collective-permute-start.5 = (f32[64,128]{1,0:T(8,128)}, f32[64,128]{1,0:T(8,128)S(1)}, u32[]{:S(2)}, u32[]{:S(2)}) collective-permute-start(f32[64,128]{1,0:T(8,128)} %bitcast.29), channel_id=1, source_target_pairs={{0,16},{16,0},{1,17},{17,1},{2,18},{18,2},{3,19},{19,3},{4,20},{20... | collective-permute-start | bytes 98312 | tf_op jit(solution)/shard_map/ppermute | solution.py:75
  7.7 1.1 %copy-start = (f32[19,16,4,128]{3,2,1,0:T(4,128)S(1)}, f32[19,16,4,128]{3,2,1,0:T(4,128)}, u32[]{:S(2)}) copy-start(f32[19,16,4,128]{3,2,1,0:T(4,128)} %param.17) | copy-start | bytes 1867780
  8.8 17.0 %copy-start.1 = (f32[19,16,4,128]{3,2,1,0:T(4,128)S(1)}, f32[19,16,4,128]{3,2,1,0:T(4,128)}, u32[]{:S(2)}) copy-start(f32[19,16,4,128]{3,2,1,0:T(4,128)} %param.17) | copy-start | bytes 1867780
  9.7 4.0 %collective-permute-start = (f32[64,128]{1,0:T(8,128)S(1)}, f32[64,128]{1,0:T(8,128)S(1)}, u32[]{:S(2)}, u32[]{:S(2)}) collective-permute-start(f32[64,128]{1,0:T(8,128)S(1)} %get-tuple-element.41.refs_6_), channel_id=1, source_target_pairs={{0,16},{16,0},{1,17},{17,1},{2,18},{18,2},{3,19},{19,3},{4,20},{20... | collective-permute-start | bytes 98312 | tf_op jit(solution)/shard_map/ppermute | solution.py:75
  14.4 0.8 %copy-start.3 = (f32[32,1,2,128]{3,2,1,0:T(2,128)S(1)}, f32[32,1,2,128]{3,2,1,0:T(2,128)}, u32[]{:S(2)}) copy-start(f32[32,1,2,128]{3,2,1,0:T(2,128)} %param.12) | copy-start | bytes 98308
  18.2 7.6 %copy-start.2 = (f32[19,19]{1,0:T(8,128)S(1)}, f32[19,19]{1,0:T(8,128)}, u32[]{:S(2)}) copy-start(f32[19,19]{1,0:T(8,128)} %refs_3_.3) | copy-start | bytes 4336
  18.5 7.2 %collective-permute-start.8 = (f32[21,16,128]{2,1,0:T(8,128)S(1)}, f32[21,16,128]{2,1,0:T(8,128)S(1)}, u32[]{:S(2)}, u32[]{:S(2)}) collective-permute-start(f32[21,16,128]{2,1,0:T(8,128)S(1)} %get-tuple-element.45), channel_id=1, source_target_pairs={{0,1},{1,0},{2,3},{3,2},{4,5},{5,4},{6,7},{7,6},{8,9},{9,8},{10,11... | collective-permute-start | bytes 516104 | tf_op jit(solution)/shard_map/ppermute | solution.py:473
  18.6 7.1 %collective-permute-start.9 = (f32[21,16,128]{2,1,0:T(8,128)S(1)}, f32[21,16,128]{2,1,0:T(8,128)S(1)}, u32[]{:S(2)}, u32[]{:S(2)}) collective-permute-start(f32[21,16,128]{2,1,0:T(8,128)S(1)} %get-tuple-element.46), channel_id=1, source_target_pairs={{0,16},{1,2},{2,1},{3,19},{4,20},{5,6},{6,5},{7,23},{8,24},{9,10},... | collective-permute-start | bytes 516104 | tf_op jit(solution)/shard_map/ppermute | solution.py:474
  19.3 6.4 %collective-permute-start.10 = (f32[19,8,128]{2,1,0:T(8,128)S(1)}, f32[19,8,128]{2,1,0:T(8,128)S(1)}, u32[]{:S(2)}, u32[]{:S(2)}) collective-permute-start(f32[19,8,128]{2,1,0:T(8,128)S(1)} %get-tuple-element.47), channel_id=1, source_target_pairs={{0,16},{16,0},{1,17},{17,1},{2,18},{18,2},{3,19},{19,3},{4,20},{20... | collective-permute-start | bytes 233480 | tf_op jit(solution)/shard_map/ppermute | solution.py:75
  20.7 3.9 %collective-permute-start.6 = (f32[64,128]{1,0:T(8,128)S(1)}, f32[64,128]{1,0:T(8,128)S(1)}, u32[]{:S(2)}, u32[]{:S(2)}) collective-permute-start(f32[64,128]{1,0:T(8,128)S(1)} %get-tuple-element.43), channel_id=1, source_target_pairs={{0,4},{1,5},{2,6},{3,7},{4,0},{5,1},{6,2},{7,3},{8,12},{9,13},{10,... | collective-permute-start | bytes 98312 | tf_op jit(solution)/shard_map/ppermute | solution.py:471
  22.3 3.5 %copy-start.11 = (f32[19]{0:T(128)S(1)}, f32[19]{0:T(128)}, u32[]{:S(2)}) copy-start(f32[19]{0:T(128)} %refs_0_.7) | copy-start | bytes 232
  22.3 3.5 %copy-start.12 = (f32[19]{0:T(128)S(1)}, f32[19]{0:T(128)}, u32[]{:S(2)}) copy-start(f32[19]{0:T(128)} %refs_1_.7) | copy-start | bytes 232
  22.3 2.3 %collective-permute-start.7 = (f32[64,128]{1,0:T(8,128)S(1)}, f32[64,128]{1,0:T(8,128)S(1)}, u32[]{:S(2)}, u32[]{:S(2)}) collective-permute-start(f32[64,128]{1,0:T(8,128)S(1)} %get-tuple-element.44), channel_id=1, source_target_pairs={{0,1},{1,0},{2,3},{3,2},{4,8},{5,9},{6,10},{7,11},{8,4},{9,5},{10,... | collective-permute-start | bytes 98312 | tf_op jit(solution)/shard_map/ppermute | solution.py:472
  28.0 4.0 %collective-permute-start.11 = (f32[64,128]{1,0:T(8,128)S(1)}, f32[64,128]{1,0:T(8,128)S(1)}, u32[]{:S(2)}, u32[]{:S(2)}) collective-permute-start(f32[64,128]{1,0:T(8,128)S(1)} %get-tuple-element.52.refs_6_), channel_id=1, source_target_pairs={{0,16},{16,0},{1,17},{17,1},{2,18},{18,2},{3,19},{19,3},{4,20},{20... | collective-permute-start | bytes 98312 | tf_op jit(solution)/shard_map/ppermute | solution.py:75
  32.9 6.6 %collective-permute-start.14 = (f32[21,16,128]{2,1,0:T(8,128)S(1)}, f32[21,16,128]{2,1,0:T(8,128)S(1)}, u32[]{:S(2)}, u32[]{:S(2)}) collective-permute-start(f32[21,16,128]{2,1,0:T(8,128)S(1)} %get-tuple-element.66), channel_id=1, source_target_pairs={{0,1},{1,0},{2,3},{3,2},{4,5},{5,4},{6,7},{7,6},{8,9},{9,8},{10,11... | collective-permute-start | bytes 516104 | tf_op jit(solution)/shard_map/ppermute | solution.py:473
  32.9 6.6 %collective-permute-start.15 = (f32[21,16,128]{2,1,0:T(8,128)S(1)}, f32[21,16,128]{2,1,0:T(8,128)S(1)}, u32[]{:S(2)}, u32[]{:S(2)}) collective-permute-start(f32[21,16,128]{2,1,0:T(8,128)S(1)} %get-tuple-element.67), channel_id=1, source_target_pairs={{0,16},{1,2},{2,1},{3,19},{4,20},{5,6},{6,5},{7,23},{8,24},{9,10},... | collective-permute-start | bytes 516104 | tf_op jit(solution)/shard_map/ppermute | solution.py:474
  33.6 5.9 %collective-permute-start.16 = (f32[19,8,128]{2,1,0:T(8,128)S(1)}, f32[19,8,128]{2,1,0:T(8,128)S(1)}, u32[]{:S(2)}, u32[]{:S(2)}) collective-permute-start(f32[19,8,128]{2,1,0:T(8,128)S(1)} %get-tuple-element.68), channel_id=1, source_target_pairs={{0,16},{16,0},{1,17},{17,1},{2,18},{18,2},{3,19},{19,3},{4,20},{20... | collective-permute-start | bytes 233480 | tf_op jit(solution)/shard_map/ppermute | solution.py:75
  35.0 3.9 %collective-permute-start.12 = (f32[64,128]{1,0:T(8,128)S(1)}, f32[64,128]{1,0:T(8,128)S(1)}, u32[]{:S(2)}, u32[]{:S(2)}) collective-permute-start(f32[64,128]{1,0:T(8,128)S(1)} %get-tuple-element.64), channel_id=1, source_target_pairs={{0,4},{1,5},{2,6},{3,7},{4,0},{5,1},{6,2},{7,3},{8,12},{9,13},{10,... | collective-permute-start | bytes 98312 | tf_op jit(solution)/shard_map/ppermute | solution.py:471
  36.6 2.3 %collective-permute-start.13 = (f32[64,128]{1,0:T(8,128)S(1)}, f32[64,128]{1,0:T(8,128)S(1)}, u32[]{:S(2)}, u32[]{:S(2)}) collective-permute-start(f32[64,128]{1,0:T(8,128)S(1)} %get-tuple-element.65), channel_id=1, source_target_pairs={{0,1},{1,0},{2,3},{3,2},{4,8},{5,9},{6,10},{7,11},{8,4},{9,5},{10,... | collective-permute-start | bytes 98312 | tf_op jit(solution)/shard_map/ppermute | solution.py:472
  (6 other events, 4.4 us)

commit v2 on v1

v2 whole, which is shorter than its diff:
```python
import functools

import jax
import jax.numpy as jnp
from jax import lax
from jax.experimental import pallas as pl
from jax.experimental.pallas import tpu as pltpu
from jax.sharding import PartitionSpec as P

STEPS = 2

WATER_ATTEN = 0.01
PIGMENT_ATTEN = 0.05
WARMING_UPTAKE = 5.0
WARM_EXPANSION = 0.2
SALT_EXPANSION = 0.8
CONVECT_MIX = 0.15
SIDE_DIFFUSE = 0.05
WARMING_FACTOR = 0.0633
TIME_STEP = 0.5

SUB = 8
AXES = ("grp", "gx", "gy")
VMEM_LIMIT = 48 * 1024 * 1024

F32 = jnp.float32


def vmem():
    return pl.BlockSpec(memory_space=pltpu.VMEM)


def hbm():
    return pl.BlockSpec(memory_space=pltpu.HBM)


def smem():
    return pl.BlockSpec(memory_space=pltpu.SMEM)


def shape(*dims):
    return jax.ShapeDtypeStruct(dims, F32)


def turn(x, shift, axis):
    shift = shift % x.shape[axis]
    return x if shift == 0 else pltpu.roll(x, shift, axis)


def iota(x, axis):
    return lax.broadcasted_iota(jnp.int32, x, axis)


def pairing(sizes, axis, odd):
    size_g, size_x, size_y = sizes

    def partner(g, x, y):
        i, n = (x, size_x) if axis == "gx" else (y, size_y)
        j = i + 1 if i % 2 == odd else i - 1
        if 0 <= j < n:
            return (g, j, y) if axis == "gx" else (g, x, j)
        if axis == "gx":
            return (g, x, y ^ 1) if (y ^ 1) < size_y else (g, x, y)
        return (g ^ 1, x, y) if (g ^ 1) < size_g else (g, x, y)

    def index(g, x, y):
        return (g * size_x + x) * size_y + y

    return [
        (index(g, x, y), index(*partner(g, x, y)))
        for g in range(size_g)
        for x in range(size_x)
        for y in range(size_y)
    ]


def from_others(value, count):
    return [
        lax.ppermute(value, "grp", [(i, (i + k) % count) for i in range(count)])
        for k in range(1, count)
    ]


class Refs:
    def __init__(self, refs):
        self.refs = list(refs)

    def take(self, n):
        out, self.refs = self.refs[:n], self.refs[n:]
        return out


def pick(mine, others, k):
    value = mine
    for at, other in enumerate(others):
        value = jnp.where(k == at + 1, other, value)
    return value


def pack_sides(c, slot, left, right):
    lane = iota(c.shape, 1)
    left = jnp.where(lane == slot, turn(c, slot, 1), left)
    right = jnp.where(lane == slot, turn(c, slot + 1, 1), right)
    return left, right


def level_base(cells, count):
    return cells if count == 2 else SUB


def message_shapes(tracers, rows, cells, width, count):
    height = level_base(cells, count) + tracers * rows + SUB
    height += -height % SUB
    if count == 2:
        return [shape(height, width)]
    return [shape(cells, width), shape(height, width), shape(height, width)]


def write_levels(last, first, t, rows, cells, msgs, g):
    if len(msgs) == 1:
        msgs[0][pl.ds(cells + t * rows, rows), :] = jnp.where(g == 0, last[SUB - rows :], first[:rows])
    else:
        msgs[1][pl.ds(SUB + t * rows, rows), :] = last[SUB - rows :]
        msgs[2][pl.ds(SUB + t * rows, rows), :] = first[:rows]


def raw_kernel(rows, *refs):
    *fields, depth_hbm, solar_hbm, out_ref, depth_ref, solar_ref, depth_s, solar_s, sems = refs
    copies = [pltpu.make_async_copy(f, out_ref.at[at], sems.at[at]) for at, f in enumerate(fields)]
    n = len(fields)
    copies.append(pltpu.make_async_copy(depth_hbm, depth_s, sems.at[n]))
    copies.append(pltpu.make_async_copy(solar_hbm, solar_s, sems.at[n + 1]))
    for copy in copies:
        copy.start()
    for copy in copies:
        copy.wait()
    for r in range(0, SUB, rows):
        depth_ref[pl.ds(r, rows), :] = depth_s[...]
        solar_ref[pl.ds(r, rows), :] = solar_s[...]


def chunks(n, parts):
    step = -(-n // parts)
    return [(a, min(step, n - a)) for a in range(0, n, step)]


def prep_kernel(rows, count, pig_ref, c_hbm, c_ref, *refs):
    *msgs, sems = refs
    g = lax.axis_index("grp")
    tracers, cells, _ = c_ref.shape
    cuts = chunks(tracers, sems.shape[0])
    copies = [
        pltpu.make_async_copy(c_hbm.at[pl.ds(a, n)], c_ref.at[pl.ds(a, n)], sems.at[i])
        for i, (a, n) in enumerate(cuts)
    ]
    for copy in copies:
        copy.start()
    pigment = jnp.zeros(c_ref.shape[1:], F32)
    for copy, (a, n) in zip(copies, cuts):
        copy.wait()
        for t in range(a, a + n):
            c = c_ref[t]
            pigment = pigment + pig_ref[t] * c
            write_levels(c[cells - SUB :], c[:SUB], t, rows, cells, msgs, g)
    msgs[0][pl.ds(0, cells), :] = pigment


def halves(v):
    high = v.astype(jnp.bfloat16)
    return high, (v - high.astype(F32)).astype(jnp.bfloat16)


def dot(a, b, **kw):
    return jnp.dot(a, b, preferred_element_type=F32, **kw)


def spread_rates(rates, tracers):
    exact = functools.partial(dot, precision=lax.Precision.HIGHEST)
    depth = tracers * SUB
    spread = jnp.where(iota((depth, tracers), 0) // SUB == iota((depth, tracers), 1), 1.0, 0.0)
    spread_t = jnp.where(iota((tracers, depth), 1) // SUB == iota((tracers, depth), 0), 1.0, 0.0)
    weights = exact(exact(spread, rates), spread_t)
    return jnp.where(
        lax.rem(iota((depth, depth), 0), SUB) == lax.rem(iota((depth, depth), 1), SUB), weights, 0.0
    )


def mix(weights, c_ref, mix_ref):
    tracers, cells, width = c_ref.shape
    w_high, w_low = halves(weights)
    for b in range(cells // SUB):
        here = pl.ds(b * SUB, SUB)
        c_high, c_low = halves(c_ref[:, here, :].reshape(tracers * SUB, width))
        mixed = dot(w_high, c_high) + (dot(w_high, c_low) + dot(w_low, c_high))
        mix_ref[:, here, :] = mixed.reshape(tracers, SUB, width)


def pack(rows, c_ref, pigment, msg_xa, msg_xb, msg_ya, msg_yb, p_s):
    tracers, cells, _ = c_ref.shape
    levels = cells // rows
    x_even = lax.rem(lax.axis_index("gx"), 2) == 0
    y_even = lax.rem(lax.axis_index("gy"), 2) == 0
    p_s[...] = pigment
    left = right = jnp.zeros(c_ref.shape[1:], F32)
    left, right = pack_sides(pigment, tracers + 2, left, right)
    for t in range(tracers):
        left, right = pack_sides(c_ref[t], t, left, right)
    msg_xa[...] = jnp.where(x_even, right, left)
    msg_xb[...] = jnp.where(x_even, left, right)

    def put(slot, first, last):
        msg_ya[slot] = jnp.where(y_even, last, first)
        msg_yb[slot] = jnp.where(y_even, first, last)

    for t in range(tracers):
        put(
            t,
            c_ref[t, pl.ds(0, levels, stride=rows), :],
            c_ref[t, pl.ds(rows - 1, levels, stride=rows), :],
        )
    put(
        tracers + 2,
        p_s[pl.ds(0, levels, stride=rows), :],
        p_s[pl.ds(rows - 1, levels, stride=rows), :],
    )


def pack_kernel(rows, *refs):
    c_ref, rates_ref, p_msg, msg_xa, msg_xb, msg_ya, msg_yb, w_ref, mix_ref, p_s = refs
    tracers, cells, _ = c_ref.shape
    pack(rows, c_ref, p_msg[pl.ds(0, cells), :], msg_xa, msg_xb, msg_ya, msg_yb, p_s)
    weights = spread_rates(rates_ref[...], tracers)
    w_ref[...] = weights
    mix(weights, c_ref, mix_ref)


def ocean_kernel(rows, count, tracers, first_step, *refs):
    refs = Refs(refs)
    depth_ref, solar_ref = refs.take(2)
    in_xa, in_xb, in_ya, in_yb = refs.take(4)
    p_own, *p_others = refs.take(count)
    if first_step:
        own_fields, *other_fields = refs.take(count)
    else:
        fields = refs.take(5)
    band_ref, msg_xa, msg_xb, msg_ya, msg_yb = refs.take(5)
    full_out = refs.take(5 if first_step else 4)
    (p_full,) = refs.take(1)
    if first_step:
        fields = refs.take(5)
    face_s, par_s, wet_s = refs.take(3)
    g = lax.axis_index("grp")
    cells, width = in_xa.shape
    levels = cells // rows
    total = count * cells
    all_levels = total // rows
    strip = rows // count

    for b in range(count):
        k = lax.rem(g - b + count, count)
        p_full[pl.ds(b * cells, cells), :] = pick(
            p_own[pl.ds(0, cells), :], [o[pl.ds(0, cells), :] for o in p_others], k
        )
    if first_step:
        for at in range(5):
            for s in range(count):
                k = lax.rem(g - s + count, count)
                for r in range(strip):
                    here = pl.ds(r, all_levels, stride=strip)
                    fields[at][pl.ds(s * strip + r, all_levels, stride=rows), :] = pick(
                        own_fields[at, here, :], [o[at, here, :] for o in other_fields], k
                    )

    def spread(ref):
        return jnp.broadcast_to(ref[...][None], (total // SUB, SUB, width)).reshape(total, width)

    row = iota((total, width), 0)
    wet = jnp.where(row // rows < spread(depth_ref), 1.0, 0.0)
    att = WATER_ATTEN + PIGMENT_ATTEN * p_full[...]
    summed = att
    step = rows
    while step < total:
        summed = summed + jnp.where(row >= step, turn(summed, step, 0), 0.0)
        step *= 2
    top = spread(solar_ref) * jnp.exp(att - summed)
    par = top * jnp.exp(-0.5 * att)
    east, north, temp, sal, mixing = [f[...] for f in fields]
    temp = temp + WARMING_UPTAKE * (top * (1.0 - jnp.exp(-att))) * wet

    def below(v):
        return turn(v, -rows, 0)

    density = SALT_EXPANSION * sal - WARM_EXPANSION * temp
    face = 0.5 * (mixing + below(mixing)) + CONVECT_MIX / (1.0 + jnp.exp(below(density) - density))
    face = jnp.where(row < total - rows, face * below(wet), 0.0)

    def stir(v):
        flux = face * (below(v) - v)
        return v + flux - turn(flux, rows, 0)

    for at, v in enumerate((east, north, temp, sal)):
        full_out[at][...] = stir(v)
    if first_step:
        full_out[4][...] = mixing
    face_s[...] = face
    par_s[...] = par
    wet_s[...] = wet

    band = pl.ds(pl.multiple_of(g * cells, SUB), cells)
    above = pl.ds(pl.multiple_of(lax.max(g * cells - SUB, 0), SUB), SUB)
    face_band = face_s[band, :]
    lifted = turn(jnp.concatenate([face_s[above, :], face_band], axis=0), rows, 0)[SUB:]
    lifted = jnp.where((iota((cells, width), 0) < rows) & (g == 0), 0.0, lifted)
    u = full_out[0][band, :]
    wet_band = wet_s[band, :]
    band_ref[0] = u
    band_ref[1] = full_out[1][band, :]
    band_ref[2] = full_out[2][band, :]
    band_ref[3] = face_band
    band_ref[4] = lifted
    band_ref[5] = par_s[band, :]
    band_ref[6] = wet_band

    x_even = lax.rem(lax.axis_index("gx"), 2) == 0
    y_even = lax.rem(lax.axis_index("gy"), 2) == 0
    xa, xb = in_xa[...], in_xb[...]
    left, right = jnp.where(x_even, xb, xa), jnp.where(x_even, xa, xb)
    left, right = pack_sides(wet_band, tracers + 1, left, right)
    _, right = pack_sides(u, tracers, left, right)
    msg_xa[...] = jnp.where(x_even, right, left)
    msg_xb[...] = jnp.where(x_even, left, right)
    for t in (*range(tracers), tracers + 2):
        msg_ya[t] = in_ya[t]
        msg_yb[t] = in_yb[t]
    speed = band_ref[1, pl.ds(rows - 1, levels, stride=rows), :]
    wet_first = band_ref[6, pl.ds(0, levels, stride=rows), :]
    wet_last = band_ref[6, pl.ds(rows - 1, levels, stride=rows), :]
    msg_ya[tracers] = speed
    msg_yb[tracers] = speed
    msg_ya[tracers + 1] = jnp.where(y_even, wet_last, wet_first)
    msg_yb[tracers + 1] = jnp.where(y_even, wet_first, wet_last)


def own_strip_kernel(rows, count, *refs):
    refs = Refs(refs)
    full, outs, strips = refs.take(4), refs.take(4), refs.take(4)
    (sems,) = refs.take(1)
    g = lax.axis_index("grp")
    strip = rows // count
    all_levels = full[0].shape[0] // rows
    copies = [pltpu.make_async_copy(strips[at], outs[at], sems.at[at]) for at in range(4)]
    for at in range(4):
        for r in range(strip):
            value = full[at][pl.ds(r, all_levels, stride=rows), :]
            for s in range(1, count):
                value = jnp.where(g == s, full[at][pl.ds(s * strip + r, all_levels, stride=rows), :], value)
            strips[at][pl.ds(r, all_levels, stride=strip), :] = value
        copies[at].start()
    for copy in copies:
        copy.wait()


def inner_kernel(rows, count, last_step, *refs):
    refs = Refs(refs)
    photo_ref, sat_ref, pig_ref, c_ref, mix_ref, band_ref = refs.take(6)
    lev_in = refs.take(1 if count == 2 else 2)
    (part_ref,) = refs.take(1)
    p_part = None if last_step else refs.take(1)[0]
    tracers, cells, width = c_ref.shape
    k_d = band_ref[3]
    k_u = band_ref[4]
    k_c = 1.0 - k_d - k_u
    par = band_ref[5]
    lit = TIME_STEP * band_ref[6]
    warm = lit * jnp.exp(WARMING_FACTOR * (band_ref[2] - 20.0))
    lit = lit * par
    pigment = jnp.zeros((cells, width), F32)
    for t in range(tracers):
        c = c_ref[t]
        at = level_base(cells, count) + t * rows
        up8 = lev_in[0][pl.ds(at + rows - SUB, SUB), :]
        down8 = lev_in[-1][pl.ds(at, SUB), :]
        c_u = turn(jnp.concatenate([up8, c], axis=0), rows, 0)[SUB:]
        c_d = turn(jnp.concatenate([c, down8], axis=0), -rows, 0)[:cells]
        part = (
            (k_c + photo_ref[t] * (lit / (par + sat_ref[t]))) * c + k_u * c_u + k_d * c_d + warm * mix_ref[t]
        )
        part_ref[t] = part
        if not last_step:
            pigment = pigment + pig_ref[t] * part
    if not last_step:
        p_part[...] = pigment


class Sides:
    def __init__(self, rows, cells, width, got, spread_s):
        got_xa, got_xb, self.got_ya, self.got_yb = got
        self.rows, self.spread_s = rows, spread_s
        x_even = lax.rem(lax.axis_index("gx"), 2) == 0
        self.y_even = lax.rem(lax.axis_index("gy"), 2) == 0
        self.west = jnp.where(x_even, got_xb[...], got_xa[...])
        self.east = jnp.where(x_even, got_xa[...], got_xb[...])
        self.lane = iota((cells, width), 1)
        self.at_row = lax.rem(iota((cells, width), 0), rows)
        self.levels = cells // rows

    def columns(self, v, slot):
        last = v.shape[1] - 1
        return (
            jnp.where(self.lane == 0, turn(self.west, -slot, 1), turn(v, 1, 1)),
            jnp.where(self.lane == last, turn(self.east, -1 - slot, 1), turn(v, -1, 1)),
        )

    def spread(self, slot):
        ya, yb = self.got_ya[slot], self.got_yb[slot]
        self.spread_s[slot, pl.ds(0, self.levels, stride=self.rows), :] = jnp.where(self.y_even, yb, ya)
        self.spread_s[slot, pl.ds(self.rows - 1, self.levels, stride=self.rows), :] = jnp.where(
            self.y_even, ya, yb
        )

    def rows_of(self, v, slot):
        outer = self.spread_s[slot]
        return (
            jnp.where(self.at_row == 0, outer, turn(v, 1, 0)),
            jnp.where(self.at_row == self.rows - 1, outer, turn(v, -1, 0)),
        )


def side_coefficients(sides, band_ref, tracers, sizes):
    _, size_x, size_y = sizes
    x = lax.axis_index("gx")
    y = lax.axis_index("gy")
    lane, at_row = sides.lane, sides.at_row
    u = band_ref[0]
    v = band_ref[1]
    wet = band_ref[6]
    wet_w, wet_e = sides.columns(wet, tracers + 1)
    wet_s, wet_n = sides.rows_of(wet, tracers + 1)
    open_w = wet * jnp.where((lane == 0) & (x == 0), 0.0, wet_w)
    open_e = wet * jnp.where((lane == wet.shape[1] - 1) & (x == size_x - 1), 0.0, wet_e)
    open_s = wet * jnp.where((at_row == 0) & (y == 0), 0.0, wet_s)
    open_n = wet * jnp.where((at_row == sides.rows - 1) & (y == size_y - 1), 0.0, wet_n)

    def lower(opening, speed):
        return opening * (jnp.maximum(speed, 0.0) + SIDE_DIFFUSE)

    def upper(opening, speed):
        return opening * (jnp.minimum(speed, 0.0) - SIDE_DIFFUSE)

    u_w, _ = sides.columns(u, tracers)
    v_s, _ = sides.rows_of(v, tracers)
    k_h = upper(open_w, u_w) - lower(open_e, u) + upper(open_s, v_s) - lower(open_n, v)
    return lower(open_w, u_w), -upper(open_e, u), lower(open_s, v_s), -upper(open_n, v), k_h


def sideways(sides, factors, v, slot):
    k_w, k_e, k_s, k_n, k_h = factors
    v_w, v_e = sides.columns(v, slot)
    v_s, v_n = sides.rows_of(v, slot)
    return (k_w * v_w + k_e * v_e) + (k_s * v_s + k_n * v_n) + k_h * v


def early_kernel(rows, count, sizes, *refs):
    refs = Refs(refs)
    c_ref, band_ref = refs.take(2)
    got = refs.take(4)
    p_msg, part_ref, p_part = refs.take(3)
    k_ref, spread_s = refs.take(2)
    msgs = refs.take(1 if count == 2 else 3)
    g = lax.axis_index("grp")
    tracers, cells, width = c_ref.shape
    sides = Sides(rows, cells, width, got, spread_s)
    for slot in range(tracers + 3):
        sides.spread(slot)
    factors = side_coefficients(sides, band_ref, tracers, sizes)
    for at, k in enumerate(factors):
        k_ref[at] = k
    msgs[0][pl.ds(0, cells), :] = p_part[...] + sideways(sides, factors, p_msg[pl.ds(0, cells), :], tracers + 2)

    lane = sides.lane[:SUB]
    at_row = sides.at_row[:SUB]

    def block(at, outermost, t):
        k_w, k_e, k_s, k_n, k_h = [k_ref[i, pl.ds(at, SUB), :] for i in range(5)]
        v = c_ref[t, pl.ds(at, SUB), :]
        outer = spread_s[t, pl.ds(at, SUB), :]
        v_w = jnp.where(lane == 0, turn(sides.west[at : at + SUB], -t, 1), turn(v, 1, 1))
        v_e = jnp.where(lane == width - 1, turn(sides.east[at : at + SUB], -1 - t, 1), turn(v, -1, 1))
        v_s = jnp.where(at_row == 0, outer, turn(v, 1, 0))
        v_n = jnp.where(at_row == rows - 1, outer, turn(v, -1, 0))
        side = (k_w * v_w + k_e * v_e) + (k_s * v_s + k_n * v_n) + k_h * v
        return part_ref[t, pl.ds(at, SUB), :] + side

    for t in range(tracers):
        write_levels(block(cells - SUB, True, t), block(0, False, t), t, rows, cells, msgs, g)


def step_kernel(rows, *refs):
    refs = Refs(refs)
    c_ref, part_ref, k_ref, spread_s = refs.take(4)
    got_xa, got_xb = refs.take(2)
    w_ref, p_msg = refs.take(2)
    out_ref, msg_xa, msg_xb, msg_ya, msg_yb, mix_ref, p_s = refs.take(7)
    tracers, cells, width = c_ref.shape
    sides = Sides(rows, cells, width, (got_xa, got_xb, None, None), spread_s)
    factors = [k_ref[i] for i in range(5)]
    for t in range(tracers):
        out_ref[t] = part_ref[t] + sideways(sides, factors, c_ref[t], t)
    pack(rows, out_ref, p_msg[pl.ds(0, cells), :], msg_xa, msg_xb, msg_ya, msg_yb, p_s)
    mix(w_ref[...], out_ref, mix_ref)


def final_kernel(rows, sizes, *refs):
    refs = Refs(refs)
    c_ref, part_ref, band_ref = refs.take(3)
    got = refs.take(4)
    out_hbm, spread_s, new_s, sems = refs.take(4)
    tracers, cells, width = c_ref.shape
    sides = Sides(rows, cells, width, got, spread_s)
    for slot in (tracers, tracers + 1):
        sides.spread(slot)
    factors = side_coefficients(sides, band_ref, tracers, sizes)
    copies = []
    for i, (a, n) in enumerate(chunks(tracers, sems.shape[0])):
        for t in range(a, a + n):
            sides.spread(t)
            new_s[t] = part_ref[t] + sideways(sides, factors, c_ref[t], t)
        copies.append(pltpu.make_async_copy(new_s.at[pl.ds(a, n)], out_hbm.at[pl.ds(a, n)], sems.at[i]))
        copies[-1].start()
    for copy in copies:
        copy.wait()


def call(kernel, ins, outs, in_specs=None, out_specs=None, scratch=(), flops=1 << 20):
    return pl.pallas_call(
        kernel,
        in_specs=[vmem() for _ in ins] if in_specs is None else in_specs,
        out_specs=[vmem() for _ in outs] if out_specs is None else out_specs,
        out_shape=outs,
        scratch_shapes=list(scratch),
        compiler_params=pltpu.CompilerParams(vmem_limit_bytes=VMEM_LIMIT),
        cost_estimate=pl.CostEstimate(flops=flops, bytes_accessed=1 << 20, transcendentals=0),
    )(*ins)


def per_device(
    sizes,
    zonal_boundary_speed,
    meridional_boundary_speed,
    potential_warmth,
    saltiness_field,
    quiescent_mixing_profile,
    substance_amounts,
    submerged_layer_number,
    solar_radiation,
    interaction_rates,
    photosynthetic_rates,
    saturation_irradiance,
    pigment_per_tracer,
):
    count = sizes[0]
    result_dimensions = zonal_boundary_speed.shape
    all_levels, _, strip, width = result_dimensions
    tracers, levels, rows, _ = substance_amounts.shape
    cells = levels * rows
    total = all_levels * rows
    strip_cells = all_levels * strip
    dma = pltpu.SemaphoreType.DMA
    column = pltpu.VMEM((total, width), F32)
    band_s = pltpu.VMEM((cells, width), F32)
    params = [photosynthetic_rates, saturation_irradiance, pigment_per_tracer]

    own = [
        f.reshape(strip_cells, width)
        for f in (
            zonal_boundary_speed,
            meridional_boundary_speed,
            potential_warmth,
            saltiness_field,
            quiescent_mixing_profile,
        )
    ]
    surface = [submerged_layer_number, solar_radiation]
    raw, depth, solar = call(
        functools.partial(raw_kernel, rows),
        own + surface,
        [shape(5, strip_cells, width), jax.ShapeDtypeStruct((SUB, width), jnp.int32), shape(SUB, width)],
        in_specs=[hbm()] * 7,
        scratch=[pltpu.VMEM((rows, width), jnp.int32), pltpu.VMEM((rows, width), F32), dma((7,))],
    )
    raw_others = from_others(raw, count)

    msg_levels = message_shapes(tracers, rows, cells, width, count)
    cols = shape(cells, width)
    lines = shape(tracers + 3, levels, width)
    sides = [cols, cols, lines, lines]
    field = shape(tracers, cells, width)
    c, *msgs = call(
        functools.partial(prep_kernel, rows, count),
        [pigment_per_tracer, substance_amounts.reshape(tracers, cells, width)],
        [field, *msg_levels],
        in_specs=[smem(), hbm()],
        scratch=[dma((4,))],
    )
    full = None
    for step in range(STEPS):
        first_step, last_step = step == 0, step == STEPS - 1
        p_others = from_others(msgs[0], count)
        if count == 2:
            lev = p_others
        else:
            lev = [
                lax.ppermute(msgs[1], "grp", [(i, (i + 1) % count) for i in range(count)]),
                lax.ppermute(msgs[2], "grp", [((i + 1) % count, i) for i in range(count)]),
            ]
        if first_step:
            xa, xb, ya, yb, weights, mixed = call(
                functools.partial(pack_kernel, rows),
                [c, interaction_rates, msgs[0]],
                [*sides, shape(tracers * SUB, tracers * SUB), field],
                scratch=[band_s],
                flops=1 << 24,
            )
        band, xa, xb, ya, yb, *full = call(
            functools.partial(ocean_kernel, rows, count, tracers, first_step),
            [depth, solar, xa, xb, ya, yb, msgs[0], *p_others, *([raw, *raw_others] if first_step else full)],
            [shape(7, cells, width), *sides, *[shape(total, width)] * (5 if first_step else 4)],
            scratch=[column] * (9 if first_step else 4),
        )
        xa = lax.ppermute(xa, AXES, pairing(sizes, "gx", 0))
        xb = lax.ppermute(xb, AXES, pairing(sizes, "gx", 1))
        ya = lax.ppermute(ya, AXES, pairing(sizes, "gy", 0))
        yb = lax.ppermute(yb, AXES, pairing(sizes, "gy", 1))
        part, *p_part = call(
            functools.partial(inner_kernel, rows, count, last_step),
            [*params, c, mixed, band, *lev],
            [field] + ([] if last_step else [cols]),
            in_specs=[smem()] * 3 + [vmem()] * (3 + len(lev)),
            flops=1 << 24,
        )
        if not last_step:
            k, spread, *msgs_next = call(
                functools.partial(early_kernel, rows, count, sizes),
                [c, band, xa, xb, ya, yb, msgs[0], part, *p_part],
                [shape(5, cells, width), shape(tracers + 3, cells, width), *msg_levels],
            )
            c, xa, xb, ya, yb, mixed = call(
                functools.partial(step_kernel, rows),
                [c, part, k, spread, xa, xb, weights, msgs_next[0]],
                [field, *sides, field],
                scratch=[band_s],
                flops=1 << 24,
            )
            msgs = msgs_next
        else:
            outs = call(
                functools.partial(own_strip_kernel, rows, count),
                full,
                [shape(strip_cells, width)] * 4,
                out_specs=[hbm()] * 4,
                scratch=[pltpu.VMEM((strip_cells, width), F32)] * 4 + [dma((4,))],
                flops=1 << 24,
            )
            (c,) = call(
                functools.partial(final_kernel, rows, sizes),
                [c, part, band, xa, xb, ya, yb],
                [field],
                out_specs=[hbm()],
                scratch=[
                    pltpu.VMEM((tracers + 3, cells, width), F32),
                    pltpu.VMEM((tracers, cells, width), F32),
                    dma((5,)),
                ],
            )
    return tuple(f.reshape(result_dimensions) for f in outs) + (c.reshape(substance_amounts.shape),)


def solution(mesh):
    ocean = P(None, "gy", "grp", "gx")
    tracer = P(None, "grp", "gy", "gx")
    surface = P("gy", "gx")
    sizes = tuple(mesh.shape[a] for a in AXES)
    return jax.shard_map(
        functools.partial(per_device, sizes),
        mesh=mesh,
        in_specs=(ocean,) * 5 + (tracer, surface, surface) + (P(),) * 4,
        out_specs=(ocean,) * 4 + (tracer,),
        check_vma=False,
    )
```

time: 42.9 us -> 34.2 us (0.80)
  waiting for transfers between devices: 13 us -> 6.7 us
  starting transfers between devices: 15.9 us -> 10.7 us
  Pallas kernels: 7.28 us -> 9.34 us
  local copies, waits for them, and re-layouts: 5.58 us -> 6.22 us
    ppermute x9 -> x3, starting transfers between devices: 11.2 us -> 4.33 us  [from_others(): lax.ppermute(value, 'grp', [(i, (i + k) % count) for i in range(count)])]
    ppermute x2, waiting for transfers between devices: 4.65 us -> 0.56 us  [per_device(): xa = lax.ppermute(xa, AXES, pairing(sizes, 'gx', 0))]
    ppermute x9 -> x3, waiting for transfers between devices: 8.3 us -> 5.04 us  [from_others(): lax.ppermute(value, 'grp', [(i, (i + k) % count) for i in range(count)])]
    pallas_call x5 -> x11, Pallas kernels: 7.28 us -> 9.34 us  [call(): pl.pallas_call(kernel, in_specs=[vmem() for _ in ins] if in_specs is None...]
    ppermute x2, waiting for transfers between devices: 0.01 us -> 1.09 us  [per_device(): yb = lax.ppermute(yb, AXES, pairing(sizes, 'gy', 1))]
    ppermute x2, starting transfers between devices: 3.17 us -> 4.12 us  [per_device(): xa = lax.ppermute(xa, AXES, pairing(sizes, 'gx', 0))]
    ppermute x2, starting transfers between devices: 0.01 us -> 0.74 us  [per_device(): xb = lax.ppermute(xb, AXES, pairing(sizes, 'gx', 1))]
    unnamed x26 -> x24, local copies, waits for them, and re-layouts: 5.58 us -> 6.22 us
  transfers between devices with their start and end apart: 17 -> 11, of which waited for: 6 -> 6; matrix products, arithmetic and copies ran while one was open for 0% -> 0% of each run, Pallas kernels for 2% -> 19%
where the time goes in v2:
time: 34.2 us; the launch traced here: 33.7 us
  starting transfers between devices  10.7 us (31%)
  Pallas kernels  9.34 us (27%)
  waiting for transfers between devices  6.7 us (20%)
  local copies, waits for them, and re-layouts  6.22 us (18%)
  between operations  0.74 us (2%)
    pallas_call x11, Pallas kernels, call(): pl.pallas_call(kernel, in_specs=[vmem() for _ in ins] if in_specs is None...  9.34 us
    unnamed x24, local copies, waits for them, and re-layouts  6.22 us
    ppermute x3, waiting for transfers between devices, from_others(): lax.ppermute(value, 'grp', [(i, (i + k) % count) for i in range(count)])  5.04 us
    ppermute x3, starting transfers between devices, from_others(): lax.ppermute(value, 'grp', [(i, (i + k) % count) for i in range(count)])  4.33 us
    ppermute x2, starting transfers between devices, per_device(): xa = lax.ppermute(xa, AXES, pairing(sizes, 'gx', 0))  4.12 us
    ppermute x2, starting transfers between devices, per_device(): yb = lax.ppermute(yb, AXES, pairing(sizes, 'gy', 1))  1.37 us
    ppermute x2, waiting for transfers between devices, per_device(): yb = lax.ppermute(yb, AXES, pairing(sizes, 'gy', 1))  1.09 us
    ppermute x2, starting transfers between devices, per_device(): xb = lax.ppermute(xb, AXES, pairing(sizes, 'gx', 1))  0.74 us
  transfers between devices with their start and end apart: 11, of which 6 were waited for; matrix products, arithmetic and copies ran while one was open for 0% of the time, Pallas kernels for 19%

profile of v2, /device:TPU:0, one launch (start us, length us, event | category | flops | bytes accessed | tf_op | source)
XLA Modules:
  0.0 33.7 jit_solution(17125143682594190940)
XLA Ops:
  0.7 0.7 %copy-done.11 = f32[4,128]{1,0:T(4,128)S(1)} copy-done((f32[4,128]{1,0:T(4,128)S(1)}, f32[4,128]{1,0:T(4,128)}, u32[]{:S(2)}) %copy-start.11) | copy-done | bytes 2072
  1.3 0.8 %copy-done.1 = f32[32,1,2,128]{3,2,1,0:T(2,128)S(1)} copy-done((f32[32,1,2,128]{3,2,1,0:T(2,128)S(1)}, f32[32,1,2,128]{3,2,1,0:T(2,128)}, u32[]{:S(2)}) %copy-start.1) | copy-done | bytes 32792
  2.1 0.8 %copy-done.2 = f32[32,1,2,128]{3,2,1,0:T(2,128)S(1)} copy-done((f32[32,1,2,128]{3,2,1,0:T(2,128)S(1)}, f32[32,1,2,128]{3,2,1,0:T(2,128)}, u32[]{:S(2)}) %copy-start.2) | copy-done | bytes 32792
  2.9 0.8 %copy-done.3 = f32[32,1,2,128]{3,2,1,0:T(2,128)S(1)} copy-done((f32[32,1,2,128]{3,2,1,0:T(2,128)S(1)}, f32[32,1,2,128]{3,2,1,0:T(2,128)}, u32[]{:S(2)}) %copy-start.3) | copy-done | bytes 32792
  3.6 0.8 %copy-done.4 = f32[32,1,2,128]{3,2,1,0:T(2,128)S(1)} copy-done((f32[32,1,2,128]{3,2,1,0:T(2,128)S(1)}, f32[32,1,2,128]{3,2,1,0:T(2,128)}, u32[]{:S(2)}) %copy-start.4) | copy-done | bytes 32792
  4.4 0.8 %copy-done.5 = f32[32,1,2,128]{3,2,1,0:T(2,128)S(1)} copy-done((f32[32,1,2,128]{3,2,1,0:T(2,128)S(1)}, f32[32,1,2,128]{3,2,1,0:T(2,128)}, u32[]{:S(2)}) %copy-start.5) | copy-done | bytes 32792
  5.4 3.0 %collective-permute-start.1 = (f32[5,64,128]{2,1,0:T(8,128)S(1)}, f32[5,64,128]{2,1,0:T(8,128)S(1)}, u32[]{:S(2)}, u32[]{:S(2)}) collective-permute-start(f32[5,64,128]{2,1,0:T(8,128)S(1)} %get-tuple-element.59.refs_8_), channel_id=1, source_target_pairs={{0,16},{16,0},{1,17},{17,1},{2,18},{18,2},{3,19},{19,3},{4,20},{20... | collective-permute-start | bytes 491528 | tf_op jit(solution)/shard_map/ppermute | solution.py:79
  8.4 1.1 %copy-done = f32[19,16,4,128]{3,2,1,0:T(4,128)S(1)} copy-done((f32[19,16,4,128]{3,2,1,0:T(4,128)S(1)}, f32[19,16,4,128]{3,2,1,0:T(4,128)}, u32[]{:S(2)}) %copy-start) | copy-done | bytes 622616
  9.5 1.5 %shard_map.156 = (f32[19,64,128]{2,1,0:T(8,128)S(1)}, f32[152,128]{1,0:T(8,128)S(1)}) custom-call(f32[19]{0:T(128)S(1)} %copy-done.7, f32[19,64,128]{2,1,0:T(8,128)S(1)} %bitcast.19), custom_call_target="tpu_custom_call" | custom-call | flops 1048576 | bytes 1048576 | tf_op jit(solution)/shard_map/pallas_call | solution.py:535
  11.6 1.3 %shard_map.157 = (f32[64,128]{1,0:T(8,128)S(1)}, f32[64,128]{1,0:T(8,128)S(1)}, f32[22,16,128]{2,1,0:T(8,128)S(1)}, f32[22,16,128]{2,1,0:T(8,128)S(1)}, f32[152,...) custom-call(f32[19,64,128]{2,1,0:T(8,128)S(1)} %get-tuple-element.52.refs_0_.refs_3_, f32[19,19]{1,0:T(8,128)S(1)} %copy-done.6, ...), custom_call_target="tpu_custom_call" | custom-call | flops 16777216 | bytes 1048576 | tf_op jit(solution)/shard_map/pallas_call | solution.py:535
  12.9 2.5 %collective-permute-done.refs_7_.refs_6_ = f32[152,128]{1,0:T(8,128)S(1)} collective-permute-done((f32[152,128]{1,0:T(8,128)S(1)}, f32[152,128]{1,0:T(8,128)S(1)}, u32[]{:S(2)}, u32[]{:S(2)}) %collective-permute-start) | collective-permute-done | bytes 77856 | tf_op jit(solution)/shard_map/ppermute | solution.py:79
  15.8 0.7 %collective-permute-start.5 = (f32[22,16,128]{2,1,0:T(8,128)S(1)}, f32[22,16,128]{2,1,0:T(8,128)S(1)}, u32[]{:S(2)}, u32[]{:S(2)}) collective-permute-start(f32[22,16,128]{2,1,0:T(8,128)S(1)} %get-tuple-element.65), channel_id=1, source_target_pairs={{0,16},{1,2},{2,1},{3,19},{4,20},{5,6},{6,5},{7,23},{8,24},{9,10},... | collective-permute-start | bytes 540680 | tf_op jit(solution)/shard_map/ppermute | solution.py:633
  16.5 1.6 %collective-permute-start.2 = (f32[64,128]{1,0:T(8,128)S(1)}, f32[64,128]{1,0:T(8,128)S(1)}, u32[]{:S(2)}, u32[]{:S(2)}) collective-permute-start(f32[64,128]{1,0:T(8,128)S(1)} %get-tuple-element.62), channel_id=1, source_target_pairs={{0,4},{1,5},{2,6},{3,7},{4,0},{5,1},{6,2},{7,3},{8,12},{9,13},{10,... | collective-permute-start | bytes 98312 | tf_op jit(solution)/shard_map/ppermute | solution.py:630
  18.1 0.7 %collective-permute-start.3 = (f32[64,128]{1,0:T(8,128)S(1)}, f32[64,128]{1,0:T(8,128)S(1)}, u32[]{:S(2)}, u32[]{:S(2)}) collective-permute-start(f32[64,128]{1,0:T(8,128)S(1)} %get-tuple-element.63), channel_id=1, source_target_pairs={{0,1},{1,0},{2,3},{3,2},{4,8},{5,9},{6,10},{7,11},{8,4},{9,5},{10,... | collective-permute-start | bytes 98312 | tf_op jit(solution)/shard_map/ppermute | solution.py:631
  19.5 1.0 %shard_map.159 = (f32[19,64,128]{2,1,0:T(8,128)S(1)}, f32[64,128]{1,0:T(8,128)S(1)}) custom-call(f32[19]{0:T(128)S(1)} %copy-done.8, f32[19]{0:T(128)S(1)} %copy-done.9, f32[19]{0:T(128)S(1)} %copy-done.7, f32[19,64,128]{2,1,0:T(8,128)S(1)} %get-tuple-element.52.refs_0_.refs_3_, f32[19,64,128]{2,1,0:T(8,128)S(1)} %get-tuple-element.54.refs_4_, ...), custom_call_target="tpu_custom_call" | custom-call | flops 16777216 | bytes 1048576 | tf_op jit(solution)/shard_map/pallas_call | solution.py:535
  20.7 0.7 %collective-permute-done.5.refs_5_ = f32[22,16,128]{2,1,0:T(8,128)S(1)} collective-permute-done((f32[22,16,128]{2,1,0:T(8,128)S(1)}, f32[22,16,128]{2,1,0:T(8,128)S(1)}, u32[]{:S(2)}, u32[]{:S(2)}) %collective-permute-start.5) | collective-permute-done | bytes 180256 | tf_op jit(solution)/shard_map/ppermute | solution.py:633
  21.7 0.7 %collective-permute-start.6 = (f32[152,128]{1,0:T(8,128)S(1)}, f32[152,128]{1,0:T(8,128)S(1)}, u32[]{:S(2)}, u32[]{:S(2)}) collective-permute-start(f32[152,128]{1,0:T(8,128)S(1)} %get-tuple-element.70.refs_7_.refs_6_), channel_id=1, source_target_pairs={{0,16},{16,0},{1,17},{17,1},{2,18},{18,2},{3,19},{19,3},{4,20},{20... | collective-permute-start | bytes 233480 | tf_op jit(solution)/shard_map/ppermute | solution.py:79
  22.4 1.2 %shard_map.161 = (f32[19,64,128]{2,1,0:T(8,128)S(1)}, f32[64,128]{1,0:T(8,128)S(1)}, f32[64,128]{1,0:T(8,128)S(1)}, f32[22,16,128]{2,1,0:T(8,128)S(1)}, f32[22,1...) custom-call(f32[19,64,128]{2,1,0:T(8,128)S(1)} %get-tuple-element.52.refs_0_.refs_3_, ...), custom_call_target="tpu_custom_call" | custom-call | flops 16777216 | bytes 1048576 | tf_op jit(solution)/shard_map/pallas_call | solution.py:535
  23.7 2.5 %collective-permute-done.6.refs_7_.refs_6_ = f32[152,128]{1,0:T(8,128)S(1)} collective-permute-done((f32[152,128]{1,0:T(8,128)S(1)}, f32[152,128]{1,0:T(8,128)S(1)}, u32[]{:S(2)}, u32[]{:S(2)}) %collective-permute-start.6) | collective-permute-done | bytes 77856 | tf_op jit(solution)/shard_map/ppermute | solution.py:79
  26.6 0.7 %collective-permute-start.10 = (f32[22,16,128]{2,1,0:T(8,128)S(1)}, f32[22,16,128]{2,1,0:T(8,128)S(1)}, u32[]{:S(2)}, u32[]{:S(2)}) collective-permute-start(f32[22,16,128]{2,1,0:T(8,128)S(1)} %get-tuple-element.94), channel_id=1, source_target_pairs={{0,16},{1,2},{2,1},{3,19},{4,20},{5,6},{6,5},{7,23},{8,24},{9,10},... | collective-permute-start | bytes 540680 | tf_op jit(solution)/shard_map/ppermute | solution.py:633
  27.3 2.5 %collective-permute-start.7 = (f32[64,128]{1,0:T(8,128)S(1)}, f32[64,128]{1,0:T(8,128)S(1)}, u32[]{:S(2)}, u32[]{:S(2)}) collective-permute-start(f32[64,128]{1,0:T(8,128)S(1)} %get-tuple-element.91), channel_id=1, source_target_pairs={{0,4},{1,5},{2,6},{3,7},{4,0},{5,1},{6,2},{7,3},{8,12},{9,13},{10,... | collective-permute-start | bytes 98312 | tf_op jit(solution)/shard_map/ppermute | solution.py:630
  29.8 0.7 %shard_map.163 = (f32[64,128]{1,0:T(8,128)}, f32[64,128]{1,0:T(8,128)}, f32[64,128]{1,0:T(8,128)}, f32[64,128]{1,0:T(8,128)}) custom-call(f32[128,128]{1,0:T(8,128)S(1)} %get-tuple-element.80.refs_0_, f32[128,128]{1,0:T(8,128)S(1)} %get-tuple-element.81.refs_1_, f32[128,128]{1,0:T(8,128)S(1)} %get-tuple-element.82.refs_2_, ...), custom_call_target="tpu_custom_call" | custom-call | flops 16777216 | bytes 1048576 | tf_op jit(solution)/shard_map/pallas_call | solution.py:535
  30.5 0.9 %shard_map.164.refs_1_ = f32[19,64,128]{2,1,0:T(8,128)S(1)} custom-call(f32[19]{0:T(128)S(1)} %copy-done.8, f32[19]{0:T(128)S(1)} %copy-done.9, f32[19]{0:T(128)S(1)} %copy-done.7, f32[19,64,128]{2,1,0:T(8,128)S(1)} %get-tuple-element.88.refs_3_.refs_0_, f32[19,64,128]{2,1,0:T(8,128)S(1)} %get-tuple-element.89.refs_4_, ...), custom_call_target="tpu_custom_call" | custom-call | flops 16777216 | bytes 1048576 | tf_op jit(solution)/shard_map/pallas_call | solution.py:535
  32.1 1.5 %shard_map.165 = f32[19,64,128]{2,1,0:T(8,128)} custom-call(f32[19,64,128]{2,1,0:T(8,128)S(1)} %get-tuple-element.88.refs_3_.refs_0_, f32[19,64,128]{2,1,0:T(8,128)S(1)} %shard_map.164.refs_1_, f32[7,64,128]{2,1,0:T(8,128)S(1)} %get-tuple-element.90.refs_5_.refs_2_, f32[64,128]{1,0:T(8,128)S(1)} %collective-permute-done.7.refs_3_, ...), custom_call_target="tpu_custom_call" | custom-call | flops 1048576 | bytes 1048576 | tf_op jit(solution)/shard_map/pallas_call | solution.py:535
  (33 shorter events, 3.7 us)
Async XLA Ops:
  0.6 0.7 %copy-start.11 = (f32[4,128]{1,0:T(4,128)S(1)}, f32[4,128]{1,0:T(4,128)}, u32[]{:S(2)}) copy-start(f32[4,128]{1,0:T(4,128)} %refs_6_.1) | copy-start | bytes 6148
  0.6 0.7 %copy-start.10 = (s32[4,128]{1,0:T(4,128)S(1)}, s32[4,128]{1,0:T(4,128)}, u32[]{:S(2)}) copy-start(s32[4,128]{1,0:T(4,128)} %refs_5_.1) | copy-start | bytes 6148
  1.3 0.8 %copy-start.1 = (f32[32,1,2,128]{3,2,1,0:T(2,128)S(1)}, f32[32,1,2,128]{3,2,1,0:T(2,128)}, u32[]{:S(2)}) copy-start(f32[32,1,2,128]{3,2,1,0:T(2,128)} %param.12) | copy-start | bytes 98308
  2.1 0.8 %copy-start.2 = (f32[32,1,2,128]{3,2,1,0:T(2,128)S(1)}, f32[32,1,2,128]{3,2,1,0:T(2,128)}, u32[]{:S(2)}) copy-start(f32[32,1,2,128]{3,2,1,0:T(2,128)} %param.13) | copy-start | bytes 98308
  2.8 0.8 %copy-start.3 = (f32[32,1,2,128]{3,2,1,0:T(2,128)S(1)}, f32[32,1,2,128]{3,2,1,0:T(2,128)}, u32[]{:S(2)}) copy-start(f32[32,1,2,128]{3,2,1,0:T(2,128)} %param.14) | copy-start | bytes 98308
  3.6 0.8 %copy-start.4 = (f32[32,1,2,128]{3,2,1,0:T(2,128)S(1)}, f32[32,1,2,128]{3,2,1,0:T(2,128)}, u32[]{:S(2)}) copy-start(f32[32,1,2,128]{3,2,1,0:T(2,128)} %param.15) | copy-start | bytes 98308
  4.4 0.8 %copy-start.5 = (f32[32,1,2,128]{3,2,1,0:T(2,128)S(1)}, f32[32,1,2,128]{3,2,1,0:T(2,128)}, u32[]{:S(2)}) copy-start(f32[32,1,2,128]{3,2,1,0:T(2,128)} %param.16) | copy-start | bytes 98308
  5.4 3.0 %copy-start.7 = (f32[19]{0:T(128)S(1)}, f32[19]{0:T(128)}, u32[]{:S(2)}) copy-start(f32[19]{0:T(128)} %refs_2_.3) | copy-start | bytes 232
  5.4 10.0 %collective-permute-start.1 = (f32[5,64,128]{2,1,0:T(8,128)S(1)}, f32[5,64,128]{2,1,0:T(8,128)S(1)}, u32[]{:S(2)}, u32[]{:S(2)}) collective-permute-start(f32[5,64,128]{2,1,0:T(8,128)S(1)} %get-tuple-element.59.refs_8_), channel_id=1, source_target_pairs={{0,16},{16,0},{1,17},{17,1},{2,18},{18,2},{3,19},{19,3},{4,20},{20... | collective-permute-start | bytes 491528 | tf_op jit(solution)/shard_map/ppermute | solution.py:79
  8.4 1.1 %copy-start = (f32[19,16,4,128]{3,2,1,0:T(4,128)S(1)}, f32[19,16,4,128]{3,2,1,0:T(4,128)}, u32[]{:S(2)}) copy-start(f32[19,16,4,128]{3,2,1,0:T(4,128)} %param.17) | copy-start | bytes 1867780
  9.5 2.1 %copy-start.6 = (f32[19,19]{1,0:T(8,128)S(1)}, f32[19,19]{1,0:T(8,128)}, u32[]{:S(2)}) copy-start(f32[19,19]{1,0:T(8,128)} %refs_1_.3) | copy-start | bytes 4336
  10.9 4.5 %collective-permute-start = (f32[152,128]{1,0:T(8,128)S(1)}, f32[152,128]{1,0:T(8,128)S(1)}, u32[]{:S(2)}, u32[]{:S(2)}) collective-permute-start(f32[152,128]{1,0:T(8,128)S(1)} %get-tuple-element.53.refs_2_.refs_6_), channel_id=1, source_target_pairs={{0,16},{16,0},{1,17},{17,1},{2,18},{18,2},{3,19},{19,3},{4,20},{20... | collective-permute-start | bytes 233480 | tf_op jit(solution)/shard_map/ppermute | solution.py:79
  15.8 5.0 %collective-permute-start.4 = (f32[22,16,128]{2,1,0:T(8,128)S(1)}, f32[22,16,128]{2,1,0:T(8,128)S(1)}, u32[]{:S(2)}, u32[]{:S(2)}) collective-permute-start(f32[22,16,128]{2,1,0:T(8,128)S(1)} %get-tuple-element.64), channel_id=1, source_target_pairs={{0,1},{1,0},{2,3},{3,2},{4,5},{5,4},{6,7},{7,6},{8,9},{9,8},{10,11... | collective-permute-start | bytes 540680 | tf_op jit(solution)/shard_map/ppermute | solution.py:632
  15.8 5.6 %collective-permute-start.5 = (f32[22,16,128]{2,1,0:T(8,128)S(1)}, f32[22,16,128]{2,1,0:T(8,128)S(1)}, u32[]{:S(2)}, u32[]{:S(2)}) collective-permute-start(f32[22,16,128]{2,1,0:T(8,128)S(1)} %get-tuple-element.65), channel_id=1, source_target_pairs={{0,16},{1,2},{2,1},{3,19},{4,20},{5,6},{6,5},{7,23},{8,24},{9,10},... | collective-permute-start | bytes 540680 | tf_op jit(solution)/shard_map/ppermute | solution.py:633
  16.5 4.2 %collective-permute-start.2 = (f32[64,128]{1,0:T(8,128)S(1)}, f32[64,128]{1,0:T(8,128)S(1)}, u32[]{:S(2)}, u32[]{:S(2)}) collective-permute-start(f32[64,128]{1,0:T(8,128)S(1)} %get-tuple-element.62), channel_id=1, source_target_pairs={{0,4},{1,5},{2,6},{3,7},{4,0},{5,1},{6,2},{7,3},{8,12},{9,13},{10,... | collective-permute-start | bytes 98312 | tf_op jit(solution)/shard_map/ppermute | solution.py:630
  18.1 2.6 %collective-permute-start.3 = (f32[64,128]{1,0:T(8,128)S(1)}, f32[64,128]{1,0:T(8,128)S(1)}, u32[]{:S(2)}, u32[]{:S(2)}) collective-permute-start(f32[64,128]{1,0:T(8,128)S(1)} %get-tuple-element.63), channel_id=1, source_target_pairs={{0,1},{1,0},{2,3},{3,2},{4,8},{5,9},{6,10},{7,11},{8,4},{9,5},{10,... | collective-permute-start | bytes 98312 | tf_op jit(solution)/shard_map/ppermute | solution.py:631
  18.8 0.7 %copy-start.8 = (f32[19]{0:T(128)S(1)}, f32[19]{0:T(128)}, u32[]{:S(2)}) copy-start(f32[19]{0:T(128)} %refs_0_.3) | copy-start | bytes 232
  18.8 0.7 %copy-start.9 = (f32[19]{0:T(128)S(1)}, f32[19]{0:T(128)}, u32[]{:S(2)}) copy-start(f32[19]{0:T(128)} %refs_1_.5) | copy-start | bytes 232
  21.7 4.5 %collective-permute-start.6 = (f32[152,128]{1,0:T(8,128)S(1)}, f32[152,128]{1,0:T(8,128)S(1)}, u32[]{:S(2)}, u32[]{:S(2)}) collective-permute-start(f32[152,128]{1,0:T(8,128)S(1)} %get-tuple-element.70.refs_7_.refs_6_), channel_id=1, source_target_pairs={{0,16},{16,0},{1,17},{17,1},{2,18},{18,2},{3,19},{19,3},{4,20},{20... | collective-permute-start | bytes 233480 | tf_op jit(solution)/shard_map/ppermute | solution.py:79
  26.5 5.2 %collective-permute-start.9 = (f32[22,16,128]{2,1,0:T(8,128)S(1)}, f32[22,16,128]{2,1,0:T(8,128)S(1)}, u32[]{:S(2)}, u32[]{:S(2)}) collective-permute-start(f32[22,16,128]{2,1,0:T(8,128)S(1)} %get-tuple-element.93), channel_id=1, source_target_pairs={{0,1},{1,0},{2,3},{3,2},{4,5},{5,4},{6,7},{7,6},{8,9},{9,8},{10,11... | collective-permute-start | bytes 540680 | tf_op jit(solution)/shard_map/ppermute | solution.py:632
  26.6 5.6 %collective-permute-start.10 = (f32[22,16,128]{2,1,0:T(8,128)S(1)}, f32[22,16,128]{2,1,0:T(8,128)S(1)}, u32[]{:S(2)}, u32[]{:S(2)}) collective-permute-start(f32[22,16,128]{2,1,0:T(8,128)S(1)} %get-tuple-element.94), channel_id=1, source_target_pairs={{0,16},{1,2},{2,1},{3,19},{4,20},{5,6},{6,5},{7,23},{8,24},{9,10},... | collective-permute-start | bytes 540680 | tf_op jit(solution)/shard_map/ppermute | solution.py:633
  27.3 4.4 %collective-permute-start.7 = (f32[64,128]{1,0:T(8,128)S(1)}, f32[64,128]{1,0:T(8,128)S(1)}, u32[]{:S(2)}, u32[]{:S(2)}) collective-permute-start(f32[64,128]{1,0:T(8,128)S(1)} %get-tuple-element.91), channel_id=1, source_target_pairs={{0,4},{1,5},{2,6},{3,7},{4,0},{5,1},{6,2},{7,3},{8,12},{9,13},{10,... | collective-permute-start | bytes 98312 | tf_op jit(solution)/shard_map/ppermute | solution.py:630
  29.8 1.9 %collective-permute-start.8 = (f32[64,128]{1,0:T(8,128)S(1)}, f32[64,128]{1,0:T(8,128)S(1)}, u32[]{:S(2)}, u32[]{:S(2)}) collective-permute-start(f32[64,128]{1,0:T(8,128)S(1)} %get-tuple-element.92), channel_id=1, source_target_pairs={{0,1},{1,0},{2,3},{3,2},{4,8},{5,9},{6,10},{7,11},{8,4},{9,5},{10,... | collective-permute-start | bytes 98312 | tf_op jit(solution)/shard_map/ppermute | solution.py:631

commit v3 on v2

--- a/solution.py
+++ b/solution.py
@@ -81,6 +81,11 @@
     ]
 
 
+def chunks(n, parts):
+    step = -(-n // parts)
+    return [(a, min(step, n - a)) for a in range(0, n, step)]
+
+
 class Refs:
     def __init__(self, refs):
         self.refs = list(refs)
@@ -109,7 +114,7 @@
 
 
 def message_shapes(tracers, rows, cells, width, count):
-    height = level_base(cells, count) + tracers * rows + SUB
+    height = level_base(cells, count) + tracers * rows + (SUB - rows)
     height += -height % SUB
     if count == 2:
         return [shape(height, width)]
@@ -124,44 +129,30 @@
         msgs[2][pl.ds(SUB + t * rows, rows), :] = first[:rows]
 
 
-def raw_kernel(rows, *refs):
-    *fields, depth_hbm, solar_hbm, out_ref, depth_ref, solar_ref, depth_s, solar_s, sems = refs
-    copies = [pltpu.make_async_copy(f, out_ref.at[at], sems.at[at]) for at, f in enumerate(fields)]
-    n = len(fields)
-    copies.append(pltpu.make_async_copy(depth_hbm, depth_s, sems.at[n]))
-    copies.append(pltpu.make_async_copy(solar_hbm, solar_s, sems.at[n + 1]))
-    for copy in copies:
-        copy.start()
-    for copy in copies:
-        copy.wait()
-    for r in range(0, SUB, rows):
-        depth_ref[pl.ds(r, rows), :] = depth_s[...]
-        solar_ref[pl.ds(r, rows), :] = solar_s[...]
-
-
-def chunks(n, parts):
-    step = -(-n // parts)
-    return [(a, min(step, n - a)) for a in range(0, n, step)]
-
-
-def prep_kernel(rows, count, pig_ref, c_hbm, c_ref, *refs):
-    *msgs, sems = refs
+def raw_window(rows, count, strip_cells, member):
+    if count != 2:
+        return 0, strip_cells
+    height = strip_cells // 2 + SUB
+    return member * (strip_cells - height), height
+
+
+def window_kernel(rows, count, raw_ref, out_ref):
+    g = lax.axis_index("grp")
+    low, height = raw_window(rows, count, raw_ref.shape[1], lax.rem(g + 1, count))
+    if count == 2:
+        low = pl.multiple_of(low, SUB)
+    for at in range(raw_ref.shape[0]):
+        out_ref[at] = raw_ref[at, pl.ds(low, height), :]
+
+
+def prep_kernel(rows, count, pig_ref, c_ref, *msgs):
     g = lax.axis_index("grp")
     tracers, cells, _ = c_ref.shape
-    cuts = chunks(tracers, sems.shape[0])
-    copies = [
-        pltpu.make_async_copy(c_hbm.at[pl.ds(a, n)], c_ref.at[pl.ds(a, n)], sems.at[i])
-        for i, (a, n) in enumerate(cuts)
-    ]
-    for copy in copies:
-        copy.start()
     pigment = jnp.zeros(c_ref.shape[1:], F32)
-    for copy, (a, n) in zip(copies, cuts):
-        copy.wait()
-        for t in range(a, a + n):
-            c = c_ref[t]
-            pigment = pigment + pig_ref[t] * c
-            write_levels(c[cells - SUB :], c[:SUB], t, rows, cells, msgs, g)
+    for t in range(tracers):
+        c = c_ref[t]
+        pigment = pigment + pig_ref[t] * c
+        write_levels(c[cells - SUB :], c[:SUB], t, rows, cells, msgs, g)
     msgs[0][pl.ds(0, cells), :] = pigment
 
 
@@ -226,8 +217,16 @@
 
 
 def pack_kernel(rows, *refs):
-    c_ref, rates_ref, p_msg, msg_xa, msg_xb, msg_ya, msg_yb, w_ref, mix_ref, p_s = refs
-    tracers, cells, _ = c_ref.shape
+    refs = Refs(refs)
+    photo_ref, sat_ref, depth_in, solar_in, c_ref, rates_ref, p_msg = refs.take(7)
+    msg_xa, msg_xb, msg_ya, msg_yb, w_ref, mix_ref, tiles_ref, depth_ref, solar_ref, p_s = refs.take(10)
+    tracers, cells, width = c_ref.shape
+    for r in range(0, SUB, rows):
+        depth_ref[pl.ds(r, rows), :] = depth_in[...]
+        solar_ref[pl.ds(r, rows), :] = solar_in[...]
+    for t in range(tracers):
+        tiles_ref[0, t] = jnp.full((SUB, width), photo_ref[t], F32)
+        tiles_ref[1, t] = jnp.full((SUB, width), sat_ref[t], F32)
     pack(rows, c_ref, p_msg[pl.ds(0, cells), :], msg_xa, msg_xb, msg_ya, msg_yb, p_s)
     weights = spread_rates(rates_ref[...], tracers)
     w_ref[...] = weights
@@ -248,6 +247,7 @@
     (p_full,) = refs.take(1)
     if first_step:
         fields = refs.take(5)
+        other_s = refs.take(5 * (count - 1))
     face_s, par_s, wet_s = refs.take(3)
     g = lax.axis_index("grp")
     cells, width = in_xa.shape
@@ -262,13 +262,19 @@
             p_own[pl.ds(0, cells), :], [o[pl.ds(0, cells), :] for o in p_others], k
         )
     if first_step:
+        low, height = raw_window(rows, count, all_levels * strip, g)
+        if count == 2:
+            low = pl.multiple_of(low, SUB)
         for at in range(5):
+            for k in range(count - 1):
+                other_s[5 * k + at][...] = jnp.zeros((all_levels * strip, width), F32)
+                other_s[5 * k + at][pl.ds(low, height), :] = other_fields[k][at]
             for s in range(count):
                 k = lax.rem(g - s + count, count)
                 for r in range(strip):
                     here = pl.ds(r, all_levels, stride=strip)
                     fields[at][pl.ds(s * strip + r, all_levels, stride=rows), :] = pick(
-                        own_fields[at, here, :], [o[at, here, :] for o in other_fields], k
+                        own_fields[at, here, :], [other_s[5 * j + at][here, :] for j in range(count - 1)], k
                     )
 
     def spread(ref):
@@ -362,7 +368,7 @@
 
 def inner_kernel(rows, count, last_step, *refs):
     refs = Refs(refs)
-    photo_ref, sat_ref, pig_ref, c_ref, mix_ref, band_ref = refs.take(6)
+    pig_ref, tiles_ref, c_ref, mix_ref, band_ref = refs.take(5)
     lev_in = refs.take(1 if count == 2 else 2)
     (part_ref,) = refs.take(1)
     p_part = None if last_step else refs.take(1)[0]
@@ -375,6 +381,11 @@
     warm = lit * jnp.exp(WARMING_FACTOR * (band_ref[2] - 20.0))
     lit = lit * par
     pigment = jnp.zeros((cells, width), F32)
+
+    def tile(which, t):
+        v = tiles_ref[which, t]
+        return jnp.broadcast_to(v[None], (cells // SUB, SUB, width)).reshape(cells, width)
+
     for t in range(tracers):
         c = c_ref[t]
         at = level_base(cells, count) + t * rows
@@ -383,7 +394,7 @@
         c_u = turn(jnp.concatenate([up8, c], axis=0), rows, 0)[SUB:]
         c_d = turn(jnp.concatenate([c, down8], axis=0), -rows, 0)[:cells]
         part = (
-            (k_c + photo_ref[t] * (lit / (par + sat_ref[t]))) * c + k_u * c_u + k_d * c_d + warm * mix_ref[t]
+            (k_c + tile(0, t) * (lit / (par + tile(1, t)))) * c + k_u * c_u + k_d * c_d + warm * mix_ref[t]
         )
         part_ref[t] = part
         if not last_step:
@@ -531,14 +542,14 @@
         copy.wait()
 
 
-def call(kernel, ins, outs, in_specs=None, out_specs=None, scratch=(), flops=1 << 20):
+def call(kernel, ins, outs, in_specs=None, out_specs=None, scratch=(), flops=1 << 20, vmem_limit=VMEM_LIMIT):
     return pl.pallas_call(
         kernel,
         in_specs=[vmem() for _ in ins] if in_specs is None else in_specs,
         out_specs=[vmem() for _ in outs] if out_specs is None else out_specs,
         out_shape=outs,
         scratch_shapes=list(scratch),
-        compiler_params=pltpu.CompilerParams(vmem_limit_bytes=VMEM_LIMIT),
+        compiler_params=pltpu.CompilerParams(vmem_limit_bytes=vmem_limit),
         cost_estimate=pl.CostEstimate(flops=flops, bytes_accessed=1 << 20, transcendentals=0),
     )(*ins)
 
@@ -568,7 +579,6 @@
     dma = pltpu.SemaphoreType.DMA
     column = pltpu.VMEM((total, width), F32)
     band_s = pltpu.VMEM((cells, width), F32)
-    params = [photosynthetic_rates, saturation_irradiance, pigment_per_tracer]
 
     own = [
         f.reshape(strip_cells, width)
@@ -580,27 +590,31 @@
             quiescent_mixing_profile,
         )
     ]
-    surface = [submerged_layer_number, solar_radiation]
-    raw, depth, solar = call(
-        functools.partial(raw_kernel, rows),
-        own + surface,
-        [shape(5, strip_cells, width), jax.ShapeDtypeStruct((SUB, width), jnp.int32), shape(SUB, width)],
-        in_specs=[hbm()] * 7,
-        scratch=[pltpu.VMEM((rows, width), jnp.int32), pltpu.VMEM((rows, width), F32), dma((7,))],
+    which = iota((5, strip_cells, width), 0)
+    raw = jnp.broadcast_to(own[0][None], which.shape)
+    for at in range(1, 5):
+        raw = jnp.where(which == at, own[at][None], raw)
+    _, height = raw_window(rows, count, strip_cells, 0)
+    (window,) = call(
+        functools.partial(window_kernel, rows, count),
+        [raw],
+        [shape(5, height, width)],
+        flops=1 << 30,
     )
-    raw_others = from_others(raw, count)
+    raw_others = from_others(window, count)
 
     msg_levels = message_shapes(tracers, rows, cells, width, count)
     cols = shape(cells, width)
     lines = shape(tracers + 3, levels, width)
     sides = [cols, cols, lines, lines]
     field = shape(tracers, cells, width)
-    c, *msgs = call(
+    c = substance_amounts.reshape(tracers, cells, width)
+    msgs = call(
         functools.partial(prep_kernel, rows, count),
-        [pigment_per_tracer, substance_amounts.reshape(tracers, cells, width)],
-        [field, *msg_levels],
-        in_specs=[smem(), hbm()],
-        scratch=[dma((4,))],
+        [pigment_per_tracer, c],
+        msg_levels,
+        in_specs=[smem(), vmem()],
+        vmem_limit=VMEM_LIMIT,
     )
     full = None
     for step in range(STEPS):
@@ -614,10 +628,26 @@
                 lax.ppermute(msgs[2], "grp", [((i + 1) % count, i) for i in range(count)]),
             ]
         if first_step:
-            xa, xb, ya, yb, weights, mixed = call(
+            xa, xb, ya, yb, weights, mixed, tiles, depth, solar = call(
                 functools.partial(pack_kernel, rows),
-                [c, interaction_rates, msgs[0]],
-                [*sides, shape(tracers * SUB, tracers * SUB), field],
+                [
+                    photosynthetic_rates,
+                    saturation_irradiance,
+                    submerged_layer_number,
+                    solar_radiation,
+                    c,
+                    interaction_rates,
+                    msgs[0],
+                ],
+                [
+                    *sides,
+                    shape(tracers * SUB, tracers * SUB),
+                    field,
+                    shape(2, tracers, SUB, width),
+                    jax.ShapeDtypeStruct((SUB, width), jnp.int32),
+                    shape(SUB, width),
+                ],
+                in_specs=[smem()] * 2 + [vmem()] * 5,
                 scratch=[band_s],
                 flops=1 << 24,
             )
@@ -625,7 +655,9 @@
             functools.partial(ocean_kernel, rows, count, tracers, first_step),
             [depth, solar, xa, xb, ya, yb, msgs[0], *p_others, *([raw, *raw_others] if first_step else full)],
             [shape(7, cells, width), *sides, *[shape(total, width)] * (5 if first_step else 4)],
-            scratch=[column] * (9 if first_step else 4),
+            scratch=[column] * (6 if first_step else 1)
+            + [pltpu.VMEM((strip_cells, width), F32)] * (5 * (count - 1) if first_step else 0)
+            + [column] * 3,
         )
         xa = lax.ppermute(xa, AXES, pairing(sizes, "gx", 0))
         xb = lax.ppermute(xb, AXES, pairing(sizes, "gx", 1))
@@ -633,9 +665,9 @@
         yb = lax.ppermute(yb, AXES, pairing(sizes, "gy", 1))
         part, *p_part = call(
             functools.partial(inner_kernel, rows, count, last_step),
-            [*params, c, mixed, band, *lev],
+            [pigment_per_tracer, tiles, c, mixed, band, *lev],
             [field] + ([] if last_step else [cols]),
-            in_specs=[smem()] * 3 + [vmem()] * (3 + len(lev)),
+            in_specs=[smem()] + [vmem()] * (4 + len(lev)),
             flops=1 << 24,
         )
         if not last_step:

time: 34.2 us -> 28.1 us (0.82)
  local copies, waits for them, and re-layouts: 6.22 us -> 0.04 us
  starting transfers between devices: 10.7 us -> 11.8 us
  waiting for transfers between devices: 6.7 us -> 5.75 us
  other arithmetic: 0 us -> 0.93 us
  Pallas kernels: 9.34 us -> 8.62 us
    unnamed x24 -> x14, local copies, waits for them, and re-layouts: 6.22 us -> 0.04 us
    ppermute x3, waiting for transfers between devices: 5.04 us -> 3.52 us  [from_others(): lax.ppermute(value, 'grp', [(i, (i + k) % count) for i in range(count)])]
    ppermute x2, starting transfers between devices: 1.37 us -> 2.49 us  [per_device(): yb = lax.ppermute(yb, AXES, pairing(sizes, 'gy', 1))]
    ppermute x2, waiting for transfers between devices: 0.56 us -> 1.56 us  [per_device(): xa = lax.ppermute(xa, AXES, pairing(sizes, 'gx', 0))]
    ppermute x3, starting transfers between devices: 4.33 us -> 5.25 us  [from_others(): lax.ppermute(value, 'grp', [(i, (i + k) % count) for i in range(count)])]
    select_n x0 -> x1, other arithmetic: none -> 0.92 us  [per_device(): raw = jnp.where(which == at, own[at][None], raw)]
    pallas_call x11, Pallas kernels: 9.34 us -> 8.62 us  [call(): pl.pallas_call(kernel, in_specs=[vmem() for _ in ins] if in_specs is None...]
    ppermute x2, starting transfers between devices: 0.74 us -> 0.18 us  [per_device(): xb = lax.ppermute(xb, AXES, pairing(sizes, 'gx', 1))]
  transfers between devices with their start and end apart: 11 -> 11, of which waited for: 6 -> 6; matrix products, arithmetic and copies ran while one was open for 0% -> 0% of each run, Pallas kernels for 19% -> 22%
where the time goes in v3:
time: 28.1 us; the launch traced here: 27.9 us
  starting transfers between devices  11.8 us (42%)
  Pallas kernels  8.62 us (31%)
  waiting for transfers between devices  5.75 us (20%)
  other arithmetic  0.93 us (3%)
  between operations  0.78 us (3%)
    pallas_call x11, Pallas kernels, call(): pl.pallas_call(kernel, in_specs=[vmem() for _ in ins] if in_specs is None...  8.62 us
    ppermute x3, starting transfers between devices, from_others(): lax.ppermute(value, 'grp', [(i, (i + k) % count) for i in range(count)])  5.25 us
    ppermute x2, starting transfers between devices, per_device(): xa = lax.ppermute(xa, AXES, pairing(sizes, 'gx', 0))  3.73 us
    ppermute x3, waiting for transfers between devices, from_others(): lax.ppermute(value, 'grp', [(i, (i + k) % count) for i in range(count)])  3.52 us
    ppermute x2, starting transfers between devices, per_device(): yb = lax.ppermute(yb, AXES, pairing(sizes, 'gy', 1))  2.49 us
    ppermute x2, waiting for transfers between devices, per_device(): xa = lax.ppermute(xa, AXES, pairing(sizes, 'gx', 0))  1.56 us
    select_n x1, other arithmetic, per_device(): raw = jnp.where(which == at, own[at][None], raw)  0.92 us
    ppermute x2, waiting for transfers between devices, per_device(): yb = lax.ppermute(yb, AXES, pairing(sizes, 'gy', 1))  0.66 us
  transfers between devices with their start and end apart: 11, of which 6 were waited for; matrix products, arithmetic and copies ran while one was open for 0% of the time, Pallas kernels for 22%

profile of v3, /device:TPU:0, one launch (start us, length us, event | category | flops | bytes accessed | tf_op | source)
XLA Modules:
  0.0 27.9 jit_solution(9535323329186171710)
XLA Ops:
  0.7 0.9 %select_select_fusion.raw_ref.refs_8_ = f32[5,64,128]{2,1,0:T(8,128)S(1)} fusion(f32[64,128]{1,0:T(8,128)} %bitcast.25, f32[64,128]{1,0:T(8,128)} %bitcast.26, f32[64,128]{1,0:T(8,128)} %bitcast.27, f32[64,128]{1,0:T(8,128)} %bitcast.28, f32[64,128]{1,0:T(8,128)} %bitcast.29, pred[5]{0:T(512)(128)(4,1)S(1)} %get-tuple-element.96, ...), kind=kLoop, calls=%fused_computation | loop fusion | flops 163840 | bytes 327700 | tf_op jit(solution)/shard_map/jit(_where)/select_n | solution.py:596
  1.6 3.0 %collective-permute-start.1 = (f32[5,40,128]{2,1,0:T(8,128)S(1)}, f32[5,40,128]{2,1,0:T(8,128)S(1)}, u32[]{:S(2)}, u32[]{:S(2)}) collective-permute-start(f32[5,40,128]{2,1,0:T(8,128)S(1)} %shard_map.157), channel_id=1, source_target_pairs={{0,16},{16,0},{1,17},{17,1},{2,18},{18,2},{3,19},{19,3},{4,20},{20... | collective-permute-start | bytes 307208 | tf_op jit(solution)/shard_map/ppermute | solution.py:79
  4.7 0.6 %shard_map.155.refs_6_ = f32[144,128]{1,0:T(8,128)S(1)} custom-call(f32[19]{0:T(128)S(1)} %copy-done.2, f32[19,64,128]{2,1,0:T(8,128)S(1)} %bitcast.19), custom_call_target="tpu_custom_call" | custom-call | flops 1048576 | bytes 1048576 | tf_op jit(solution)/shard_map/pallas_call | solution.py:546
  5.3 1.0 %collective-permute-start = (f32[144,128]{1,0:T(8,128)S(1)}, f32[144,128]{1,0:T(8,128)S(1)}, u32[]{:S(2)}, u32[]{:S(2)}) collective-permute-start(f32[144,128]{1,0:T(8,128)S(1)} %shard_map.155.refs_6_), channel_id=1, source_target_pairs={{0,16},{16,0},{1,17},{17,1},{2,18},{18,2},{3,19},{19,3},{4,20},{20... | collective-permute-start | bytes 221192 | tf_op jit(solution)/shard_map/ppermute | solution.py:79
  6.3 1.8 %shard_map.156 = (f32[64,128]{1,0:T(8,128)S(1)}, f32[64,128]{1,0:T(8,128)S(1)}, f32[22,16,128]{2,1,0:T(8,128)S(1)}, f32[22,16,128]{2,1,0:T(8,128)S(1)}, f32[152,...) custom-call(f32[19]{0:T(128)S(1)} %copy-done.5, ...), custom_call_target="tpu_custom_call" | custom-call | flops 16777216 | bytes 1048576 | tf_op jit(solution)/shard_map/pallas_call | solution.py:546
  8.2 1.5 %collective-permute-done.refs_7_.refs_5_ = f32[144,128]{1,0:T(8,128)S(1)} collective-permute-done((f32[144,128]{1,0:T(8,128)S(1)}, f32[144,128]{1,0:T(8,128)S(1)}, u32[]{:S(2)}, u32[]{:S(2)}) %collective-permute-start) | collective-permute-done | bytes 73760 | tf_op jit(solution)/shard_map/ppermute | solution.py:79
  9.7 0.4 %shard_map.158 = (f32[7,64,128]{2,1,0:T(8,128)S(1)}, f32[64,128]{1,0:T(8,128)S(1)}, f32[64,128]{1,0:T(8,128)S(1)}, f32[22,16,128]{2,1,0:T(8,128)S(1)}, f32[22,16...) custom-call(s32[8,128]{1,0:T(8,128)S(1)} %get-tuple-element.48.refs_, ...), custom_call_target="tpu_custom_call" | custom-call | flops 1048576 | bytes 1048576 | tf_op jit(solution)/shard_map/pallas_call | solution.py:546
  10.2 1.2 %collective-permute-start.5 = (f32[22,16,128]{2,1,0:T(8,128)S(1)}, f32[22,16,128]{2,1,0:T(8,128)S(1)}, u32[]{:S(2)}, u32[]{:S(2)}) collective-permute-start(f32[22,16,128]{2,1,0:T(8,128)S(1)} %get-tuple-element.61), channel_id=1, source_target_pairs={{0,16},{1,2},{2,1},{3,19},{4,20},{5,6},{6,5},{7,23},{8,24},{9,10},... | collective-permute-start | bytes 540680 | tf_op jit(solution)/shard_map/ppermute | solution.py:665
  11.4 1.6 %collective-permute-start.2 = (f32[64,128]{1,0:T(8,128)S(1)}, f32[64,128]{1,0:T(8,128)S(1)}, u32[]{:S(2)}, u32[]{:S(2)}) collective-permute-start(f32[64,128]{1,0:T(8,128)S(1)} %get-tuple-element.58), channel_id=1, source_target_pairs={{0,4},{1,5},{2,6},{3,7},{4,0},{5,1},{6,2},{7,3},{8,12},{9,13},{10,... | collective-permute-start | bytes 98312 | tf_op jit(solution)/shard_map/ppermute | solution.py:662
  13.1 0.9 %shard_map.159 = (f32[19,64,128]{2,1,0:T(8,128)S(1)}, f32[64,128]{1,0:T(8,128)S(1)}) custom-call(f32[19]{0:T(128)S(1)} %copy-done.2, f32[2,19,8,128]{3,2,1,0:T(8,128)S(1)} %get-tuple-element.50.refs_1_, f32[19,64,128]{2,1,0:T(8,128)S(1)} %bitcast.21, f32[19,64,128]{2,1,0:T(8,128)S(1)} %get-tuple-element.51.refs_3_, ...), custom_call_target="tpu_custom_call" | custom-call | flops 16777216 | bytes 1048576 | tf_op jit(solution)/shard_map/pallas_call | solution.py:546
  14.1 1.2 %collective-permute-done.2.refs_2_.refs_4_ = f32[64,128]{1,0:T(8,128)S(1)} collective-permute-done((f32[64,128]{1,0:T(8,128)S(1)}, f32[64,128]{1,0:T(8,128)S(1)}, u32[]{:S(2)}, u32[]{:S(2)}) %collective-permute-start.2) | collective-permute-done | bytes 32800 | tf_op jit(solution)/shard_map/ppermute | solution.py:662
  15.3 0.4 %collective-permute-done.5.refs_5_ = f32[22,16,128]{2,1,0:T(8,128)S(1)} collective-permute-done((f32[22,16,128]{2,1,0:T(8,128)S(1)}, f32[22,16,128]{2,1,0:T(8,128)S(1)}, u32[]{:S(2)}, u32[]{:S(2)}) %collective-permute-start.5) | collective-permute-done | bytes 180256 | tf_op jit(solution)/shard_map/ppermute | solution.py:665
  15.7 0.3 %shard_map.160 = (f32[5,64,128]{2,1,0:T(8,128)S(1)}, f32[22,64,128]{2,1,0:T(8,128)S(1)}, f32[144,128]{1,0:T(8,128)S(1)}) custom-call(f32[19,64,128]{2,1,0:T(8,128)S(1)} %bitcast.22, f32[7,64,128]{2,1,0:T(8,128)S(1)} %get-tuple-element.56.refs_4_.refs_1_, f32[64,128]{1,0:T(8,128)S(1)} %collective-permute-done.2.refs_2_.refs_4_, ...), custom_call_target="tpu_custom_call" | custom-call | flops 1048576 | bytes 1048576 | tf_op jit(solution)/shard_map/pallas_call | solution.py:546
  16.1 1.2 %collective-permute-start.6 = (f32[144,128]{1,0:T(8,128)S(1)}, f32[144,128]{1,0:T(8,128)S(1)}, u32[]{:S(2)}, u32[]{:S(2)}) collective-permute-start(f32[144,128]{1,0:T(8,128)S(1)} %get-tuple-element.66.refs_7_.refs_6_), channel_id=1, source_target_pairs={{0,16},{16,0},{1,17},{17,1},{2,18},{18,2},{3,19},{19,3},{4,20},{20... | collective-permute-start | bytes 221192 | tf_op jit(solution)/shard_map/ppermute | solution.py:79
  17.3 1.2 %shard_map.161 = (f32[19,64,128]{2,1,0:T(8,128)S(1)}, f32[64,128]{1,0:T(8,128)S(1)}, f32[64,128]{1,0:T(8,128)S(1)}, f32[22,16,128]{2,1,0:T(8,128)S(1)}, f32[22,1...) custom-call(f32[19,64,128]{2,1,0:T(8,128)S(1)} %bitcast.23, f32[19,64,128]{2,1,0:T(8,128)S(1)} %get-tuple-element.57.refs_7_.refs_1_, ...), custom_call_target="tpu_custom_call" | custom-call | flops 16777216 | bytes 1048576 | tf_op jit(solution)/shard_map/pallas_call | solution.py:546
  18.5 2.0 %collective-permute-done.6.refs_7_.refs_5_ = f32[144,128]{1,0:T(8,128)S(1)} collective-permute-done((f32[144,128]{1,0:T(8,128)S(1)}, f32[144,128]{1,0:T(8,128)S(1)}, u32[]{:S(2)}, u32[]{:S(2)}) %collective-permute-start.6) | collective-permute-done | bytes 73760 | tf_op jit(solution)/shard_map/ppermute | solution.py:79
  20.5 0.3 %shard_map.162 = (f32[7,64,128]{2,1,0:T(8,128)S(1)}, f32[64,128]{1,0:T(8,128)S(1)}, f32[64,128]{1,0:T(8,128)S(1)}, f32[22,16,128]{2,1,0:T(8,128)S(1)}, f32[22,16...) custom-call(s32[8,128]{1,0:T(8,128)S(1)} %get-tuple-element.48.refs_, ...), custom_call_target="tpu_custom_call" | custom-call | flops 1048576 | bytes 1048576 | tf_op jit(solution)/shard_map/pallas_call | solution.py:546
  20.9 1.2 %collective-permute-start.10 = (f32[22,16,128]{2,1,0:T(8,128)S(1)}, f32[22,16,128]{2,1,0:T(8,128)S(1)}, u32[]{:S(2)}, u32[]{:S(2)}) collective-permute-start(f32[22,16,128]{2,1,0:T(8,128)S(1)} %get-tuple-element.90), channel_id=1, source_target_pairs={{0,16},{1,2},{2,1},{3,19},{4,20},{5,6},{6,5},{7,23},{8,24},{9,10},... | collective-permute-start | bytes 540680 | tf_op jit(solution)/shard_map/ppermute | solution.py:665
  22.1 2.2 %collective-permute-start.7 = (f32[64,128]{1,0:T(8,128)S(1)}, f32[64,128]{1,0:T(8,128)S(1)}, u32[]{:S(2)}, u32[]{:S(2)}) collective-permute-start(f32[64,128]{1,0:T(8,128)S(1)} %get-tuple-element.87), channel_id=1, source_target_pairs={{0,4},{1,5},{2,6},{3,7},{4,0},{5,1},{6,2},{7,3},{8,12},{9,13},{10,... | collective-permute-start | bytes 98312 | tf_op jit(solution)/shard_map/ppermute | solution.py:662
  24.3 0.7 %shard_map.163 = (f32[64,128]{1,0:T(8,128)}, f32[64,128]{1,0:T(8,128)}, f32[64,128]{1,0:T(8,128)}, f32[64,128]{1,0:T(8,128)}) custom-call(f32[128,128]{1,0:T(8,128)S(1)} %get-tuple-element.76.refs_0_, f32[128,128]{1,0:T(8,128)S(1)} %get-tuple-element.77.refs_1_, f32[128,128]{1,0:T(8,128)S(1)} %get-tuple-element.78.refs_2_, ...), custom_call_target="tpu_custom_call" | custom-call | flops 16777216 | bytes 1048576 | tf_op jit(solution)/shard_map/pallas_call | solution.py:546
  25.0 0.9 %shard_map.164.refs_1_ = f32[19,64,128]{2,1,0:T(8,128)S(1)} custom-call(f32[19]{0:T(128)S(1)} %copy-done.2, f32[2,19,8,128]{3,2,1,0:T(8,128)S(1)} %get-tuple-element.50.refs_1_, f32[19,64,128]{2,1,0:T(8,128)S(1)} %get-tuple-element.84.refs_2_.refs_0_, f32[19,64,128]{2,1,0:T(8,128)S(1)} %get-tuple-element.85.refs_3_, ...), custom_call_target="tpu_custom_call" | custom-call | flops 16777216 | bytes 1048576 | tf_op jit(solution)/shard_map/pallas_call | solution.py:546
  25.8 0.3 %collective-permute-done.7.refs_3_ = f32[64,128]{1,0:T(8,128)S(1)} collective-permute-done((f32[64,128]{1,0:T(8,128)S(1)}, f32[64,128]{1,0:T(8,128)S(1)}, u32[]{:S(2)}, u32[]{:S(2)}) %collective-permute-start.7) | collective-permute-done | bytes 32800 | tf_op jit(solution)/shard_map/ppermute | solution.py:662
  26.1 0.3 collective-permute-done.10.refs_6_
  26.4 1.5 %shard_map.165 = f32[19,64,128]{2,1,0:T(8,128)} custom-call(f32[19,64,128]{2,1,0:T(8,128)S(1)} %get-tuple-element.84.refs_2_.refs_0_, f32[19,64,128]{2,1,0:T(8,128)S(1)} %shard_map.164.refs_1_, f32[7,64,128]{2,1,0:T(8,128)S(1)} %get-tuple-element.86.refs_4_.refs_2_, f32[64,128]{1,0:T(8,128)S(1)} %collective-permute-done.7.refs_3_, ...), custom_call_target="tpu_custom_call" | custom-call | flops 1048576 | bytes 1048576 | tf_op jit(solution)/shard_map/pallas_call | solution.py:546
  (26 shorter events, 0.4 us)
Async XLA Ops:
  1.6 3.1 %copy-start = (f32[19,16,4,128]{3,2,1,0:T(4,128)S(1)}, f32[19,16,4,128]{3,2,1,0:T(4,128)}, u32[]{:S(2)}) copy-start(f32[19,16,4,128]{3,2,1,0:T(4,128)} %param.17) | copy-start | bytes 1867780
  1.6 3.0 %copy-start.2 = (f32[19]{0:T(128)S(1)}, f32[19]{0:T(128)}, u32[]{:S(2)}) copy-start(f32[19]{0:T(128)} %refs_0_.5) | copy-start | bytes 232
  1.6 8.1 %collective-permute-start.1 = (f32[5,40,128]{2,1,0:T(8,128)S(1)}, f32[5,40,128]{2,1,0:T(8,128)S(1)}, u32[]{:S(2)}, u32[]{:S(2)}) collective-permute-start(f32[5,40,128]{2,1,0:T(8,128)S(1)} %shard_map.157), channel_id=1, source_target_pairs={{0,16},{16,0},{1,17},{17,1},{2,18},{18,2},{3,19},{19,3},{4,20},{20... | collective-permute-start | bytes 307208 | tf_op jit(solution)/shard_map/ppermute | solution.py:79
  4.6 1.7 %copy-start.1 = (f32[19,19]{1,0:T(8,128)S(1)}, f32[19,19]{1,0:T(8,128)}, u32[]{:S(2)}) copy-start(f32[19,19]{1,0:T(8,128)} %refs_5_.1) | copy-start | bytes 4336
  4.6 1.7 %copy-start.3 = (s32[4,128]{1,0:T(4,128)S(1)}, s32[4,128]{1,0:T(4,128)}, u32[]{:S(2)}) copy-start(s32[4,128]{1,0:T(4,128)} %refs_2_.1) | copy-start | bytes 6148
  4.7 1.7 %copy-start.4 = (f32[4,128]{1,0:T(4,128)S(1)}, f32[4,128]{1,0:T(4,128)}, u32[]{:S(2)}) copy-start(f32[4,128]{1,0:T(4,128)} %refs_3_.1) | copy-start | bytes 6148
  4.7 1.7 %copy-start.5 = (f32[19]{0:T(128)S(1)}, f32[19]{0:T(128)}, u32[]{:S(2)}) copy-start(f32[19]{0:T(128)} %refs_0_.3) | copy-start | bytes 232
  4.7 1.6 %copy-start.6 = (f32[19]{0:T(128)S(1)}, f32[19]{0:T(128)}, u32[]{:S(2)}) copy-start(f32[19]{0:T(128)} %refs_1_.1) | copy-start | bytes 232
  5.3 4.4 %collective-permute-start = (f32[144,128]{1,0:T(8,128)S(1)}, f32[144,128]{1,0:T(8,128)S(1)}, u32[]{:S(2)}, u32[]{:S(2)}) collective-permute-start(f32[144,128]{1,0:T(8,128)S(1)} %shard_map.155.refs_6_), channel_id=1, source_target_pairs={{0,16},{16,0},{1,17},{17,1},{2,18},{18,2},{3,19},{19,3},{4,20},{20... | collective-permute-start | bytes 221192 | tf_op jit(solution)/shard_map/ppermute | solution.py:79
  10.1 5.2 %collective-permute-start.4 = (f32[22,16,128]{2,1,0:T(8,128)S(1)}, f32[22,16,128]{2,1,0:T(8,128)S(1)}, u32[]{:S(2)}, u32[]{:S(2)}) collective-permute-start(f32[22,16,128]{2,1,0:T(8,128)S(1)} %get-tuple-element.60), channel_id=1, source_target_pairs={{0,1},{1,0},{2,3},{3,2},{4,5},{5,4},{6,7},{7,6},{8,9},{9,8},{10,11... | collective-permute-start | bytes 540680 | tf_op jit(solution)/shard_map/ppermute | solution.py:664
  10.2 5.6 %collective-permute-start.5 = (f32[22,16,128]{2,1,0:T(8,128)S(1)}, f32[22,16,128]{2,1,0:T(8,128)S(1)}, u32[]{:S(2)}, u32[]{:S(2)}) collective-permute-start(f32[22,16,128]{2,1,0:T(8,128)S(1)} %get-tuple-element.61), channel_id=1, source_target_pairs={{0,16},{1,2},{2,1},{3,19},{4,20},{5,6},{6,5},{7,23},{8,24},{9,10},... | collective-permute-start | bytes 540680 | tf_op jit(solution)/shard_map/ppermute | solution.py:665
  11.4 3.9 %collective-permute-start.2 = (f32[64,128]{1,0:T(8,128)S(1)}, f32[64,128]{1,0:T(8,128)S(1)}, u32[]{:S(2)}, u32[]{:S(2)}) collective-permute-start(f32[64,128]{1,0:T(8,128)S(1)} %get-tuple-element.58), channel_id=1, source_target_pairs={{0,4},{1,5},{2,6},{3,7},{4,0},{5,1},{6,2},{7,3},{8,12},{9,13},{10,... | collective-permute-start | bytes 98312 | tf_op jit(solution)/shard_map/ppermute | solution.py:662
  13.0 2.3 %collective-permute-start.3 = (f32[64,128]{1,0:T(8,128)S(1)}, f32[64,128]{1,0:T(8,128)S(1)}, u32[]{:S(2)}, u32[]{:S(2)}) collective-permute-start(f32[64,128]{1,0:T(8,128)S(1)} %get-tuple-element.59), channel_id=1, source_target_pairs={{0,1},{1,0},{2,3},{3,2},{4,8},{5,9},{6,10},{7,11},{8,4},{9,5},{10,... | collective-permute-start | bytes 98312 | tf_op jit(solution)/shard_map/ppermute | solution.py:663
  16.1 4.4 %collective-permute-start.6 = (f32[144,128]{1,0:T(8,128)S(1)}, f32[144,128]{1,0:T(8,128)S(1)}, u32[]{:S(2)}, u32[]{:S(2)}) collective-permute-start(f32[144,128]{1,0:T(8,128)S(1)} %get-tuple-element.66.refs_7_.refs_6_), channel_id=1, source_target_pairs={{0,16},{16,0},{1,17},{17,1},{2,18},{18,2},{3,19},{19,3},{4,20},{20... | collective-permute-start | bytes 221192 | tf_op jit(solution)/shard_map/ppermute | solution.py:79
  20.8 5.4 %collective-permute-start.9 = (f32[22,16,128]{2,1,0:T(8,128)S(1)}, f32[22,16,128]{2,1,0:T(8,128)S(1)}, u32[]{:S(2)}, u32[]{:S(2)}) collective-permute-start(f32[22,16,128]{2,1,0:T(8,128)S(1)} %get-tuple-element.89), channel_id=1, source_target_pairs={{0,1},{1,0},{2,3},{3,2},{4,5},{5,4},{6,7},{7,6},{8,9},{9,8},{10,11... | collective-permute-start | bytes 540680 | tf_op jit(solution)/shard_map/ppermute | solution.py:664
  20.9 5.6 %collective-permute-start.10 = (f32[22,16,128]{2,1,0:T(8,128)S(1)}, f32[22,16,128]{2,1,0:T(8,128)S(1)}, u32[]{:S(2)}, u32[]{:S(2)}) collective-permute-start(f32[22,16,128]{2,1,0:T(8,128)S(1)} %get-tuple-element.90), channel_id=1, source_target_pairs={{0,16},{1,2},{2,1},{3,19},{4,20},{5,6},{6,5},{7,23},{8,24},{9,10},... | collective-permute-start | bytes 540680 | tf_op jit(solution)/shard_map/ppermute | solution.py:665
  22.1 4.0 %collective-permute-start.7 = (f32[64,128]{1,0:T(8,128)S(1)}, f32[64,128]{1,0:T(8,128)S(1)}, u32[]{:S(2)}, u32[]{:S(2)}) collective-permute-start(f32[64,128]{1,0:T(8,128)S(1)} %get-tuple-element.87), channel_id=1, source_target_pairs={{0,4},{1,5},{2,6},{3,7},{4,0},{5,1},{6,2},{7,3},{8,12},{9,13},{10,... | collective-permute-start | bytes 98312 | tf_op jit(solution)/shard_map/ppermute | solution.py:662
  24.3 1.9 %collective-permute-start.8 = (f32[64,128]{1,0:T(8,128)S(1)}, f32[64,128]{1,0:T(8,128)S(1)}, u32[]{:S(2)}, u32[]{:S(2)}) collective-permute-start(f32[64,128]{1,0:T(8,128)S(1)} %get-tuple-element.88), channel_id=1, source_target_pairs={{0,1},{1,0},{2,3},{3,2},{4,8},{5,9},{6,10},{7,11},{8,4},{9,5},{10,... | collective-permute-start | bytes 98312 | tf_op jit(solution)/shard_map/ppermute | solution.py:663

commit v4 on v3

v4 whole, which is shorter than its diff:
```python
import functools

import jax
import jax.numpy as jnp
from jax import lax
from jax.experimental import pallas as pl
from jax.experimental.pallas import tpu as pltpu
from jax.sharding import PartitionSpec as P

STEPS = 2

WATER_ATTEN = 0.01
PIGMENT_ATTEN = 0.05
WARMING_UPTAKE = 5.0
WARM_EXPANSION = 0.2
SALT_EXPANSION = 0.8
CONVECT_MIX = 0.15
SIDE_DIFFUSE = 0.05
WARMING_FACTOR = 0.0633
TIME_STEP = 0.5

SUB = 8
AXES = ("grp", "gx", "gy")
VMEM_LIMIT = 48 * 1024 * 1024

F32 = jnp.float32


def vmem():
    return pl.BlockSpec(memory_space=pltpu.VMEM)


def hbm():
    return pl.BlockSpec(memory_space=pltpu.HBM)


def shape(*dims):
    return jax.ShapeDtypeStruct(dims, F32)


def turn(x, shift, axis):
    shift = shift % x.shape[axis]
    return x if shift == 0 else pltpu.roll(x, shift, axis)


def iota(x, axis):
    return lax.broadcasted_iota(jnp.int32, x, axis)


def pairing(sizes, axis, odd):
    size_g, size_x, size_y = sizes

    def partner(g, x, y):
        i, n = (x, size_x) if axis == "gx" else (y, size_y)
        j = i + 1 if i % 2 == odd else i - 1
        if 0 <= j < n:
            return (g, j, y) if axis == "gx" else (g, x, j)
        if axis == "gx":
            return (g, x, y ^ 1) if (y ^ 1) < size_y else (g, x, y)
        return (g ^ 1, x, y) if (g ^ 1) < size_g else (g, x, y)

    def index(g, x, y):
        return (g * size_x + x) * size_y + y

    return [
        (index(g, x, y), index(*partner(g, x, y)))
        for g in range(size_g)
        for x in range(size_x)
        for y in range(size_y)
    ]


def from_others(value, count):
    return [
        lax.ppermute(value, "grp", [(i, (i + k) % count) for i in range(count)])
        for k in range(1, count)
    ]


def chunks(n, parts):
    step = -(-n // parts)
    return [(a, min(step, n - a)) for a in range(0, n, step)]


class Refs:
    def __init__(self, refs):
        self.refs = list(refs)

    def take(self, n):
        out, self.refs = self.refs[:n], self.refs[n:]
        return out


def pick(mine, others, k):
    value = mine
    for at, other in enumerate(others):
        value = jnp.where(k == at + 1, other, value)
    return value


def pack_sides(c, slot, left, right):
    lane = iota(c.shape, 1)
    width = c.shape[1]
    left = jnp.where(lane == (2 * slot - 1) % width, turn(c, 2 * slot - 1, 1), left)
    right = jnp.where(lane == 2 * slot, turn(c, 2 * slot + 1, 1), right)
    return left, right


def compact(rows, cells, count):
    return count == 2 and SUB == 2 * rows and cells >= 2 * SUB


def level_base(rows, cells, count):
    if count != 2:
        return SUB
    return cells // 2 + SUB if compact(rows, cells, count) else cells


def message_shapes(tracers, rows, cells, width, count):
    height = level_base(rows, cells, count) + tracers * rows + (SUB - rows)
    height += -height % SUB
    if count == 2:
        return [shape(height, width)]
    return [shape(cells, width), shape(height, width), shape(height, width)]


def write_levels(last, first, t, rows, base, msgs, g):
    here = pl.ds(base + t * rows, rows)
    if len(msgs) == 1:
        msgs[0][here, :] = jnp.where(g == 0, last[SUB - rows :], first[:rows])
    else:
        msgs[1][here, :] = last[SUB - rows :]
        msgs[2][here, :] = first[:rows]


def in_strip(rows, count, width, member):
    at_row = lax.rem(iota((SUB, width), 0), rows)
    strip = rows // count
    return (at_row >= member * strip) & (at_row < (member + 1) * strip)


def write_pigment(rows, count, p_ref, msg, g):
    cells, width = p_ref.shape
    if not compact(rows, cells, count):
        msg[pl.ds(0, cells), :] = p_ref[...]
        return
    levels, strip = cells // rows, rows // count
    for r in range(strip):
        msg[pl.ds(r, levels, stride=strip), :] = jnp.where(
            g == 0, p_ref[pl.ds(strip + r, levels, stride=rows), :], p_ref[pl.ds(r, levels, stride=rows), :]
        )
    blocks = [p_ref[pl.ds(at, SUB), :] for at in range(0, cells, SUB)]
    inner = blocks[1]
    for block in blocks[2:-1]:
        inner = inner + block
    inner = jnp.zeros_like(inner) if len(blocks) == 2 else inner
    near = jnp.where(g == 0, blocks[-1], blocks[0])
    rest = inner + jnp.where(g == 0, blocks[0], blocks[-1])
    rest = rest + turn(rest, rows, 0)
    msg[pl.ds(cells // 2, SUB), :] = jnp.where(in_strip(rows, count, width, g), near, turn(rest, strip, 0))


def read_pigment(rows, count, msg, other_s, g):
    cells, width = other_s.shape
    if not compact(rows, cells, count):
        return msg[pl.ds(0, cells), :]
    levels, strip = cells // rows, rows // count
    for s in range(count):
        for r in range(strip):
            other_s[pl.ds(s * strip + r, levels, stride=rows), :] = jnp.where(
                g == s, msg[pl.ds(r, levels, stride=strip), :], 0.0
            )
    edge = msg[pl.ds(cells // 2, SUB), :]
    theirs = in_strip(rows, count, width, 1 - g)
    first = other_s[pl.ds(0, SUB), :]
    rest = jnp.where(iota((SUB, width), 0) < rows, turn(edge, strip, 0), 0.0)
    other_s[pl.ds(0, SUB), :] = jnp.where(theirs, jnp.where(g == 0, edge, rest), first)
    last = other_s[pl.ds(cells - SUB, SUB), :]
    other_s[pl.ds(cells - SUB, SUB), :] = jnp.where(theirs & (g == 1), edge, last)
    return other_s[...]


def raw_window(rows, count, strip_cells, member):
    if count != 2:
        return 0, strip_cells
    height = strip_cells // 2 + 2 * (rows // count)
    return member * (strip_cells - height), height


def first_kernel(out_ref):
    out_ref[...] = jnp.zeros(out_ref.shape, F32)


def raw_kernel(rows, count, first_ref, pig_in, *refs):
    *fields, raw_ref, out_ref, pig_out = refs
    g = lax.axis_index("grp")
    pig_out[...] = pig_in[...]
    strip_cells = raw_ref.shape[1]
    low, height = raw_window(rows, count, strip_cells, 0)
    high, _ = raw_window(rows, count, strip_cells, 1)
    for at, field in enumerate(fields):
        raw_ref[at] = field[...]
        lower_part, upper_part = field[pl.ds(low, height), :], field[pl.ds(high, height), :]
        out_ref[pl.ds(at * height, height), :] = jnp.where(g == 0, upper_part, lower_part)


def tile(v, cells):
    width = v.shape[1]
    return jnp.broadcast_to(v[None], (cells // SUB, SUB, width)).reshape(cells, width)


def prep_kernel(rows, count, pig_ref, c_ref, p_ref, *msgs):
    g = lax.axis_index("grp")
    tracers, cells, width = c_ref.shape
    base = level_base(rows, cells, count)
    weights = pig_ref[...]
    pigment = jnp.zeros((cells, width), F32)
    for t in range(tracers):
        c = c_ref[t]
        pigment = pigment + tile(jnp.broadcast_to(weights[:, t : t + 1], (SUB, width)), cells) * c
        write_levels(c[cells - SUB :], c[:SUB], t, rows, base, msgs, g)
    p_ref[...] = pigment
    write_pigment(rows, count, p_ref, msgs[0], g)


def halves(v):
    high = v.astype(jnp.bfloat16)
    return high, (v - high.astype(F32)).astype(jnp.bfloat16)


def dot(a, b, **kw):
    return jnp.dot(a, b, preferred_element_type=F32, **kw)


def spread_rates(rates, tracers):
    exact = functools.partial(dot, precision=lax.Precision.HIGHEST)
    depth = tracers * SUB
    spread = jnp.where(iota((depth, tracers), 0) // SUB == iota((depth, tracers), 1), 1.0, 0.0)
    spread_t = jnp.where(iota((tracers, depth), 1) // SUB == iota((tracers, depth), 0), 1.0, 0.0)
    weights = exact(exact(spread, rates), spread_t)
    return jnp.where(
        lax.rem(iota((depth, depth), 0), SUB) == lax.rem(iota((depth, depth), 1), SUB), weights, 0.0
    )


def mix(weights, c_ref, mix_ref):
    tracers, cells, width = c_ref.shape
    w_high, w_low = halves(weights)
    for b in range(cells // SUB):
        here = pl.ds(b * SUB, SUB)
        c_high, c_low = halves(c_ref[:, here, :].reshape(tracers * SUB, width))
        mixed = dot(w_high, c_high) + (dot(w_high, c_low) + dot(w_low, c_high))
        mix_ref[:, here, :] = mixed.reshape(tracers, SUB, width)


def pack(rows, c_ref, p_ref, msg_xa, msg_xb, msg_ya, msg_yb):
    tracers, cells, _ = c_ref.shape
    levels = cells // rows
    x_even = lax.rem(lax.axis_index("gx"), 2) == 0
    y_even = lax.rem(lax.axis_index("gy"), 2) == 0
    left = right = jnp.zeros(c_ref.shape[1:], F32)
    left, right = pack_sides(p_ref[...], tracers + 2, left, right)
    for t in range(tracers):
        left, right = pack_sides(c_ref[t], t, left, right)
    msg_xa[...] = jnp.where(x_even, right, left)
    msg_xb[...] = jnp.where(x_even, left, right)

    def put(slot, first, last):
        msg_ya[slot] = jnp.where(y_even, last, first)
        msg_yb[slot] = jnp.where(y_even, first, last)

    for t in range(tracers):
        put(
            t,
            c_ref[t, pl.ds(0, levels, stride=rows), :],
            c_ref[t, pl.ds(rows - 1, levels, stride=rows), :],
        )
    put(
        tracers + 2,
        p_ref[pl.ds(0, levels, stride=rows), :],
        p_ref[pl.ds(rows - 1, levels, stride=rows), :],
    )


def pack_kernel(rows, *refs):
    refs = Refs(refs)
    photo_ref, sat_ref, pig_ref, depth_in, solar_in, c_ref, rates_ref, p_ref = refs.take(8)
    msg_xa, msg_xb, msg_ya, msg_yb, w_ref, mix_ref, tiles_ref, depth_ref, solar_ref = refs.take(9)
    tracers, cells, width = c_ref.shape
    for r in range(0, SUB, rows):
        depth_ref[pl.ds(r, rows), :] = depth_in[...]
        solar_ref[pl.ds(r, rows), :] = solar_in[...]
    for at, param in enumerate((photo_ref, sat_ref, pig_ref)):
        values = param[...]
        for t in range(tracers):
            tiles_ref[at, t] = jnp.broadcast_to(values[:, t : t + 1], (SUB, width))
    pack(rows, c_ref, p_ref, msg_xa, msg_xb, msg_ya, msg_yb)
    weights = spread_rates(rates_ref[...], tracers)
    w_ref[...] = weights
    mix(weights, c_ref, mix_ref)


def ocean_kernel(rows, count, tracers, first_step, *refs):
    refs = Refs(refs)
    depth_ref, solar_ref = refs.take(2)
    in_xa, in_xb, in_ya, in_yb = refs.take(4)
    p_own, *p_others = refs.take(count)
    if first_step:
        own_fields, *other_fields = refs.take(count)
    else:
        fields = refs.take(5)
    band_ref, msg_xa, msg_xb, msg_ya, msg_yb = refs.take(5)
    full_out = refs.take(5 if first_step else 4)
    p_full, p_other_s = refs.take(2)
    if first_step:
        fields = refs.take(5)
        other_s = refs.take(5 * (count - 1))
    face_s, par_s, wet_s = refs.take(3)
    g = lax.axis_index("grp")
    cells, width = in_xa.shape
    levels = cells // rows
    total = count * cells
    all_levels = total // rows
    strip = rows // count

    pigments = [read_pigment(rows, count, o, p_other_s, g) for o in p_others]
    for b in range(count):
        k = lax.rem(g - b + count, count)
        p_full[pl.ds(b * cells, cells), :] = pick(p_own[...], pigments, k)
    if first_step:
        strip_cells = all_levels * strip
        for at in range(5):
            for k in range(count - 1):
                other = other_s[5 * k + at]
                low, height = raw_window(rows, count, strip_cells, 0)
                value = other_fields[k][pl.ds(at * height, height), :]
                if count != 2:
                    other[...] = value
                    continue
                high, _ = raw_window(rows, count, strip_cells, 1)
                other[...] = jnp.zeros((strip_cells, width), F32)
                other[pl.ds(low, height), :] = jnp.where(g == 0, value, 0.0)
                kept = jnp.where(iota(value.shape, 0) < low + height - high, other[pl.ds(high, height), :], 0.0)
                other[pl.ds(high, height), :] = jnp.where(g == 1, value, kept)
            for s in range(count):
                k = lax.rem(g - s + count, count)
                for r in range(strip):
                    here = pl.ds(r, all_levels, stride=strip)
                    fields[at][pl.ds(s * strip + r, all_levels, stride=rows), :] = pick(
                        own_fields[at, here, :], [other_s[5 * j + at][here, :] for j in range(count - 1)], k
                    )

    row = iota((total, width), 0)
    wet = jnp.where(row // rows < tile(depth_ref[...], total), 1.0, 0.0)
    att = WATER_ATTEN + PIGMENT_ATTEN * p_full[...]
    summed = att
    step = rows
    while step < total:
        summed = summed + jnp.where(row >= step, turn(summed, step, 0), 0.0)
        step *= 2
    top = tile(solar_ref[...], total) * jnp.exp(att - summed)
    par = top * jnp.exp(-0.5 * att)
    east, north, temp, sal, mixing = [f[...] for f in fields]
    temp = temp + WARMING_UPTAKE * (top * (1.0 - jnp.exp(-att))) * wet

    def below(v):
        return turn(v, -rows, 0)

    density = SALT_EXPANSION * sal - WARM_EXPANSION * temp
    face = 0.5 * (mixing + below(mixing)) + CONVECT_MIX / (1.0 + jnp.exp(below(density) - density))
    face = jnp.where(row < total - rows, face * below(wet), 0.0)

    def stir(v):
        flux = face * (below(v) - v)
        return v + flux - turn(flux, rows, 0)

    for at, v in enumerate((east, north, temp, sal)):
        full_out[at][...] = stir(v)
    if first_step:
        full_out[4][...] = mixing
    face_s[...] = face
    par_s[...] = par
    wet_s[...] = wet

    band = pl.ds(pl.multiple_of(g * cells, SUB), cells)
    above = pl.ds(pl.multiple_of(lax.max(g * cells - SUB, 0), SUB), SUB)
    face_band = face_s[band, :]
    lifted = turn(jnp.concatenate([face_s[above, :], face_band], axis=0), rows, 0)[SUB:]
    lifted = jnp.where((iota((cells, width), 0) < rows) & (g == 0), 0.0, lifted)
    u = full_out[0][band, :]
    wet_band = wet_s[band, :]
    band_ref[0] = u
    band_ref[1] = full_out[1][band, :]
    band_ref[2] = full_out[2][band, :]
    band_ref[3] = face_band
    band_ref[4] = lifted
    band_ref[5] = par_s[band, :]
    band_ref[6] = wet_band

    x_even = lax.rem(lax.axis_index("gx"), 2) == 0
    y_even = lax.rem(lax.axis_index("gy"), 2) == 0
    xa, xb = in_xa[...], in_xb[...]
    left, right = jnp.where(x_even, xb, xa), jnp.where(x_even, xa, xb)
    left, right = pack_sides(wet_band, tracers + 1, left, right)
    _, right = pack_sides(u, tracers, left, right)
    msg_xa[...] = jnp.where(x_even, right, left)
    msg_xb[...] = jnp.where(x_even, left, right)
    for t in (*range(tracers), tracers + 2):
        msg_ya[t] = in_ya[t]
        msg_yb[t] = in_yb[t]
    speed = band_ref[1, pl.ds(rows - 1, levels, stride=rows), :]
    wet_first = band_ref[6, pl.ds(0, levels, stride=rows), :]
    wet_last = band_ref[6, pl.ds(rows - 1, levels, stride=rows), :]
    msg_ya[tracers] = speed
    msg_yb[tracers] = speed
    msg_ya[tracers + 1] = jnp.where(y_even, wet_last, wet_first)
    msg_yb[tracers + 1] = jnp.where(y_even, wet_first, wet_last)


def start_own_strip(rows, count, g, full, outs, strips, sems):
    strip = rows // count
    all_levels = full[0].shape[0] // rows
    copies = [pltpu.make_async_copy(strips[at], outs[at], sems.at[at]) for at in range(4)]
    for at in range(4):
        for r in range(strip):
            value = full[at][pl.ds(r, all_levels, stride=rows), :]
            for s in range(1, count):
                value = jnp.where(g == s, full[at][pl.ds(s * strip + r, all_levels, stride=rows), :], value)
            strips[at][pl.ds(r, all_levels, stride=strip), :] = value
        copies[at].start()
    return copies


def lower(opening, speed):
    return opening * (jnp.maximum(speed, 0.0) + SIDE_DIFFUSE)


def upper(opening, speed):
    return opening * (jnp.minimum(speed, 0.0) - SIDE_DIFFUSE)


def inner_kernel(rows, count, last_step, *refs):
    refs = Refs(refs)
    tiles_ref, c_ref, mix_ref, band_ref = refs.take(4)
    lev_in = refs.take(1 if count == 2 else 2)
    if last_step:
        full = refs.take(4)
    (part_ref,) = refs.take(1)
    if last_step:
        outs, strips = refs.take(4), refs.take(4)
        (sems,) = refs.take(1)
        copies = start_own_strip(rows, count, lax.axis_index("grp"), full, outs, strips, sems)
    else:
        (p_part,) = refs.take(1)
    tracers, cells, width = c_ref.shape
    base = level_base(rows, cells, count)
    lane = iota((cells, width), 1)
    at_row = lax.rem(iota((cells, width), 0), rows)
    u = band_ref[0]
    v = band_ref[1]
    wet = band_ref[6]

    def west(x):
        return turn(x, 1, 1)

    def east(x):
        return turn(x, -1, 1)

    def south(x):
        return turn(x, 1, 0)

    def north(x):
        return turn(x, -1, 0)

    open_w = jnp.where(lane == 0, 0.0, wet * west(wet))
    open_e = jnp.where(lane == width - 1, 0.0, wet * east(wet))
    open_s = jnp.where(at_row == 0, 0.0, wet * south(wet))
    open_n = jnp.where(at_row == rows - 1, 0.0, wet * north(wet))
    k_w = lower(open_w, west(u))
    k_e = -upper(open_e, u)
    k_s = lower(open_s, south(v))
    k_n = -upper(open_n, v)
    k_d = band_ref[3]
    k_u = band_ref[4]
    k_c = (upper(open_w, west(u)) - lower(open_e, u)) + (upper(open_s, south(v)) - lower(open_n, v))
    k_c = 1.0 + (k_c - k_d - k_u)
    par = band_ref[5]
    lit = TIME_STEP * wet
    warm = lit * jnp.exp(WARMING_FACTOR * (band_ref[2] - 20.0))
    lit = lit * par
    pigment = jnp.zeros((cells, width), F32)
    for t in range(tracers):
        c = c_ref[t]
        at = base + t * rows
        up8 = lev_in[0][pl.ds(at + rows - SUB, SUB), :]
        down8 = lev_in[-1][pl.ds(at, SUB), :]
        c_u = turn(jnp.concatenate([up8, c], axis=0), rows, 0)[SUB:]
        c_d = turn(jnp.concatenate([c, down8], axis=0), -rows, 0)[:cells]
        part = (
            (k_c + tile(tiles_ref[0, t], cells) * (lit / (par + tile(tiles_ref[1, t], cells)))) * c
            + (k_u * c_u + k_d * c_d)
            + (k_w * west(c) + k_e * east(c))
            + (k_s * south(c) + k_n * north(c))
            + warm * mix_ref[t]
        )
        part_ref[t] = part
        if not last_step:
            pigment = pigment + tile(tiles_ref[2, t], cells) * part
    if last_step:
        for copy in copies:
            copy.wait()
    else:
        p_part[...] = pigment


def x_halo(got_xa, got_xb):
    x_even = lax.rem(lax.axis_index("gx"), 2) == 0
    xa, xb = got_xa[...], got_xb[...]
    lane = iota(xa.shape, 1)
    return jnp.where((lax.rem(lane, 2) == 0) == x_even, xb, xa)


def spread_rows(rows, got_ya, got_yb, out_ref, slot):
    y_even = lax.rem(lax.axis_index("gy"), 2) == 0
    levels = got_ya.shape[1]
    ya, yb = got_ya[slot], got_yb[slot]
    out_ref[slot, pl.ds(0, levels, stride=rows), :] = jnp.where(y_even, yb, ya)
    out_ref[slot, pl.ds(rows - 1, levels, stride=rows), :] = jnp.where(y_even, ya, yb)


def side_factors(rows, sizes, halo, spread_s, band_ref, tracers):
    _, size_x, size_y = sizes
    x = lax.axis_index("gx")
    y = lax.axis_index("gy")
    u = band_ref[0]
    v = band_ref[1]
    wet = band_ref[6]
    shape2 = wet.shape
    lane = iota(shape2, 1)
    at_row = lax.rem(iota(shape2, 0), rows)
    at_w, at_e, at_s, at_n = lane == 0, lane == shape2[1] - 1, at_row == 0, at_row == rows - 1
    wet_x = wet * turn(halo, -2 * (tracers + 1), 1)
    wet_y = wet * spread_s[tracers + 1]
    open_w = jnp.where(at_w & (x > 0), wet_x, 0.0)
    open_e = jnp.where(at_e & (x < size_x - 1), wet_x, 0.0)
    open_s = jnp.where(at_s & (y > 0), wet_y, 0.0)
    open_n = jnp.where(at_n & (y < size_y - 1), wet_y, 0.0)
    u_w = turn(halo, -2 * tracers, 1)
    v_s = jnp.where(at_s, spread_s[tracers], 0.0)
    k_x = lower(open_w, u_w) - upper(open_e, u)
    k_y = lower(open_s, v_s) - upper(open_n, v)
    k_c = (upper(open_w, u_w) - lower(open_e, u)) + (upper(open_s, v_s) - lower(open_n, v))
    return k_x, k_y, k_c


def sideways(rows, factors, halo, outer, c, slot):
    k_x, k_y, k_c = factors
    at_row = lax.rem(iota(c.shape, 0), rows)
    edge = (at_row == 0) | (at_row == rows - 1)
    return (k_x * turn(halo, -2 * slot, 1) + k_c * c) + jnp.where(edge, k_y * outer, 0.0)


def early_kernel(rows, count, sizes, *refs):
    refs = Refs(refs)
    c_ref, band_ref, got_xa, got_xb, got_ya, got_yb, p_in, part_ref, p_part = refs.take(9)
    k_ref, halo_ref, spread_s, p_ref = refs.take(4)
    msgs = refs.refs
    g = lax.axis_index("grp")
    tracers, cells, width = c_ref.shape
    base = level_base(rows, cells, count)
    halo = x_halo(got_xa, got_xb)
    halo_ref[...] = halo
    for slot in range(tracers + 3):
        spread_rows(rows, got_ya, got_yb, spread_s, slot)
    factors = side_factors(rows, sizes, halo, spread_s, band_ref, tracers)
    for at, k in enumerate(factors):
        k_ref[at] = k
    slot = tracers + 2
    p_ref[...] = p_part[...] + sideways(rows, factors, halo, spread_s[slot], p_in[...], slot)
    write_pigment(rows, count, p_ref, msgs[0], g)

    def block(at, t):
        here = pl.ds(at, SUB)
        cut = [k[at : at + SUB] for k in factors]
        change = sideways(rows, cut, halo[at : at + SUB], spread_s[t, here, :], c_ref[t, here, :], t)
        return part_ref[t, here, :] + change

    for t in range(tracers):
        write_levels(block(cells - SUB, t), block(0, t), t, rows, base, msgs, g)


def step_kernel(rows, *refs):
    refs = Refs(refs)
    c_ref, part_ref, k_ref, halo_ref, spread_s, w_ref, p_ref = refs.take(7)
    out_ref, msg_xa, msg_xb, msg_ya, msg_yb, mix_ref = refs.take(6)
    tracers = c_ref.shape[0]
    factors = [k_ref[i] for i in range(3)]
    halo = halo_ref[...]
    for t in range(tracers):
        out_ref[t] = part_ref[t] + sideways(rows, factors, halo, spread_s[t], c_ref[t], t)
    pack(rows, out_ref, p_ref, msg_xa, msg_xb, msg_ya, msg_yb)
    mix(w_ref[...], out_ref, mix_ref)


def final_kernel(rows, sizes, *refs):
    refs = Refs(refs)
    c_ref, part_ref, band_ref, got_xa, got_xb, got_ya, got_yb = refs.take(7)
    out_hbm, spread_s, new_s, sems = refs.take(4)
    tracers = c_ref.shape[0]
    halo = x_halo(got_xa, got_xb)
    for slot in (tracers, tracers + 1):
        spread_rows(rows, got_ya, got_yb, spread_s, slot)
    factors = side_factors(rows, sizes, halo, spread_s, band_ref, tracers)
    copies = []
    for i, (a, n) in enumerate(chunks(tracers, sems.shape[0])):
        for t in range(a, a + n):
            spread_rows(rows, got_ya, got_yb, spread_s, t)
            new_s[t] = part_ref[t] + sideways(rows, factors, halo, spread_s[t], c_ref[t], t)
        copies.append(pltpu.make_async_copy(new_s.at[pl.ds(a, n)], out_hbm.at[pl.ds(a, n)], sems.at[i]))
        copies[-1].start()
    for copy in copies:
        copy.wait()


def call(kernel, ins, outs, in_specs=None, out_specs=None, scratch=(), flops=1 << 20, vmem_limit=VMEM_LIMIT):
    return pl.pallas_call(
        kernel,
        in_specs=[vmem() for _ in ins] if in_specs is None else in_specs,
        out_specs=[vmem() for _ in outs] if out_specs is None else out_specs,
        out_shape=outs,
        scratch_shapes=list(scratch),
        compiler_params=pltpu.CompilerParams(vmem_limit_bytes=vmem_limit),
        cost_estimate=pl.CostEstimate(flops=flops, bytes_accessed=1 << 20, transcendentals=0),
    )(*ins)


def per_device(
    sizes,
    zonal_boundary_speed,
    meridional_boundary_speed,
    potential_warmth,
    saltiness_field,
    quiescent_mixing_profile,
    substance_amounts,
    submerged_layer_number,
    solar_radiation,
    interaction_rates,
    photosynthetic_rates,
    saturation_irradiance,
    pigment_per_tracer,
):
    count = sizes[0]
    result_dimensions = zonal_boundary_speed.shape
    all_levels, _, strip, width = result_dimensions
    tracers, levels, rows, _ = substance_amounts.shape
    cells = levels * rows
    total = all_levels * rows
    strip_cells = all_levels * strip
    dma = pltpu.SemaphoreType.DMA
    column = pltpu.VMEM((total, width), F32)
    band_s = pltpu.VMEM((cells, width), F32)

    own = [
        f.reshape(strip_cells, width)
        for f in (
            zonal_boundary_speed,
            meridional_boundary_speed,
            potential_warmth,
            saltiness_field,
            quiescent_mixing_profile,
        )
    ]
    _, height = raw_window(rows, count, strip_cells, 0)
    params = [
        p.reshape(1, tracers) for p in (photosynthetic_rates, saturation_irradiance, pigment_per_tracer)
    ]
    (first,) = call(first_kernel, [], [shape(SUB, width)], flops=1 << 30)
    raw, window, pig = call(
        functools.partial(raw_kernel, rows, count),
        [first, params[2], *own],
        [shape(5, strip_cells, width), shape(5 * height, width), shape(1, tracers)],
    )
    raw_others = from_others(window, count)

    msg_levels = message_shapes(tracers, rows, cells, width, count)
    cols = shape(cells, width)
    lines = shape(tracers + 3, levels, width)
    sides = [cols, cols, lines, lines]
    field = shape(tracers, cells, width)
    c = substance_amounts.reshape(tracers, cells, width)
    pigment, *msgs = call(
        functools.partial(prep_kernel, rows, count),
        [pig, c],
        [cols, *msg_levels],
    )
    full = None
    for step in range(STEPS):
        first_step, last_step = step == 0, step == STEPS - 1
        p_others = from_others(msgs[0], count)
        if count == 2:
            lev = p_others
        else:
            lev = [
                lax.ppermute(msgs[1], "grp", [(i, (i + 1) % count) for i in range(count)]),
                lax.ppermute(msgs[2], "grp", [((i + 1) % count, i) for i in range(count)]),
            ]
        if first_step:
            xa, xb, ya, yb, weights, mixed, tiles, depth, solar = call(
                functools.partial(pack_kernel, rows),
                [
                    *params,
                    submerged_layer_number,
                    solar_radiation,
                    c,
                    interaction_rates,
                    pigment,
                ],
                [
                    *sides,
                    shape(tracers * SUB, tracers * SUB),
                    field,
                    shape(3, tracers, SUB, width),
                    jax.ShapeDtypeStruct((SUB, width), jnp.int32),
                    shape(SUB, width),
                ],
                flops=1 << 24,
            )
        band, xa, xb, ya, yb, *full = call(
            functools.partial(ocean_kernel, rows, count, tracers, first_step),
            [depth, solar, xa, xb, ya, yb, pigment, *p_others, *([raw, *raw_others] if first_step else full)],
            [shape(7, cells, width), *sides, *[shape(total, width)] * (5 if first_step else 4)],
            scratch=[column, band_s]
            + [column] * (5 if first_step else 0)
            + [pltpu.VMEM((strip_cells, width), F32)] * (5 * (count - 1) if first_step else 0)
            + [column] * 3,
        )
        xa = lax.ppermute(xa, AXES, pairing(sizes, "gx", 0))
        xb = lax.ppermute(xb, AXES, pairing(sizes, "gx", 1))
        ya = lax.ppermute(ya, AXES, pairing(sizes, "gy", 0))
        yb = lax.ppermute(yb, AXES, pairing(sizes, "gy", 1))
        part, *rest = call(
            functools.partial(inner_kernel, rows, count, last_step),
            [tiles, c, mixed, band, *lev, *(full if last_step else [])],
            [field] + ([shape(strip_cells, width)] * 4 if last_step else [cols]),
            out_specs=[vmem()] + ([hbm()] * 4 if last_step else [vmem()]),
            scratch=[pltpu.VMEM((strip_cells, width), F32)] * 4 + [dma((4,))] if last_step else [],
            flops=1 << 24,
        )
        if not last_step:
            k, halo, spread, pigment_next, *msgs = call(
                functools.partial(early_kernel, rows, count, sizes),
                [c, band, xa, xb, ya, yb, pigment, part, *rest],
                [shape(3, cells, width), cols, shape(tracers + 3, cells, width), cols, *msg_levels],
            )
            pigment = pigment_next
            c, xa, xb, ya, yb, mixed = call(
                functools.partial(step_kernel, rows),
                [c, part, k, halo, spread, weights, pigment],
                [field, *sides, field],
                flops=1 << 24,
            )
        else:
            ocean = rest
            (c,) = call(
                functools.partial(final_kernel, rows, sizes),
                [c, part, band, xa, xb, ya, yb],
                [field],
                out_specs=[hbm()],
                scratch=[
                    pltpu.VMEM((tracers + 3, cells, width), F32),
                    pltpu.VMEM((tracers, cells, width), F32),
                    dma((5,)),
                ],
            )
    return tuple(f.reshape(result_dimensions) for f in ocean) + (c.reshape(substance_amounts.shape),)


def solution(mesh):
    ocean = P(None, "gy", "grp", "gx")
    tracer = P(None, "grp", "gy", "gx")
    surface = P("gy", "gx")
    sizes = tuple(mesh.shape[a] for a in AXES)
    return jax.shard_map(
        functools.partial(per_device, sizes),
        mesh=mesh,
        in_specs=(ocean,) * 5 + (tracer, surface, surface) + (P(),) * 4,
        out_specs=(ocean,) * 4 + (tracer,),
        check_vma=False,
    )
```

time: 28.1 us -> 26.8 us (0.954)
  Pallas kernels: 8.62 us -> 6.4 us
  local copies, waits for them, and re-layouts: 0.04 us -> 1.53 us
  other arithmetic: 0.93 us -> 0 us
  waiting for transfers between devices: 5.75 us -> 6.27 us
  starting transfers between devices: 11.8 us -> 11.4 us
    pallas_call x11, Pallas kernels: 8.62 us -> 6.4 us  [call(): pl.pallas_call(kernel, in_specs=[vmem() for _ in ins] if in_specs is None...]
    unnamed x14 -> x24, local copies, waits for them, and re-layouts: 0.04 us -> 1.53 us
    select_n x1 -> x0, other arithmetic: 0.92 us -> none  [per_device(): raw = jnp.where(which == at, own[at][None], raw)]
    ppermute x3, starting transfers between devices: 5.25 us -> 4.68 us  [from_others(): lax.ppermute(value, 'grp', [(i, (i + k) % count) for i in range(count)])]
    ppermute x3, waiting for transfers between devices: 3.52 us -> 4 us  [from_others(): lax.ppermute(value, 'grp', [(i, (i + k) % count) for i in range(count)])]
    ppermute x2, waiting for transfers between devices: 1.56 us -> 1.97 us  [per_device(): xa = lax.ppermute(xa, AXES, pairing(sizes, 'gx', 0))]
    ppermute x2, starting transfers between devices: 2.49 us -> 2.86 us  [per_device(): yb = lax.ppermute(yb, AXES, pairing(sizes, 'gy', 1))]
    ppermute x2, waiting for transfers between devices: 0.66 us -> 0.29 us  [per_device(): yb = lax.ppermute(yb, AXES, pairing(sizes, 'gy', 1))]
  transfers between devices with their start and end apart: 11 -> 11, of which waited for: 6 -> 6; matrix products, arithmetic and copies ran while one was open for 0% -> 0% of each run, Pallas kernels for 22% -> 17%
where the time goes in v4:
time: 26.8 us; the launch traced here: 26.4 us
  starting transfers between devices  11.4 us (43%)
  Pallas kernels  6.4 us (24%)
  waiting for transfers between devices  6.27 us (23%)
  local copies, waits for them, and re-layouts  1.53 us (6%)
  between operations  0.78 us (3%)
    pallas_call x11, Pallas kernels, call(): pl.pallas_call(kernel, in_specs=[vmem() for _ in ins] if in_specs is None...  6.4 us
    ppermute x3, starting transfers between devices, from_others(): lax.ppermute(value, 'grp', [(i, (i + k) % count) for i in range(count)])  4.68 us
    ppermute x3, waiting for transfers between devices, from_others(): lax.ppermute(value, 'grp', [(i, (i + k) % count) for i in range(count)])  4 us
    ppermute x2, starting transfers between devices, per_device(): xa = lax.ppermute(xa, AXES, pairing(sizes, 'gx', 0))  3.72 us
    ppermute x2, starting transfers between devices, per_device(): yb = lax.ppermute(yb, AXES, pairing(sizes, 'gy', 1))  2.86 us
    ppermute x2, waiting for transfers between devices, per_device(): xa = lax.ppermute(xa, AXES, pairing(sizes, 'gx', 0))  1.97 us
    unnamed x24, local copies, waits for them, and re-layouts  1.53 us
  transfers between devices with their start and end apart: 11, of which 6 were waited for; matrix products, arithmetic and copies ran while one was open for 0% of the time, Pallas kernels for 17%

profile of v4, /device:TPU:0, one launch (start us, length us, event | category | flops | bytes accessed | tf_op | source)
XLA Modules:
  0.0 26.4 jit_solution(16173533324253353699)
XLA Ops:
  0.7 0.7 %copy-done.1 = f32[32,1,2,128]{3,2,1,0:T(2,128)S(1)} copy-done((f32[32,1,2,128]{3,2,1,0:T(2,128)S(1)}, f32[32,1,2,128]{3,2,1,0:T(2,128)}, u32[]{:S(2)}) %copy-start.1) | copy-done | bytes 32792
  1.6 3.0 %collective-permute-start.1 = (f32[180,128]{1,0:T(8,128)S(1)}, f32[180,128]{1,0:T(8,128)S(1)}, u32[]{:S(2)}, u32[]{:S(2)}) collective-permute-start(f32[180,128]{1,0:T(8,128)S(1)} %get-tuple-element.68), channel_id=1, source_target_pairs={{0,16},{16,0},{1,17},{17,1},{2,18},{18,2},{3,19},{19,3},{4,20},{20... | collective-permute-start | bytes 276488 | tf_op jit(solution)/shard_map/ppermute | solution.py:75
  4.6 0.1 shard_map.157
  4.7 0.2 collective-permute-start
  4.9 0.3 %copy-done.6 = f32[19,19]{1,0:T(8,128)S(1)} copy-done((f32[19,19]{1,0:T(8,128)S(1)}, f32[19,19]{1,0:T(8,128)}, u32[]{:S(2)}) %copy-start.6) | copy-done | bytes 1468
  5.3 0.3 %copy-done.8 = f32[4,128]{1,0:T(4,128)S(1)} copy-done((f32[4,128]{1,0:T(4,128)S(1)}, f32[4,128]{1,0:T(4,128)}, u32[]{:S(2)}) %copy-start.8) | copy-done | bytes 2072
  5.6 1.3 %shard_map.158 = (f32[64,128]{1,0:T(8,128)S(1)}, f32[64,128]{1,0:T(8,128)S(1)}, f32[22,16,128]{2,1,0:T(8,128)S(1)}, f32[22,16,128]{2,1,0:T(8,128)S(1)}, f32[152,...) custom-call(f32[1,19]{1,0:T(1,128)S(1)} %bitcast.34, ...), custom_call_target="tpu_custom_call" | custom-call | flops 16777216 | bytes 1048576 | tf_op jit(solution)/shard_map/pallas_call | solution.py:626
  7.0 2.0 %collective-permute-done.refs_7_.refs_4_ = f32[120,128]{1,0:T(8,128)S(1)} collective-permute-done((f32[120,128]{1,0:T(8,128)S(1)}, f32[120,128]{1,0:T(8,128)S(1)}, u32[]{:S(2)}, u32[]{:S(2)}) %collective-permute-start) | collective-permute-done | bytes 61472 | tf_op jit(solution)/shard_map/ppermute | solution.py:75
  9.0 0.4 %shard_map.159 = (f32[7,64,128]{2,1,0:T(8,128)S(1)}, f32[64,128]{1,0:T(8,128)S(1)}, f32[64,128]{1,0:T(8,128)S(1)}, f32[22,16,128]{2,1,0:T(8,128)S(1)}, f32[22,16...) custom-call(s32[8,128]{1,0:T(8,128)S(1)} %get-tuple-element.60.refs_, ...), custom_call_target="tpu_custom_call" | custom-call | flops 1048576 | bytes 1048576 | tf_op jit(solution)/shard_map/pallas_call | solution.py:626
  9.4 1.4 %collective-permute-start.5 = (f32[22,16,128]{2,1,0:T(8,128)S(1)}, f32[22,16,128]{2,1,0:T(8,128)S(1)}, u32[]{:S(2)}, u32[]{:S(2)}) collective-permute-start(f32[22,16,128]{2,1,0:T(8,128)S(1)} %get-tuple-element.74), channel_id=1, source_target_pairs={{0,16},{1,2},{2,1},{3,19},{4,20},{5,6},{6,5},{7,23},{8,24},{9,10},... | collective-permute-start | bytes 540680 | tf_op jit(solution)/shard_map/ppermute | solution.py:740
  10.8 1.6 %collective-permute-start.2 = (f32[64,128]{1,0:T(8,128)S(1)}, f32[64,128]{1,0:T(8,128)S(1)}, u32[]{:S(2)}, u32[]{:S(2)}) collective-permute-start(f32[64,128]{1,0:T(8,128)S(1)} %get-tuple-element.71), channel_id=1, source_target_pairs={{0,4},{1,5},{2,6},{3,7},{4,0},{5,1},{6,2},{7,3},{8,12},{9,13},{10,... | collective-permute-start | bytes 98312 | tf_op jit(solution)/shard_map/ppermute | solution.py:737
  12.4 0.8 %shard_map.160 = (f32[19,64,128]{2,1,0:T(8,128)S(1)}, f32[64,128]{1,0:T(8,128)S(1)}) custom-call(f32[3,19,8,128]{3,2,1,0:T(8,128)S(1)} %get-tuple-element.58.refs_0_, f32[19,64,128]{2,1,0:T(8,128)S(1)} %bitcast.24, f32[19,64,128]{2,1,0:T(8,128)S(1)} %get-tuple-element.59.refs_2_, f32[7,64,128]{2,1,0:T(8,128)S(1)} %get-tuple-element.69.refs_3_.refs_1_, ...), custom_call_target="tpu_custom_call" | custom-call | flops 16777216 | bytes 1048576 | tf_op jit(solution)/shard_map/pallas_call | solution.py:626
  13.2 1.5 %collective-permute-done.2.refs_2_ = f32[64,128]{1,0:T(8,128)S(1)} collective-permute-done((f32[64,128]{1,0:T(8,128)S(1)}, f32[64,128]{1,0:T(8,128)S(1)}, u32[]{:S(2)}, u32[]{:S(2)}) %collective-permute-start.2) | collective-permute-done | bytes 32800 | tf_op jit(solution)/shard_map/ppermute | solution.py:737
  14.8 0.2 collective-permute-done.5.refs_5_
  15.0 0.2 shard_map.161
  15.1 1.4 %collective-permute-start.6 = (f32[120,128]{1,0:T(8,128)S(1)}, f32[120,128]{1,0:T(8,128)S(1)}, u32[]{:S(2)}, u32[]{:S(2)}) collective-permute-start(f32[120,128]{1,0:T(8,128)S(1)} %get-tuple-element.87), channel_id=1, source_target_pairs={{0,16},{16,0},{1,17},{17,1},{2,18},{18,2},{3,19},{19,3},{4,20},{20... | collective-permute-start | bytes 184328 | tf_op jit(solution)/shard_map/ppermute | solution.py:75
  16.6 0.9 %shard_map.162 = (f32[19,64,128]{2,1,0:T(8,128)S(1)}, f32[64,128]{1,0:T(8,128)S(1)}, f32[64,128]{1,0:T(8,128)S(1)}, f32[22,16,128]{2,1,0:T(8,128)S(1)}, f32[22,1...) custom-call(f32[19,64,128]{2,1,0:T(8,128)S(1)} %bitcast.26, f32[19,64,128]{2,1,0:T(8,128)S(1)} %get-tuple-element.70.refs_7_.refs_1_, ...), custom_call_target="tpu_custom_call" | custom-call | flops 16777216 | bytes 1048576 | tf_op jit(solution)/shard_map/pallas_call | solution.py:626
  17.4 2.0 %collective-permute-done.6.refs_7_.refs_4_ = f32[120,128]{1,0:T(8,128)S(1)} collective-permute-done((f32[120,128]{1,0:T(8,128)S(1)}, f32[120,128]{1,0:T(8,128)S(1)}, u32[]{:S(2)}, u32[]{:S(2)}) %collective-permute-start.6) | collective-permute-done | bytes 61472 | tf_op jit(solution)/shard_map/ppermute | solution.py:75
  19.4 0.3 %shard_map.163 = (f32[7,64,128]{2,1,0:T(8,128)S(1)}, f32[64,128]{1,0:T(8,128)S(1)}, f32[64,128]{1,0:T(8,128)S(1)}, f32[22,16,128]{2,1,0:T(8,128)S(1)}, f32[22,16...) custom-call(s32[8,128]{1,0:T(8,128)S(1)} %get-tuple-element.60.refs_, ...), custom_call_target="tpu_custom_call" | custom-call | flops 1048576 | bytes 1048576 | tf_op jit(solution)/shard_map/pallas_call | solution.py:626
  19.8 1.4 %collective-permute-start.10 = (f32[22,16,128]{2,1,0:T(8,128)S(1)}, f32[22,16,128]{2,1,0:T(8,128)S(1)}, u32[]{:S(2)}, u32[]{:S(2)}) collective-permute-start(f32[22,16,128]{2,1,0:T(8,128)S(1)} %get-tuple-element.106), channel_id=1, source_target_pairs={{0,16},{1,2},{2,1},{3,19},{4,20},{5,6},{6,5},{7,23},{8,24},{9,10},... | collective-permute-start | bytes 540680 | tf_op jit(solution)/shard_map/ppermute | solution.py:740
  21.2 2.1 %collective-permute-start.7 = (f32[64,128]{1,0:T(8,128)S(1)}, f32[64,128]{1,0:T(8,128)S(1)}, u32[]{:S(2)}, u32[]{:S(2)}) collective-permute-start(f32[64,128]{1,0:T(8,128)S(1)} %get-tuple-element.103), channel_id=1, source_target_pairs={{0,4},{1,5},{2,6},{3,7},{4,0},{5,1},{6,2},{7,3},{8,12},{9,13},{10,... | collective-permute-start | bytes 98312 | tf_op jit(solution)/shard_map/ppermute | solution.py:737
  23.4 1.4 %shard_map.164 = (f32[19,64,128]{2,1,0:T(8,128)S(1)}, f32[64,128]{1,0:T(8,128)}, f32[64,128]{1,0:T(8,128)}, f32[64,128]{1,0:T(8,128)}, f32[64,128]{1,0:T(8,128)}) custom-call(f32[3,19,8,128]{3,2,1,0:T(8,128)S(1)} %get-tuple-element.58.refs_0_, f32[19,64,128]{2,1,0:T(8,128)S(1)} %get-tuple-element.81.refs_1_.refs_0_, ...), custom_call_target="tpu_custom_call" | custom-call | flops 16777216 | bytes 1048576 | tf_op jit(solution)/shard_map/pallas_call | solution.py:626
  24.8 0.5 %collective-permute-done.7.refs_3_ = f32[64,128]{1,0:T(8,128)S(1)} collective-permute-done((f32[64,128]{1,0:T(8,128)S(1)}, f32[64,128]{1,0:T(8,128)S(1)}, u32[]{:S(2)}, u32[]{:S(2)}) %collective-permute-start.7) | collective-permute-done | bytes 32800 | tf_op jit(solution)/shard_map/ppermute | solution.py:737
  25.4 1.0 %shard_map.165 = f32[19,64,128]{2,1,0:T(8,128)} custom-call(f32[19,64,128]{2,1,0:T(8,128)S(1)} %get-tuple-element.81.refs_1_.refs_0_, f32[19,64,128]{2,1,0:T(8,128)S(1)} %get-tuple-element.102.refs_1_, f32[7,64,128]{2,1,0:T(8,128)S(1)} %get-tuple-element.93.refs_3_.refs_2_, f32[64,128]{1,0:T(8,128)S(1)} %collective-permute-done.7.refs_3_, ...), custom_call_target="tpu_custom_call" | custom-call | flops 1048576 | bytes 1048576 | tf_op jit(solution)/shard_map/pallas_call | solution.py:626
  (33 shorter events, 0.3 us)
Async XLA Ops:
  0.6 3.9 %copy-start = (f32[19,16,4,128]{3,2,1,0:T(4,128)S(1)}, f32[19,16,4,128]{3,2,1,0:T(4,128)}, u32[]{:S(2)}) copy-start(f32[19,16,4,128]{3,2,1,0:T(4,128)} %param.17) | copy-start | bytes 1867780
  0.6 0.8 %copy-start.1 = (f32[32,1,2,128]{3,2,1,0:T(2,128)S(1)}, f32[32,1,2,128]{3,2,1,0:T(2,128)}, u32[]{:S(2)}) copy-start(f32[32,1,2,128]{3,2,1,0:T(2,128)} %param.12) | copy-start | bytes 98308
  0.7 0.8 %copy-start.2 = (f32[32,1,2,128]{3,2,1,0:T(2,128)S(1)}, f32[32,1,2,128]{3,2,1,0:T(2,128)}, u32[]{:S(2)}) copy-start(f32[32,1,2,128]{3,2,1,0:T(2,128)} %param.13) | copy-start | bytes 98308
  0.7 0.8 %copy-start.3 = (f32[32,1,2,128]{3,2,1,0:T(2,128)S(1)}, f32[32,1,2,128]{3,2,1,0:T(2,128)}, u32[]{:S(2)}) copy-start(f32[32,1,2,128]{3,2,1,0:T(2,128)} %param.14) | copy-start | bytes 98308
  0.7 0.8 %copy-start.4 = (f32[32,1,2,128]{3,2,1,0:T(2,128)S(1)}, f32[32,1,2,128]{3,2,1,0:T(2,128)}, u32[]{:S(2)}) copy-start(f32[32,1,2,128]{3,2,1,0:T(2,128)} %param.15) | copy-start | bytes 98308
  0.7 0.8 %copy-start.5 = (f32[32,1,2,128]{3,2,1,0:T(2,128)S(1)}, f32[32,1,2,128]{3,2,1,0:T(2,128)}, u32[]{:S(2)}) copy-start(f32[32,1,2,128]{3,2,1,0:T(2,128)} %param.16) | copy-start | bytes 98308
  0.7 0.8 %copy-start.9 = (f32[19]{0:T(128)S(1)}, f32[19]{0:T(128)}, u32[]{:S(2)}) copy-start(f32[19]{0:T(128)} %param.23) | copy-start | bytes 232
  1.6 7.4 %collective-permute-start.1 = (f32[180,128]{1,0:T(8,128)S(1)}, f32[180,128]{1,0:T(8,128)S(1)}, u32[]{:S(2)}, u32[]{:S(2)}) collective-permute-start(f32[180,128]{1,0:T(8,128)S(1)} %get-tuple-element.68), channel_id=1, source_target_pairs={{0,16},{16,0},{1,17},{17,1},{2,18},{18,2},{3,19},{19,3},{4,20},{20... | collective-permute-start | bytes 276488 | tf_op jit(solution)/shard_map/ppermute | solution.py:75
  4.6 0.7 %copy-start.6 = (f32[19,19]{1,0:T(8,128)S(1)}, f32[19,19]{1,0:T(8,128)}, u32[]{:S(2)}) copy-start(f32[19,19]{1,0:T(8,128)} %refs_6_.1) | copy-start | bytes 4336
  4.7 4.3 %collective-permute-start = (f32[120,128]{1,0:T(8,128)S(1)}, f32[120,128]{1,0:T(8,128)S(1)}, u32[]{:S(2)}, u32[]{:S(2)}) collective-permute-start(f32[120,128]{1,0:T(8,128)S(1)} %get-tuple-element.66), channel_id=1, source_target_pairs={{0,16},{16,0},{1,17},{17,1},{2,18},{18,2},{3,19},{19,3},{4,20},{20... | collective-permute-start | bytes 184328 | tf_op jit(solution)/shard_map/ppermute | solution.py:75
  4.9 0.7 %copy-start.8 = (f32[4,128]{1,0:T(4,128)S(1)}, f32[4,128]{1,0:T(4,128)}, u32[]{:S(2)}) copy-start(f32[4,128]{1,0:T(4,128)} %refs_4_.1) | copy-start | bytes 6148
  4.9 0.7 %copy-start.7 = (s32[4,128]{1,0:T(4,128)S(1)}, s32[4,128]{1,0:T(4,128)}, u32[]{:S(2)}) copy-start(s32[4,128]{1,0:T(4,128)} %refs_3_.1) | copy-start | bytes 6148
  4.9 0.7 %copy-start.10 = (f32[19]{0:T(128)S(1)}, f32[19]{0:T(128)}, u32[]{:S(2)}) copy-start(f32[19]{0:T(128)} %param.21) | copy-start | bytes 232
  4.9 0.7 %copy-start.11 = (f32[19]{0:T(128)S(1)}, f32[19]{0:T(128)}, u32[]{:S(2)}) copy-start(f32[19]{0:T(128)} %param.22) | copy-start | bytes 232
  9.3 5.4 %collective-permute-start.4 = (f32[22,16,128]{2,1,0:T(8,128)S(1)}, f32[22,16,128]{2,1,0:T(8,128)S(1)}, u32[]{:S(2)}, u32[]{:S(2)}) collective-permute-start(f32[22,16,128]{2,1,0:T(8,128)S(1)} %get-tuple-element.73), channel_id=1, source_target_pairs={{0,1},{1,0},{2,3},{3,2},{4,5},{5,4},{6,7},{7,6},{8,9},{9,8},{10,11... | collective-permute-start | bytes 540680 | tf_op jit(solution)/shard_map/ppermute | solution.py:739
  9.4 5.6 %collective-permute-start.5 = (f32[22,16,128]{2,1,0:T(8,128)S(1)}, f32[22,16,128]{2,1,0:T(8,128)S(1)}, u32[]{:S(2)}, u32[]{:S(2)}) collective-permute-start(f32[22,16,128]{2,1,0:T(8,128)S(1)} %get-tuple-element.74), channel_id=1, source_target_pairs={{0,16},{1,2},{2,1},{3,19},{4,20},{5,6},{6,5},{7,23},{8,24},{9,10},... | collective-permute-start | bytes 540680 | tf_op jit(solution)/shard_map/ppermute | solution.py:740
  10.8 3.9 %collective-permute-start.2 = (f32[64,128]{1,0:T(8,128)S(1)}, f32[64,128]{1,0:T(8,128)S(1)}, u32[]{:S(2)}, u32[]{:S(2)}) collective-permute-start(f32[64,128]{1,0:T(8,128)S(1)} %get-tuple-element.71), channel_id=1, source_target_pairs={{0,4},{1,5},{2,6},{3,7},{4,0},{5,1},{6,2},{7,3},{8,12},{9,13},{10,... | collective-permute-start | bytes 98312 | tf_op jit(solution)/shard_map/ppermute | solution.py:737
  12.4 2.3 %collective-permute-start.3 = (f32[64,128]{1,0:T(8,128)S(1)}, f32[64,128]{1,0:T(8,128)S(1)}, u32[]{:S(2)}, u32[]{:S(2)}) collective-permute-start(f32[64,128]{1,0:T(8,128)S(1)} %get-tuple-element.72), channel_id=1, source_target_pairs={{0,1},{1,0},{2,3},{3,2},{4,8},{5,9},{6,10},{7,11},{8,4},{9,5},{10,... | collective-permute-start | bytes 98312 | tf_op jit(solution)/shard_map/ppermute | solution.py:738
  15.1 4.3 %collective-permute-start.6 = (f32[120,128]{1,0:T(8,128)S(1)}, f32[120,128]{1,0:T(8,128)S(1)}, u32[]{:S(2)}, u32[]{:S(2)}) collective-permute-start(f32[120,128]{1,0:T(8,128)S(1)} %get-tuple-element.87), channel_id=1, source_target_pairs={{0,16},{16,0},{1,17},{17,1},{2,18},{18,2},{3,19},{19,3},{4,20},{20... | collective-permute-start | bytes 184328 | tf_op jit(solution)/shard_map/ppermute | solution.py:75
  19.8 5.5 %collective-permute-start.9 = (f32[22,16,128]{2,1,0:T(8,128)S(1)}, f32[22,16,128]{2,1,0:T(8,128)S(1)}, u32[]{:S(2)}, u32[]{:S(2)}) collective-permute-start(f32[22,16,128]{2,1,0:T(8,128)S(1)} %get-tuple-element.105), channel_id=1, source_target_pairs={{0,1},{1,0},{2,3},{3,2},{4,5},{5,4},{6,7},{7,6},{8,9},{9,8},{10,11... | collective-permute-start | bytes 540680 | tf_op jit(solution)/shard_map/ppermute | solution.py:739
  19.8 5.6 %collective-permute-start.10 = (f32[22,16,128]{2,1,0:T(8,128)S(1)}, f32[22,16,128]{2,1,0:T(8,128)S(1)}, u32[]{:S(2)}, u32[]{:S(2)}) collective-permute-start(f32[22,16,128]{2,1,0:T(8,128)S(1)} %get-tuple-element.106), channel_id=1, source_target_pairs={{0,16},{1,2},{2,1},{3,19},{4,20},{5,6},{6,5},{7,23},{8,24},{9,10},... | collective-permute-start | bytes 540680 | tf_op jit(solution)/shard_map/ppermute | solution.py:740
  21.2 4.0 %collective-permute-start.7 = (f32[64,128]{1,0:T(8,128)S(1)}, f32[64,128]{1,0:T(8,128)S(1)}, u32[]{:S(2)}, u32[]{:S(2)}) collective-permute-start(f32[64,128]{1,0:T(8,128)S(1)} %get-tuple-element.103), channel_id=1, source_target_pairs={{0,4},{1,5},{2,6},{3,7},{4,0},{5,1},{6,2},{7,3},{8,12},{9,13},{10,... | collective-permute-start | bytes 98312 | tf_op jit(solution)/shard_map/ppermute | solution.py:737
  23.4 1.9 %collective-permute-start.8 = (f32[64,128]{1,0:T(8,128)S(1)}, f32[64,128]{1,0:T(8,128)S(1)}, u32[]{:S(2)}, u32[]{:S(2)}) collective-permute-start(f32[64,128]{1,0:T(8,128)S(1)} %get-tuple-element.104), channel_id=1, source_target_pairs={{0,1},{1,0},{2,3},{3,2},{4,8},{5,9},{6,10},{7,11},{8,4},{9,5},{10,... | collective-permute-start | bytes 98312 | tf_op jit(solution)/shard_map/ppermute | solution.py:738

commit v5 on v4

--- a/solution.py
+++ b/solution.py
@@ -57,7 +57,7 @@
             return (g, j, y) if axis == "gx" else (g, x, j)
         if axis == "gx":
             return (g, x, y ^ 1) if (y ^ 1) < size_y else (g, x, y)
-        return (g ^ 1, x, y) if (g ^ 1) < size_g else (g, x, y)
+        return (g, x ^ 1, y) if (x ^ 1) < size_x else (g, x, y)
 
     def index(g, x, y):
         return (g * size_x + x) * size_y + y
@@ -70,6 +70,16 @@
     ]
 
 
+def upward(sizes):
+    size_g, size_x, size_y = sizes
+    return [
+        ((g * size_x + x) * size_y + y, (g * size_x + x) * size_y + (y + 1) % size_y)
+        for g in range(size_g)
+        for x in range(size_x)
+        for y in range(size_y)
+    ]
+
+
 def from_others(value, count):
     return [
         lax.ppermute(value, "grp", [(i, (i + k) % count) for i in range(count)])
@@ -100,10 +110,28 @@
 
 def pack_sides(c, slot, left, right):
     lane = iota(c.shape, 1)
-    width = c.shape[1]
-    left = jnp.where(lane == (2 * slot - 1) % width, turn(c, 2 * slot - 1, 1), left)
+    left = jnp.where(lane == 2 * slot, turn(c, 2 * slot, 1), left)
     right = jnp.where(lane == 2 * slot, turn(c, 2 * slot + 1, 1), right)
     return left, right
+
+
+def folds(slots, cells, width):
+    return 4 * slots <= width and cells % (2 * SUB) == 0
+
+
+def fold(v, slots):
+    cells, width = v.shape
+    if not folds(slots, cells, width):
+        return v
+    half = cells // 2
+    return jnp.where(iota((half, width), 1) < width // 2, v[:half], turn(v[half:], width // 2, 1))
+
+
+def unfold(v, slots, cells):
+    width = v.shape[1]
+    if not folds(slots, cells, width):
+        return v
+    return jnp.concatenate([v, turn(v, width // 2, 1)], axis=0)
 
 
 def compact(rows, cells, count):
@@ -253,33 +281,27 @@
         mix_ref[:, here, :] = mixed.reshape(tracers, SUB, width)
 
 
+def put_rows(msg_ya, msg_yb, slot, first, last):
+    y_even = lax.rem(lax.axis_index("gy"), 2) == 0
+    msg_ya[slot] = jnp.where(y_even, last, first)
+    msg_yb[slot] = jnp.where(y_even, first, last)
+
+
 def pack(rows, c_ref, p_ref, msg_xa, msg_xb, msg_ya, msg_yb):
     tracers, cells, _ = c_ref.shape
     levels = cells // rows
     x_even = lax.rem(lax.axis_index("gx"), 2) == 0
-    y_even = lax.rem(lax.axis_index("gy"), 2) == 0
     left = right = jnp.zeros(c_ref.shape[1:], F32)
     left, right = pack_sides(p_ref[...], tracers + 2, left, right)
     for t in range(tracers):
         left, right = pack_sides(c_ref[t], t, left, right)
     msg_xa[...] = jnp.where(x_even, right, left)
     msg_xb[...] = jnp.where(x_even, left, right)
-
-    def put(slot, first, last):
-        msg_ya[slot] = jnp.where(y_even, last, first)
-        msg_yb[slot] = jnp.where(y_even, first, last)
-
+    first, last = pl.ds(0, levels, stride=rows), pl.ds(rows - 1, levels, stride=rows)
     for t in range(tracers):
-        put(
-            t,
-            c_ref[t, pl.ds(0, levels, stride=rows), :],
-            c_ref[t, pl.ds(rows - 1, levels, stride=rows), :],
-        )
-    put(
-        tracers + 2,
-        p_ref[pl.ds(0, levels, stride=rows), :],
-        p_ref[pl.ds(rows - 1, levels, stride=rows), :],
-    )
+        put_rows(msg_ya, msg_yb, t, c_ref[t, first, :], c_ref[t, last, :])
+    if msg_ya.shape[0] > tracers:
+        put_rows(msg_ya, msg_yb, tracers, p_ref[first, :], p_ref[last, :])
 
 
 def pack_kernel(rows, *refs):
@@ -295,6 +317,11 @@
         for t in range(tracers):
             tiles_ref[at, t] = jnp.broadcast_to(values[:, t : t + 1], (SUB, width))
     pack(rows, c_ref, p_ref, msg_xa, msg_xb, msg_ya, msg_yb)
+    levels = cells // rows
+    level = lax.axis_index("grp") * levels + iota((levels, width), 0)
+    wet_first = jnp.where(level < depth_in[pl.ds(0, 1), :], 1.0, 0.0)
+    wet_last = jnp.where(level < depth_in[pl.ds(rows - 1, 1), :], 1.0, 0.0)
+    put_rows(msg_ya, msg_yb, tracers + 1, wet_first, wet_last)
     weights = spread_rates(rates_ref[...], tracers)
     w_ref[...] = weights
     mix(weights, c_ref, mix_ref)
@@ -303,13 +330,13 @@
 def ocean_kernel(rows, count, tracers, first_step, *refs):
     refs = Refs(refs)
     depth_ref, solar_ref = refs.take(2)
-    in_xa, in_xb, in_ya, in_yb = refs.take(4)
+    in_xa, in_xb = refs.take(2)
     p_own, *p_others = refs.take(count)
     if first_step:
         own_fields, *other_fields = refs.take(count)
     else:
         fields = refs.take(5)
-    band_ref, msg_xa, msg_xb, msg_ya, msg_yb = refs.take(5)
+    band_ref, msg_xa, msg_xb, speed_ref = refs.take(4)
     full_out = refs.take(5 if first_step else 4)
     p_full, p_other_s = refs.take(2)
     if first_step:
@@ -398,23 +425,15 @@
     band_ref[6] = wet_band
 
     x_even = lax.rem(lax.axis_index("gx"), 2) == 0
-    y_even = lax.rem(lax.axis_index("gy"), 2) == 0
     xa, xb = in_xa[...], in_xb[...]
     left, right = jnp.where(x_even, xb, xa), jnp.where(x_even, xa, xb)
     left, right = pack_sides(wet_band, tracers + 1, left, right)
     _, right = pack_sides(u, tracers, left, right)
-    msg_xa[...] = jnp.where(x_even, right, left)
-    msg_xb[...] = jnp.where(x_even, left, right)
-    for t in (*range(tracers), tracers + 2):
-        msg_ya[t] = in_ya[t]
-        msg_yb[t] = in_yb[t]
-    speed = band_ref[1, pl.ds(rows - 1, levels, stride=rows), :]
-    wet_first = band_ref[6, pl.ds(0, levels, stride=rows), :]
-    wet_last = band_ref[6, pl.ds(rows - 1, levels, stride=rows), :]
-    msg_ya[tracers] = speed
-    msg_yb[tracers] = speed
-    msg_ya[tracers + 1] = jnp.where(y_even, wet_last, wet_first)
-    msg_yb[tracers + 1] = jnp.where(y_even, wet_first, wet_last)
+    msg_xa[...] = fold(jnp.where(x_even, right, left), tracers + 3)
+    msg_xb[...] = fold(jnp.where(x_even, left, right), tracers + 3)
+    speed_ref[pl.ds(0, levels), :] = band_ref[1, pl.ds(rows - 1, levels, stride=rows), :]
+    speed_ref[pl.ds(levels, levels), :] = jnp.zeros((levels, width), F32)
+    speed_ref[pl.ds(2 * levels, levels), :] = jnp.zeros((levels, width), F32)
 
 
 def start_own_strip(rows, count, g, full, outs, strips, sems):
@@ -513,11 +532,12 @@
         p_part[...] = pigment
 
 
-def x_halo(got_xa, got_xb):
+def x_halo(got_xa, got_xb, slots, cells):
     x_even = lax.rem(lax.axis_index("gx"), 2) == 0
     xa, xb = got_xa[...], got_xb[...]
-    lane = iota(xa.shape, 1)
-    return jnp.where((lax.rem(lane, 2) == 0) == x_even, xb, xa)
+    west = jnp.where(x_even, xb, xa)
+    east = turn(jnp.where(x_even, xa, xb), -1, 1)
+    return unfold(jnp.where(lax.rem(iota(xa.shape, 1), 2) == 0, west, east), slots, cells)
 
 
 def spread_rows(rows, got_ya, got_yb, out_ref, slot):
@@ -528,25 +548,26 @@
     out_ref[slot, pl.ds(rows - 1, levels, stride=rows), :] = jnp.where(y_even, ya, yb)
 
 
-def side_factors(rows, sizes, halo, spread_s, band_ref, tracers):
+def side_factors(rows, sizes, halo, wet_out, speed, speed_s, band_ref, tracers):
     _, size_x, size_y = sizes
     x = lax.axis_index("gx")
     y = lax.axis_index("gy")
     u = band_ref[0]
     v = band_ref[1]
     wet = band_ref[6]
-    shape2 = wet.shape
-    lane = iota(shape2, 1)
-    at_row = lax.rem(iota(shape2, 0), rows)
-    at_w, at_e, at_s, at_n = lane == 0, lane == shape2[1] - 1, at_row == 0, at_row == rows - 1
+    cells, width = wet.shape
+    speed_s[pl.ds(0, cells // rows, stride=rows), :] = speed[pl.ds(0, cells // rows), :]
+    lane = iota((cells, width), 1)
+    at_row = lax.rem(iota((cells, width), 0), rows)
+    at_w, at_e, at_s, at_n = lane == 0, lane == width - 1, at_row == 0, at_row == rows - 1
     wet_x = wet * turn(halo, -2 * (tracers + 1), 1)
-    wet_y = wet * spread_s[tracers + 1]
+    wet_y = wet * wet_out
     open_w = jnp.where(at_w & (x > 0), wet_x, 0.0)
     open_e = jnp.where(at_e & (x < size_x - 1), wet_x, 0.0)
     open_s = jnp.where(at_s & (y > 0), wet_y, 0.0)
     open_n = jnp.where(at_n & (y < size_y - 1), wet_y, 0.0)
     u_w = turn(halo, -2 * tracers, 1)
-    v_s = jnp.where(at_s, spread_s[tracers], 0.0)
+    v_s = jnp.where(at_s, speed_s[...], 0.0)
     k_x = lower(open_w, u_w) - upper(open_e, u)
     k_y = lower(open_s, v_s) - upper(open_n, v)
     k_c = (upper(open_w, u_w) - lower(open_e, u)) + (upper(open_s, v_s) - lower(open_n, v))
@@ -560,23 +581,28 @@
     return (k_x * turn(halo, -2 * slot, 1) + k_c * c) + jnp.where(edge, k_y * outer, 0.0)
 
 
-def early_kernel(rows, count, sizes, *refs):
+def early_kernel(rows, count, sizes, first_step, *refs):
     refs = Refs(refs)
-    c_ref, band_ref, got_xa, got_xb, got_ya, got_yb, p_in, part_ref, p_part = refs.take(9)
-    k_ref, halo_ref, spread_s, p_ref = refs.take(4)
-    msgs = refs.refs
+    c_ref, band_ref, got_xa, got_xb, got_ya, got_yb = refs.take(6)
+    (speed,) = refs.take(1)
+    p_in, part_ref, p_part = refs.take(3)
+    if not first_step:
+        (wet_in,) = refs.take(1)
+    k_ref, halo_ref, spread_s, wet_out, p_ref = refs.take(5)
+    msgs, speed_s = refs.refs[:-1], refs.refs[-1]
     g = lax.axis_index("grp")
     tracers, cells, width = c_ref.shape
     base = level_base(rows, cells, count)
-    halo = x_halo(got_xa, got_xb)
+    halo = x_halo(got_xa, got_xb, tracers + 3, cells)
     halo_ref[...] = halo
-    for slot in range(tracers + 3):
+    for slot in range(got_ya.shape[0]):
         spread_rows(rows, got_ya, got_yb, spread_s, slot)
-    factors = side_factors(rows, sizes, halo, spread_s, band_ref, tracers)
+    wet_out[...] = spread_s[tracers + 1] if first_step else wet_in[...]
+    factors = side_factors(rows, sizes, halo, wet_out[...], speed, speed_s, band_ref, tracers)
     for at, k in enumerate(factors):
         k_ref[at] = k
-    slot = tracers + 2
-    p_ref[...] = p_part[...] + sideways(rows, factors, halo, spread_s[slot], p_in[...], slot)
+    change = sideways(rows, factors, halo, spread_s[tracers], p_in[...], tracers + 2)
+    p_ref[...] = p_part[...] + change
     write_pigment(rows, count, p_ref, msgs[0], g)
 
     def block(at, t):
@@ -602,15 +628,19 @@
     mix(w_ref[...], out_ref, mix_ref)
 
 
-def final_kernel(rows, sizes, *refs):
+def final_kernel(rows, sizes, first_step, *refs):
     refs = Refs(refs)
     c_ref, part_ref, band_ref, got_xa, got_xb, got_ya, got_yb = refs.take(7)
-    out_hbm, spread_s, new_s, sems = refs.take(4)
-    tracers = c_ref.shape[0]
-    halo = x_halo(got_xa, got_xb)
-    for slot in (tracers, tracers + 1):
-        spread_rows(rows, got_ya, got_yb, spread_s, slot)
-    factors = side_factors(rows, sizes, halo, spread_s, band_ref, tracers)
+    (speed,) = refs.take(1)
+    if not first_step:
+        (wet_in,) = refs.take(1)
+    out_hbm, spread_s, speed_s, new_s, sems = refs.take(5)
+    tracers, cells, _ = c_ref.shape
+    halo = x_halo(got_xa, got_xb, tracers + 3, cells)
+    if first_step:
+        spread_rows(rows, got_ya, got_yb, spread_s, tracers + 1)
+    wet_out = spread_s[tracers + 1] if first_step else wet_in[...]
+    factors = side_factors(rows, sizes, halo, wet_out, speed, speed_s, band_ref, tracers)
     copies = []
     for i, (a, n) in enumerate(chunks(tracers, sems.shape[0])):
         for t in range(a, a + n):
@@ -622,15 +652,15 @@
         copy.wait()
 
 
-def call(kernel, ins, outs, in_specs=None, out_specs=None, scratch=(), flops=1 << 20, vmem_limit=VMEM_LIMIT):
+def call(kernel, ins, outs, in_specs=None, out_specs=None, scratch=(), flops=1 << 20, moved=1 << 20):
     return pl.pallas_call(
         kernel,
         in_specs=[vmem() for _ in ins] if in_specs is None else in_specs,
         out_specs=[vmem() for _ in outs] if out_specs is None else out_specs,
         out_shape=outs,
         scratch_shapes=list(scratch),
-        compiler_params=pltpu.CompilerParams(vmem_limit_bytes=vmem_limit),
-        cost_estimate=pl.CostEstimate(flops=flops, bytes_accessed=1 << 20, transcendentals=0),
+        compiler_params=pltpu.CompilerParams(vmem_limit_bytes=VMEM_LIMIT),
+        cost_estimate=pl.CostEstimate(flops=flops, bytes_accessed=moved, transcendentals=0),
     )(*ins)
 
 
@@ -682,29 +712,22 @@
     )
     raw_others = from_others(window, count)
 
-    msg_levels = message_shapes(tracers, rows, cells, width, count)
+    messages = message_shapes(tracers, rows, cells, width, count)
     cols = shape(cells, width)
-    lines = shape(tracers + 3, levels, width)
-    sides = [cols, cols, lines, lines]
+    sent_cols = shape(cells // 2, width) if folds(tracers + 3, cells, width) else cols
     field = shape(tracers, cells, width)
     c = substance_amounts.reshape(tracers, cells, width)
     pigment, *msgs = call(
         functools.partial(prep_kernel, rows, count),
         [pig, c],
-        [cols, *msg_levels],
+        [cols, *messages],
     )
     full = None
     for step in range(STEPS):
         first_step, last_step = step == 0, step == STEPS - 1
         p_others = from_others(msgs[0], count)
-        if count == 2:
-            lev = p_others
-        else:
-            lev = [
-                lax.ppermute(msgs[1], "grp", [(i, (i + 1) % count) for i in range(count)]),
-                lax.ppermute(msgs[2], "grp", [((i + 1) % count, i) for i in range(count)]),
-            ]
         if first_step:
+            lines = shape(tracers + 2, levels, width)
             xa, xb, ya, yb, weights, mixed, tiles, depth, solar = call(
                 functools.partial(pack_kernel, rows),
                 [
@@ -716,58 +739,80 @@
                     pigment,
                 ],
                 [
-                    *sides,
+                    cols,
+                    cols,
+                    lines,
+                    lines,
                     shape(tracers * SUB, tracers * SUB),
                     field,
                     shape(3, tracers, SUB, width),
                     jax.ShapeDtypeStruct((SUB, width), jnp.int32),
                     shape(SUB, width),
                 ],
-                flops=1 << 24,
+                flops=1<<24,
             )
-        band, xa, xb, ya, yb, *full = call(
+        ya = lax.ppermute(ya, AXES, pairing(sizes, "gy", 0))
+        yb = lax.ppermute(yb, AXES, pairing(sizes, "gy", 1))
+        if count == 2:
+            lev = p_others
+        else:
+            lev = [
+                lax.ppermute(msgs[1], "grp", [(i, (i + 1) % count) for i in range(count)]),
+                lax.ppermute(msgs[2], "grp", [((i + 1) % count, i) for i in range(count)]),
+            ]
+        band, xa, xb, speed, *full = call(
             functools.partial(ocean_kernel, rows, count, tracers, first_step),
-            [depth, solar, xa, xb, ya, yb, pigment, *p_others, *([raw, *raw_others] if first_step else full)],
-            [shape(7, cells, width), *sides, *[shape(total, width)] * (5 if first_step else 4)],
+            [depth, solar, xa, xb, pigment, *p_others, *([raw, *raw_others] if first_step else full)],
+            [
+                shape(7, cells, width),
+                sent_cols,
+                sent_cols,
+                shape(3 * levels, width),
+                *[shape(total, width)] * (5 if first_step else 4),
+            ],
             scratch=[column, band_s]
             + [column] * (5 if first_step else 0)
             + [pltpu.VMEM((strip_cells, width), F32)] * (5 * (count - 1) if first_step else 0)
             + [column] * 3,
+            flops=1<<32,
         )
         xa = lax.ppermute(xa, AXES, pairing(sizes, "gx", 0))
         xb = lax.ppermute(xb, AXES, pairing(sizes, "gx", 1))
-        ya = lax.ppermute(ya, AXES, pairing(sizes, "gy", 0))
-        yb = lax.ppermute(yb, AXES, pairing(sizes, "gy", 1))
+        speed = lax.ppermute(speed, AXES, upward(sizes))
         part, *rest = call(
             functools.partial(inner_kernel, rows, count, last_step),
             [tiles, c, mixed, band, *lev, *(full if last_step else [])],
             [field] + ([shape(strip_cells, width)] * 4 if last_step else [cols]),
             out_specs=[vmem()] + ([hbm()] * 4 if last_step else [vmem()]),
             scratch=[pltpu.VMEM((strip_cells, width), F32)] * 4 + [dma((4,))] if last_step else [],
-            flops=1 << 24,
+            flops=1<<10,
         )
+        known = [] if first_step else [wet_out]
         if not last_step:
-            k, halo, spread, pigment_next, *msgs = call(
-                functools.partial(early_kernel, rows, count, sizes),
-                [c, band, xa, xb, ya, yb, pigment, part, *rest],
-                [shape(3, cells, width), cols, shape(tracers + 3, cells, width), cols, *msg_levels],
+            k, halo, spread, wet_out, pigment_next, *msgs = call(
+                functools.partial(early_kernel, rows, count, sizes, first_step),
+                [c, band, xa, xb, ya, yb, speed, pigment, part, *rest, *known],
+                [shape(3, cells, width), cols, shape(tracers + 2, cells, width), cols, cols, *messages],
+                scratch=[band_s],
             )
             pigment = pigment_next
+            lines = shape(tracers + (0 if step + 1 == STEPS - 1 else 1), levels, width)
             c, xa, xb, ya, yb, mixed = call(
                 functools.partial(step_kernel, rows),
                 [c, part, k, halo, spread, weights, pigment],
-                [field, *sides, field],
-                flops=1 << 24,
+                [field, cols, cols, lines, lines, field],
+                flops=1<<32,
             )
         else:
             ocean = rest
             (c,) = call(
-                functools.partial(final_kernel, rows, sizes),
-                [c, part, band, xa, xb, ya, yb],
+                functools.partial(final_kernel, rows, sizes, first_step),
+                [c, part, band, xa, xb, ya, yb, speed, *known],
                 [field],
                 out_specs=[hbm()],
                 scratch=[
-                    pltpu.VMEM((tracers + 3, cells, width), F32),
+                    pltpu.VMEM((tracers + 2, cells, width), F32),
+                    band_s,
                     pltpu.VMEM((tracers, cells, width), F32),
                     dma((5,)),
                 ],

time: 26.8 us -> 25.1 us (0.937)
  waiting for transfers between devices: 6.27 us -> 0.18 us
  starting transfers between devices: 11.4 us -> 15.7 us
    ppermute x3, waiting for transfers between devices: 4 us -> 0.01 us  [from_others(): lax.ppermute(value, 'grp', [(i, (i + k) % count) for i in range(count)])]
    ppermute x2, starting transfers between devices: 0.01 us -> 2.4 us  [per_device(): xb = lax.ppermute(xb, AXES, pairing(sizes, 'gx', 1))]
    ppermute x2, starting transfers between devices: 2.86 us -> 4.73 us  [per_device(): yb = lax.ppermute(yb, AXES, pairing(sizes, 'gy', 1))]
    ppermute x2, waiting for transfers between devices: 1.97 us -> 0.15 us  [per_device(): xa = lax.ppermute(xa, AXES, pairing(sizes, 'gx', 0))]
    ppermute x2, starting transfers between devices: 3.72 us -> 3.4 us  [per_device(): xa = lax.ppermute(xa, AXES, pairing(sizes, 'gx', 0))]
    ppermute x2, waiting for transfers between devices: 0.29 us -> 0.01 us  [per_device(): yb = lax.ppermute(yb, AXES, pairing(sizes, 'gy', 1))]
  transfers between devices with their start and end apart: 11 -> 13, of which waited for: 6 -> 1; matrix products, arithmetic and copies ran while one was open for 0% -> 0% of each run, Pallas kernels for 17% -> 21%
where the time goes in v5:
time: 25.1 us; the launch traced here: 24.9 us
  starting transfers between devices  15.7 us (63%)
  Pallas kernels  6.64 us (26%)
  local copies, waits for them, and re-layouts  1.53 us (6%)
  between operations  0.84 us (3%)
    pallas_call x11, Pallas kernels, call(): pl.pallas_call(kernel, in_specs=[vmem() for _ in ins] if in_specs is None...  6.64 us
    ppermute x3, starting transfers between devices, from_others(): lax.ppermute(value, 'grp', [(i, (i + k) % count) for i in range(count)])  4.82 us
    ppermute x2, starting transfers between devices, per_device(): yb = lax.ppermute(yb, AXES, pairing(sizes, 'gy', 1))  4.73 us
    ppermute x2, starting transfers between devices, per_device(): xa = lax.ppermute(xa, AXES, pairing(sizes, 'gx', 0))  3.4 us
    ppermute x2, starting transfers between devices, per_device(): xb = lax.ppermute(xb, AXES, pairing(sizes, 'gx', 1))  2.4 us
    unnamed x24, local copies, waits for them, and re-layouts  1.53 us
  transfers between devices with their start and end apart: 13, of which 1 were waited for; matrix products, arithmetic and copies ran while one was open for 0% of the time, Pallas kernels for 21%

profile of v5, /device:TPU:0, one launch (start us, length us, event | category | flops | bytes accessed | tf_op | source)
XLA Modules:
  0.0 24.9 jit_solution(8701421585740378785)
XLA Ops:
  0.7 0.7 %copy-done.1 = f32[32,1,2,128]{3,2,1,0:T(2,128)S(1)} copy-done((f32[32,1,2,128]{3,2,1,0:T(2,128)S(1)}, f32[32,1,2,128]{3,2,1,0:T(2,128)}, u32[]{:S(2)}) %copy-start.1) | copy-done | bytes 32792
  1.6 3.0 %collective-permute-start.1 = (f32[180,128]{1,0:T(8,128)S(1)}, f32[180,128]{1,0:T(8,128)S(1)}, u32[]{:S(2)}, u32[]{:S(2)}) collective-permute-start(f32[180,128]{1,0:T(8,128)S(1)} %get-tuple-element.65), channel_id=1, source_target_pairs={{0,16},{16,0},{1,17},{17,1},{2,18},{18,2},{3,19},{19,3},{4,20},{20... | collective-permute-start | bytes 276488 | tf_op jit(solution)/shard_map/ppermute | solution.py:85
  4.6 0.1 shard_map.157
  4.7 0.2 collective-permute-start
  4.9 0.3 %copy-done.6 = f32[19,19]{1,0:T(8,128)S(1)} copy-done((f32[19,19]{1,0:T(8,128)S(1)}, f32[19,19]{1,0:T(8,128)}, u32[]{:S(2)}) %copy-start.6) | copy-done | bytes 1468
  5.3 0.3 %copy-done.8 = f32[4,128]{1,0:T(4,128)S(1)} copy-done((f32[4,128]{1,0:T(4,128)S(1)}, f32[4,128]{1,0:T(4,128)}, u32[]{:S(2)}) %copy-start.8) | copy-done | bytes 2072
  5.6 1.3 %shard_map.158 = (f32[64,128]{1,0:T(8,128)S(1)}, f32[64,128]{1,0:T(8,128)S(1)}, f32[21,16,128]{2,1,0:T(8,128)S(1)}, f32[21,16,128]{2,1,0:T(8,128)S(1)}, f32[152,...) custom-call(f32[1,19]{1,0:T(1,128)S(1)} %bitcast.34, ...), custom_call_target="tpu_custom_call" | custom-call | flops 16777216 | bytes 1048576 | tf_op jit(solution)/shard_map/pallas_call | solution.py:656
  7.0 0.1 collective-permute-start.4
  7.1 2.0 %collective-permute-start.5 = (f32[21,16,128]{2,1,0:T(8,128)S(1)}, f32[21,16,128]{2,1,0:T(8,128)S(1)}, u32[]{:S(2)}, u32[]{:S(2)}) collective-permute-start(f32[21,16,128]{2,1,0:T(8,128)S(1)} %get-tuple-element.71), channel_id=1, source_target_pairs={{0,4},{1,2},{2,1},{3,7},{4,0},{5,6},{6,5},{7,3},{8,12},{9,10},{10,... | collective-permute-start | bytes 516104 | tf_op jit(solution)/shard_map/ppermute | solution.py:755
  9.1 0.4 %shard_map.159 = (f32[7,64,128]{2,1,0:T(8,128)S(1)}, f32[32,128]{1,0:T(8,128)S(1)}, f32[32,128]{1,0:T(8,128)S(1)}, f32[48,128]{1,0:T(8,128)S(1)}, f32[128,128]{1...) custom-call(s32[8,128]{1,0:T(8,128)S(1)} %get-tuple-element.59.refs_, ...), custom_call_target="tpu_custom_call" | custom-call | flops 4294967296 | bytes 1048576 | tf_op jit(solution)/shard_map/pallas_call | solution.py:656
  9.4 0.1 collective-permute-start.6
  9.5 1.6 %collective-permute-start.2 = (f32[32,128]{1,0:T(8,128)S(1)}, f32[32,128]{1,0:T(8,128)S(1)}, u32[]{:S(2)}, u32[]{:S(2)}) collective-permute-start(f32[32,128]{1,0:T(8,128)S(1)} %get-tuple-element.68), channel_id=1, source_target_pairs={{0,4},{1,5},{2,6},{3,7},{4,0},{5,1},{6,2},{7,3},{8,12},{9,13},{10,... | collective-permute-start | bytes 49160 | tf_op jit(solution)/shard_map/ppermute | solution.py:779
  11.1 1.2 %collective-permute-start.3 = (f32[32,128]{1,0:T(8,128)S(1)}, f32[32,128]{1,0:T(8,128)S(1)}, u32[]{:S(2)}, u32[]{:S(2)}) collective-permute-start(f32[32,128]{1,0:T(8,128)S(1)} %get-tuple-element.69), channel_id=1, source_target_pairs={{0,1},{1,0},{2,3},{3,2},{4,8},{5,9},{6,10},{7,11},{8,4},{9,5},{10,... | collective-permute-start | bytes 49160 | tf_op jit(solution)/shard_map/ppermute | solution.py:780
  12.3 0.8 %shard_map.160 = (f32[19,64,128]{2,1,0:T(8,128)S(1)}, f32[64,128]{1,0:T(8,128)S(1)}) custom-call(f32[3,19,8,128]{3,2,1,0:T(8,128)S(1)} %get-tuple-element.57.refs_0_, f32[19,64,128]{2,1,0:T(8,128)S(1)} %bitcast.24, f32[19,64,128]{2,1,0:T(8,128)S(1)} %get-tuple-element.58.refs_2_, f32[7,64,128]{2,1,0:T(8,128)S(1)} %get-tuple-element.66.refs_3_.refs_1_, ...), custom_call_target="tpu_custom_call" | custom-call | flops 1024 | bytes 1048576 | tf_op jit(solution)/shard_map/pallas_call | solution.py:656
  13.1 0.1 collective-permute-done.2.refs_2_
  13.3 0.3 %shard_map.161 = (f32[3,64,128]{2,1,0:T(8,128)S(1)}, f32[64,128]{1,0:T(8,128)S(1)}, f32[21,64,128]{2,1,0:T(8,128)S(1)}, f32[64,128]{1,0:T(8,128)S(1)}, f32[64,128]{1,0:T(8,128)S(1)}, /*index=5*/f32[120,128]{1,0:T(8,128)S(1)}) custom-call(f32[19,64,128]{2,1,0:T(8,128)S(1)} %bitcast.25, f32[7,64,128]{2,1,0:T(8,128)S(1)} %get-tuple-element.66.refs_3_.refs_1_, ...), custom_call_target="tpu_custom_call" | custom-call | flops 1048576 | bytes 1048576 | tf_op jit(solution)/shard_map/pallas_call | solution.py:656
  13.6 1.6 %collective-permute-start.7 = (f32[120,128]{1,0:T(8,128)S(1)}, f32[120,128]{1,0:T(8,128)S(1)}, u32[]{:S(2)}, u32[]{:S(2)}) collective-permute-start(f32[120,128]{1,0:T(8,128)S(1)} %get-tuple-element.83), channel_id=1, source_target_pairs={{0,16},{16,0},{1,17},{17,1},{2,18},{18,2},{3,19},{19,3},{4,20},{20... | collective-permute-start | bytes 184328 | tf_op jit(solution)/shard_map/ppermute | solution.py:85
  15.2 0.8 %shard_map.162 = (f32[19,64,128]{2,1,0:T(8,128)S(1)}, f32[64,128]{1,0:T(8,128)S(1)}, f32[64,128]{1,0:T(8,128)S(1)}, f32[19,16,128]{2,1,0:T(8,128)S(1)}, f32[19,1...) custom-call(f32[19,64,128]{2,1,0:T(8,128)S(1)} %bitcast.26, f32[19,64,128]{2,1,0:T(8,128)S(1)} %get-tuple-element.67.refs_8_.refs_1_, ...), custom_call_target="tpu_custom_call" | custom-call | flops 4294967296 | bytes 1048576 | tf_op jit(solution)/shard_map/pallas_call | solution.py:656
  16.1 2.7 %collective-permute-start.11 = (f32[19,16,128]{2,1,0:T(8,128)S(1)}, f32[19,16,128]{2,1,0:T(8,128)S(1)}, u32[]{:S(2)}, u32[]{:S(2)}) collective-permute-start(f32[19,16,128]{2,1,0:T(8,128)S(1)} %get-tuple-element.102), channel_id=1, source_target_pairs={{0,4},{1,2},{2,1},{3,7},{4,0},{5,6},{6,5},{7,3},{8,12},{9,10},{10,... | collective-permute-start | bytes 466952 | tf_op jit(solution)/shard_map/ppermute | solution.py:755
  18.8 0.3 %shard_map.163 = (f32[7,64,128]{2,1,0:T(8,128)S(1)}, f32[32,128]{1,0:T(8,128)S(1)}, f32[32,128]{1,0:T(8,128)S(1)}, f32[48,128]{1,0:T(8,128)S(1)}, f32[128,128]{1...) custom-call(s32[8,128]{1,0:T(8,128)S(1)} %get-tuple-element.59.refs_0_, ...), custom_call_target="tpu_custom_call" | custom-call | flops 4294967296 | bytes 1048576 | tf_op jit(solution)/shard_map/pallas_call | solution.py:656
  19.2 1.8 %collective-permute-start.8 = (f32[32,128]{1,0:T(8,128)S(1)}, f32[32,128]{1,0:T(8,128)S(1)}, u32[]{:S(2)}, u32[]{:S(2)}) collective-permute-start(f32[32,128]{1,0:T(8,128)S(1)} %get-tuple-element.99), channel_id=1, source_target_pairs={{0,4},{1,5},{2,6},{3,7},{4,0},{5,1},{6,2},{7,3},{8,12},{9,13},{10,... | collective-permute-start | bytes 49160 | tf_op jit(solution)/shard_map/ppermute | solution.py:779
  21.0 1.2 %collective-permute-start.9 = (f32[32,128]{1,0:T(8,128)S(1)}, f32[32,128]{1,0:T(8,128)S(1)}, u32[]{:S(2)}, u32[]{:S(2)}) collective-permute-start(f32[32,128]{1,0:T(8,128)S(1)} %get-tuple-element.100), channel_id=1, source_target_pairs={{0,1},{1,0},{2,3},{3,2},{4,8},{5,9},{6,10},{7,11},{8,4},{9,5},{10,... | collective-permute-start | bytes 49160 | tf_op jit(solution)/shard_map/ppermute | solution.py:780
  22.2 1.4 %shard_map.164 = (f32[19,64,128]{2,1,0:T(8,128)S(1)}, f32[64,128]{1,0:T(8,128)}, f32[64,128]{1,0:T(8,128)}, f32[64,128]{1,0:T(8,128)}, f32[64,128]{1,0:T(8,128)}) custom-call(f32[3,19,8,128]{3,2,1,0:T(8,128)S(1)} %get-tuple-element.57.refs_0_, f32[19,64,128]{2,1,0:T(8,128)S(1)} %get-tuple-element.79.refs_1_.refs_0_, ...), custom_call_target="tpu_custom_call" | custom-call | flops 1024 | bytes 1048576 | tf_op jit(solution)/shard_map/pallas_call | solution.py:656
  23.7 1.1 %shard_map.165 = f32[19,64,128]{2,1,0:T(8,128)} custom-call(f32[19,64,128]{2,1,0:T(8,128)S(1)} %get-tuple-element.79.refs_1_.refs_0_, f32[19,64,128]{2,1,0:T(8,128)S(1)} %get-tuple-element.98.refs_1_, f32[7,64,128]{2,1,0:T(8,128)S(1)} %get-tuple-element.89.refs_3_.refs_2_, f32[32,128]{1,0:T(8,128)S(1)} %collective-permute-done.8.refs_3_, ...), custom_call_target="tpu_custom_call" | custom-call | flops 1048576 | bytes 1048576 | tf_op jit(solution)/shard_map/pallas_call | solution.py:656
  (37 shorter events, 0.3 us)
Async XLA Ops:
  0.6 3.9 %copy-start = (f32[19,16,4,128]{3,2,1,0:T(4,128)S(1)}, f32[19,16,4,128]{3,2,1,0:T(4,128)}, u32[]{:S(2)}) copy-start(f32[19,16,4,128]{3,2,1,0:T(4,128)} %param.17) | copy-start | bytes 1867780
  0.6 0.8 %copy-start.1 = (f32[32,1,2,128]{3,2,1,0:T(2,128)S(1)}, f32[32,1,2,128]{3,2,1,0:T(2,128)}, u32[]{:S(2)}) copy-start(f32[32,1,2,128]{3,2,1,0:T(2,128)} %param.12) | copy-start | bytes 98308
  0.7 0.8 %copy-start.2 = (f32[32,1,2,128]{3,2,1,0:T(2,128)S(1)}, f32[32,1,2,128]{3,2,1,0:T(2,128)}, u32[]{:S(2)}) copy-start(f32[32,1,2,128]{3,2,1,0:T(2,128)} %param.13) | copy-start | bytes 98308
  0.7 0.8 %copy-start.3 = (f32[32,1,2,128]{3,2,1,0:T(2,128)S(1)}, f32[32,1,2,128]{3,2,1,0:T(2,128)}, u32[]{:S(2)}) copy-start(f32[32,1,2,128]{3,2,1,0:T(2,128)} %param.14) | copy-start | bytes 98308
  0.7 0.8 %copy-start.4 = (f32[32,1,2,128]{3,2,1,0:T(2,128)S(1)}, f32[32,1,2,128]{3,2,1,0:T(2,128)}, u32[]{:S(2)}) copy-start(f32[32,1,2,128]{3,2,1,0:T(2,128)} %param.15) | copy-start | bytes 98308
  0.7 0.8 %copy-start.5 = (f32[32,1,2,128]{3,2,1,0:T(2,128)S(1)}, f32[32,1,2,128]{3,2,1,0:T(2,128)}, u32[]{:S(2)}) copy-start(f32[32,1,2,128]{3,2,1,0:T(2,128)} %param.16) | copy-start | bytes 98308
  0.7 0.8 %copy-start.9 = (f32[19]{0:T(128)S(1)}, f32[19]{0:T(128)}, u32[]{:S(2)}) copy-start(f32[19]{0:T(128)} %param.23) | copy-start | bytes 232
  1.6 7.5 %collective-permute-start.1 = (f32[180,128]{1,0:T(8,128)S(1)}, f32[180,128]{1,0:T(8,128)S(1)}, u32[]{:S(2)}, u32[]{:S(2)}) collective-permute-start(f32[180,128]{1,0:T(8,128)S(1)} %get-tuple-element.65), channel_id=1, source_target_pairs={{0,16},{16,0},{1,17},{17,1},{2,18},{18,2},{3,19},{19,3},{4,20},{20... | collective-permute-start | bytes 276488 | tf_op jit(solution)/shard_map/ppermute | solution.py:85
  4.6 0.7 %copy-start.6 = (f32[19,19]{1,0:T(8,128)S(1)}, f32[19,19]{1,0:T(8,128)}, u32[]{:S(2)}) copy-start(f32[19,19]{1,0:T(8,128)} %refs_6_.1) | copy-start | bytes 4336
  4.7 4.4 %collective-permute-start = (f32[120,128]{1,0:T(8,128)S(1)}, f32[120,128]{1,0:T(8,128)S(1)}, u32[]{:S(2)}, u32[]{:S(2)}) collective-permute-start(f32[120,128]{1,0:T(8,128)S(1)} %get-tuple-element.63), channel_id=1, source_target_pairs={{0,16},{16,0},{1,17},{17,1},{2,18},{18,2},{3,19},{19,3},{4,20},{20... | collective-permute-start | bytes 184328 | tf_op jit(solution)/shard_map/ppermute | solution.py:85
  4.9 0.7 %copy-start.7 = (s32[4,128]{1,0:T(4,128)S(1)}, s32[4,128]{1,0:T(4,128)}, u32[]{:S(2)}) copy-start(s32[4,128]{1,0:T(4,128)} %refs_3_.1) | copy-start | bytes 6148
  4.9 0.7 %copy-start.10 = (f32[19]{0:T(128)S(1)}, f32[19]{0:T(128)}, u32[]{:S(2)}) copy-start(f32[19]{0:T(128)} %param.21) | copy-start | bytes 232
  4.9 0.7 %copy-start.11 = (f32[19]{0:T(128)S(1)}, f32[19]{0:T(128)}, u32[]{:S(2)}) copy-start(f32[19]{0:T(128)} %param.22) | copy-start | bytes 232
  7.0 6.3 %collective-permute-start.4 = (f32[21,16,128]{2,1,0:T(8,128)S(1)}, f32[21,16,128]{2,1,0:T(8,128)S(1)}, u32[]{:S(2)}, u32[]{:S(2)}) collective-permute-start(f32[21,16,128]{2,1,0:T(8,128)S(1)} %get-tuple-element.70), channel_id=1, source_target_pairs={{0,1},{1,0},{2,3},{3,2},{4,5},{5,4},{6,7},{7,6},{8,9},{9,8},{10,11... | collective-permute-start | bytes 516104 | tf_op jit(solution)/shard_map/ppermute | solution.py:754
  7.1 6.2 %collective-permute-start.5 = (f32[21,16,128]{2,1,0:T(8,128)S(1)}, f32[21,16,128]{2,1,0:T(8,128)S(1)}, u32[]{:S(2)}, u32[]{:S(2)}) collective-permute-start(f32[21,16,128]{2,1,0:T(8,128)S(1)} %get-tuple-element.71), channel_id=1, source_target_pairs={{0,4},{1,2},{2,1},{3,7},{4,0},{5,6},{6,5},{7,3},{8,12},{9,10},{10,... | collective-permute-start | bytes 516104 | tf_op jit(solution)/shard_map/ppermute | solution.py:755
  9.4 3.9 %collective-permute-start.6 = (f32[48,128]{1,0:T(8,128)S(1)}, f32[48,128]{1,0:T(8,128)S(1)}, u32[]{:S(2)}, u32[]{:S(2)}) collective-permute-start(f32[48,128]{1,0:T(8,128)S(1)} %get-tuple-element.72), channel_id=1, source_target_pairs={{0,1},{1,2},{2,3},{3,0},{4,5},{5,6},{6,7},{7,4},{8,9},{9,10},{10,1... | collective-permute-start | bytes 73736 | tf_op jit(solution)/shard_map/ppermute | solution.py:781
  9.5 3.8 %collective-permute-start.2 = (f32[32,128]{1,0:T(8,128)S(1)}, f32[32,128]{1,0:T(8,128)S(1)}, u32[]{:S(2)}, u32[]{:S(2)}) collective-permute-start(f32[32,128]{1,0:T(8,128)S(1)} %get-tuple-element.68), channel_id=1, source_target_pairs={{0,4},{1,5},{2,6},{3,7},{4,0},{5,1},{6,2},{7,3},{8,12},{9,13},{10,... | collective-permute-start | bytes 49160 | tf_op jit(solution)/shard_map/ppermute | solution.py:779
  11.1 2.2 %collective-permute-start.3 = (f32[32,128]{1,0:T(8,128)S(1)}, f32[32,128]{1,0:T(8,128)S(1)}, u32[]{:S(2)}, u32[]{:S(2)}) collective-permute-start(f32[32,128]{1,0:T(8,128)S(1)} %get-tuple-element.69), channel_id=1, source_target_pairs={{0,1},{1,0},{2,3},{3,2},{4,8},{5,9},{6,10},{7,11},{8,4},{9,5},{10,... | collective-permute-start | bytes 49160 | tf_op jit(solution)/shard_map/ppermute | solution.py:780
  13.6 5.2 %collective-permute-start.7 = (f32[120,128]{1,0:T(8,128)S(1)}, f32[120,128]{1,0:T(8,128)S(1)}, u32[]{:S(2)}, u32[]{:S(2)}) collective-permute-start(f32[120,128]{1,0:T(8,128)S(1)} %get-tuple-element.83), channel_id=1, source_target_pairs={{0,16},{16,0},{1,17},{17,1},{2,18},{18,2},{3,19},{19,3},{4,20},{20... | collective-permute-start | bytes 184328 | tf_op jit(solution)/shard_map/ppermute | solution.py:85
  16.0 7.7 %collective-permute-start.10 = (f32[19,16,128]{2,1,0:T(8,128)S(1)}, f32[19,16,128]{2,1,0:T(8,128)S(1)}, u32[]{:S(2)}, u32[]{:S(2)}) collective-permute-start(f32[19,16,128]{2,1,0:T(8,128)S(1)} %get-tuple-element.101), channel_id=1, source_target_pairs={{0,1},{1,0},{2,3},{3,2},{4,5},{5,4},{6,7},{7,6},{8,9},{9,8},{10,11... | collective-permute-start | bytes 466952 | tf_op jit(solution)/shard_map/ppermute | solution.py:754
  16.1 7.6 %collective-permute-start.11 = (f32[19,16,128]{2,1,0:T(8,128)S(1)}, f32[19,16,128]{2,1,0:T(8,128)S(1)}, u32[]{:S(2)}, u32[]{:S(2)}) collective-permute-start(f32[19,16,128]{2,1,0:T(8,128)S(1)} %get-tuple-element.102), channel_id=1, source_target_pairs={{0,4},{1,2},{2,1},{3,7},{4,0},{5,6},{6,5},{7,3},{8,12},{9,10},{10,... | collective-permute-start | bytes 466952 | tf_op jit(solution)/shard_map/ppermute | solution.py:755
  19.2 4.5 %collective-permute-start.12 = (f32[48,128]{1,0:T(8,128)S(1)}, f32[48,128]{1,0:T(8,128)S(1)}, u32[]{:S(2)}, u32[]{:S(2)}) collective-permute-start(f32[48,128]{1,0:T(8,128)S(1)} %get-tuple-element.103), channel_id=1, source_target_pairs={{0,1},{1,2},{2,3},{3,0},{4,5},{5,6},{6,7},{7,4},{8,9},{9,10},{10,1... | collective-permute-start | bytes 73736 | tf_op jit(solution)/shard_map/ppermute | solution.py:781
  19.2 4.4 %collective-permute-start.8 = (f32[32,128]{1,0:T(8,128)S(1)}, f32[32,128]{1,0:T(8,128)S(1)}, u32[]{:S(2)}, u32[]{:S(2)}) collective-permute-start(f32[32,128]{1,0:T(8,128)S(1)} %get-tuple-element.99), channel_id=1, source_target_pairs={{0,4},{1,5},{2,6},{3,7},{4,0},{5,1},{6,2},{7,3},{8,12},{9,13},{10,... | collective-permute-start | bytes 49160 | tf_op jit(solution)/shard_map/ppermute | solution.py:779
  21.0 2.6 %collective-permute-start.9 = (f32[32,128]{1,0:T(8,128)S(1)}, f32[32,128]{1,0:T(8,128)S(1)}, u32[]{:S(2)}, u32[]{:S(2)}) collective-permute-start(f32[32,128]{1,0:T(8,128)S(1)} %get-tuple-element.100), channel_id=1, source_target_pairs={{0,1},{1,0},{2,3},{3,2},{4,8},{5,9},{6,10},{7,11},{8,4},{9,5},{10,... | collective-permute-start | bytes 49160 | tf_op jit(solution)/shard_map/ppermute | solution.py:780
  (1 other events, 0.7 us)

commit v6 on v5

--- a/solution.py
+++ b/solution.py
@@ -108,54 +108,56 @@
     return value
 
 
-def pack_sides(c, slot, left, right):
-    lane = iota(c.shape, 1)
-    left = jnp.where(lane == 2 * slot, turn(c, 2 * slot, 1), left)
-    right = jnp.where(lane == 2 * slot, turn(c, 2 * slot + 1, 1), right)
+def folds(slots, cells, width):
+    return 4 * slots < width and cells % (2 * SUB) == 0
+
+
+def halves_of(cells, slots, width):
+    if not folds(slots, cells, width):
+        return [(slice(0, cells), 0)]
+    return [(slice(0, cells // 2), 0), (slice(cells // 2, cells), width // 2)]
+
+
+def pack_sides(c, slot, slots, left, right):
+    cells, width = c.shape
+    at = 2 * (slot + 1)
+    lane = iota(left.shape, 1)
+    for rows, base in halves_of(cells, slots, width):
+        left = jnp.where(lane == base + at - 1, turn(c[rows], base + at - 1, 1), left)
+        right = jnp.where(lane == base + at, turn(c[rows], base + at + 1, 1), right)
     return left, right
 
 
-def folds(slots, cells, width):
-    return 4 * slots <= width and cells % (2 * SUB) == 0
-
-
-def fold(v, slots):
-    cells, width = v.shape
-    if not folds(slots, cells, width):
-        return v
-    half = cells // 2
-    return jnp.where(iota((half, width), 1) < width // 2, v[:half], turn(v[half:], width // 2, 1))
-
-
-def unfold(v, slots, cells):
-    width = v.shape[1]
-    if not folds(slots, cells, width):
-        return v
-    return jnp.concatenate([v, turn(v, width // 2, 1)], axis=0)
+def sides_of(halo, slot, slots, cells):
+    at = 2 * (slot + 1)
+    width = halo.shape[1]
+    turned = [turn(halo, -at - base, 1) for _, base in halves_of(cells, slots, width)]
+    return turned[0] if len(turned) == 1 else jnp.concatenate(turned, axis=0)
 
 
 def compact(rows, cells, count):
     return count == 2 and SUB == 2 * rows and cells >= 2 * SUB
 
 
-def level_base(rows, cells, count):
-    if count != 2:
-        return SUB
+def level_base(rows, cells, count, together):
+    if not together:
+        return SUB - rows
     return cells // 2 + SUB if compact(rows, cells, count) else cells
 
 
-def message_shapes(tracers, rows, cells, width, count):
-    height = level_base(rows, cells, count) + tracers * rows + (SUB - rows)
+def message_shapes(tracers, rows, cells, width, count, together):
+    height = level_base(rows, cells, count, together) + tracers * rows + (SUB - rows)
     height += -height % SUB
-    if count == 2:
+    if together:
         return [shape(height, width)]
-    return [shape(cells, width), shape(height, width), shape(height, width)]
+    pigment = cells // 2 + SUB if compact(rows, cells, count) else cells
+    return [shape(pigment, width)] + [shape(height, width)] * (1 if count == 2 else 2)
 
 
 def write_levels(last, first, t, rows, base, msgs, g):
     here = pl.ds(base + t * rows, rows)
-    if len(msgs) == 1:
-        msgs[0][here, :] = jnp.where(g == 0, last[SUB - rows :], first[:rows])
+    if len(msgs) < 3:
+        msgs[-1][here, :] = jnp.where(g == 0, last[SUB - rows :], first[:rows])
     else:
         msgs[1][here, :] = last[SUB - rows :]
         msgs[2][here, :] = first[:rows]
@@ -219,10 +221,13 @@
     out_ref[...] = jnp.zeros(out_ref.shape, F32)
 
 
-def raw_kernel(rows, count, first_ref, pig_in, *refs):
-    *fields, raw_ref, out_ref, pig_out = refs
+def raw_kernel(rows, count, first_ref, *refs):
+    refs = Refs(refs)
+    fields, small_in = refs.take(5), refs.take(6)
+    raw_ref, out_ref = refs.take(2)
     g = lax.axis_index("grp")
-    pig_out[...] = pig_in[...]
+    for small, small_out in zip(small_in, refs.take(6)):
+        small_out[...] = small[...]
     strip_cells = raw_ref.shape[1]
     low, height = raw_window(rows, count, strip_cells, 0)
     high, _ = raw_window(rows, count, strip_cells, 1)
@@ -240,7 +245,7 @@
 def prep_kernel(rows, count, pig_ref, c_ref, p_ref, *msgs):
     g = lax.axis_index("grp")
     tracers, cells, width = c_ref.shape
-    base = level_base(rows, cells, count)
+    base = level_base(rows, cells, count, False)
     weights = pig_ref[...]
     pigment = jnp.zeros((cells, width), F32)
     for t in range(tracers):
@@ -291,10 +296,10 @@
     tracers, cells, _ = c_ref.shape
     levels = cells // rows
     x_even = lax.rem(lax.axis_index("gx"), 2) == 0
-    left = right = jnp.zeros(c_ref.shape[1:], F32)
-    left, right = pack_sides(p_ref[...], tracers + 2, left, right)
+    left = right = jnp.zeros(msg_xa.shape, F32)
+    left, right = pack_sides(p_ref[...], tracers + 2, tracers + 3, left, right)
     for t in range(tracers):
-        left, right = pack_sides(c_ref[t], t, left, right)
+        left, right = pack_sides(c_ref[t], t, tracers + 3, left, right)
     msg_xa[...] = jnp.where(x_even, right, left)
     msg_xb[...] = jnp.where(x_even, left, right)
     first, last = pl.ds(0, levels, stride=rows), pl.ds(rows - 1, levels, stride=rows)
@@ -306,25 +311,18 @@
 
 def pack_kernel(rows, *refs):
     refs = Refs(refs)
-    photo_ref, sat_ref, pig_ref, depth_in, solar_in, c_ref, rates_ref, p_ref = refs.take(8)
-    msg_xa, msg_xb, msg_ya, msg_yb, w_ref, mix_ref, tiles_ref, depth_ref, solar_ref = refs.take(9)
+    depth_in, solar_in, c_ref, p_ref = refs.take(4)
+    msg_xa, msg_xb, msg_ya, msg_yb, depth_ref, solar_ref = refs.take(6)
     tracers, cells, width = c_ref.shape
     for r in range(0, SUB, rows):
         depth_ref[pl.ds(r, rows), :] = depth_in[...]
         solar_ref[pl.ds(r, rows), :] = solar_in[...]
-    for at, param in enumerate((photo_ref, sat_ref, pig_ref)):
-        values = param[...]
-        for t in range(tracers):
-            tiles_ref[at, t] = jnp.broadcast_to(values[:, t : t + 1], (SUB, width))
     pack(rows, c_ref, p_ref, msg_xa, msg_xb, msg_ya, msg_yb)
     levels = cells // rows
     level = lax.axis_index("grp") * levels + iota((levels, width), 0)
     wet_first = jnp.where(level < depth_in[pl.ds(0, 1), :], 1.0, 0.0)
     wet_last = jnp.where(level < depth_in[pl.ds(rows - 1, 1), :], 1.0, 0.0)
     put_rows(msg_ya, msg_yb, tracers + 1, wet_first, wet_last)
-    weights = spread_rates(rates_ref[...], tracers)
-    w_ref[...] = weights
-    mix(weights, c_ref, mix_ref)
 
 
 def ocean_kernel(rows, count, tracers, first_step, *refs):
@@ -344,7 +342,7 @@
         other_s = refs.take(5 * (count - 1))
     face_s, par_s, wet_s = refs.take(3)
     g = lax.axis_index("grp")
-    cells, width = in_xa.shape
+    cells, width = p_own.shape
     levels = cells // rows
     total = count * cells
     all_levels = total // rows
@@ -427,10 +425,10 @@
     x_even = lax.rem(lax.axis_index("gx"), 2) == 0
     xa, xb = in_xa[...], in_xb[...]
     left, right = jnp.where(x_even, xb, xa), jnp.where(x_even, xa, xb)
-    left, right = pack_sides(wet_band, tracers + 1, left, right)
-    _, right = pack_sides(u, tracers, left, right)
-    msg_xa[...] = fold(jnp.where(x_even, right, left), tracers + 3)
-    msg_xb[...] = fold(jnp.where(x_even, left, right), tracers + 3)
+    left, right = pack_sides(wet_band, tracers + 1, tracers + 3, left, right)
+    _, right = pack_sides(u, tracers, tracers + 3, left, right)
+    msg_xa[...] = jnp.where(x_even, right, left)
+    msg_xb[...] = jnp.where(x_even, left, right)
     speed_ref[pl.ds(0, levels), :] = band_ref[1, pl.ds(rows - 1, levels, stride=rows), :]
     speed_ref[pl.ds(levels, levels), :] = jnp.zeros((levels, width), F32)
     speed_ref[pl.ds(2 * levels, levels), :] = jnp.zeros((levels, width), F32)
@@ -458,21 +456,36 @@
     return opening * (jnp.minimum(speed, 0.0) - SIDE_DIFFUSE)
 
 
-def inner_kernel(rows, count, last_step, *refs):
+def inner_kernel(rows, count, first_step, last_step, *refs):
     refs = Refs(refs)
-    tiles_ref, c_ref, mix_ref, band_ref = refs.take(4)
+    if first_step:
+        params, (rates_ref,) = refs.take(3), refs.take(1)
+    else:
+        tiles_ref, w_ref = refs.take(2)
+    c_ref, band_ref = refs.take(2)
     lev_in = refs.take(1 if count == 2 else 2)
     if last_step:
         full = refs.take(4)
     (part_ref,) = refs.take(1)
     if last_step:
-        outs, strips = refs.take(4), refs.take(4)
-        (sems,) = refs.take(1)
-        copies = start_own_strip(rows, count, lax.axis_index("grp"), full, outs, strips, sems)
+        outs = refs.take(4)
     else:
         (p_part,) = refs.take(1)
+    if first_step:
+        tiles_ref, w_ref = refs.take(2)
+    if last_step:
+        strips, (sems,) = refs.take(4), refs.take(1)
+        copies = start_own_strip(rows, count, lax.axis_index("grp"), full, outs, strips, sems)
+    (mix_ref,) = refs.take(1)
     tracers, cells, width = c_ref.shape
-    base = level_base(rows, cells, count)
+    if first_step:
+        w_ref[...] = spread_rates(rates_ref[...], tracers)
+        for at, param in enumerate(params):
+            values = param[...]
+            for t in range(tracers):
+                tiles_ref[at, t] = jnp.broadcast_to(values[:, t : t + 1], (SUB, width))
+    mix(w_ref[...], c_ref, mix_ref)
+    base = level_base(rows, cells, count, False)
     lane = iota((cells, width), 1)
     at_row = lax.rem(iota((cells, width), 0), rows)
     u = band_ref[0]
@@ -532,12 +545,10 @@
         p_part[...] = pigment
 
 
-def x_halo(got_xa, got_xb, slots, cells):
+def x_halo(got_xa, got_xb):
     x_even = lax.rem(lax.axis_index("gx"), 2) == 0
     xa, xb = got_xa[...], got_xb[...]
-    west = jnp.where(x_even, xb, xa)
-    east = turn(jnp.where(x_even, xa, xb), -1, 1)
-    return unfold(jnp.where(lax.rem(iota(xa.shape, 1), 2) == 0, west, east), slots, cells)
+    return jnp.where((lax.rem(iota(xa.shape, 1), 2) == 0) == x_even, xb, xa)
 
 
 def spread_rows(rows, got_ya, got_yb, out_ref, slot):
@@ -548,7 +559,7 @@
     out_ref[slot, pl.ds(rows - 1, levels, stride=rows), :] = jnp.where(y_even, ya, yb)
 
 
-def side_factors(rows, sizes, halo, wet_out, speed, speed_s, band_ref, tracers):
+def side_factors(rows, sizes, halo_ref, wet_out, speed, speed_s, band_ref, tracers):
     _, size_x, size_y = sizes
     x = lax.axis_index("gx")
     y = lax.axis_index("gy")
@@ -560,13 +571,13 @@
     lane = iota((cells, width), 1)
     at_row = lax.rem(iota((cells, width), 0), rows)
     at_w, at_e, at_s, at_n = lane == 0, lane == width - 1, at_row == 0, at_row == rows - 1
-    wet_x = wet * turn(halo, -2 * (tracers + 1), 1)
+    wet_x = wet * sides_of(halo_ref[...], tracers + 1, tracers + 3, cells)
     wet_y = wet * wet_out
     open_w = jnp.where(at_w & (x > 0), wet_x, 0.0)
     open_e = jnp.where(at_e & (x < size_x - 1), wet_x, 0.0)
     open_s = jnp.where(at_s & (y > 0), wet_y, 0.0)
     open_n = jnp.where(at_n & (y < size_y - 1), wet_y, 0.0)
-    u_w = turn(halo, -2 * tracers, 1)
+    u_w = sides_of(halo_ref[...], tracers, tracers + 3, cells)
     v_s = jnp.where(at_s, speed_s[...], 0.0)
     k_x = lower(open_w, u_w) - upper(open_e, u)
     k_y = lower(open_s, v_s) - upper(open_n, v)
@@ -574,11 +585,11 @@
     return k_x, k_y, k_c
 
 
-def sideways(rows, factors, halo, outer, c, slot):
+def sideways(rows, factors, sides, outer, c):
     k_x, k_y, k_c = factors
     at_row = lax.rem(iota(c.shape, 0), rows)
     edge = (at_row == 0) | (at_row == rows - 1)
-    return (k_x * turn(halo, -2 * slot, 1) + k_c * c) + jnp.where(edge, k_y * outer, 0.0)
+    return (k_x * sides + k_c * c) + jnp.where(edge, k_y * outer, 0.0)
 
 
 def early_kernel(rows, count, sizes, first_step, *refs):
@@ -592,40 +603,43 @@
     msgs, speed_s = refs.refs[:-1], refs.refs[-1]
     g = lax.axis_index("grp")
     tracers, cells, width = c_ref.shape
-    base = level_base(rows, cells, count)
-    halo = x_halo(got_xa, got_xb, tracers + 3, cells)
-    halo_ref[...] = halo
+    lev_base = level_base(rows, cells, count, False)
+    halo_ref[...] = x_halo(got_xa, got_xb)
     for slot in range(got_ya.shape[0]):
         spread_rows(rows, got_ya, got_yb, spread_s, slot)
     wet_out[...] = spread_s[tracers + 1] if first_step else wet_in[...]
-    factors = side_factors(rows, sizes, halo, wet_out[...], speed, speed_s, band_ref, tracers)
+    factors = side_factors(rows, sizes, halo_ref, wet_out[...], speed, speed_s, band_ref, tracers)
     for at, k in enumerate(factors):
         k_ref[at] = k
-    change = sideways(rows, factors, halo, spread_s[tracers], p_in[...], tracers + 2)
+    side = sides_of(halo_ref[...], tracers + 2, tracers + 3, cells)
+    change = sideways(rows, factors, side, spread_s[tracers], p_in[...])
     p_ref[...] = p_part[...] + change
     write_pigment(rows, count, p_ref, msgs[0], g)
 
     def block(at, t):
         here = pl.ds(at, SUB)
         cut = [k[at : at + SUB] for k in factors]
-        change = sideways(rows, cut, halo[at : at + SUB], spread_s[t, here, :], c_ref[t, here, :], t)
+        for part, base in halves_of(cells, tracers + 3, width):
+            if part.start <= at < part.stop:
+                side = turn(halo_ref[pl.ds(at - part.start, SUB), :], -2 * (t + 1) - base, 1)
+        change = sideways(rows, cut, side, spread_s[t, here, :], c_ref[t, here, :])
         return part_ref[t, here, :] + change
 
     for t in range(tracers):
-        write_levels(block(cells - SUB, t), block(0, t), t, rows, base, msgs, g)
+        write_levels(block(cells - SUB, t), block(0, t), t, rows, lev_base, msgs, g)
 
 
 def step_kernel(rows, *refs):
     refs = Refs(refs)
-    c_ref, part_ref, k_ref, halo_ref, spread_s, w_ref, p_ref = refs.take(7)
-    out_ref, msg_xa, msg_xb, msg_ya, msg_yb, mix_ref = refs.take(6)
+    c_ref, part_ref, k_ref, halo_ref, spread_s, p_ref = refs.take(6)
+    out_ref, msg_xa, msg_xb, msg_ya, msg_yb = refs.take(5)
     tracers = c_ref.shape[0]
     factors = [k_ref[i] for i in range(3)]
-    halo = halo_ref[...]
     for t in range(tracers):
-        out_ref[t] = part_ref[t] + sideways(rows, factors, halo, spread_s[t], c_ref[t], t)
+        out_ref[t] = part_ref[t] + sideways(
+                rows, factors, sides_of(halo_ref[...], t, tracers + 3, c_ref.shape[1]), spread_s[t], c_ref[t]
+            )
     pack(rows, out_ref, p_ref, msg_xa, msg_xb, msg_ya, msg_yb)
-    mix(w_ref[...], out_ref, mix_ref)
 
 
 def final_kernel(rows, sizes, first_step, *refs):
@@ -634,18 +648,20 @@
     (speed,) = refs.take(1)
     if not first_step:
         (wet_in,) = refs.take(1)
-    out_hbm, spread_s, speed_s, new_s, sems = refs.take(5)
-    tracers, cells, _ = c_ref.shape
-    halo = x_halo(got_xa, got_xb, tracers + 3, cells)
+    out_hbm, spread_s, speed_s, halo_ref, new_s, sems = refs.take(6)
+    tracers = c_ref.shape[0]
+    halo_ref[...] = x_halo(got_xa, got_xb)
     if first_step:
         spread_rows(rows, got_ya, got_yb, spread_s, tracers + 1)
     wet_out = spread_s[tracers + 1] if first_step else wet_in[...]
-    factors = side_factors(rows, sizes, halo, wet_out, speed, speed_s, band_ref, tracers)
+    factors = side_factors(rows, sizes, halo_ref, wet_out, speed, speed_s, band_ref, tracers)
     copies = []
     for i, (a, n) in enumerate(chunks(tracers, sems.shape[0])):
         for t in range(a, a + n):
             spread_rows(rows, got_ya, got_yb, spread_s, t)
-            new_s[t] = part_ref[t] + sideways(rows, factors, halo, spread_s[t], c_ref[t], t)
+            new_s[t] = part_ref[t] + sideways(
+                rows, factors, sides_of(halo_ref[...], t, tracers + 3, c_ref.shape[1]), spread_s[t], c_ref[t]
+            )
         copies.append(pltpu.make_async_copy(new_s.at[pl.ds(a, n)], out_hbm.at[pl.ds(a, n)], sems.at[i]))
         copies[-1].start()
     for copy in copies:
@@ -705,22 +721,28 @@
         p.reshape(1, tracers) for p in (photosynthetic_rates, saturation_irradiance, pigment_per_tracer)
     ]
     (first,) = call(first_kernel, [], [shape(SUB, width)], flops=1 << 30)
-    raw, window, pig = call(
+    small = [*params, interaction_rates, submerged_layer_number, solar_radiation]
+    raw, window, *small = call(
         functools.partial(raw_kernel, rows, count),
-        [first, params[2], *own],
-        [shape(5, strip_cells, width), shape(5 * height, width), shape(1, tracers)],
+        [first, *own, *small],
+        [
+            shape(5, strip_cells, width),
+            shape(5 * height, width),
+            *[jax.ShapeDtypeStruct(v.shape, v.dtype) for v in small],
+        ],
     )
+    *params, rates, layers, light = small
     raw_others = from_others(window, count)
 
-    messages = message_shapes(tracers, rows, cells, width, count)
+    messages = message_shapes(tracers, rows, cells, width, count, False)
     cols = shape(cells, width)
     sent_cols = shape(cells // 2, width) if folds(tracers + 3, cells, width) else cols
     field = shape(tracers, cells, width)
     c = substance_amounts.reshape(tracers, cells, width)
     pigment, *msgs = call(
         functools.partial(prep_kernel, rows, count),
-        [pig, c],
-        [cols, *messages],
+        [params[2], c],
+        [cols, *message_shapes(tracers, rows, cells, width, count, False)],
     )
     full = None
     for step in range(STEPS):
@@ -728,33 +750,23 @@
         p_others = from_others(msgs[0], count)
         if first_step:
             lines = shape(tracers + 2, levels, width)
-            xa, xb, ya, yb, weights, mixed, tiles, depth, solar = call(
+            xa, xb, ya, yb, depth, solar = call(
                 functools.partial(pack_kernel, rows),
+                [layers, light, c, pigment],
                 [
-                    *params,
-                    submerged_layer_number,
-                    solar_radiation,
-                    c,
-                    interaction_rates,
-                    pigment,
-                ],
-                [
-                    cols,
-                    cols,
+                    sent_cols,
+                    sent_cols,
                     lines,
                     lines,
-                    shape(tracers * SUB, tracers * SUB),
-                    field,
-                    shape(3, tracers, SUB, width),
                     jax.ShapeDtypeStruct((SUB, width), jnp.int32),
                     shape(SUB, width),
                 ],
-                flops=1<<24,
+                flops=1 << 24,
             )
         ya = lax.ppermute(ya, AXES, pairing(sizes, "gy", 0))
         yb = lax.ppermute(yb, AXES, pairing(sizes, "gy", 1))
         if count == 2:
-            lev = p_others
+            lev = from_others(msgs[-1], count)
         else:
             lev = [
                 lax.ppermute(msgs[1], "grp", [(i, (i + 1) % count) for i in range(count)]),
@@ -779,28 +791,37 @@
         xa = lax.ppermute(xa, AXES, pairing(sizes, "gx", 0))
         xb = lax.ppermute(xb, AXES, pairing(sizes, "gx", 1))
         speed = lax.ppermute(speed, AXES, upward(sizes))
+        tables = [shape(3, tracers, SUB, width), shape(tracers * SUB, tracers * SUB)]
         part, *rest = call(
-            functools.partial(inner_kernel, rows, count, last_step),
-            [tiles, c, mixed, band, *lev, *(full if last_step else [])],
-            [field] + ([shape(strip_cells, width)] * 4 if last_step else [cols]),
-            out_specs=[vmem()] + ([hbm()] * 4 if last_step else [vmem()]),
-            scratch=[pltpu.VMEM((strip_cells, width), F32)] * 4 + [dma((4,))] if last_step else [],
-            flops=1<<10,
+            functools.partial(inner_kernel, rows, count, first_step, last_step),
+            [*([*params, rates] if first_step else known_rates), c, band, *lev, *(full if last_step else [])],
+            [field]
+            + ([shape(strip_cells, width)] * 4 if last_step else [cols])
+            + (tables if first_step else []),
+            out_specs=[vmem()]
+            + ([hbm()] * 4 if last_step else [vmem()])
+            + ([vmem()] * 2 if first_step else []),
+            scratch=([pltpu.VMEM((strip_cells, width), F32)] * 4 + [dma((4,))] if last_step else [])
+            + [pltpu.VMEM((tracers, cells, width), F32)],
+            flops=1 << 10,
         )
+        if first_step:
+            *rest, tiles, weights = rest
+            known_rates = [tiles, weights]
         known = [] if first_step else [wet_out]
         if not last_step:
             k, halo, spread, wet_out, pigment_next, *msgs = call(
                 functools.partial(early_kernel, rows, count, sizes, first_step),
                 [c, band, xa, xb, ya, yb, speed, pigment, part, *rest, *known],
-                [shape(3, cells, width), cols, shape(tracers + 2, cells, width), cols, cols, *messages],
+                [shape(3, cells, width), sent_cols, shape(tracers + 2, cells, width), cols, cols, *messages],
                 scratch=[band_s],
             )
             pigment = pigment_next
             lines = shape(tracers + (0 if step + 1 == STEPS - 1 else 1), levels, width)
-            c, xa, xb, ya, yb, mixed = call(
+            c, xa, xb, ya, yb = call(
                 functools.partial(step_kernel, rows),
-                [c, part, k, halo, spread, weights, pigment],
-                [field, cols, cols, lines, lines, field],
+                [c, part, k, halo, spread, pigment],
+                [field, sent_cols, sent_cols, lines, lines],
                 flops=1<<32,
             )
         else:
@@ -813,6 +834,7 @@
                 scratch=[
                     pltpu.VMEM((tracers + 2, cells, width), F32),
                     band_s,
+                    pltpu.VMEM(sent_cols.shape, F32),
                     pltpu.VMEM((tracers, cells, width), F32),
                     dma((5,)),
                 ],

time: 25.1 us -> 24.2 us (0.964)
  local copies, waits for them, and re-layouts: 1.53 us -> 0.79 us
  Pallas kernels: 6.64 us -> 6.16 us
  starting transfers between devices: 15.7 us -> 16.1 us
    ppermute x3 -> x5, starting transfers between devices: 4.82 us -> 7.19 us  [from_others(): lax.ppermute(value, 'grp', [(i, (i + k) % count) for i in range(count)])]
    unnamed x24, local copies, waits for them, and re-layouts: 1.53 us -> 0.79 us
    ppermute x2, starting transfers between devices: 4.73 us -> 4.01 us  [per_device(): yb = lax.ppermute(yb, AXES, pairing(sizes, 'gy', 1))]
    ppermute x2, starting transfers between devices: 2.4 us -> 1.85 us  [per_device(): xb = lax.ppermute(xb, AXES, pairing(sizes, 'gx', 1))]
    ppermute x2, starting transfers between devices: 3.4 us -> 2.87 us  [per_device(): xa = lax.ppermute(xa, AXES, pairing(sizes, 'gx', 0))]
    pallas_call x11, Pallas kernels: 6.64 us -> 6.16 us  [call(): pl.pallas_call(kernel, in_specs=[vmem() for _ in ins] if in_specs is None...]
  transfers between devices with their start and end apart: 13 -> 15, of which waited for: 1 -> 0; matrix products, arithmetic and copies ran while one was open for 0% -> 0% of each run, Pallas kernels for 21% -> 21%
where the time goes in v6:
time: 24.2 us; the launch traced here: 24 us
  starting transfers between devices  16.1 us (67%)
  Pallas kernels  6.16 us (25%)
  between operations  0.9 us (4%)
  local copies, waits for them, and re-layouts  0.79 us (3%)
    ppermute x5, starting transfers between devices, from_others(): lax.ppermute(value, 'grp', [(i, (i + k) % count) for i in range(count)])  7.19 us
    pallas_call x11, Pallas kernels, call(): pl.pallas_call(kernel, in_specs=[vmem() for _ in ins] if in_specs is None...  6.16 us
    ppermute x2, starting transfers between devices, per_device(): yb = lax.ppermute(yb, AXES, pairing(sizes, 'gy', 1))  4.01 us
    ppermute x2, starting transfers between devices, per_device(): xa = lax.ppermute(xa, AXES, pairing(sizes, 'gx', 0))  2.87 us
    ppermute x2, starting transfers between devices, per_device(): xb = lax.ppermute(xb, AXES, pairing(sizes, 'gx', 1))  1.85 us
    unnamed x24, local copies, waits for them, and re-layouts  0.79 us
  transfers between devices with their start and end apart: 15, of which 0 were waited for; matrix products, arithmetic and copies ran while one was open for 0% of the time, Pallas kernels for 21%

profile of v6, /device:TPU:0, one launch (start us, length us, event | category | flops | bytes accessed | tf_op | source)
XLA Modules:
  0.0 24.0 jit_solution(5329606769010611976)
XLA Ops:
  0.8 0.6 %copy-done.1 = f32[32,1,2,128]{3,2,1,0:T(2,128)S(1)} copy-done((f32[32,1,2,128]{3,2,1,0:T(2,128)S(1)}, f32[32,1,2,128]{3,2,1,0:T(2,128)}, u32[]{:S(2)}) %copy-start.1) | copy-done | bytes 32792
  1.6 3.0 %collective-permute-start.1 = (f32[180,128]{1,0:T(8,128)S(1)}, f32[180,128]{1,0:T(8,128)S(1)}, u32[]{:S(2)}, u32[]{:S(2)}) collective-permute-start(f32[180,128]{1,0:T(8,128)S(1)} %get-tuple-element.73), channel_id=1, source_target_pairs={{0,16},{16,0},{1,17},{17,1},{2,18},{18,2},{3,19},{19,3},{4,20},{20... | collective-permute-start | bytes 276488 | tf_op jit(solution)/shard_map/ppermute | solution.py:85
  4.6 0.1 shard_map.157
  4.7 0.3 %collective-permute-start = (f32[40,128]{1,0:T(8,128)S(1)}, f32[40,128]{1,0:T(8,128)S(1)}, u32[]{:S(2)}, u32[]{:S(2)}) collective-permute-start(f32[40,128]{1,0:T(8,128)S(1)} %get-tuple-element.71), channel_id=1, source_target_pairs={{0,16},{16,0},{1,17},{17,1},{2,18},{18,2},{3,19},{19,3},{4,20},{20... | collective-permute-start | bytes 61448 | tf_op jit(solution)/shard_map/ppermute | solution.py:85
  5.0 1.8 %collective-permute-start.2 = (f32[88,128]{1,0:T(8,128)S(1)}, f32[88,128]{1,0:T(8,128)S(1)}, u32[]{:S(2)}, u32[]{:S(2)}) collective-permute-start(f32[88,128]{1,0:T(8,128)S(1)} %get-tuple-element.75), channel_id=1, source_target_pairs={{0,16},{16,0},{1,17},{17,1},{2,18},{18,2},{3,19},{19,3},{4,20},{20... | collective-permute-start | bytes 135176 | tf_op jit(solution)/shard_map/ppermute | solution.py:85
  6.8 0.4 %shard_map.158 = (f32[32,128]{1,0:T(8,128)S(1)}, f32[32,128]{1,0:T(8,128)S(1)}, f32[21,16,128]{2,1,0:T(8,128)S(1)}, f32[21,16,128]{2,1,0:T(8,128)S(1)}, s32[8,128]{1,0:T(8,128)S(1)}, /*index=5*/f32[8,128]{1,0:T(8,128)S(1)}) custom-call(s32[4,128]{1,0:T(4,128)S(1)} %get-tuple-element.64.refs_0_, f32[4,128]{1,0:T(4,128)S(1)} %get-tuple-element.65.refs_1_, ...), custom_call_target="tpu_custom_call" | custom-call | flops 16777216 | bytes 1048576 | tf_op jit(solution)/shard_map/pallas_call | solution.py:672
  7.2 0.1 collective-permute-start.5
  7.3 1.6 %collective-permute-start.6 = (f32[21,16,128]{2,1,0:T(8,128)S(1)}, f32[21,16,128]{2,1,0:T(8,128)S(1)}, u32[]{:S(2)}, u32[]{:S(2)}) collective-permute-start(f32[21,16,128]{2,1,0:T(8,128)S(1)} %get-tuple-element.82), channel_id=1, source_target_pairs={{0,4},{1,2},{2,1},{3,7},{4,0},{5,6},{6,5},{7,3},{8,12},{9,10},{10,... | collective-permute-start | bytes 516104 | tf_op jit(solution)/shard_map/ppermute | solution.py:767
  8.9 0.3 %shard_map.159 = (f32[7,64,128]{2,1,0:T(8,128)S(1)}, f32[32,128]{1,0:T(8,128)S(1)}, f32[32,128]{1,0:T(8,128)S(1)}, f32[48,128]{1,0:T(8,128)S(1)}, f32[128,128]{1...) custom-call(s32[8,128]{1,0:T(8,128)S(1)} %get-tuple-element.67.refs_, ...), custom_call_target="tpu_custom_call" | custom-call | flops 4294967296 | bytes 1048576 | tf_op jit(solution)/shard_map/pallas_call | solution.py:672
  9.3 0.1 collective-permute-start.7
  9.3 1.6 %collective-permute-start.3 = (f32[32,128]{1,0:T(8,128)S(1)}, f32[32,128]{1,0:T(8,128)S(1)}, u32[]{:S(2)}, u32[]{:S(2)}) collective-permute-start(f32[32,128]{1,0:T(8,128)S(1)} %get-tuple-element.79), channel_id=1, source_target_pairs={{0,4},{1,5},{2,6},{3,7},{4,0},{5,1},{6,2},{7,3},{8,12},{9,13},{10,... | collective-permute-start | bytes 49160 | tf_op jit(solution)/shard_map/ppermute | solution.py:791
  10.9 1.0 %collective-permute-start.4 = (f32[32,128]{1,0:T(8,128)S(1)}, f32[32,128]{1,0:T(8,128)S(1)}, u32[]{:S(2)}, u32[]{:S(2)}) collective-permute-start(f32[32,128]{1,0:T(8,128)S(1)} %get-tuple-element.80), channel_id=1, source_target_pairs={{0,1},{1,0},{2,3},{3,2},{4,8},{5,9},{6,10},{7,11},{8,4},{9,5},{10,... | collective-permute-start | bytes 49160 | tf_op jit(solution)/shard_map/ppermute | solution.py:792
  11.9 1.6 %shard_map.160 = (f32[19,64,128]{2,1,0:T(8,128)S(1)}, f32[64,128]{1,0:T(8,128)S(1)}, f32[3,19,8,128]{3,2,1,0:T(8,128)S(1)}, f32[152,152]{1,0:T(8,128)S(1)}) custom-call(f32[1,19]{1,0:T(1,128)S(1)} %get-tuple-element.60.refs_0_, f32[1,19]{1,0:T(1,128)S(1)} %get-tuple-element.61.refs_1_, f32[1,19]{1,0:T(1,128)S(1)} %get-tuple-element.62.pig_ref.refs_2_, ...), custom_call_target="tpu_custom_call" | custom-call | flops 1024 | bytes 1048576 | tf_op jit(solution)/shard_map/pallas_call | solution.py:672
  13.5 0.2 shard_map.161
  13.7 1.5 %collective-permute-start.8 = (f32[40,128]{1,0:T(8,128)S(1)}, f32[40,128]{1,0:T(8,128)S(1)}, u32[]{:S(2)}, u32[]{:S(2)}) collective-permute-start(f32[40,128]{1,0:T(8,128)S(1)} %get-tuple-element.92), channel_id=1, source_target_pairs={{0,16},{16,0},{1,17},{17,1},{2,18},{18,2},{3,19},{19,3},{4,20},{20... | collective-permute-start | bytes 61448 | tf_op jit(solution)/shard_map/ppermute | solution.py:85
  15.1 0.6 %collective-permute-start.9 = (f32[88,128]{1,0:T(8,128)S(1)}, f32[88,128]{1,0:T(8,128)S(1)}, u32[]{:S(2)}, u32[]{:S(2)}) collective-permute-start(f32[88,128]{1,0:T(8,128)S(1)} %get-tuple-element.99), channel_id=1, source_target_pairs={{0,16},{16,0},{1,17},{17,1},{2,18},{18,2},{3,19},{19,3},{4,20},{20... | collective-permute-start | bytes 135176 | tf_op jit(solution)/shard_map/ppermute | solution.py:85
  15.8 0.6 %shard_map.162 = (f32[19,64,128]{2,1,0:T(8,128)S(1)}, f32[32,128]{1,0:T(8,128)S(1)}, f32[32,128]{1,0:T(8,128)S(1)}, f32[19,16,128]{2,1,0:T(8,128)S(1)}, f32[19,16,128]{2,1,0:T(8,128)S(1)}) custom-call(f32[19,64,128]{2,1,0:T(8,128)S(1)} %bitcast.26, f32[19,64,128]{2,1,0:T(8,128)S(1)} %get-tuple-element.78.refs_8_.refs_1_, ...), custom_call_target="tpu_custom_call" | custom-call | flops 4294967296 | bytes 1048576 | tf_op jit(solution)/shard_map/pallas_call | solution.py:672
  16.4 0.1 collective-permute-start.12
  16.5 2.4 %collective-permute-start.13 = (f32[19,16,128]{2,1,0:T(8,128)S(1)}, f32[19,16,128]{2,1,0:T(8,128)S(1)}, u32[]{:S(2)}, u32[]{:S(2)}) collective-permute-start(f32[19,16,128]{2,1,0:T(8,128)S(1)} %get-tuple-element.112), channel_id=1, source_target_pairs={{0,4},{1,2},{2,1},{3,7},{4,0},{5,6},{6,5},{7,3},{8,12},{9,10},{10,... | collective-permute-start | bytes 466952 | tf_op jit(solution)/shard_map/ppermute | solution.py:767
  18.8 0.3 %shard_map.163 = (f32[7,64,128]{2,1,0:T(8,128)S(1)}, f32[32,128]{1,0:T(8,128)S(1)}, f32[32,128]{1,0:T(8,128)S(1)}, f32[48,128]{1,0:T(8,128)S(1)}, f32[128,128]{1...) custom-call(s32[8,128]{1,0:T(8,128)S(1)} %get-tuple-element.67.refs_0_, ...), custom_call_target="tpu_custom_call" | custom-call | flops 4294967296 | bytes 1048576 | tf_op jit(solution)/shard_map/pallas_call | solution.py:672
  19.2 1.3 %collective-permute-start.10 = (f32[32,128]{1,0:T(8,128)S(1)}, f32[32,128]{1,0:T(8,128)S(1)}, u32[]{:S(2)}, u32[]{:S(2)}) collective-permute-start(f32[32,128]{1,0:T(8,128)S(1)} %get-tuple-element.109), channel_id=1, source_target_pairs={{0,4},{1,5},{2,6},{3,7},{4,0},{5,1},{6,2},{7,3},{8,12},{9,13},{10,... | collective-permute-start | bytes 49160 | tf_op jit(solution)/shard_map/ppermute | solution.py:791
  20.5 0.9 %collective-permute-start.11 = (f32[32,128]{1,0:T(8,128)S(1)}, f32[32,128]{1,0:T(8,128)S(1)}, u32[]{:S(2)}, u32[]{:S(2)}) collective-permute-start(f32[32,128]{1,0:T(8,128)S(1)} %get-tuple-element.110), channel_id=1, source_target_pairs={{0,1},{1,0},{2,3},{3,2},{4,8},{5,9},{6,10},{7,11},{8,4},{9,5},{10,... | collective-permute-start | bytes 49160 | tf_op jit(solution)/shard_map/ppermute | solution.py:792
  21.4 1.6 %shard_map.164 = (f32[19,64,128]{2,1,0:T(8,128)S(1)}, f32[64,128]{1,0:T(8,128)}, f32[64,128]{1,0:T(8,128)}, f32[64,128]{1,0:T(8,128)}, f32[64,128]{1,0:T(8,128)}) custom-call(f32[3,19,8,128]{3,2,1,0:T(8,128)S(1)} %get-tuple-element.76.refs_0_, f32[152,152]{1,0:T(8,128)S(1)} %get-tuple-element.77.refs_1_, ...), custom_call_target="tpu_custom_call" | custom-call | flops 1024 | bytes 1048576 | tf_op jit(solution)/shard_map/pallas_call | solution.py:672
  23.0 1.0 %shard_map.165 = f32[19,64,128]{2,1,0:T(8,128)} custom-call(f32[19,64,128]{2,1,0:T(8,128)S(1)} %get-tuple-element.89.refs_2_.refs_0_, f32[19,64,128]{2,1,0:T(8,128)S(1)} %get-tuple-element.108.refs_1_, f32[7,64,128]{2,1,0:T(8,128)S(1)} %get-tuple-element.98.refs_3_.refs_2_, f32[32,128]{1,0:T(8,128)S(1)} %collective-permute-done.10.refs_3_, ...), custom_call_target="tpu_custom_call" | custom-call | flops 1048576 | bytes 1048576 | tf_op jit(solution)/shard_map/pallas_call | solution.py:672
  (41 shorter events, 0.2 us)
Async XLA Ops:
  0.7 0.8 %copy-start.3 = (f32[32,1,2,128]{3,2,1,0:T(2,128)S(1)}, f32[32,1,2,128]{3,2,1,0:T(2,128)}, u32[]{:S(2)}) copy-start(f32[32,1,2,128]{3,2,1,0:T(2,128)} %param.14) | copy-start | bytes 98308
  0.7 0.8 %copy-start.4 = (f32[32,1,2,128]{3,2,1,0:T(2,128)S(1)}, f32[32,1,2,128]{3,2,1,0:T(2,128)}, u32[]{:S(2)}) copy-start(f32[32,1,2,128]{3,2,1,0:T(2,128)} %param.15) | copy-start | bytes 98308
  0.7 0.8 %copy-start.5 = (f32[32,1,2,128]{3,2,1,0:T(2,128)S(1)}, f32[32,1,2,128]{3,2,1,0:T(2,128)}, u32[]{:S(2)}) copy-start(f32[32,1,2,128]{3,2,1,0:T(2,128)} %param.16) | copy-start | bytes 98308
  0.7 0.8 %copy-start.8 = (f32[4,128]{1,0:T(4,128)S(1)}, f32[4,128]{1,0:T(4,128)}, u32[]{:S(2)}) copy-start(f32[4,128]{1,0:T(4,128)} %refs_10_.1) | copy-start | bytes 6148
  0.7 0.8 %copy-start.11 = (f32[19]{0:T(128)S(1)}, f32[19]{0:T(128)}, u32[]{:S(2)}) copy-start(f32[19]{0:T(128)} %param.23) | copy-start | bytes 232
  0.7 3.9 %copy-start = (f32[19,16,4,128]{3,2,1,0:T(4,128)S(1)}, f32[19,16,4,128]{3,2,1,0:T(4,128)}, u32[]{:S(2)}) copy-start(f32[19,16,4,128]{3,2,1,0:T(4,128)} %param.17) | copy-start | bytes 1867780
  0.7 0.8 %copy-start.6 = (f32[19,19]{1,0:T(8,128)S(1)}, f32[19,19]{1,0:T(8,128)}, u32[]{:S(2)}) copy-start(f32[19,19]{1,0:T(8,128)} %refs_8_.1) | copy-start | bytes 4336
  0.7 0.8 %copy-start.7 = (s32[4,128]{1,0:T(4,128)S(1)}, s32[4,128]{1,0:T(4,128)}, u32[]{:S(2)}) copy-start(s32[4,128]{1,0:T(4,128)} %refs_9_.1) | copy-start | bytes 6148
  0.7 0.8 %copy-start.9 = (f32[19]{0:T(128)S(1)}, f32[19]{0:T(128)}, u32[]{:S(2)}) copy-start(f32[19]{0:T(128)} %param.21) | copy-start | bytes 232
  1.6 7.4 %collective-permute-start.1 = (f32[180,128]{1,0:T(8,128)S(1)}, f32[180,128]{1,0:T(8,128)S(1)}, u32[]{:S(2)}, u32[]{:S(2)}) collective-permute-start(f32[180,128]{1,0:T(8,128)S(1)} %get-tuple-element.73), channel_id=1, source_target_pairs={{0,16},{16,0},{1,17},{17,1},{2,18},{18,2},{3,19},{19,3},{4,20},{20... | collective-permute-start | bytes 276488 | tf_op jit(solution)/shard_map/ppermute | solution.py:85
  4.7 4.2 %collective-permute-start = (f32[40,128]{1,0:T(8,128)S(1)}, f32[40,128]{1,0:T(8,128)S(1)}, u32[]{:S(2)}, u32[]{:S(2)}) collective-permute-start(f32[40,128]{1,0:T(8,128)S(1)} %get-tuple-element.71), channel_id=1, source_target_pairs={{0,16},{16,0},{1,17},{17,1},{2,18},{18,2},{3,19},{19,3},{4,20},{20... | collective-permute-start | bytes 61448 | tf_op jit(solution)/shard_map/ppermute | solution.py:85
  5.0 5.9 %collective-permute-start.2 = (f32[88,128]{1,0:T(8,128)S(1)}, f32[88,128]{1,0:T(8,128)S(1)}, u32[]{:S(2)}, u32[]{:S(2)}) collective-permute-start(f32[88,128]{1,0:T(8,128)S(1)} %get-tuple-element.75), channel_id=1, source_target_pairs={{0,16},{16,0},{1,17},{17,1},{2,18},{18,2},{3,19},{19,3},{4,20},{20... | collective-permute-start | bytes 135176 | tf_op jit(solution)/shard_map/ppermute | solution.py:85
  7.2 6.3 %collective-permute-start.5 = (f32[21,16,128]{2,1,0:T(8,128)S(1)}, f32[21,16,128]{2,1,0:T(8,128)S(1)}, u32[]{:S(2)}, u32[]{:S(2)}) collective-permute-start(f32[21,16,128]{2,1,0:T(8,128)S(1)} %get-tuple-element.81), channel_id=1, source_target_pairs={{0,1},{1,0},{2,3},{3,2},{4,5},{5,4},{6,7},{7,6},{8,9},{9,8},{10,11... | collective-permute-start | bytes 516104 | tf_op jit(solution)/shard_map/ppermute | solution.py:766
  7.3 6.2 %collective-permute-start.6 = (f32[21,16,128]{2,1,0:T(8,128)S(1)}, f32[21,16,128]{2,1,0:T(8,128)S(1)}, u32[]{:S(2)}, u32[]{:S(2)}) collective-permute-start(f32[21,16,128]{2,1,0:T(8,128)S(1)} %get-tuple-element.82), channel_id=1, source_target_pairs={{0,4},{1,2},{2,1},{3,7},{4,0},{5,6},{6,5},{7,3},{8,12},{9,10},{10,... | collective-permute-start | bytes 516104 | tf_op jit(solution)/shard_map/ppermute | solution.py:767
  9.3 4.2 %collective-permute-start.7 = (f32[48,128]{1,0:T(8,128)S(1)}, f32[48,128]{1,0:T(8,128)S(1)}, u32[]{:S(2)}, u32[]{:S(2)}) collective-permute-start(f32[48,128]{1,0:T(8,128)S(1)} %get-tuple-element.83), channel_id=1, source_target_pairs={{0,1},{1,2},{2,3},{3,0},{4,5},{5,6},{6,7},{7,4},{8,9},{9,10},{10,1... | collective-permute-start | bytes 73736 | tf_op jit(solution)/shard_map/ppermute | solution.py:793
  9.3 4.1 %collective-permute-start.3 = (f32[32,128]{1,0:T(8,128)S(1)}, f32[32,128]{1,0:T(8,128)S(1)}, u32[]{:S(2)}, u32[]{:S(2)}) collective-permute-start(f32[32,128]{1,0:T(8,128)S(1)} %get-tuple-element.79), channel_id=1, source_target_pairs={{0,4},{1,5},{2,6},{3,7},{4,0},{5,1},{6,2},{7,3},{8,12},{9,13},{10,... | collective-permute-start | bytes 49160 | tf_op jit(solution)/shard_map/ppermute | solution.py:791
  10.9 2.5 %collective-permute-start.4 = (f32[32,128]{1,0:T(8,128)S(1)}, f32[32,128]{1,0:T(8,128)S(1)}, u32[]{:S(2)}, u32[]{:S(2)}) collective-permute-start(f32[32,128]{1,0:T(8,128)S(1)} %get-tuple-element.80), channel_id=1, source_target_pairs={{0,1},{1,0},{2,3},{3,2},{4,8},{5,9},{6,10},{7,11},{8,4},{9,5},{10,... | collective-permute-start | bytes 49160 | tf_op jit(solution)/shard_map/ppermute | solution.py:792
  13.7 5.2 %collective-permute-start.8 = (f32[40,128]{1,0:T(8,128)S(1)}, f32[40,128]{1,0:T(8,128)S(1)}, u32[]{:S(2)}, u32[]{:S(2)}) collective-permute-start(f32[40,128]{1,0:T(8,128)S(1)} %get-tuple-element.92), channel_id=1, source_target_pairs={{0,16},{16,0},{1,17},{17,1},{2,18},{18,2},{3,19},{19,3},{4,20},{20... | collective-permute-start | bytes 61448 | tf_op jit(solution)/shard_map/ppermute | solution.py:85
  15.1 5.3 %collective-permute-start.9 = (f32[88,128]{1,0:T(8,128)S(1)}, f32[88,128]{1,0:T(8,128)S(1)}, u32[]{:S(2)}, u32[]{:S(2)}) collective-permute-start(f32[88,128]{1,0:T(8,128)S(1)} %get-tuple-element.99), channel_id=1, source_target_pairs={{0,16},{16,0},{1,17},{17,1},{2,18},{18,2},{3,19},{19,3},{4,20},{20... | collective-permute-start | bytes 135176 | tf_op jit(solution)/shard_map/ppermute | solution.py:85
  16.4 6.6 %collective-permute-start.12 = (f32[19,16,128]{2,1,0:T(8,128)S(1)}, f32[19,16,128]{2,1,0:T(8,128)S(1)}, u32[]{:S(2)}, u32[]{:S(2)}) collective-permute-start(f32[19,16,128]{2,1,0:T(8,128)S(1)} %get-tuple-element.111), channel_id=1, source_target_pairs={{0,1},{1,0},{2,3},{3,2},{4,5},{5,4},{6,7},{7,6},{8,9},{9,8},{10,11... | collective-permute-start | bytes 466952 | tf_op jit(solution)/shard_map/ppermute | solution.py:766
  16.5 6.5 %collective-permute-start.13 = (f32[19,16,128]{2,1,0:T(8,128)S(1)}, f32[19,16,128]{2,1,0:T(8,128)S(1)}, u32[]{:S(2)}, u32[]{:S(2)}) collective-permute-start(f32[19,16,128]{2,1,0:T(8,128)S(1)} %get-tuple-element.112), channel_id=1, source_target_pairs={{0,4},{1,2},{2,1},{3,7},{4,0},{5,6},{6,5},{7,3},{8,12},{9,10},{10,... | collective-permute-start | bytes 466952 | tf_op jit(solution)/shard_map/ppermute | solution.py:767
  19.1 3.9 %collective-permute-start.14 = (f32[48,128]{1,0:T(8,128)S(1)}, f32[48,128]{1,0:T(8,128)S(1)}, u32[]{:S(2)}, u32[]{:S(2)}) collective-permute-start(f32[48,128]{1,0:T(8,128)S(1)} %get-tuple-element.113), channel_id=1, source_target_pairs={{0,1},{1,2},{2,3},{3,0},{4,5},{5,6},{6,7},{7,4},{8,9},{9,10},{10,1... | collective-permute-start | bytes 73736 | tf_op jit(solution)/shard_map/ppermute | solution.py:793
  19.2 3.8 %collective-permute-start.10 = (f32[32,128]{1,0:T(8,128)S(1)}, f32[32,128]{1,0:T(8,128)S(1)}, u32[]{:S(2)}, u32[]{:S(2)}) collective-permute-start(f32[32,128]{1,0:T(8,128)S(1)} %get-tuple-element.109), channel_id=1, source_target_pairs={{0,4},{1,5},{2,6},{3,7},{4,0},{5,1},{6,2},{7,3},{8,12},{9,13},{10,... | collective-permute-start | bytes 49160 | tf_op jit(solution)/shard_map/ppermute | solution.py:791
  20.5 2.5 %collective-permute-start.11 = (f32[32,128]{1,0:T(8,128)S(1)}, f32[32,128]{1,0:T(8,128)S(1)}, u32[]{:S(2)}, u32[]{:S(2)}) collective-permute-start(f32[32,128]{1,0:T(8,128)S(1)} %get-tuple-element.110), channel_id=1, source_target_pairs={{0,1},{1,0},{2,3},{3,2},{4,8},{5,9},{6,10},{7,11},{8,4},{9,5},{10,... | collective-permute-start | bytes 49160 | tf_op jit(solution)/shard_map/ppermute | solution.py:792
  (3 other events, 2.3 us)

commit v7 on v6

--- a/solution.py
+++ b/solution.py
@@ -139,28 +139,24 @@
     return count == 2 and SUB == 2 * rows and cells >= 2 * SUB
 
 
-def level_base(rows, cells, count, together):
-    if not together:
-        return SUB - rows
+def pigment_rows(rows, cells, count):
     return cells // 2 + SUB if compact(rows, cells, count) else cells
 
 
-def message_shapes(tracers, rows, cells, width, count, together):
-    height = level_base(rows, cells, count, together) + tracers * rows + (SUB - rows)
+def level_shapes(tracers, rows, width, count):
+    height = tracers * rows + 2 * (SUB - rows)
     height += -height % SUB
-    if together:
-        return [shape(height, width)]
-    pigment = cells // 2 + SUB if compact(rows, cells, count) else cells
-    return [shape(pigment, width)] + [shape(height, width)] * (1 if count == 2 else 2)
-
-
-def write_levels(last, first, t, rows, base, msgs, g):
-    here = pl.ds(base + t * rows, rows)
-    if len(msgs) < 3:
-        msgs[-1][here, :] = jnp.where(g == 0, last[SUB - rows :], first[:rows])
+    return [shape(height, width)] * (1 if count == 2 else 2)
+
+
+def write_levels(c, t, rows, levs, g):
+    cells = c.shape[0]
+    here = pl.ds(SUB - rows + t * rows, rows)
+    if len(levs) == 1:
+        levs[0][here, :] = jnp.where(g == 0, c[cells - rows :], c[:rows])
     else:
-        msgs[1][here, :] = last[SUB - rows :]
-        msgs[2][here, :] = first[:rows]
+        levs[0][here, :] = c[cells - rows :]
+        levs[1][here, :] = c[:rows]
 
 
 def in_strip(rows, count, width, member):
@@ -242,18 +238,16 @@
     return jnp.broadcast_to(v[None], (cells // SUB, SUB, width)).reshape(cells, width)
 
 
-def prep_kernel(rows, count, pig_ref, c_ref, p_ref, *msgs):
+def prep_kernel(rows, count, pig_ref, c_ref, p_ref, p_msg):
     g = lax.axis_index("grp")
     tracers, cells, width = c_ref.shape
-    base = level_base(rows, cells, count, False)
     weights = pig_ref[...]
     pigment = jnp.zeros((cells, width), F32)
     for t in range(tracers):
         c = c_ref[t]
         pigment = pigment + tile(jnp.broadcast_to(weights[:, t : t + 1], (SUB, width)), cells) * c
-        write_levels(c[cells - SUB :], c[:SUB], t, rows, base, msgs, g)
     p_ref[...] = pigment
-    write_pigment(rows, count, p_ref, msgs[0], g)
+    write_pigment(rows, count, p_ref, p_msg, g)
 
 
 def halves(v):
@@ -292,14 +286,16 @@
     msg_yb[slot] = jnp.where(y_even, first, last)
 
 
-def pack(rows, c_ref, p_ref, msg_xa, msg_xb, msg_ya, msg_yb):
+def pack(rows, c_ref, p_ref, msg_xa, msg_xb, msg_ya, msg_yb, levs):
     tracers, cells, _ = c_ref.shape
     levels = cells // rows
     x_even = lax.rem(lax.axis_index("gx"), 2) == 0
     left = right = jnp.zeros(msg_xa.shape, F32)
     left, right = pack_sides(p_ref[...], tracers + 2, tracers + 3, left, right)
+    g = lax.axis_index("grp")
     for t in range(tracers):
         left, right = pack_sides(c_ref[t], t, tracers + 3, left, right)
+        write_levels(c_ref[t], t, rows, levs, g)
     msg_xa[...] = jnp.where(x_even, right, left)
     msg_xb[...] = jnp.where(x_even, left, right)
     first, last = pl.ds(0, levels, stride=rows), pl.ds(rows - 1, levels, stride=rows)
@@ -313,11 +309,12 @@
     refs = Refs(refs)
     depth_in, solar_in, c_ref, p_ref = refs.take(4)
     msg_xa, msg_xb, msg_ya, msg_yb, depth_ref, solar_ref = refs.take(6)
+    levs = refs.refs
     tracers, cells, width = c_ref.shape
     for r in range(0, SUB, rows):
         depth_ref[pl.ds(r, rows), :] = depth_in[...]
         solar_ref[pl.ds(r, rows), :] = solar_in[...]
-    pack(rows, c_ref, p_ref, msg_xa, msg_xb, msg_ya, msg_yb)
+    pack(rows, c_ref, p_ref, msg_xa, msg_xb, msg_ya, msg_yb, levs)
     levels = cells // rows
     level = lax.axis_index("grp") * levels + iota((levels, width), 0)
     wet_first = jnp.where(level < depth_in[pl.ds(0, 1), :], 1.0, 0.0)
@@ -485,7 +482,6 @@
             for t in range(tracers):
                 tiles_ref[at, t] = jnp.broadcast_to(values[:, t : t + 1], (SUB, width))
     mix(w_ref[...], c_ref, mix_ref)
-    base = level_base(rows, cells, count, False)
     lane = iota((cells, width), 1)
     at_row = lax.rem(iota((cells, width), 0), rows)
     u = band_ref[0]
@@ -523,7 +519,7 @@
     pigment = jnp.zeros((cells, width), F32)
     for t in range(tracers):
         c = c_ref[t]
-        at = base + t * rows
+        at = SUB - rows + t * rows
         up8 = lev_in[0][pl.ds(at + rows - SUB, SUB), :]
         down8 = lev_in[-1][pl.ds(at, SUB), :]
         c_u = turn(jnp.concatenate([up8, c], axis=0), rows, 0)[SUB:]
@@ -599,11 +595,9 @@
     p_in, part_ref, p_part = refs.take(3)
     if not first_step:
         (wet_in,) = refs.take(1)
-    k_ref, halo_ref, spread_s, wet_out, p_ref = refs.take(5)
-    msgs, speed_s = refs.refs[:-1], refs.refs[-1]
+    k_ref, halo_ref, spread_s, wet_out, p_ref, p_msg, speed_s = refs.take(7)
     g = lax.axis_index("grp")
     tracers, cells, width = c_ref.shape
-    lev_base = level_base(rows, cells, count, False)
     halo_ref[...] = x_halo(got_xa, got_xb)
     for slot in range(got_ya.shape[0]):
         spread_rows(rows, got_ya, got_yb, spread_s, slot)
@@ -614,19 +608,7 @@
     side = sides_of(halo_ref[...], tracers + 2, tracers + 3, cells)
     change = sideways(rows, factors, side, spread_s[tracers], p_in[...])
     p_ref[...] = p_part[...] + change
-    write_pigment(rows, count, p_ref, msgs[0], g)
-
-    def block(at, t):
-        here = pl.ds(at, SUB)
-        cut = [k[at : at + SUB] for k in factors]
-        for part, base in halves_of(cells, tracers + 3, width):
-            if part.start <= at < part.stop:
-                side = turn(halo_ref[pl.ds(at - part.start, SUB), :], -2 * (t + 1) - base, 1)
-        change = sideways(rows, cut, side, spread_s[t, here, :], c_ref[t, here, :])
-        return part_ref[t, here, :] + change
-
-    for t in range(tracers):
-        write_levels(block(cells - SUB, t), block(0, t), t, rows, lev_base, msgs, g)
+    write_pigment(rows, count, p_ref, p_msg, g)
 
 
 def step_kernel(rows, *refs):
@@ -639,7 +621,7 @@
         out_ref[t] = part_ref[t] + sideways(
                 rows, factors, sides_of(halo_ref[...], t, tracers + 3, c_ref.shape[1]), spread_s[t], c_ref[t]
             )
-    pack(rows, out_ref, p_ref, msg_xa, msg_xb, msg_ya, msg_yb)
+    pack(rows, out_ref, p_ref, msg_xa, msg_xb, msg_ya, msg_yb, refs.refs)
 
 
 def final_kernel(rows, sizes, first_step, *refs):
@@ -734,23 +716,24 @@
     *params, rates, layers, light = small
     raw_others = from_others(window, count)
 
-    messages = message_shapes(tracers, rows, cells, width, count, False)
+    sent_pigment = shape(pigment_rows(rows, cells, count), width)
+    sent_levels = level_shapes(tracers, rows, width, count)
     cols = shape(cells, width)
     sent_cols = shape(cells // 2, width) if folds(tracers + 3, cells, width) else cols
     field = shape(tracers, cells, width)
     c = substance_amounts.reshape(tracers, cells, width)
-    pigment, *msgs = call(
+    pigment, p_msg = call(
         functools.partial(prep_kernel, rows, count),
         [params[2], c],
-        [cols, *message_shapes(tracers, rows, cells, width, count, False)],
+        [cols, sent_pigment],
     )
     full = None
     for step in range(STEPS):
         first_step, last_step = step == 0, step == STEPS - 1
-        p_others = from_others(msgs[0], count)
+        p_others = from_others(p_msg, count)
         if first_step:
             lines = shape(tracers + 2, levels, width)
-            xa, xb, ya, yb, depth, solar = call(
+            xa, xb, ya, yb, depth, solar, *levs = call(
                 functools.partial(pack_kernel, rows),
                 [layers, light, c, pigment],
                 [
@@ -760,17 +743,18 @@
                     lines,
                     jax.ShapeDtypeStruct((SUB, width), jnp.int32),
                     shape(SUB, width),
+                    *sent_levels,
                 ],
                 flops=1 << 24,
             )
         ya = lax.ppermute(ya, AXES, pairing(sizes, "gy", 0))
         yb = lax.ppermute(yb, AXES, pairing(sizes, "gy", 1))
         if count == 2:
-            lev = from_others(msgs[-1], count)
+            lev = from_others(levs[0], count)
         else:
             lev = [
-                lax.ppermute(msgs[1], "grp", [(i, (i + 1) % count) for i in range(count)]),
-                lax.ppermute(msgs[2], "grp", [((i + 1) % count, i) for i in range(count)]),
+                lax.ppermute(levs[0], "grp", [(i, (i + 1) % count) for i in range(count)]),
+                lax.ppermute(levs[1], "grp", [((i + 1) % count, i) for i in range(count)]),
             ]
         band, xa, xb, speed, *full = call(
             functools.partial(ocean_kernel, rows, count, tracers, first_step),
@@ -810,18 +794,18 @@
             known_rates = [tiles, weights]
         known = [] if first_step else [wet_out]
         if not last_step:
-            k, halo, spread, wet_out, pigment_next, *msgs = call(
+            k, halo, spread, wet_out, pigment_next, p_msg = call(
                 functools.partial(early_kernel, rows, count, sizes, first_step),
                 [c, band, xa, xb, ya, yb, speed, pigment, part, *rest, *known],
-                [shape(3, cells, width), sent_cols, shape(tracers + 2, cells, width), cols, cols, *messages],
+                [shape(3, cells, width), sent_cols, shape(tracers + 2, cells, width), cols, cols, sent_pigment],
                 scratch=[band_s],
             )
             pigment = pigment_next
             lines = shape(tracers + (0 if step + 1 == STEPS - 1 else 1), levels, width)
-            c, xa, xb, ya, yb = call(
+            c, xa, xb, ya, yb, *levs = call(
                 functools.partial(step_kernel, rows),
                 [c, part, k, halo, spread, pigment],
-                [field, sent_cols, sent_cols, lines, lines],
+                [field, sent_cols, sent_cols, lines, lines, *sent_levels],
                 flops=1<<32,
             )
         else:

time: 24.2 us -> 24.1 us (level)
  transfers between devices with their start and end apart: 15 -> 15, of which waited for: 0 -> 1; matrix products, arithmetic and copies ran while one was open for 0% -> 0% of each run, Pallas kernels for 21% -> 21%
where the time goes in v7:
time: 24.1 us; the launch traced here: 24 us
  starting transfers between devices  15.9 us (66%)
  Pallas kernels  6.25 us (26%)
  between operations  0.86 us (4%)
  local copies, waits for them, and re-layouts  0.79 us (3%)
    ppermute x5, starting transfers between devices, from_others(): lax.ppermute(value, 'grp', [(i, (i + k) % count) for i in range(count)])  7.32 us
    pallas_call x11, Pallas kernels, call(): pl.pallas_call(kernel, in_specs=[vmem() for _ in ins] if in_specs is None...  6.25 us
    ppermute x2, starting transfers between devices, per_device(): yb = lax.ppermute(yb, AXES, pairing(sizes, 'gy', 1))  3.91 us
    ppermute x2, starting transfers between devices, per_device(): xa = lax.ppermute(xa, AXES, pairing(sizes, 'gx', 0))  2.78 us
    ppermute x2, starting transfers between devices, per_device(): xb = lax.ppermute(xb, AXES, pairing(sizes, 'gx', 1))  1.77 us
    unnamed x24, local copies, waits for them, and re-layouts  0.79 us
  transfers between devices with their start and end apart: 15, of which 1 were waited for; matrix products, arithmetic and copies ran while one was open for 0% of the time, Pallas kernels for 21%

profile of v7, /device:TPU:0, one launch (start us, length us, event | category | flops | bytes accessed | tf_op | source)
XLA Modules:
  0.0 24.0 jit_solution(5630875387465404144)
XLA Ops:
  0.8 0.6 %copy-done.1 = f32[32,1,2,128]{3,2,1,0:T(2,128)S(1)} copy-done((f32[32,1,2,128]{3,2,1,0:T(2,128)S(1)}, f32[32,1,2,128]{3,2,1,0:T(2,128)}, u32[]{:S(2)}) %copy-start.1) | copy-done | bytes 32792
  1.5 0.1 copy-done.6
  1.6 3.0 %collective-permute-start.1 = (f32[180,128]{1,0:T(8,128)S(1)}, f32[180,128]{1,0:T(8,128)S(1)}, u32[]{:S(2)}, u32[]{:S(2)}) collective-permute-start(f32[180,128]{1,0:T(8,128)S(1)} %get-tuple-element.73), channel_id=1, source_target_pairs={{0,16},{16,0},{1,17},{17,1},{2,18},{18,2},{3,19},{19,3},{4,20},{20... | collective-permute-start | bytes 276488 | tf_op jit(solution)/shard_map/ppermute | solution.py:85
  4.6 0.1 shard_map.157
  4.7 0.3 %collective-permute-start = (f32[40,128]{1,0:T(8,128)S(1)}, f32[40,128]{1,0:T(8,128)S(1)}, u32[]{:S(2)}, u32[]{:S(2)}) collective-permute-start(f32[40,128]{1,0:T(8,128)S(1)} %get-tuple-element.71), channel_id=1, source_target_pairs={{0,16},{16,0},{1,17},{17,1},{2,18},{18,2},{3,19},{19,3},{4,20},{20... | collective-permute-start | bytes 61448 | tf_op jit(solution)/shard_map/ppermute | solution.py:85
  5.0 0.4 %shard_map.158 = (f32[32,128]{1,0:T(8,128)S(1)}, f32[32,128]{1,0:T(8,128)S(1)}, f32[21,16,128]{2,1,0:T(8,128)S(1)}, f32[21,16,128]{2,1,0:T(8,128)S(1)}, s32[8,12...) custom-call(s32[4,128]{1,0:T(4,128)S(1)} %get-tuple-element.64.refs_0_, ...), custom_call_target="tpu_custom_call" | custom-call | flops 16777216 | bytes 1048576 | tf_op jit(solution)/shard_map/pallas_call | solution.py:654
  5.4 1.8 %collective-permute-start.2 = (f32[88,128]{1,0:T(8,128)S(1)}, f32[88,128]{1,0:T(8,128)S(1)}, u32[]{:S(2)}, u32[]{:S(2)}) collective-permute-start(f32[88,128]{1,0:T(8,128)S(1)} %get-tuple-element.75), channel_id=1, source_target_pairs={{0,16},{16,0},{1,17},{17,1},{2,18},{18,2},{3,19},{19,3},{4,20},{20... | collective-permute-start | bytes 135176 | tf_op jit(solution)/shard_map/ppermute | solution.py:85
  7.3 1.6 %collective-permute-start.6 = (f32[21,16,128]{2,1,0:T(8,128)S(1)}, f32[21,16,128]{2,1,0:T(8,128)S(1)}, u32[]{:S(2)}, u32[]{:S(2)}) collective-permute-start(f32[21,16,128]{2,1,0:T(8,128)S(1)} %get-tuple-element.82), channel_id=1, source_target_pairs={{0,4},{1,2},{2,1},{3,7},{4,0},{5,6},{6,5},{7,3},{8,12},{9,10},{10,... | collective-permute-start | bytes 516104 | tf_op jit(solution)/shard_map/ppermute | solution.py:751
  8.9 0.3 %shard_map.159 = (f32[7,64,128]{2,1,0:T(8,128)S(1)}, f32[32,128]{1,0:T(8,128)S(1)}, f32[32,128]{1,0:T(8,128)S(1)}, f32[48,128]{1,0:T(8,128)S(1)}, f32[128,128]{1...) custom-call(s32[8,128]{1,0:T(8,128)S(1)} %get-tuple-element.67.refs_, ...), custom_call_target="tpu_custom_call" | custom-call | flops 4294967296 | bytes 1048576 | tf_op jit(solution)/shard_map/pallas_call | solution.py:654
  9.2 0.1 collective-permute-start.7
  9.3 1.6 %collective-permute-start.3 = (f32[32,128]{1,0:T(8,128)S(1)}, f32[32,128]{1,0:T(8,128)S(1)}, u32[]{:S(2)}, u32[]{:S(2)}) collective-permute-start(f32[32,128]{1,0:T(8,128)S(1)} %get-tuple-element.79), channel_id=1, source_target_pairs={{0,4},{1,5},{2,6},{3,7},{4,0},{5,1},{6,2},{7,3},{8,12},{9,13},{10,... | collective-permute-start | bytes 49160 | tf_op jit(solution)/shard_map/ppermute | solution.py:775
  10.8 1.0 %collective-permute-start.4 = (f32[32,128]{1,0:T(8,128)S(1)}, f32[32,128]{1,0:T(8,128)S(1)}, u32[]{:S(2)}, u32[]{:S(2)}) collective-permute-start(f32[32,128]{1,0:T(8,128)S(1)} %get-tuple-element.80), channel_id=1, source_target_pairs={{0,1},{1,0},{2,3},{3,2},{4,8},{5,9},{6,10},{7,11},{8,4},{9,5},{10,... | collective-permute-start | bytes 49160 | tf_op jit(solution)/shard_map/ppermute | solution.py:776
  11.9 1.6 %shard_map.160 = (f32[19,64,128]{2,1,0:T(8,128)S(1)}, f32[64,128]{1,0:T(8,128)S(1)}, f32[3,19,8,128]{3,2,1,0:T(8,128)S(1)}, f32[152,152]{1,0:T(8,128)S(1)}) custom-call(f32[1,19]{1,0:T(1,128)S(1)} %get-tuple-element.60.refs_0_, f32[1,19]{1,0:T(1,128)S(1)} %get-tuple-element.61.refs_1_, f32[1,19]{1,0:T(1,128)S(1)} %get-tuple-element.62.pig_ref.refs_2_, ...), custom_call_target="tpu_custom_call" | custom-call | flops 1024 | bytes 1048576 | tf_op jit(solution)/shard_map/pallas_call | solution.py:654
  13.6 0.1 shard_map.161
  13.7 1.3 %collective-permute-start.8 = (f32[40,128]{1,0:T(8,128)S(1)}, f32[40,128]{1,0:T(8,128)S(1)}, u32[]{:S(2)}, u32[]{:S(2)}) collective-permute-start(f32[40,128]{1,0:T(8,128)S(1)} %get-tuple-element.92), channel_id=1, source_target_pairs={{0,16},{16,0},{1,17},{17,1},{2,18},{18,2},{3,19},{19,3},{4,20},{20... | collective-permute-start | bytes 61448 | tf_op jit(solution)/shard_map/ppermute | solution.py:85
  15.0 0.6 %shard_map.162 = (f32[19,64,128]{2,1,0:T(8,128)S(1)}, f32[32,128]{1,0:T(8,128)S(1)}, f32[32,128]{1,0:T(8,128)S(1)}, f32[19,16,128]{2,1,0:T(8,128)S(1)}, f32[19,1...) custom-call(f32[19,64,128]{2,1,0:T(8,128)S(1)} %bitcast.26, f32[19,64,128]{2,1,0:T(8,128)S(1)} %get-tuple-element.78.refs_8_.refs_1_, ...), custom_call_target="tpu_custom_call" | custom-call | flops 4294967296 | bytes 1048576 | tf_op jit(solution)/shard_map/pallas_call | solution.py:654
  15.6 0.9 %collective-permute-start.9 = (f32[88,128]{1,0:T(8,128)S(1)}, f32[88,128]{1,0:T(8,128)S(1)}, u32[]{:S(2)}, u32[]{:S(2)}) collective-permute-start(f32[88,128]{1,0:T(8,128)S(1)} %get-tuple-element.99), channel_id=1, source_target_pairs={{0,16},{16,0},{1,17},{17,1},{2,18},{18,2},{3,19},{19,3},{4,20},{20... | collective-permute-start | bytes 135176 | tf_op jit(solution)/shard_map/ppermute | solution.py:85
  16.5 2.3 %collective-permute-start.13 = (f32[19,16,128]{2,1,0:T(8,128)S(1)}, f32[19,16,128]{2,1,0:T(8,128)S(1)}, u32[]{:S(2)}, u32[]{:S(2)}) collective-permute-start(f32[19,16,128]{2,1,0:T(8,128)S(1)} %get-tuple-element.112), channel_id=1, source_target_pairs={{0,4},{1,2},{2,1},{3,7},{4,0},{5,6},{6,5},{7,3},{8,12},{9,10},{10,... | collective-permute-start | bytes 466952 | tf_op jit(solution)/shard_map/ppermute | solution.py:751
  18.8 0.3 %shard_map.163 = (f32[7,64,128]{2,1,0:T(8,128)S(1)}, f32[32,128]{1,0:T(8,128)S(1)}, f32[32,128]{1,0:T(8,128)S(1)}, f32[48,128]{1,0:T(8,128)S(1)}, f32[128,128]{1...) custom-call(s32[8,128]{1,0:T(8,128)S(1)} %get-tuple-element.67.refs_0_, ...), custom_call_target="tpu_custom_call" | custom-call | flops 4294967296 | bytes 1048576 | tf_op jit(solution)/shard_map/pallas_call | solution.py:654
  19.2 1.2 %collective-permute-start.10 = (f32[32,128]{1,0:T(8,128)S(1)}, f32[32,128]{1,0:T(8,128)S(1)}, u32[]{:S(2)}, u32[]{:S(2)}) collective-permute-start(f32[32,128]{1,0:T(8,128)S(1)} %get-tuple-element.109), channel_id=1, source_target_pairs={{0,4},{1,5},{2,6},{3,7},{4,0},{5,1},{6,2},{7,3},{8,12},{9,13},{10,... | collective-permute-start | bytes 49160 | tf_op jit(solution)/shard_map/ppermute | solution.py:775
  20.4 0.8 %collective-permute-start.11 = (f32[32,128]{1,0:T(8,128)S(1)}, f32[32,128]{1,0:T(8,128)S(1)}, u32[]{:S(2)}, u32[]{:S(2)}) collective-permute-start(f32[32,128]{1,0:T(8,128)S(1)} %get-tuple-element.110), channel_id=1, source_target_pairs={{0,1},{1,0},{2,3},{3,2},{4,8},{5,9},{6,10},{7,11},{8,4},{9,5},{10,... | collective-permute-start | bytes 49160 | tf_op jit(solution)/shard_map/ppermute | solution.py:776
  21.1 1.6 %shard_map.164 = (f32[19,64,128]{2,1,0:T(8,128)S(1)}, f32[64,128]{1,0:T(8,128)}, f32[64,128]{1,0:T(8,128)}, f32[64,128]{1,0:T(8,128)}, f32[64,128]{1,0:T(8,128)}) custom-call(f32[3,19,8,128]{3,2,1,0:T(8,128)S(1)} %get-tuple-element.76.refs_0_, f32[152,152]{1,0:T(8,128)S(1)} %get-tuple-element.77.refs_1_, ...), custom_call_target="tpu_custom_call" | custom-call | flops 1024 | bytes 1048576 | tf_op jit(solution)/shard_map/pallas_call | solution.py:654
  22.8 0.2 collective-permute-done.10.refs_3_
  23.0 1.0 %shard_map.165 = f32[19,64,128]{2,1,0:T(8,128)} custom-call(f32[19,64,128]{2,1,0:T(8,128)S(1)} %get-tuple-element.89.refs_2_.refs_0_, f32[19,64,128]{2,1,0:T(8,128)S(1)} %get-tuple-element.108.refs_1_, f32[7,64,128]{2,1,0:T(8,128)S(1)} %get-tuple-element.98.refs_3_.refs_2_, f32[32,128]{1,0:T(8,128)S(1)} %collective-permute-done.10.refs_3_, ...), custom_call_target="tpu_custom_call" | custom-call | flops 1048576 | bytes 1048576 | tf_op jit(solution)/shard_map/pallas_call | solution.py:654
  (41 shorter events, 0.2 us)
Async XLA Ops:
  0.7 0.8 %copy-start.3 = (f32[32,1,2,128]{3,2,1,0:T(2,128)S(1)}, f32[32,1,2,128]{3,2,1,0:T(2,128)}, u32[]{:S(2)}) copy-start(f32[32,1,2,128]{3,2,1,0:T(2,128)} %param.14) | copy-start | bytes 98308
  0.7 0.8 %copy-start.4 = (f32[32,1,2,128]{3,2,1,0:T(2,128)S(1)}, f32[32,1,2,128]{3,2,1,0:T(2,128)}, u32[]{:S(2)}) copy-start(f32[32,1,2,128]{3,2,1,0:T(2,128)} %param.15) | copy-start | bytes 98308
  0.7 0.8 %copy-start.5 = (f32[32,1,2,128]{3,2,1,0:T(2,128)S(1)}, f32[32,1,2,128]{3,2,1,0:T(2,128)}, u32[]{:S(2)}) copy-start(f32[32,1,2,128]{3,2,1,0:T(2,128)} %param.16) | copy-start | bytes 98308
  0.7 0.8 %copy-start.8 = (f32[4,128]{1,0:T(4,128)S(1)}, f32[4,128]{1,0:T(4,128)}, u32[]{:S(2)}) copy-start(f32[4,128]{1,0:T(4,128)} %refs_10_.1) | copy-start | bytes 6148
  0.7 0.8 %copy-start.11 = (f32[19]{0:T(128)S(1)}, f32[19]{0:T(128)}, u32[]{:S(2)}) copy-start(f32[19]{0:T(128)} %param.23) | copy-start | bytes 232
  0.7 3.9 %copy-start = (f32[19,16,4,128]{3,2,1,0:T(4,128)S(1)}, f32[19,16,4,128]{3,2,1,0:T(4,128)}, u32[]{:S(2)}) copy-start(f32[19,16,4,128]{3,2,1,0:T(4,128)} %param.17) | copy-start | bytes 1867780
  0.7 0.8 %copy-start.6 = (f32[19,19]{1,0:T(8,128)S(1)}, f32[19,19]{1,0:T(8,128)}, u32[]{:S(2)}) copy-start(f32[19,19]{1,0:T(8,128)} %refs_8_.1) | copy-start | bytes 4336
  0.7 0.8 %copy-start.7 = (s32[4,128]{1,0:T(4,128)S(1)}, s32[4,128]{1,0:T(4,128)}, u32[]{:S(2)}) copy-start(s32[4,128]{1,0:T(4,128)} %refs_9_.1) | copy-start | bytes 6148
  0.7 0.8 %copy-start.9 = (f32[19]{0:T(128)S(1)}, f32[19]{0:T(128)}, u32[]{:S(2)}) copy-start(f32[19]{0:T(128)} %param.21) | copy-start | bytes 232
  1.6 7.3 %collective-permute-start.1 = (f32[180,128]{1,0:T(8,128)S(1)}, f32[180,128]{1,0:T(8,128)S(1)}, u32[]{:S(2)}, u32[]{:S(2)}) collective-permute-start(f32[180,128]{1,0:T(8,128)S(1)} %get-tuple-element.73), channel_id=1, source_target_pairs={{0,16},{16,0},{1,17},{17,1},{2,18},{18,2},{3,19},{19,3},{4,20},{20... | collective-permute-start | bytes 276488 | tf_op jit(solution)/shard_map/ppermute | solution.py:85
  4.7 4.2 %collective-permute-start = (f32[40,128]{1,0:T(8,128)S(1)}, f32[40,128]{1,0:T(8,128)S(1)}, u32[]{:S(2)}, u32[]{:S(2)}) collective-permute-start(f32[40,128]{1,0:T(8,128)S(1)} %get-tuple-element.71), channel_id=1, source_target_pairs={{0,16},{16,0},{1,17},{17,1},{2,18},{18,2},{3,19},{19,3},{4,20},{20... | collective-permute-start | bytes 61448 | tf_op jit(solution)/shard_map/ppermute | solution.py:85
  5.4 5.4 %collective-permute-start.2 = (f32[88,128]{1,0:T(8,128)S(1)}, f32[88,128]{1,0:T(8,128)S(1)}, u32[]{:S(2)}, u32[]{:S(2)}) collective-permute-start(f32[88,128]{1,0:T(8,128)S(1)} %get-tuple-element.75), channel_id=1, source_target_pairs={{0,16},{16,0},{1,17},{17,1},{2,18},{18,2},{3,19},{19,3},{4,20},{20... | collective-permute-start | bytes 135176 | tf_op jit(solution)/shard_map/ppermute | solution.py:85
  7.3 6.3 %collective-permute-start.5 = (f32[21,16,128]{2,1,0:T(8,128)S(1)}, f32[21,16,128]{2,1,0:T(8,128)S(1)}, u32[]{:S(2)}, u32[]{:S(2)}) collective-permute-start(f32[21,16,128]{2,1,0:T(8,128)S(1)} %get-tuple-element.81), channel_id=1, source_target_pairs={{0,1},{1,0},{2,3},{3,2},{4,5},{5,4},{6,7},{7,6},{8,9},{9,8},{10,11... | collective-permute-start | bytes 516104 | tf_op jit(solution)/shard_map/ppermute | solution.py:750
  7.3 6.3 %collective-permute-start.6 = (f32[21,16,128]{2,1,0:T(8,128)S(1)}, f32[21,16,128]{2,1,0:T(8,128)S(1)}, u32[]{:S(2)}, u32[]{:S(2)}) collective-permute-start(f32[21,16,128]{2,1,0:T(8,128)S(1)} %get-tuple-element.82), channel_id=1, source_target_pairs={{0,4},{1,2},{2,1},{3,7},{4,0},{5,6},{6,5},{7,3},{8,12},{9,10},{10,... | collective-permute-start | bytes 516104 | tf_op jit(solution)/shard_map/ppermute | solution.py:751
  9.2 4.3 %collective-permute-start.7 = (f32[48,128]{1,0:T(8,128)S(1)}, f32[48,128]{1,0:T(8,128)S(1)}, u32[]{:S(2)}, u32[]{:S(2)}) collective-permute-start(f32[48,128]{1,0:T(8,128)S(1)} %get-tuple-element.83), channel_id=1, source_target_pairs={{0,1},{1,2},{2,3},{3,0},{4,5},{5,6},{6,7},{7,4},{8,9},{9,10},{10,1... | collective-permute-start | bytes 73736 | tf_op jit(solution)/shard_map/ppermute | solution.py:777
  9.3 4.2 %collective-permute-start.3 = (f32[32,128]{1,0:T(8,128)S(1)}, f32[32,128]{1,0:T(8,128)S(1)}, u32[]{:S(2)}, u32[]{:S(2)}) collective-permute-start(f32[32,128]{1,0:T(8,128)S(1)} %get-tuple-element.79), channel_id=1, source_target_pairs={{0,4},{1,5},{2,6},{3,7},{4,0},{5,1},{6,2},{7,3},{8,12},{9,13},{10,... | collective-permute-start | bytes 49160 | tf_op jit(solution)/shard_map/ppermute | solution.py:775
  10.8 2.7 %collective-permute-start.4 = (f32[32,128]{1,0:T(8,128)S(1)}, f32[32,128]{1,0:T(8,128)S(1)}, u32[]{:S(2)}, u32[]{:S(2)}) collective-permute-start(f32[32,128]{1,0:T(8,128)S(1)} %get-tuple-element.80), channel_id=1, source_target_pairs={{0,1},{1,0},{2,3},{3,2},{4,8},{5,9},{6,10},{7,11},{8,4},{9,5},{10,... | collective-permute-start | bytes 49160 | tf_op jit(solution)/shard_map/ppermute | solution.py:776
  13.7 5.1 %collective-permute-start.8 = (f32[40,128]{1,0:T(8,128)S(1)}, f32[40,128]{1,0:T(8,128)S(1)}, u32[]{:S(2)}, u32[]{:S(2)}) collective-permute-start(f32[40,128]{1,0:T(8,128)S(1)} %get-tuple-element.92), channel_id=1, source_target_pairs={{0,16},{16,0},{1,17},{17,1},{2,18},{18,2},{3,19},{19,3},{4,20},{20... | collective-permute-start | bytes 61448 | tf_op jit(solution)/shard_map/ppermute | solution.py:85
  15.6 4.7 %collective-permute-start.9 = (f32[88,128]{1,0:T(8,128)S(1)}, f32[88,128]{1,0:T(8,128)S(1)}, u32[]{:S(2)}, u32[]{:S(2)}) collective-permute-start(f32[88,128]{1,0:T(8,128)S(1)} %get-tuple-element.99), channel_id=1, source_target_pairs={{0,16},{16,0},{1,17},{17,1},{2,18},{18,2},{3,19},{19,3},{4,20},{20... | collective-permute-start | bytes 135176 | tf_op jit(solution)/shard_map/ppermute | solution.py:85
  16.5 6.5 %collective-permute-start.12 = (f32[19,16,128]{2,1,0:T(8,128)S(1)}, f32[19,16,128]{2,1,0:T(8,128)S(1)}, u32[]{:S(2)}, u32[]{:S(2)}) collective-permute-start(f32[19,16,128]{2,1,0:T(8,128)S(1)} %get-tuple-element.111), channel_id=1, source_target_pairs={{0,1},{1,0},{2,3},{3,2},{4,5},{5,4},{6,7},{7,6},{8,9},{9,8},{10,11... | collective-permute-start | bytes 466952 | tf_op jit(solution)/shard_map/ppermute | solution.py:750
  16.5 6.5 %collective-permute-start.13 = (f32[19,16,128]{2,1,0:T(8,128)S(1)}, f32[19,16,128]{2,1,0:T(8,128)S(1)}, u32[]{:S(2)}, u32[]{:S(2)}) collective-permute-start(f32[19,16,128]{2,1,0:T(8,128)S(1)} %get-tuple-element.112), channel_id=1, source_target_pairs={{0,4},{1,2},{2,1},{3,7},{4,0},{5,6},{6,5},{7,3},{8,12},{9,10},{10,... | collective-permute-start | bytes 466952 | tf_op jit(solution)/shard_map/ppermute | solution.py:751
  19.1 3.8 %collective-permute-start.14 = (f32[48,128]{1,0:T(8,128)S(1)}, f32[48,128]{1,0:T(8,128)S(1)}, u32[]{:S(2)}, u32[]{:S(2)}) collective-permute-start(f32[48,128]{1,0:T(8,128)S(1)} %get-tuple-element.113), channel_id=1, source_target_pairs={{0,1},{1,2},{2,3},{3,0},{4,5},{5,6},{6,7},{7,4},{8,9},{9,10},{10,1... | collective-permute-start | bytes 73736 | tf_op jit(solution)/shard_map/ppermute | solution.py:777
  19.2 3.8 %collective-permute-start.10 = (f32[32,128]{1,0:T(8,128)S(1)}, f32[32,128]{1,0:T(8,128)S(1)}, u32[]{:S(2)}, u32[]{:S(2)}) collective-permute-start(f32[32,128]{1,0:T(8,128)S(1)} %get-tuple-element.109), channel_id=1, source_target_pairs={{0,4},{1,5},{2,6},{3,7},{4,0},{5,1},{6,2},{7,3},{8,12},{9,13},{10,... | collective-permute-start | bytes 49160 | tf_op jit(solution)/shard_map/ppermute | solution.py:775
  20.4 2.6 %collective-permute-start.11 = (f32[32,128]{1,0:T(8,128)S(1)}, f32[32,128]{1,0:T(8,128)S(1)}, u32[]{:S(2)}, u32[]{:S(2)}) collective-permute-start(f32[32,128]{1,0:T(8,128)S(1)} %get-tuple-element.110), channel_id=1, source_target_pairs={{0,1},{1,0},{2,3},{3,2},{4,8},{5,9},{6,10},{7,11},{8,4},{9,5},{10,... | collective-permute-start | bytes 49160 | tf_op jit(solution)/shard_map/ppermute | solution.py:776
  (3 other events, 2.3 us)

commit v8 on v7

--- a/solution.py
+++ b/solution.py
@@ -333,11 +333,10 @@
         fields = refs.take(5)
     band_ref, msg_xa, msg_xb, speed_ref = refs.take(4)
     full_out = refs.take(5 if first_step else 4)
-    p_full, p_other_s = refs.take(2)
+    (p_other_s,) = refs.take(1)
     if first_step:
         fields = refs.take(5)
         other_s = refs.take(5 * (count - 1))
-    face_s, par_s, wet_s = refs.take(3)
     g = lax.axis_index("grp")
     cells, width = p_own.shape
     levels = cells // rows
@@ -346,9 +345,8 @@
     strip = rows // count
 
     pigments = [read_pigment(rows, count, o, p_other_s, g) for o in p_others]
-    for b in range(count):
-        k = lax.rem(g - b + count, count)
-        p_full[pl.ds(b * cells, cells), :] = pick(p_own[...], pigments, k)
+    bands = [pick(p_own[...], pigments, lax.rem(g - b + count, count)) for b in range(count)]
+    pigment = jnp.concatenate(bands, axis=0)
     if first_step:
         strip_cells = all_levels * strip
         for at in range(5):
@@ -374,7 +372,7 @@
 
     row = iota((total, width), 0)
     wet = jnp.where(row // rows < tile(depth_ref[...], total), 1.0, 0.0)
-    att = WATER_ATTEN + PIGMENT_ATTEN * p_full[...]
+    att = WATER_ATTEN + PIGMENT_ATTEN * pigment
     summed = att
     step = rows
     while step < total:
@@ -396,28 +394,21 @@
         flux = face * (below(v) - v)
         return v + flux - turn(flux, rows, 0)
 
-    for at, v in enumerate((east, north, temp, sal)):
-        full_out[at][...] = stir(v)
-    if first_step:
-        full_out[4][...] = mixing
-    face_s[...] = face
-    par_s[...] = par
-    wet_s[...] = wet
-
-    band = pl.ds(pl.multiple_of(g * cells, SUB), cells)
-    above = pl.ds(pl.multiple_of(lax.max(g * cells - SUB, 0), SUB), SUB)
-    face_band = face_s[band, :]
-    lifted = turn(jnp.concatenate([face_s[above, :], face_band], axis=0), rows, 0)[SUB:]
-    lifted = jnp.where((iota((cells, width), 0) < rows) & (g == 0), 0.0, lifted)
-    u = full_out[0][band, :]
-    wet_band = wet_s[band, :]
+    mixed = [stir(v) for v in (east, north, temp, sal)]
+
+    def band_of(v):
+        value = v[:cells]
+        for b in range(1, count):
+            value = jnp.where(g == b, v[b * cells : (b + 1) * cells], value)
+        return value
+
+    u = band_of(mixed[0])
+    wet_band = band_of(wet)
     band_ref[0] = u
-    band_ref[1] = full_out[1][band, :]
-    band_ref[2] = full_out[2][band, :]
-    band_ref[3] = face_band
-    band_ref[4] = lifted
-    band_ref[5] = par_s[band, :]
-    band_ref[6] = wet_band
+    band_ref[1] = band_of(mixed[1])
+    speed_ref[pl.ds(0, levels), :] = band_ref[1, pl.ds(rows - 1, levels, stride=rows), :]
+    speed_ref[pl.ds(levels, levels), :] = jnp.zeros((levels, width), F32)
+    speed_ref[pl.ds(2 * levels, levels), :] = jnp.zeros((levels, width), F32)
 
     x_even = lax.rem(lax.axis_index("gx"), 2) == 0
     xa, xb = in_xa[...], in_xb[...]
@@ -426,9 +417,15 @@
     _, right = pack_sides(u, tracers, tracers + 3, left, right)
     msg_xa[...] = jnp.where(x_even, right, left)
     msg_xb[...] = jnp.where(x_even, left, right)
-    speed_ref[pl.ds(0, levels), :] = band_ref[1, pl.ds(rows - 1, levels, stride=rows), :]
-    speed_ref[pl.ds(levels, levels), :] = jnp.zeros((levels, width), F32)
-    speed_ref[pl.ds(2 * levels, levels), :] = jnp.zeros((levels, width), F32)
+    band_ref[2] = band_of(mixed[2])
+    band_ref[3] = band_of(face)
+    band_ref[4] = band_of(turn(face, rows, 0))
+    band_ref[5] = band_of(par)
+    band_ref[6] = wet_band
+    for at, v in enumerate(mixed):
+        full_out[at][...] = v
+    if first_step:
+        full_out[4][...] = mixing
 
 
 def start_own_strip(rows, count, g, full, outs, strips, sems):
@@ -766,10 +763,9 @@
                 shape(3 * levels, width),
                 *[shape(total, width)] * (5 if first_step else 4),
             ],
-            scratch=[column, band_s]
+            scratch=[band_s]
             + [column] * (5 if first_step else 0)
-            + [pltpu.VMEM((strip_cells, width), F32)] * (5 * (count - 1) if first_step else 0)
-            + [column] * 3,
+            + [pltpu.VMEM((strip_cells, width), F32)] * (5 * (count - 1) if first_step else 0),
             flops=1<<32,
         )
         xa = lax.ppermute(xa, AXES, pairing(sizes, "gx", 0))

time: 24.1 us -> 24.1 us (level)
  no operation moved by 1% of the time
where the time goes in v8:
time: 24.1 us; the launch traced here: 24 us
  starting transfers between devices  15.9 us (66%)
  Pallas kernels  6.18 us (26%)
  between operations  0.86 us (4%)
  local copies, waits for them, and re-layouts  0.79 us (3%)
    ppermute x5, starting transfers between devices, from_others(): lax.ppermute(value, 'grp', [(i, (i + k) % count) for i in range(count)])  7.32 us
    pallas_call x11, Pallas kernels, call(): pl.pallas_call(kernel, in_specs=[vmem() for _ in ins] if in_specs is None...  6.18 us
    ppermute x2, starting transfers between devices, per_device(): yb = lax.ppermute(yb, AXES, pairing(sizes, 'gy', 1))  3.9 us
    ppermute x2, starting transfers between devices, per_device(): xa = lax.ppermute(xa, AXES, pairing(sizes, 'gx', 0))  2.78 us
    ppermute x2, starting transfers between devices, per_device(): xb = lax.ppermute(xb, AXES, pairing(sizes, 'gx', 1))  1.77 us
    unnamed x24, local copies, waits for them, and re-layouts  0.79 us
  transfers between devices with their start and end apart: 15, of which 1 were waited for; matrix products, arithmetic and copies ran while one was open for 0% of the time, Pallas kernels for 21%

profile of v8, /device:TPU:0, one launch (start us, length us, event | category | flops | bytes accessed | tf_op | source)
XLA Modules:
  0.0 24.0 jit_solution(4389111186299033921)
XLA Ops:
  0.8 0.6 %copy-done.1 = f32[32,1,2,128]{3,2,1,0:T(2,128)S(1)} copy-done((f32[32,1,2,128]{3,2,1,0:T(2,128)S(1)}, f32[32,1,2,128]{3,2,1,0:T(2,128)}, u32[]{:S(2)}) %copy-start.1) | copy-done | bytes 32792
  1.5 0.1 copy-done.6
  1.6 3.0 %collective-permute-start.1 = (f32[180,128]{1,0:T(8,128)S(1)}, f32[180,128]{1,0:T(8,128)S(1)}, u32[]{:S(2)}, u32[]{:S(2)}) collective-permute-start(f32[180,128]{1,0:T(8,128)S(1)} %get-tuple-element.73), channel_id=1, source_target_pairs={{0,16},{16,0},{1,17},{17,1},{2,18},{18,2},{3,19},{19,3},{4,20},{20... | collective-permute-start | bytes 276488 | tf_op jit(solution)/shard_map/ppermute | solution.py:85
  4.6 0.1 shard_map.157
  4.7 0.3 %collective-permute-start = (f32[40,128]{1,0:T(8,128)S(1)}, f32[40,128]{1,0:T(8,128)S(1)}, u32[]{:S(2)}, u32[]{:S(2)}) collective-permute-start(f32[40,128]{1,0:T(8,128)S(1)} %get-tuple-element.71), channel_id=1, source_target_pairs={{0,16},{16,0},{1,17},{17,1},{2,18},{18,2},{3,19},{19,3},{4,20},{20... | collective-permute-start | bytes 61448 | tf_op jit(solution)/shard_map/ppermute | solution.py:85
  5.0 0.4 %shard_map.158 = (f32[32,128]{1,0:T(8,128)S(1)}, f32[32,128]{1,0:T(8,128)S(1)}, f32[21,16,128]{2,1,0:T(8,128)S(1)}, f32[21,16,128]{2,1,0:T(8,128)S(1)}, s32[8,12...) custom-call(s32[4,128]{1,0:T(4,128)S(1)} %get-tuple-element.64.refs_0_, ...), custom_call_target="tpu_custom_call" | custom-call | flops 16777216 | bytes 1048576 | tf_op jit(solution)/shard_map/pallas_call | solution.py:651
  5.4 1.8 %collective-permute-start.2 = (f32[88,128]{1,0:T(8,128)S(1)}, f32[88,128]{1,0:T(8,128)S(1)}, u32[]{:S(2)}, u32[]{:S(2)}) collective-permute-start(f32[88,128]{1,0:T(8,128)S(1)} %get-tuple-element.75), channel_id=1, source_target_pairs={{0,16},{16,0},{1,17},{17,1},{2,18},{18,2},{3,19},{19,3},{4,20},{20... | collective-permute-start | bytes 135176 | tf_op jit(solution)/shard_map/ppermute | solution.py:85
  7.3 1.6 %collective-permute-start.6 = (f32[21,16,128]{2,1,0:T(8,128)S(1)}, f32[21,16,128]{2,1,0:T(8,128)S(1)}, u32[]{:S(2)}, u32[]{:S(2)}) collective-permute-start(f32[21,16,128]{2,1,0:T(8,128)S(1)} %get-tuple-element.82), channel_id=1, source_target_pairs={{0,4},{1,2},{2,1},{3,7},{4,0},{5,6},{6,5},{7,3},{8,12},{9,10},{10,... | collective-permute-start | bytes 516104 | tf_op jit(solution)/shard_map/ppermute | solution.py:748
  8.9 0.3 %shard_map.159 = (f32[7,64,128]{2,1,0:T(8,128)S(1)}, f32[32,128]{1,0:T(8,128)S(1)}, f32[32,128]{1,0:T(8,128)S(1)}, f32[48,128]{1,0:T(8,128)S(1)}, f32[128,128]{1...) custom-call(s32[8,128]{1,0:T(8,128)S(1)} %get-tuple-element.67.refs_, ...), custom_call_target="tpu_custom_call" | custom-call | flops 4294967296 | bytes 1048576 | tf_op jit(solution)/shard_map/pallas_call | solution.py:651
  9.1 0.1 collective-permute-start.7
  9.2 1.6 %collective-permute-start.3 = (f32[32,128]{1,0:T(8,128)S(1)}, f32[32,128]{1,0:T(8,128)S(1)}, u32[]{:S(2)}, u32[]{:S(2)}) collective-permute-start(f32[32,128]{1,0:T(8,128)S(1)} %get-tuple-element.79), channel_id=1, source_target_pairs={{0,4},{1,5},{2,6},{3,7},{4,0},{5,1},{6,2},{7,3},{8,12},{9,13},{10,... | collective-permute-start | bytes 49160 | tf_op jit(solution)/shard_map/ppermute | solution.py:771
  10.8 1.0 %collective-permute-start.4 = (f32[32,128]{1,0:T(8,128)S(1)}, f32[32,128]{1,0:T(8,128)S(1)}, u32[]{:S(2)}, u32[]{:S(2)}) collective-permute-start(f32[32,128]{1,0:T(8,128)S(1)} %get-tuple-element.80), channel_id=1, source_target_pairs={{0,1},{1,0},{2,3},{3,2},{4,8},{5,9},{6,10},{7,11},{8,4},{9,5},{10,... | collective-permute-start | bytes 49160 | tf_op jit(solution)/shard_map/ppermute | solution.py:772
  11.8 1.6 %shard_map.160 = (f32[19,64,128]{2,1,0:T(8,128)S(1)}, f32[64,128]{1,0:T(8,128)S(1)}, f32[3,19,8,128]{3,2,1,0:T(8,128)S(1)}, f32[152,152]{1,0:T(8,128)S(1)}) custom-call(f32[1,19]{1,0:T(1,128)S(1)} %get-tuple-element.60.refs_0_, f32[1,19]{1,0:T(1,128)S(1)} %get-tuple-element.61.refs_1_, f32[1,19]{1,0:T(1,128)S(1)} %get-tuple-element.62.pig_ref.refs_2_, ...), custom_call_target="tpu_custom_call" | custom-call | flops 1024 | bytes 1048576 | tf_op jit(solution)/shard_map/pallas_call | solution.py:651
  13.5 0.1 shard_map.161
  13.7 1.3 %collective-permute-start.8 = (f32[40,128]{1,0:T(8,128)S(1)}, f32[40,128]{1,0:T(8,128)S(1)}, u32[]{:S(2)}, u32[]{:S(2)}) collective-permute-start(f32[40,128]{1,0:T(8,128)S(1)} %get-tuple-element.92), channel_id=1, source_target_pairs={{0,16},{16,0},{1,17},{17,1},{2,18},{18,2},{3,19},{19,3},{4,20},{20... | collective-permute-start | bytes 61448 | tf_op jit(solution)/shard_map/ppermute | solution.py:85
  14.9 0.6 %shard_map.162 = (f32[19,64,128]{2,1,0:T(8,128)S(1)}, f32[32,128]{1,0:T(8,128)S(1)}, f32[32,128]{1,0:T(8,128)S(1)}, f32[19,16,128]{2,1,0:T(8,128)S(1)}, f32[19,1...) custom-call(f32[19,64,128]{2,1,0:T(8,128)S(1)} %bitcast.26, f32[19,64,128]{2,1,0:T(8,128)S(1)} %get-tuple-element.78.refs_8_.refs_1_, ...), custom_call_target="tpu_custom_call" | custom-call | flops 4294967296 | bytes 1048576 | tf_op jit(solution)/shard_map/pallas_call | solution.py:651
  15.6 0.9 %collective-permute-start.9 = (f32[88,128]{1,0:T(8,128)S(1)}, f32[88,128]{1,0:T(8,128)S(1)}, u32[]{:S(2)}, u32[]{:S(2)}) collective-permute-start(f32[88,128]{1,0:T(8,128)S(1)} %get-tuple-element.99), channel_id=1, source_target_pairs={{0,16},{16,0},{1,17},{17,1},{2,18},{18,2},{3,19},{19,3},{4,20},{20... | collective-permute-start | bytes 135176 | tf_op jit(solution)/shard_map/ppermute | solution.py:85
  16.5 2.3 %collective-permute-start.13 = (f32[19,16,128]{2,1,0:T(8,128)S(1)}, f32[19,16,128]{2,1,0:T(8,128)S(1)}, u32[]{:S(2)}, u32[]{:S(2)}) collective-permute-start(f32[19,16,128]{2,1,0:T(8,128)S(1)} %get-tuple-element.112), channel_id=1, source_target_pairs={{0,4},{1,2},{2,1},{3,7},{4,0},{5,6},{6,5},{7,3},{8,12},{9,10},{10,... | collective-permute-start | bytes 466952 | tf_op jit(solution)/shard_map/ppermute | solution.py:748
  18.8 0.3 %shard_map.163 = (f32[7,64,128]{2,1,0:T(8,128)S(1)}, f32[32,128]{1,0:T(8,128)S(1)}, f32[32,128]{1,0:T(8,128)S(1)}, f32[48,128]{1,0:T(8,128)S(1)}, f32[128,128]{1...) custom-call(s32[8,128]{1,0:T(8,128)S(1)} %get-tuple-element.67.refs_0_, ...), custom_call_target="tpu_custom_call" | custom-call | flops 4294967296 | bytes 1048576 | tf_op jit(solution)/shard_map/pallas_call | solution.py:651
  19.1 1.2 %collective-permute-start.10 = (f32[32,128]{1,0:T(8,128)S(1)}, f32[32,128]{1,0:T(8,128)S(1)}, u32[]{:S(2)}, u32[]{:S(2)}) collective-permute-start(f32[32,128]{1,0:T(8,128)S(1)} %get-tuple-element.109), channel_id=1, source_target_pairs={{0,4},{1,5},{2,6},{3,7},{4,0},{5,1},{6,2},{7,3},{8,12},{9,13},{10,... | collective-permute-start | bytes 49160 | tf_op jit(solution)/shard_map/ppermute | solution.py:771
  20.3 0.8 %collective-permute-start.11 = (f32[32,128]{1,0:T(8,128)S(1)}, f32[32,128]{1,0:T(8,128)S(1)}, u32[]{:S(2)}, u32[]{:S(2)}) collective-permute-start(f32[32,128]{1,0:T(8,128)S(1)} %get-tuple-element.110), channel_id=1, source_target_pairs={{0,1},{1,0},{2,3},{3,2},{4,8},{5,9},{6,10},{7,11},{8,4},{9,5},{10,... | collective-permute-start | bytes 49160 | tf_op jit(solution)/shard_map/ppermute | solution.py:772
  21.1 1.7 %shard_map.164 = (f32[19,64,128]{2,1,0:T(8,128)S(1)}, f32[64,128]{1,0:T(8,128)}, f32[64,128]{1,0:T(8,128)}, f32[64,128]{1,0:T(8,128)}, f32[64,128]{1,0:T(8,128)}) custom-call(f32[3,19,8,128]{3,2,1,0:T(8,128)S(1)} %get-tuple-element.76.refs_0_, f32[152,152]{1,0:T(8,128)S(1)} %get-tuple-element.77.refs_1_, ...), custom_call_target="tpu_custom_call" | custom-call | flops 1024 | bytes 1048576 | tf_op jit(solution)/shard_map/pallas_call | solution.py:651
  22.8 0.2 collective-permute-done.10.refs_3_
  23.0 1.0 %shard_map.165 = f32[19,64,128]{2,1,0:T(8,128)} custom-call(f32[19,64,128]{2,1,0:T(8,128)S(1)} %get-tuple-element.89.refs_2_.refs_0_, f32[19,64,128]{2,1,0:T(8,128)S(1)} %get-tuple-element.108.refs_1_, f32[7,64,128]{2,1,0:T(8,128)S(1)} %get-tuple-element.98.refs_3_.refs_2_, f32[32,128]{1,0:T(8,128)S(1)} %collective-permute-done.10.refs_3_, ...), custom_call_target="tpu_custom_call" | custom-call | flops 1048576 | bytes 1048576 | tf_op jit(solution)/shard_map/pallas_call | solution.py:651
  (41 shorter events, 0.2 us)
Async XLA Ops:
  0.7 0.8 %copy-start.3 = (f32[32,1,2,128]{3,2,1,0:T(2,128)S(1)}, f32[32,1,2,128]{3,2,1,0:T(2,128)}, u32[]{:S(2)}) copy-start(f32[32,1,2,128]{3,2,1,0:T(2,128)} %param.14) | copy-start | bytes 98308
  0.7 0.8 %copy-start.4 = (f32[32,1,2,128]{3,2,1,0:T(2,128)S(1)}, f32[32,1,2,128]{3,2,1,0:T(2,128)}, u32[]{:S(2)}) copy-start(f32[32,1,2,128]{3,2,1,0:T(2,128)} %param.15) | copy-start | bytes 98308
  0.7 0.8 %copy-start.5 = (f32[32,1,2,128]{3,2,1,0:T(2,128)S(1)}, f32[32,1,2,128]{3,2,1,0:T(2,128)}, u32[]{:S(2)}) copy-start(f32[32,1,2,128]{3,2,1,0:T(2,128)} %param.16) | copy-start | bytes 98308
  0.7 0.8 %copy-start.8 = (f32[4,128]{1,0:T(4,128)S(1)}, f32[4,128]{1,0:T(4,128)}, u32[]{:S(2)}) copy-start(f32[4,128]{1,0:T(4,128)} %refs_10_.1) | copy-start | bytes 6148
  0.7 0.8 %copy-start.11 = (f32[19]{0:T(128)S(1)}, f32[19]{0:T(128)}, u32[]{:S(2)}) copy-start(f32[19]{0:T(128)} %param.23) | copy-start | bytes 232
  0.7 3.9 %copy-start = (f32[19,16,4,128]{3,2,1,0:T(4,128)S(1)}, f32[19,16,4,128]{3,2,1,0:T(4,128)}, u32[]{:S(2)}) copy-start(f32[19,16,4,128]{3,2,1,0:T(4,128)} %param.17) | copy-start | bytes 1867780
  0.7 0.8 %copy-start.6 = (f32[19,19]{1,0:T(8,128)S(1)}, f32[19,19]{1,0:T(8,128)}, u32[]{:S(2)}) copy-start(f32[19,19]{1,0:T(8,128)} %refs_8_.1) | copy-start | bytes 4336
  0.7 0.8 %copy-start.7 = (s32[4,128]{1,0:T(4,128)S(1)}, s32[4,128]{1,0:T(4,128)}, u32[]{:S(2)}) copy-start(s32[4,128]{1,0:T(4,128)} %refs_9_.1) | copy-start | bytes 6148
  0.7 0.8 %copy-start.9 = (f32[19]{0:T(128)S(1)}, f32[19]{0:T(128)}, u32[]{:S(2)}) copy-start(f32[19]{0:T(128)} %param.21) | copy-start | bytes 232
  1.6 7.3 %collective-permute-start.1 = (f32[180,128]{1,0:T(8,128)S(1)}, f32[180,128]{1,0:T(8,128)S(1)}, u32[]{:S(2)}, u32[]{:S(2)}) collective-permute-start(f32[180,128]{1,0:T(8,128)S(1)} %get-tuple-element.73), channel_id=1, source_target_pairs={{0,16},{16,0},{1,17},{17,1},{2,18},{18,2},{3,19},{19,3},{4,20},{20... | collective-permute-start | bytes 276488 | tf_op jit(solution)/shard_map/ppermute | solution.py:85
  4.7 4.2 %collective-permute-start = (f32[40,128]{1,0:T(8,128)S(1)}, f32[40,128]{1,0:T(8,128)S(1)}, u32[]{:S(2)}, u32[]{:S(2)}) collective-permute-start(f32[40,128]{1,0:T(8,128)S(1)} %get-tuple-element.71), channel_id=1, source_target_pairs={{0,16},{16,0},{1,17},{17,1},{2,18},{18,2},{3,19},{19,3},{4,20},{20... | collective-permute-start | bytes 61448 | tf_op jit(solution)/shard_map/ppermute | solution.py:85
  5.4 5.4 %collective-permute-start.2 = (f32[88,128]{1,0:T(8,128)S(1)}, f32[88,128]{1,0:T(8,128)S(1)}, u32[]{:S(2)}, u32[]{:S(2)}) collective-permute-start(f32[88,128]{1,0:T(8,128)S(1)} %get-tuple-element.75), channel_id=1, source_target_pairs={{0,16},{16,0},{1,17},{17,1},{2,18},{18,2},{3,19},{19,3},{4,20},{20... | collective-permute-start | bytes 135176 | tf_op jit(solution)/shard_map/ppermute | solution.py:85
  7.3 6.3 %collective-permute-start.5 = (f32[21,16,128]{2,1,0:T(8,128)S(1)}, f32[21,16,128]{2,1,0:T(8,128)S(1)}, u32[]{:S(2)}, u32[]{:S(2)}) collective-permute-start(f32[21,16,128]{2,1,0:T(8,128)S(1)} %get-tuple-element.81), channel_id=1, source_target_pairs={{0,1},{1,0},{2,3},{3,2},{4,5},{5,4},{6,7},{7,6},{8,9},{9,8},{10,11... | collective-permute-start | bytes 516104 | tf_op jit(solution)/shard_map/ppermute | solution.py:747
  7.3 6.3 %collective-permute-start.6 = (f32[21,16,128]{2,1,0:T(8,128)S(1)}, f32[21,16,128]{2,1,0:T(8,128)S(1)}, u32[]{:S(2)}, u32[]{:S(2)}) collective-permute-start(f32[21,16,128]{2,1,0:T(8,128)S(1)} %get-tuple-element.82), channel_id=1, source_target_pairs={{0,4},{1,2},{2,1},{3,7},{4,0},{5,6},{6,5},{7,3},{8,12},{9,10},{10,... | collective-permute-start | bytes 516104 | tf_op jit(solution)/shard_map/ppermute | solution.py:748
  9.1 4.4 %collective-permute-start.7 = (f32[48,128]{1,0:T(8,128)S(1)}, f32[48,128]{1,0:T(8,128)S(1)}, u32[]{:S(2)}, u32[]{:S(2)}) collective-permute-start(f32[48,128]{1,0:T(8,128)S(1)} %get-tuple-element.83), channel_id=1, source_target_pairs={{0,1},{1,2},{2,3},{3,0},{4,5},{5,6},{6,7},{7,4},{8,9},{9,10},{10,1... | collective-permute-start | bytes 73736 | tf_op jit(solution)/shard_map/ppermute | solution.py:773
  9.2 4.2 %collective-permute-start.3 = (f32[32,128]{1,0:T(8,128)S(1)}, f32[32,128]{1,0:T(8,128)S(1)}, u32[]{:S(2)}, u32[]{:S(2)}) collective-permute-start(f32[32,128]{1,0:T(8,128)S(1)} %get-tuple-element.79), channel_id=1, source_target_pairs={{0,4},{1,5},{2,6},{3,7},{4,0},{5,1},{6,2},{7,3},{8,12},{9,13},{10,... | collective-permute-start | bytes 49160 | tf_op jit(solution)/shard_map/ppermute | solution.py:771
  10.8 2.7 %collective-permute-start.4 = (f32[32,128]{1,0:T(8,128)S(1)}, f32[32,128]{1,0:T(8,128)S(1)}, u32[]{:S(2)}, u32[]{:S(2)}) collective-permute-start(f32[32,128]{1,0:T(8,128)S(1)} %get-tuple-element.80), channel_id=1, source_target_pairs={{0,1},{1,0},{2,3},{3,2},{4,8},{5,9},{6,10},{7,11},{8,4},{9,5},{10,... | collective-permute-start | bytes 49160 | tf_op jit(solution)/shard_map/ppermute | solution.py:772
  13.7 5.1 %collective-permute-start.8 = (f32[40,128]{1,0:T(8,128)S(1)}, f32[40,128]{1,0:T(8,128)S(1)}, u32[]{:S(2)}, u32[]{:S(2)}) collective-permute-start(f32[40,128]{1,0:T(8,128)S(1)} %get-tuple-element.92), channel_id=1, source_target_pairs={{0,16},{16,0},{1,17},{17,1},{2,18},{18,2},{3,19},{19,3},{4,20},{20... | collective-permute-start | bytes 61448 | tf_op jit(solution)/shard_map/ppermute | solution.py:85
  15.6 4.8 %collective-permute-start.9 = (f32[88,128]{1,0:T(8,128)S(1)}, f32[88,128]{1,0:T(8,128)S(1)}, u32[]{:S(2)}, u32[]{:S(2)}) collective-permute-start(f32[88,128]{1,0:T(8,128)S(1)} %get-tuple-element.99), channel_id=1, source_target_pairs={{0,16},{16,0},{1,17},{17,1},{2,18},{18,2},{3,19},{19,3},{4,20},{20... | collective-permute-start | bytes 135176 | tf_op jit(solution)/shard_map/ppermute | solution.py:85
  16.5 6.5 %collective-permute-start.12 = (f32[19,16,128]{2,1,0:T(8,128)S(1)}, f32[19,16,128]{2,1,0:T(8,128)S(1)}, u32[]{:S(2)}, u32[]{:S(2)}) collective-permute-start(f32[19,16,128]{2,1,0:T(8,128)S(1)} %get-tuple-element.111), channel_id=1, source_target_pairs={{0,1},{1,0},{2,3},{3,2},{4,5},{5,4},{6,7},{7,6},{8,9},{9,8},{10,11... | collective-permute-start | bytes 466952 | tf_op jit(solution)/shard_map/ppermute | solution.py:747
  16.5 6.5 %collective-permute-start.13 = (f32[19,16,128]{2,1,0:T(8,128)S(1)}, f32[19,16,128]{2,1,0:T(8,128)S(1)}, u32[]{:S(2)}, u32[]{:S(2)}) collective-permute-start(f32[19,16,128]{2,1,0:T(8,128)S(1)} %get-tuple-element.112), channel_id=1, source_target_pairs={{0,4},{1,2},{2,1},{3,7},{4,0},{5,6},{6,5},{7,3},{8,12},{9,10},{10,... | collective-permute-start | bytes 466952 | tf_op jit(solution)/shard_map/ppermute | solution.py:748
  19.1 3.9 %collective-permute-start.14 = (f32[48,128]{1,0:T(8,128)S(1)}, f32[48,128]{1,0:T(8,128)S(1)}, u32[]{:S(2)}, u32[]{:S(2)}) collective-permute-start(f32[48,128]{1,0:T(8,128)S(1)} %get-tuple-element.113), channel_id=1, source_target_pairs={{0,1},{1,2},{2,3},{3,0},{4,5},{5,6},{6,7},{7,4},{8,9},{9,10},{10,1... | collective-permute-start | bytes 73736 | tf_op jit(solution)/shard_map/ppermute | solution.py:773
  19.1 3.8 %collective-permute-start.10 = (f32[32,128]{1,0:T(8,128)S(1)}, f32[32,128]{1,0:T(8,128)S(1)}, u32[]{:S(2)}, u32[]{:S(2)}) collective-permute-start(f32[32,128]{1,0:T(8,128)S(1)} %get-tuple-element.109), channel_id=1, source_target_pairs={{0,4},{1,5},{2,6},{3,7},{4,0},{5,1},{6,2},{7,3},{8,12},{9,13},{10,... | collective-permute-start | bytes 49160 | tf_op jit(solution)/shard_map/ppermute | solution.py:771
  20.3 2.6 %collective-permute-start.11 = (f32[32,128]{1,0:T(8,128)S(1)}, f32[32,128]{1,0:T(8,128)S(1)}, u32[]{:S(2)}, u32[]{:S(2)}) collective-permute-start(f32[32,128]{1,0:T(8,128)S(1)} %get-tuple-element.110), channel_id=1, source_target_pairs={{0,1},{1,0},{2,3},{3,2},{4,8},{5,9},{6,10},{7,11},{8,4},{9,5},{10,... | collective-permute-start | bytes 49160 | tf_op jit(solution)/shard_map/ppermute | solution.py:772
  (3 other events, 2.3 us)

commit v9 on v7

--- a/solution.py
+++ b/solution.py
@@ -459,7 +459,7 @@
         params, (rates_ref,) = refs.take(3), refs.take(1)
     else:
         tiles_ref, w_ref = refs.take(2)
-    c_ref, band_ref = refs.take(2)
+    c_ref, band_ref, _ = refs.take(3)
     lev_in = refs.take(1 if count == 2 else 2)
     if last_step:
         full = refs.take(4)
@@ -778,7 +778,7 @@
         tables = [shape(3, tracers, SUB, width), shape(tracers * SUB, tracers * SUB)]
         part, *rest = call(
             functools.partial(inner_kernel, rows, count, first_step, last_step),
-            [*([*params, rates] if first_step else known_rates), c, band, *lev, *(full if last_step else [])],
+            [*([*params, rates] if first_step else known_rates), c, band, ya, *lev, *(full if last_step else [])],
             [field]
             + ([shape(strip_cells, width)] * 4 if last_step else [cols])
             + (tables if first_step else []),

time: 24.1 us -> 24.1 us (level)
  no operation moved by 1% of the time
where the time goes in v9:
time: 24.1 us; the launch traced here: 23.9 us
  starting transfers between devices  15.9 us (66%)
  Pallas kernels  6.25 us (26%)
  between operations  0.85 us (4%)
  local copies, waits for them, and re-layouts  0.79 us (3%)
    ppermute x5, starting transfers between devices, from_others(): lax.ppermute(value, 'grp', [(i, (i + k) % count) for i in range(count)])  7.32 us
    pallas_call x11, Pallas kernels, call(): pl.pallas_call(kernel, in_specs=[vmem() for _ in ins] if in_specs is None...  6.25 us
    ppermute x2, starting transfers between devices, per_device(): yb = lax.ppermute(yb, AXES, pairing(sizes, 'gy', 1))  3.89 us
    ppermute x2, starting transfers between devices, per_device(): xa = lax.ppermute(xa, AXES, pairing(sizes, 'gx', 0))  2.78 us
    ppermute x2, starting transfers between devices, per_device(): xb = lax.ppermute(xb, AXES, pairing(sizes, 'gx', 1))  1.78 us
    unnamed x24, local copies, waits for them, and re-layouts  0.79 us
  transfers between devices with their start and end apart: 15, of which 1 were waited for; matrix products, arithmetic and copies ran while one was open for 0% of the time, Pallas kernels for 21%

profile of v9, /device:TPU:0, one launch (start us, length us, event | category | flops | bytes accessed | tf_op | source)
XLA Modules:
  0.0 23.9 jit_solution(9910641094766824790)
XLA Ops:
  0.8 0.6 %copy-done.1 = f32[32,1,2,128]{3,2,1,0:T(2,128)S(1)} copy-done((f32[32,1,2,128]{3,2,1,0:T(2,128)S(1)}, f32[32,1,2,128]{3,2,1,0:T(2,128)}, u32[]{:S(2)}) %copy-start.1) | copy-done | bytes 32792
  1.5 0.1 copy-done.6
  1.6 3.0 %collective-permute-start.1 = (f32[180,128]{1,0:T(8,128)S(1)}, f32[180,128]{1,0:T(8,128)S(1)}, u32[]{:S(2)}, u32[]{:S(2)}) collective-permute-start(f32[180,128]{1,0:T(8,128)S(1)} %get-tuple-element.73), channel_id=1, source_target_pairs={{0,16},{16,0},{1,17},{17,1},{2,18},{18,2},{3,19},{19,3},{4,20},{20... | collective-permute-start | bytes 276488 | tf_op jit(solution)/shard_map/ppermute | solution.py:85
  4.6 0.1 shard_map.157
  4.7 0.3 %collective-permute-start = (f32[40,128]{1,0:T(8,128)S(1)}, f32[40,128]{1,0:T(8,128)S(1)}, u32[]{:S(2)}, u32[]{:S(2)}) collective-permute-start(f32[40,128]{1,0:T(8,128)S(1)} %get-tuple-element.71), channel_id=1, source_target_pairs={{0,16},{16,0},{1,17},{17,1},{2,18},{18,2},{3,19},{19,3},{4,20},{20... | collective-permute-start | bytes 61448 | tf_op jit(solution)/shard_map/ppermute | solution.py:85
  5.0 0.4 %shard_map.158 = (f32[32,128]{1,0:T(8,128)S(1)}, f32[32,128]{1,0:T(8,128)S(1)}, f32[21,16,128]{2,1,0:T(8,128)S(1)}, f32[21,16,128]{2,1,0:T(8,128)S(1)}, s32[8,12...) custom-call(s32[4,128]{1,0:T(4,128)S(1)} %get-tuple-element.64.refs_0_, ...), custom_call_target="tpu_custom_call" | custom-call | flops 16777216 | bytes 1048576 | tf_op jit(solution)/shard_map/pallas_call | solution.py:654
  5.4 1.8 %collective-permute-start.3 = (f32[88,128]{1,0:T(8,128)S(1)}, f32[88,128]{1,0:T(8,128)S(1)}, u32[]{:S(2)}, u32[]{:S(2)}) collective-permute-start(f32[88,128]{1,0:T(8,128)S(1)} %get-tuple-element.76), channel_id=1, source_target_pairs={{0,16},{16,0},{1,17},{17,1},{2,18},{18,2},{3,19},{19,3},{4,20},{20... | collective-permute-start | bytes 135176 | tf_op jit(solution)/shard_map/ppermute | solution.py:85
  7.3 1.6 %collective-permute-start.6 = (f32[21,16,128]{2,1,0:T(8,128)S(1)}, f32[21,16,128]{2,1,0:T(8,128)S(1)}, u32[]{:S(2)}, u32[]{:S(2)}) collective-permute-start(f32[21,16,128]{2,1,0:T(8,128)S(1)} %get-tuple-element.82), channel_id=1, source_target_pairs={{0,4},{1,2},{2,1},{3,7},{4,0},{5,6},{6,5},{7,3},{8,12},{9,10},{10,... | collective-permute-start | bytes 516104 | tf_op jit(solution)/shard_map/ppermute | solution.py:751
  8.9 0.3 %shard_map.159 = (f32[7,64,128]{2,1,0:T(8,128)S(1)}, f32[32,128]{1,0:T(8,128)S(1)}, f32[32,128]{1,0:T(8,128)S(1)}, f32[48,128]{1,0:T(8,128)S(1)}, f32[128,128]{1...) custom-call(s32[8,128]{1,0:T(8,128)S(1)} %get-tuple-element.67.refs_, ...), custom_call_target="tpu_custom_call" | custom-call | flops 4294967296 | bytes 1048576 | tf_op jit(solution)/shard_map/pallas_call | solution.py:654
  9.2 0.1 collective-permute-start.7
  9.3 1.6 %collective-permute-start.4 = (f32[32,128]{1,0:T(8,128)S(1)}, f32[32,128]{1,0:T(8,128)S(1)}, u32[]{:S(2)}, u32[]{:S(2)}) collective-permute-start(f32[32,128]{1,0:T(8,128)S(1)} %get-tuple-element.80), channel_id=1, source_target_pairs={{0,4},{1,5},{2,6},{3,7},{4,0},{5,1},{6,2},{7,3},{8,12},{9,13},{10,... | collective-permute-start | bytes 49160 | tf_op jit(solution)/shard_map/ppermute | solution.py:775
  10.8 1.0 %collective-permute-start.5 = (f32[32,128]{1,0:T(8,128)S(1)}, f32[32,128]{1,0:T(8,128)S(1)}, u32[]{:S(2)}, u32[]{:S(2)}) collective-permute-start(f32[32,128]{1,0:T(8,128)S(1)} %get-tuple-element.81), channel_id=1, source_target_pairs={{0,1},{1,0},{2,3},{3,2},{4,8},{5,9},{6,10},{7,11},{8,4},{9,5},{10,... | collective-permute-start | bytes 49160 | tf_op jit(solution)/shard_map/ppermute | solution.py:776
  11.9 1.6 %shard_map.160 = (f32[19,64,128]{2,1,0:T(8,128)S(1)}, f32[64,128]{1,0:T(8,128)S(1)}, f32[3,19,8,128]{3,2,1,0:T(8,128)S(1)}, f32[152,152]{1,0:T(8,128)S(1)}) custom-call(f32[1,19]{1,0:T(1,128)S(1)} %get-tuple-element.60.refs_0_, f32[1,19]{1,0:T(1,128)S(1)} %get-tuple-element.61.refs_1_, f32[1,19]{1,0:T(1,128)S(1)} %get-tuple-element.62.pig_ref.refs_2_, ...), custom_call_target="tpu_custom_call" | custom-call | flops 1024 | bytes 1048576 | tf_op jit(solution)/shard_map/pallas_call | solution.py:654
  13.5 0.1 shard_map.161
  13.7 1.3 %collective-permute-start.8 = (f32[40,128]{1,0:T(8,128)S(1)}, f32[40,128]{1,0:T(8,128)S(1)}, u32[]{:S(2)}, u32[]{:S(2)}) collective-permute-start(f32[40,128]{1,0:T(8,128)S(1)} %get-tuple-element.92), channel_id=1, source_target_pairs={{0,16},{16,0},{1,17},{17,1},{2,18},{18,2},{3,19},{19,3},{4,20},{20... | collective-permute-start | bytes 61448 | tf_op jit(solution)/shard_map/ppermute | solution.py:85
  15.0 0.6 %shard_map.162 = (f32[19,64,128]{2,1,0:T(8,128)S(1)}, f32[32,128]{1,0:T(8,128)S(1)}, f32[32,128]{1,0:T(8,128)S(1)}, f32[19,16,128]{2,1,0:T(8,128)S(1)}, f32[19,1...) custom-call(f32[19,64,128]{2,1,0:T(8,128)S(1)} %bitcast.26, f32[19,64,128]{2,1,0:T(8,128)S(1)} %get-tuple-element.79.refs_8_.refs_1_, ...), custom_call_target="tpu_custom_call" | custom-call | flops 4294967296 | bytes 1048576 | tf_op jit(solution)/shard_map/pallas_call | solution.py:654
  15.6 0.9 %collective-permute-start.10 = (f32[88,128]{1,0:T(8,128)S(1)}, f32[88,128]{1,0:T(8,128)S(1)}, u32[]{:S(2)}, u32[]{:S(2)}) collective-permute-start(f32[88,128]{1,0:T(8,128)S(1)} %get-tuple-element.100), channel_id=1, source_target_pairs={{0,16},{16,0},{1,17},{17,1},{2,18},{18,2},{3,19},{19,3},{4,20},{20... | collective-permute-start | bytes 135176 | tf_op jit(solution)/shard_map/ppermute | solution.py:85
  16.5 2.3 %collective-permute-start.13 = (f32[19,16,128]{2,1,0:T(8,128)S(1)}, f32[19,16,128]{2,1,0:T(8,128)S(1)}, u32[]{:S(2)}, u32[]{:S(2)}) collective-permute-start(f32[19,16,128]{2,1,0:T(8,128)S(1)} %get-tuple-element.112), channel_id=1, source_target_pairs={{0,4},{1,2},{2,1},{3,7},{4,0},{5,6},{6,5},{7,3},{8,12},{9,10},{10,... | collective-permute-start | bytes 466952 | tf_op jit(solution)/shard_map/ppermute | solution.py:751
  18.8 0.3 %shard_map.163 = (f32[7,64,128]{2,1,0:T(8,128)S(1)}, f32[32,128]{1,0:T(8,128)S(1)}, f32[32,128]{1,0:T(8,128)S(1)}, f32[48,128]{1,0:T(8,128)S(1)}, f32[128,128]{1...) custom-call(s32[8,128]{1,0:T(8,128)S(1)} %get-tuple-element.67.refs_0_, ...), custom_call_target="tpu_custom_call" | custom-call | flops 4294967296 | bytes 1048576 | tf_op jit(solution)/shard_map/pallas_call | solution.py:654
  19.1 1.2 %collective-permute-start.11 = (f32[32,128]{1,0:T(8,128)S(1)}, f32[32,128]{1,0:T(8,128)S(1)}, u32[]{:S(2)}, u32[]{:S(2)}) collective-permute-start(f32[32,128]{1,0:T(8,128)S(1)} %get-tuple-element.110), channel_id=1, source_target_pairs={{0,4},{1,5},{2,6},{3,7},{4,0},{5,1},{6,2},{7,3},{8,12},{9,13},{10,... | collective-permute-start | bytes 49160 | tf_op jit(solution)/shard_map/ppermute | solution.py:775
  20.3 0.8 %collective-permute-start.12 = (f32[32,128]{1,0:T(8,128)S(1)}, f32[32,128]{1,0:T(8,128)S(1)}, u32[]{:S(2)}, u32[]{:S(2)}) collective-permute-start(f32[32,128]{1,0:T(8,128)S(1)} %get-tuple-element.111), channel_id=1, source_target_pairs={{0,1},{1,0},{2,3},{3,2},{4,8},{5,9},{6,10},{7,11},{8,4},{9,5},{10,... | collective-permute-start | bytes 49160 | tf_op jit(solution)/shard_map/ppermute | solution.py:776
  21.1 1.6 %shard_map.164 = (f32[19,64,128]{2,1,0:T(8,128)S(1)}, f32[64,128]{1,0:T(8,128)}, f32[64,128]{1,0:T(8,128)}, f32[64,128]{1,0:T(8,128)}, f32[64,128]{1,0:T(8,128)}) custom-call(f32[3,19,8,128]{3,2,1,0:T(8,128)S(1)} %get-tuple-element.77.refs_0_, f32[152,152]{1,0:T(8,128)S(1)} %get-tuple-element.78.refs_1_, ...), custom_call_target="tpu_custom_call" | custom-call | flops 1024 | bytes 1048576 | tf_op jit(solution)/shard_map/pallas_call | solution.py:654
  22.8 0.2 collective-permute-done.11.refs_3_
  22.9 1.0 %shard_map.165 = f32[19,64,128]{2,1,0:T(8,128)} custom-call(f32[19,64,128]{2,1,0:T(8,128)S(1)} %get-tuple-element.89.refs_2_.refs_0_, f32[19,64,128]{2,1,0:T(8,128)S(1)} %get-tuple-element.109.refs_1_, f32[7,64,128]{2,1,0:T(8,128)S(1)} %get-tuple-element.98.refs_3_.refs_2_, f32[32,128]{1,0:T(8,128)S(1)} %collective-permute-done.11.refs_3_, ...), custom_call_target="tpu_custom_call" | custom-call | flops 1048576 | bytes 1048576 | tf_op jit(solution)/shard_map/pallas_call | solution.py:654
  (41 shorter events, 0.2 us)
Async XLA Ops:
  0.7 0.8 %copy-start.3 = (f32[32,1,2,128]{3,2,1,0:T(2,128)S(1)}, f32[32,1,2,128]{3,2,1,0:T(2,128)}, u32[]{:S(2)}) copy-start(f32[32,1,2,128]{3,2,1,0:T(2,128)} %param.14) | copy-start | bytes 98308
  0.7 0.8 %copy-start.4 = (f32[32,1,2,128]{3,2,1,0:T(2,128)S(1)}, f32[32,1,2,128]{3,2,1,0:T(2,128)}, u32[]{:S(2)}) copy-start(f32[32,1,2,128]{3,2,1,0:T(2,128)} %param.15) | copy-start | bytes 98308
  0.7 0.8 %copy-start.5 = (f32[32,1,2,128]{3,2,1,0:T(2,128)S(1)}, f32[32,1,2,128]{3,2,1,0:T(2,128)}, u32[]{:S(2)}) copy-start(f32[32,1,2,128]{3,2,1,0:T(2,128)} %param.16) | copy-start | bytes 98308
  0.7 0.8 %copy-start.8 = (f32[4,128]{1,0:T(4,128)S(1)}, f32[4,128]{1,0:T(4,128)}, u32[]{:S(2)}) copy-start(f32[4,128]{1,0:T(4,128)} %refs_10_.1) | copy-start | bytes 6148
  0.7 0.8 %copy-start.11 = (f32[19]{0:T(128)S(1)}, f32[19]{0:T(128)}, u32[]{:S(2)}) copy-start(f32[19]{0:T(128)} %param.23) | copy-start | bytes 232
  0.7 3.9 %copy-start = (f32[19,16,4,128]{3,2,1,0:T(4,128)S(1)}, f32[19,16,4,128]{3,2,1,0:T(4,128)}, u32[]{:S(2)}) copy-start(f32[19,16,4,128]{3,2,1,0:T(4,128)} %param.17) | copy-start | bytes 1867780
  0.7 0.8 %copy-start.6 = (f32[19,19]{1,0:T(8,128)S(1)}, f32[19,19]{1,0:T(8,128)}, u32[]{:S(2)}) copy-start(f32[19,19]{1,0:T(8,128)} %refs_8_.1) | copy-start | bytes 4336
  0.7 0.8 %copy-start.7 = (s32[4,128]{1,0:T(4,128)S(1)}, s32[4,128]{1,0:T(4,128)}, u32[]{:S(2)}) copy-start(s32[4,128]{1,0:T(4,128)} %refs_9_.1) | copy-start | bytes 6148
  0.7 0.8 %copy-start.9 = (f32[19]{0:T(128)S(1)}, f32[19]{0:T(128)}, u32[]{:S(2)}) copy-start(f32[19]{0:T(128)} %param.21) | copy-start | bytes 232
  1.6 7.3 %collective-permute-start.1 = (f32[180,128]{1,0:T(8,128)S(1)}, f32[180,128]{1,0:T(8,128)S(1)}, u32[]{:S(2)}, u32[]{:S(2)}) collective-permute-start(f32[180,128]{1,0:T(8,128)S(1)} %get-tuple-element.73), channel_id=1, source_target_pairs={{0,16},{16,0},{1,17},{17,1},{2,18},{18,2},{3,19},{19,3},{4,20},{20... | collective-permute-start | bytes 276488 | tf_op jit(solution)/shard_map/ppermute | solution.py:85
  4.7 4.2 %collective-permute-start = (f32[40,128]{1,0:T(8,128)S(1)}, f32[40,128]{1,0:T(8,128)S(1)}, u32[]{:S(2)}, u32[]{:S(2)}) collective-permute-start(f32[40,128]{1,0:T(8,128)S(1)} %get-tuple-element.71), channel_id=1, source_target_pairs={{0,16},{16,0},{1,17},{17,1},{2,18},{18,2},{3,19},{19,3},{4,20},{20... | collective-permute-start | bytes 61448 | tf_op jit(solution)/shard_map/ppermute | solution.py:85
  5.4 5.4 %collective-permute-start.3 = (f32[88,128]{1,0:T(8,128)S(1)}, f32[88,128]{1,0:T(8,128)S(1)}, u32[]{:S(2)}, u32[]{:S(2)}) collective-permute-start(f32[88,128]{1,0:T(8,128)S(1)} %get-tuple-element.76), channel_id=1, source_target_pairs={{0,16},{16,0},{1,17},{17,1},{2,18},{18,2},{3,19},{19,3},{4,20},{20... | collective-permute-start | bytes 135176 | tf_op jit(solution)/shard_map/ppermute | solution.py:85
  7.3 4.6 %collective-permute-start.2 = (f32[21,16,128]{2,1,0:T(8,128)S(1)}, f32[21,16,128]{2,1,0:T(8,128)S(1)}, u32[]{:S(2)}, u32[]{:S(2)}) collective-permute-start(f32[21,16,128]{2,1,0:T(8,128)S(1)} %get-tuple-element.75), channel_id=1, source_target_pairs={{0,1},{1,0},{2,3},{3,2},{4,5},{5,4},{6,7},{7,6},{8,9},{9,8},{10,11... | collective-permute-start | bytes 516104 | tf_op jit(solution)/shard_map/ppermute | solution.py:750
  7.3 6.3 %collective-permute-start.6 = (f32[21,16,128]{2,1,0:T(8,128)S(1)}, f32[21,16,128]{2,1,0:T(8,128)S(1)}, u32[]{:S(2)}, u32[]{:S(2)}) collective-permute-start(f32[21,16,128]{2,1,0:T(8,128)S(1)} %get-tuple-element.82), channel_id=1, source_target_pairs={{0,4},{1,2},{2,1},{3,7},{4,0},{5,6},{6,5},{7,3},{8,12},{9,10},{10,... | collective-permute-start | bytes 516104 | tf_op jit(solution)/shard_map/ppermute | solution.py:751
  9.2 4.3 %collective-permute-start.7 = (f32[48,128]{1,0:T(8,128)S(1)}, f32[48,128]{1,0:T(8,128)S(1)}, u32[]{:S(2)}, u32[]{:S(2)}) collective-permute-start(f32[48,128]{1,0:T(8,128)S(1)} %get-tuple-element.83), channel_id=1, source_target_pairs={{0,1},{1,2},{2,3},{3,0},{4,5},{5,6},{6,7},{7,4},{8,9},{9,10},{10,1... | collective-permute-start | bytes 73736 | tf_op jit(solution)/shard_map/ppermute | solution.py:777
  9.3 4.2 %collective-permute-start.4 = (f32[32,128]{1,0:T(8,128)S(1)}, f32[32,128]{1,0:T(8,128)S(1)}, u32[]{:S(2)}, u32[]{:S(2)}) collective-permute-start(f32[32,128]{1,0:T(8,128)S(1)} %get-tuple-element.80), channel_id=1, source_target_pairs={{0,4},{1,5},{2,6},{3,7},{4,0},{5,1},{6,2},{7,3},{8,12},{9,13},{10,... | collective-permute-start | bytes 49160 | tf_op jit(solution)/shard_map/ppermute | solution.py:775
  10.8 2.7 %collective-permute-start.5 = (f32[32,128]{1,0:T(8,128)S(1)}, f32[32,128]{1,0:T(8,128)S(1)}, u32[]{:S(2)}, u32[]{:S(2)}) collective-permute-start(f32[32,128]{1,0:T(8,128)S(1)} %get-tuple-element.81), channel_id=1, source_target_pairs={{0,1},{1,0},{2,3},{3,2},{4,8},{5,9},{6,10},{7,11},{8,4},{9,5},{10,... | collective-permute-start | bytes 49160 | tf_op jit(solution)/shard_map/ppermute | solution.py:776
  13.7 5.1 %collective-permute-start.8 = (f32[40,128]{1,0:T(8,128)S(1)}, f32[40,128]{1,0:T(8,128)S(1)}, u32[]{:S(2)}, u32[]{:S(2)}) collective-permute-start(f32[40,128]{1,0:T(8,128)S(1)} %get-tuple-element.92), channel_id=1, source_target_pairs={{0,16},{16,0},{1,17},{17,1},{2,18},{18,2},{3,19},{19,3},{4,20},{20... | collective-permute-start | bytes 61448 | tf_op jit(solution)/shard_map/ppermute | solution.py:85
  15.6 4.7 %collective-permute-start.10 = (f32[88,128]{1,0:T(8,128)S(1)}, f32[88,128]{1,0:T(8,128)S(1)}, u32[]{:S(2)}, u32[]{:S(2)}) collective-permute-start(f32[88,128]{1,0:T(8,128)S(1)} %get-tuple-element.100), channel_id=1, source_target_pairs={{0,16},{16,0},{1,17},{17,1},{2,18},{18,2},{3,19},{19,3},{4,20},{20... | collective-permute-start | bytes 135176 | tf_op jit(solution)/shard_map/ppermute | solution.py:85
  16.5 4.6 %collective-permute-start.9 = (f32[19,16,128]{2,1,0:T(8,128)S(1)}, f32[19,16,128]{2,1,0:T(8,128)S(1)}, u32[]{:S(2)}, u32[]{:S(2)}) collective-permute-start(f32[19,16,128]{2,1,0:T(8,128)S(1)} %get-tuple-element.99), channel_id=1, source_target_pairs={{0,1},{1,0},{2,3},{3,2},{4,5},{5,4},{6,7},{7,6},{8,9},{9,8},{10,11... | collective-permute-start | bytes 466952 | tf_op jit(solution)/shard_map/ppermute | solution.py:750
  16.5 6.5 %collective-permute-start.13 = (f32[19,16,128]{2,1,0:T(8,128)S(1)}, f32[19,16,128]{2,1,0:T(8,128)S(1)}, u32[]{:S(2)}, u32[]{:S(2)}) collective-permute-start(f32[19,16,128]{2,1,0:T(8,128)S(1)} %get-tuple-element.112), channel_id=1, source_target_pairs={{0,4},{1,2},{2,1},{3,7},{4,0},{5,6},{6,5},{7,3},{8,12},{9,10},{10,... | collective-permute-start | bytes 466952 | tf_op jit(solution)/shard_map/ppermute | solution.py:751
  19.1 3.8 %collective-permute-start.14 = (f32[48,128]{1,0:T(8,128)S(1)}, f32[48,128]{1,0:T(8,128)S(1)}, u32[]{:S(2)}, u32[]{:S(2)}) collective-permute-start(f32[48,128]{1,0:T(8,128)S(1)} %get-tuple-element.113), channel_id=1, source_target_pairs={{0,1},{1,2},{2,3},{3,0},{4,5},{5,6},{6,7},{7,4},{8,9},{9,10},{10,1... | collective-permute-start | bytes 73736 | tf_op jit(solution)/shard_map/ppermute | solution.py:777
  19.1 3.8 %collective-permute-start.11 = (f32[32,128]{1,0:T(8,128)S(1)}, f32[32,128]{1,0:T(8,128)S(1)}, u32[]{:S(2)}, u32[]{:S(2)}) collective-permute-start(f32[32,128]{1,0:T(8,128)S(1)} %get-tuple-element.110), channel_id=1, source_target_pairs={{0,4},{1,5},{2,6},{3,7},{4,0},{5,1},{6,2},{7,3},{8,12},{9,13},{10,... | collective-permute-start | bytes 49160 | tf_op jit(solution)/shard_map/ppermute | solution.py:775
  20.3 2.6 %collective-permute-start.12 = (f32[32,128]{1,0:T(8,128)S(1)}, f32[32,128]{1,0:T(8,128)S(1)}, u32[]{:S(2)}, u32[]{:S(2)}) collective-permute-start(f32[32,128]{1,0:T(8,128)S(1)} %get-tuple-element.111), channel_id=1, source_target_pairs={{0,1},{1,0},{2,3},{3,2},{4,8},{5,9},{6,10},{7,11},{8,4},{9,5},{10,... | collective-permute-start | bytes 49160 | tf_op jit(solution)/shard_map/ppermute | solution.py:776
  (3 other events, 2.3 us)

commit v10 on v8

--- a/solution.py
+++ b/solution.py
@@ -456,7 +456,7 @@
         params, (rates_ref,) = refs.take(3), refs.take(1)
     else:
         tiles_ref, w_ref = refs.take(2)
-    c_ref, band_ref = refs.take(2)
+    c_ref, band_ref, _ = refs.take(3)
     lev_in = refs.take(1 if count == 2 else 2)
     if last_step:
         full = refs.take(4)
@@ -774,7 +774,7 @@
         tables = [shape(3, tracers, SUB, width), shape(tracers * SUB, tracers * SUB)]
         part, *rest = call(
             functools.partial(inner_kernel, rows, count, first_step, last_step),
-            [*([*params, rates] if first_step else known_rates), c, band, *lev, *(full if last_step else [])],
+            [*([*params, rates] if first_step else known_rates), c, band, ya, *lev, *(full if last_step else [])],
             [field]
             + ([shape(strip_cells, width)] * 4 if last_step else [cols])
             + (tables if first_step else []),

time: 24.1 us -> 24.1 us (level)
  no operation moved by 1% of the time
where the time goes in v10:
time: 24.1 us; the launch traced here: 23.9 us
  starting transfers between devices  15.9 us (66%)
  Pallas kernels  6.18 us (26%)
  between operations  0.85 us (4%)
  local copies, waits for them, and re-layouts  0.79 us (3%)
    ppermute x5, starting transfers between devices, from_others(): lax.ppermute(value, 'grp', [(i, (i + k) % count) for i in range(count)])  7.32 us
    pallas_call x11, Pallas kernels, call(): pl.pallas_call(kernel, in_specs=[vmem() for _ in ins] if in_specs is None...  6.18 us
    ppermute x2, starting transfers between devices, per_device(): yb = lax.ppermute(yb, AXES, pairing(sizes, 'gy', 1))  3.9 us
    ppermute x2, starting transfers between devices, per_device(): xa = lax.ppermute(xa, AXES, pairing(sizes, 'gx', 0))  2.78 us
    ppermute x2, starting transfers between devices, per_device(): xb = lax.ppermute(xb, AXES, pairing(sizes, 'gx', 1))  1.78 us
    unnamed x24, local copies, waits for them, and re-layouts  0.79 us
  transfers between devices with their start and end apart: 15, of which 1 were waited for; matrix products, arithmetic and copies ran while one was open for 0% of the time, Pallas kernels for 21%

profile of v10, /device:TPU:0, one launch (start us, length us, event | category | flops | bytes accessed | tf_op | source)
XLA Modules:
  0.0 23.9 jit_solution(7219616465323308212)
XLA Ops:
  0.8 0.6 %copy-done.1 = f32[32,1,2,128]{3,2,1,0:T(2,128)S(1)} copy-done((f32[32,1,2,128]{3,2,1,0:T(2,128)S(1)}, f32[32,1,2,128]{3,2,1,0:T(2,128)}, u32[]{:S(2)}) %copy-start.1) | copy-done | bytes 32792
  1.5 0.1 copy-done.6
  1.6 3.0 %collective-permute-start.1 = (f32[180,128]{1,0:T(8,128)S(1)}, f32[180,128]{1,0:T(8,128)S(1)}, u32[]{:S(2)}, u32[]{:S(2)}) collective-permute-start(f32[180,128]{1,0:T(8,128)S(1)} %get-tuple-element.73), channel_id=1, source_target_pairs={{0,16},{16,0},{1,17},{17,1},{2,18},{18,2},{3,19},{19,3},{4,20},{20... | collective-permute-start | bytes 276488 | tf_op jit(solution)/shard_map/ppermute | solution.py:85
  4.6 0.1 shard_map.157
  4.7 0.3 %collective-permute-start = (f32[40,128]{1,0:T(8,128)S(1)}, f32[40,128]{1,0:T(8,128)S(1)}, u32[]{:S(2)}, u32[]{:S(2)}) collective-permute-start(f32[40,128]{1,0:T(8,128)S(1)} %get-tuple-element.71), channel_id=1, source_target_pairs={{0,16},{16,0},{1,17},{17,1},{2,18},{18,2},{3,19},{19,3},{4,20},{20... | collective-permute-start | bytes 61448 | tf_op jit(solution)/shard_map/ppermute | solution.py:85
  5.0 0.4 %shard_map.158 = (f32[32,128]{1,0:T(8,128)S(1)}, f32[32,128]{1,0:T(8,128)S(1)}, f32[21,16,128]{2,1,0:T(8,128)S(1)}, f32[21,16,128]{2,1,0:T(8,128)S(1)}, s32[8,12...) custom-call(s32[4,128]{1,0:T(4,128)S(1)} %get-tuple-element.64.refs_0_, ...), custom_call_target="tpu_custom_call" | custom-call | flops 16777216 | bytes 1048576 | tf_op jit(solution)/shard_map/pallas_call | solution.py:651
  5.4 1.8 %collective-permute-start.3 = (f32[88,128]{1,0:T(8,128)S(1)}, f32[88,128]{1,0:T(8,128)S(1)}, u32[]{:S(2)}, u32[]{:S(2)}) collective-permute-start(f32[88,128]{1,0:T(8,128)S(1)} %get-tuple-element.76), channel_id=1, source_target_pairs={{0,16},{16,0},{1,17},{17,1},{2,18},{18,2},{3,19},{19,3},{4,20},{20... | collective-permute-start | bytes 135176 | tf_op jit(solution)/shard_map/ppermute | solution.py:85
  7.3 1.6 %collective-permute-start.6 = (f32[21,16,128]{2,1,0:T(8,128)S(1)}, f32[21,16,128]{2,1,0:T(8,128)S(1)}, u32[]{:S(2)}, u32[]{:S(2)}) collective-permute-start(f32[21,16,128]{2,1,0:T(8,128)S(1)} %get-tuple-element.82), channel_id=1, source_target_pairs={{0,4},{1,2},{2,1},{3,7},{4,0},{5,6},{6,5},{7,3},{8,12},{9,10},{10,... | collective-permute-start | bytes 516104 | tf_op jit(solution)/shard_map/ppermute | solution.py:748
  8.9 0.3 %shard_map.159 = (f32[7,64,128]{2,1,0:T(8,128)S(1)}, f32[32,128]{1,0:T(8,128)S(1)}, f32[32,128]{1,0:T(8,128)S(1)}, f32[48,128]{1,0:T(8,128)S(1)}, f32[128,128]{1...) custom-call(s32[8,128]{1,0:T(8,128)S(1)} %get-tuple-element.67.refs_, ...), custom_call_target="tpu_custom_call" | custom-call | flops 4294967296 | bytes 1048576 | tf_op jit(solution)/shard_map/pallas_call | solution.py:651
  9.1 0.1 collective-permute-start.7
  9.2 1.6 %collective-permute-start.4 = (f32[32,128]{1,0:T(8,128)S(1)}, f32[32,128]{1,0:T(8,128)S(1)}, u32[]{:S(2)}, u32[]{:S(2)}) collective-permute-start(f32[32,128]{1,0:T(8,128)S(1)} %get-tuple-element.80), channel_id=1, source_target_pairs={{0,4},{1,5},{2,6},{3,7},{4,0},{5,1},{6,2},{7,3},{8,12},{9,13},{10,... | collective-permute-start | bytes 49160 | tf_op jit(solution)/shard_map/ppermute | solution.py:771
  10.8 1.0 %collective-permute-start.5 = (f32[32,128]{1,0:T(8,128)S(1)}, f32[32,128]{1,0:T(8,128)S(1)}, u32[]{:S(2)}, u32[]{:S(2)}) collective-permute-start(f32[32,128]{1,0:T(8,128)S(1)} %get-tuple-element.81), channel_id=1, source_target_pairs={{0,1},{1,0},{2,3},{3,2},{4,8},{5,9},{6,10},{7,11},{8,4},{9,5},{10,... | collective-permute-start | bytes 49160 | tf_op jit(solution)/shard_map/ppermute | solution.py:772
  11.8 1.6 %shard_map.160 = (f32[19,64,128]{2,1,0:T(8,128)S(1)}, f32[64,128]{1,0:T(8,128)S(1)}, f32[3,19,8,128]{3,2,1,0:T(8,128)S(1)}, f32[152,152]{1,0:T(8,128)S(1)}) custom-call(f32[1,19]{1,0:T(1,128)S(1)} %get-tuple-element.60.refs_0_, f32[1,19]{1,0:T(1,128)S(1)} %get-tuple-element.61.refs_1_, f32[1,19]{1,0:T(1,128)S(1)} %get-tuple-element.62.pig_ref.refs_2_, ...), custom_call_target="tpu_custom_call" | custom-call | flops 1024 | bytes 1048576 | tf_op jit(solution)/shard_map/pallas_call | solution.py:651
  13.5 0.1 shard_map.161
  13.7 1.3 %collective-permute-start.8 = (f32[40,128]{1,0:T(8,128)S(1)}, f32[40,128]{1,0:T(8,128)S(1)}, u32[]{:S(2)}, u32[]{:S(2)}) collective-permute-start(f32[40,128]{1,0:T(8,128)S(1)} %get-tuple-element.92), channel_id=1, source_target_pairs={{0,16},{16,0},{1,17},{17,1},{2,18},{18,2},{3,19},{19,3},{4,20},{20... | collective-permute-start | bytes 61448 | tf_op jit(solution)/shard_map/ppermute | solution.py:85
  14.9 0.6 %shard_map.162 = (f32[19,64,128]{2,1,0:T(8,128)S(1)}, f32[32,128]{1,0:T(8,128)S(1)}, f32[32,128]{1,0:T(8,128)S(1)}, f32[19,16,128]{2,1,0:T(8,128)S(1)}, f32[19,1...) custom-call(f32[19,64,128]{2,1,0:T(8,128)S(1)} %bitcast.26, f32[19,64,128]{2,1,0:T(8,128)S(1)} %get-tuple-element.79.refs_8_.refs_1_, ...), custom_call_target="tpu_custom_call" | custom-call | flops 4294967296 | bytes 1048576 | tf_op jit(solution)/shard_map/pallas_call | solution.py:651
  15.6 0.9 %collective-permute-start.10 = (f32[88,128]{1,0:T(8,128)S(1)}, f32[88,128]{1,0:T(8,128)S(1)}, u32[]{:S(2)}, u32[]{:S(2)}) collective-permute-start(f32[88,128]{1,0:T(8,128)S(1)} %get-tuple-element.100), channel_id=1, source_target_pairs={{0,16},{16,0},{1,17},{17,1},{2,18},{18,2},{3,19},{19,3},{4,20},{20... | collective-permute-start | bytes 135176 | tf_op jit(solution)/shard_map/ppermute | solution.py:85
  16.5 2.3 %collective-permute-start.13 = (f32[19,16,128]{2,1,0:T(8,128)S(1)}, f32[19,16,128]{2,1,0:T(8,128)S(1)}, u32[]{:S(2)}, u32[]{:S(2)}) collective-permute-start(f32[19,16,128]{2,1,0:T(8,128)S(1)} %get-tuple-element.112), channel_id=1, source_target_pairs={{0,4},{1,2},{2,1},{3,7},{4,0},{5,6},{6,5},{7,3},{8,12},{9,10},{10,... | collective-permute-start | bytes 466952 | tf_op jit(solution)/shard_map/ppermute | solution.py:748
  18.8 0.3 %shard_map.163 = (f32[7,64,128]{2,1,0:T(8,128)S(1)}, f32[32,128]{1,0:T(8,128)S(1)}, f32[32,128]{1,0:T(8,128)S(1)}, f32[48,128]{1,0:T(8,128)S(1)}, f32[128,128]{1...) custom-call(s32[8,128]{1,0:T(8,128)S(1)} %get-tuple-element.67.refs_0_, ...), custom_call_target="tpu_custom_call" | custom-call | flops 4294967296 | bytes 1048576 | tf_op jit(solution)/shard_map/pallas_call | solution.py:651
  19.1 1.2 %collective-permute-start.11 = (f32[32,128]{1,0:T(8,128)S(1)}, f32[32,128]{1,0:T(8,128)S(1)}, u32[]{:S(2)}, u32[]{:S(2)}) collective-permute-start(f32[32,128]{1,0:T(8,128)S(1)} %get-tuple-element.110), channel_id=1, source_target_pairs={{0,4},{1,5},{2,6},{3,7},{4,0},{5,1},{6,2},{7,3},{8,12},{9,13},{10,... | collective-permute-start | bytes 49160 | tf_op jit(solution)/shard_map/ppermute | solution.py:771
  20.3 0.8 %collective-permute-start.12 = (f32[32,128]{1,0:T(8,128)S(1)}, f32[32,128]{1,0:T(8,128)S(1)}, u32[]{:S(2)}, u32[]{:S(2)}) collective-permute-start(f32[32,128]{1,0:T(8,128)S(1)} %get-tuple-element.111), channel_id=1, source_target_pairs={{0,1},{1,0},{2,3},{3,2},{4,8},{5,9},{6,10},{7,11},{8,4},{9,5},{10,... | collective-permute-start | bytes 49160 | tf_op jit(solution)/shard_map/ppermute | solution.py:772
  21.1 1.7 %shard_map.164 = (f32[19,64,128]{2,1,0:T(8,128)S(1)}, f32[64,128]{1,0:T(8,128)}, f32[64,128]{1,0:T(8,128)}, f32[64,128]{1,0:T(8,128)}, f32[64,128]{1,0:T(8,128)}) custom-call(f32[3,19,8,128]{3,2,1,0:T(8,128)S(1)} %get-tuple-element.77.refs_0_, f32[152,152]{1,0:T(8,128)S(1)} %get-tuple-element.78.refs_1_, ...), custom_call_target="tpu_custom_call" | custom-call | flops 1024 | bytes 1048576 | tf_op jit(solution)/shard_map/pallas_call | solution.py:651
  22.8 0.2 collective-permute-done.11.refs_3_
  22.9 1.0 %shard_map.165 = f32[19,64,128]{2,1,0:T(8,128)} custom-call(f32[19,64,128]{2,1,0:T(8,128)S(1)} %get-tuple-element.89.refs_2_.refs_0_, f32[19,64,128]{2,1,0:T(8,128)S(1)} %get-tuple-element.109.refs_1_, f32[7,64,128]{2,1,0:T(8,128)S(1)} %get-tuple-element.98.refs_3_.refs_2_, f32[32,128]{1,0:T(8,128)S(1)} %collective-permute-done.11.refs_3_, ...), custom_call_target="tpu_custom_call" | custom-call | flops 1048576 | bytes 1048576 | tf_op jit(solution)/shard_map/pallas_call | solution.py:651
  (41 shorter events, 0.2 us)
Async XLA Ops:
  0.7 0.8 %copy-start.3 = (f32[32,1,2,128]{3,2,1,0:T(2,128)S(1)}, f32[32,1,2,128]{3,2,1,0:T(2,128)}, u32[]{:S(2)}) copy-start(f32[32,1,2,128]{3,2,1,0:T(2,128)} %param.14) | copy-start | bytes 98308
  0.7 0.8 %copy-start.4 = (f32[32,1,2,128]{3,2,1,0:T(2,128)S(1)}, f32[32,1,2,128]{3,2,1,0:T(2,128)}, u32[]{:S(2)}) copy-start(f32[32,1,2,128]{3,2,1,0:T(2,128)} %param.15) | copy-start | bytes 98308
  0.7 0.8 %copy-start.5 = (f32[32,1,2,128]{3,2,1,0:T(2,128)S(1)}, f32[32,1,2,128]{3,2,1,0:T(2,128)}, u32[]{:S(2)}) copy-start(f32[32,1,2,128]{3,2,1,0:T(2,128)} %param.16) | copy-start | bytes 98308
  0.7 0.8 %copy-start.8 = (f32[4,128]{1,0:T(4,128)S(1)}, f32[4,128]{1,0:T(4,128)}, u32[]{:S(2)}) copy-start(f32[4,128]{1,0:T(4,128)} %refs_10_.1) | copy-start | bytes 6148
  0.7 0.8 %copy-start.11 = (f32[19]{0:T(128)S(1)}, f32[19]{0:T(128)}, u32[]{:S(2)}) copy-start(f32[19]{0:T(128)} %param.23) | copy-start | bytes 232
  0.7 3.9 %copy-start = (f32[19,16,4,128]{3,2,1,0:T(4,128)S(1)}, f32[19,16,4,128]{3,2,1,0:T(4,128)}, u32[]{:S(2)}) copy-start(f32[19,16,4,128]{3,2,1,0:T(4,128)} %param.17) | copy-start | bytes 1867780
  0.7 0.8 %copy-start.6 = (f32[19,19]{1,0:T(8,128)S(1)}, f32[19,19]{1,0:T(8,128)}, u32[]{:S(2)}) copy-start(f32[19,19]{1,0:T(8,128)} %refs_8_.1) | copy-start | bytes 4336
  0.7 0.8 %copy-start.7 = (s32[4,128]{1,0:T(4,128)S(1)}, s32[4,128]{1,0:T(4,128)}, u32[]{:S(2)}) copy-start(s32[4,128]{1,0:T(4,128)} %refs_9_.1) | copy-start | bytes 6148
  0.7 0.8 %copy-start.9 = (f32[19]{0:T(128)S(1)}, f32[19]{0:T(128)}, u32[]{:S(2)}) copy-start(f32[19]{0:T(128)} %param.21) | copy-start | bytes 232
  1.6 7.3 %collective-permute-start.1 = (f32[180,128]{1,0:T(8,128)S(1)}, f32[180,128]{1,0:T(8,128)S(1)}, u32[]{:S(2)}, u32[]{:S(2)}) collective-permute-start(f32[180,128]{1,0:T(8,128)S(1)} %get-tuple-element.73), channel_id=1, source_target_pairs={{0,16},{16,0},{1,17},{17,1},{2,18},{18,2},{3,19},{19,3},{4,20},{20... | collective-permute-start | bytes 276488 | tf_op jit(solution)/shard_map/ppermute | solution.py:85
  4.7 4.2 %collective-permute-start = (f32[40,128]{1,0:T(8,128)S(1)}, f32[40,128]{1,0:T(8,128)S(1)}, u32[]{:S(2)}, u32[]{:S(2)}) collective-permute-start(f32[40,128]{1,0:T(8,128)S(1)} %get-tuple-element.71), channel_id=1, source_target_pairs={{0,16},{16,0},{1,17},{17,1},{2,18},{18,2},{3,19},{19,3},{4,20},{20... | collective-permute-start | bytes 61448 | tf_op jit(solution)/shard_map/ppermute | solution.py:85
  5.4 5.4 %collective-permute-start.3 = (f32[88,128]{1,0:T(8,128)S(1)}, f32[88,128]{1,0:T(8,128)S(1)}, u32[]{:S(2)}, u32[]{:S(2)}) collective-permute-start(f32[88,128]{1,0:T(8,128)S(1)} %get-tuple-element.76), channel_id=1, source_target_pairs={{0,16},{16,0},{1,17},{17,1},{2,18},{18,2},{3,19},{19,3},{4,20},{20... | collective-permute-start | bytes 135176 | tf_op jit(solution)/shard_map/ppermute | solution.py:85
  7.3 4.6 %collective-permute-start.2 = (f32[21,16,128]{2,1,0:T(8,128)S(1)}, f32[21,16,128]{2,1,0:T(8,128)S(1)}, u32[]{:S(2)}, u32[]{:S(2)}) collective-permute-start(f32[21,16,128]{2,1,0:T(8,128)S(1)} %get-tuple-element.75), channel_id=1, source_target_pairs={{0,1},{1,0},{2,3},{3,2},{4,5},{5,4},{6,7},{7,6},{8,9},{9,8},{10,11... | collective-permute-start | bytes 516104 | tf_op jit(solution)/shard_map/ppermute | solution.py:747
  7.3 6.2 %collective-permute-start.6 = (f32[21,16,128]{2,1,0:T(8,128)S(1)}, f32[21,16,128]{2,1,0:T(8,128)S(1)}, u32[]{:S(2)}, u32[]{:S(2)}) collective-permute-start(f32[21,16,128]{2,1,0:T(8,128)S(1)} %get-tuple-element.82), channel_id=1, source_target_pairs={{0,4},{1,2},{2,1},{3,7},{4,0},{5,6},{6,5},{7,3},{8,12},{9,10},{10,... | collective-permute-start | bytes 516104 | tf_op jit(solution)/shard_map/ppermute | solution.py:748
  9.1 4.4 %collective-permute-start.7 = (f32[48,128]{1,0:T(8,128)S(1)}, f32[48,128]{1,0:T(8,128)S(1)}, u32[]{:S(2)}, u32[]{:S(2)}) collective-permute-start(f32[48,128]{1,0:T(8,128)S(1)} %get-tuple-element.83), channel_id=1, source_target_pairs={{0,1},{1,2},{2,3},{3,0},{4,5},{5,6},{6,7},{7,4},{8,9},{9,10},{10,1... | collective-permute-start | bytes 73736 | tf_op jit(solution)/shard_map/ppermute | solution.py:773
  9.2 4.2 %collective-permute-start.4 = (f32[32,128]{1,0:T(8,128)S(1)}, f32[32,128]{1,0:T(8,128)S(1)}, u32[]{:S(2)}, u32[]{:S(2)}) collective-permute-start(f32[32,128]{1,0:T(8,128)S(1)} %get-tuple-element.80), channel_id=1, source_target_pairs={{0,4},{1,5},{2,6},{3,7},{4,0},{5,1},{6,2},{7,3},{8,12},{9,13},{10,... | collective-permute-start | bytes 49160 | tf_op jit(solution)/shard_map/ppermute | solution.py:771
  10.8 2.7 %collective-permute-start.5 = (f32[32,128]{1,0:T(8,128)S(1)}, f32[32,128]{1,0:T(8,128)S(1)}, u32[]{:S(2)}, u32[]{:S(2)}) collective-permute-start(f32[32,128]{1,0:T(8,128)S(1)} %get-tuple-element.81), channel_id=1, source_target_pairs={{0,1},{1,0},{2,3},{3,2},{4,8},{5,9},{6,10},{7,11},{8,4},{9,5},{10,... | collective-permute-start | bytes 49160 | tf_op jit(solution)/shard_map/ppermute | solution.py:772
  13.7 5.1 %collective-permute-start.8 = (f32[40,128]{1,0:T(8,128)S(1)}, f32[40,128]{1,0:T(8,128)S(1)}, u32[]{:S(2)}, u32[]{:S(2)}) collective-permute-start(f32[40,128]{1,0:T(8,128)S(1)} %get-tuple-element.92), channel_id=1, source_target_pairs={{0,16},{16,0},{1,17},{17,1},{2,18},{18,2},{3,19},{19,3},{4,20},{20... | collective-permute-start | bytes 61448 | tf_op jit(solution)/shard_map/ppermute | solution.py:85
  15.6 4.8 %collective-permute-start.10 = (f32[88,128]{1,0:T(8,128)S(1)}, f32[88,128]{1,0:T(8,128)S(1)}, u32[]{:S(2)}, u32[]{:S(2)}) collective-permute-start(f32[88,128]{1,0:T(8,128)S(1)} %get-tuple-element.100), channel_id=1, source_target_pairs={{0,16},{16,0},{1,17},{17,1},{2,18},{18,2},{3,19},{19,3},{4,20},{20... | collective-permute-start | bytes 135176 | tf_op jit(solution)/shard_map/ppermute | solution.py:85
  16.5 4.6 %collective-permute-start.9 = (f32[19,16,128]{2,1,0:T(8,128)S(1)}, f32[19,16,128]{2,1,0:T(8,128)S(1)}, u32[]{:S(2)}, u32[]{:S(2)}) collective-permute-start(f32[19,16,128]{2,1,0:T(8,128)S(1)} %get-tuple-element.99), channel_id=1, source_target_pairs={{0,1},{1,0},{2,3},{3,2},{4,5},{5,4},{6,7},{7,6},{8,9},{9,8},{10,11... | collective-permute-start | bytes 466952 | tf_op jit(solution)/shard_map/ppermute | solution.py:747
  16.5 6.5 %collective-permute-start.13 = (f32[19,16,128]{2,1,0:T(8,128)S(1)}, f32[19,16,128]{2,1,0:T(8,128)S(1)}, u32[]{:S(2)}, u32[]{:S(2)}) collective-permute-start(f32[19,16,128]{2,1,0:T(8,128)S(1)} %get-tuple-element.112), channel_id=1, source_target_pairs={{0,4},{1,2},{2,1},{3,7},{4,0},{5,6},{6,5},{7,3},{8,12},{9,10},{10,... | collective-permute-start | bytes 466952 | tf_op jit(solution)/shard_map/ppermute | solution.py:748
  19.1 3.9 %collective-permute-start.14 = (f32[48,128]{1,0:T(8,128)S(1)}, f32[48,128]{1,0:T(8,128)S(1)}, u32[]{:S(2)}, u32[]{:S(2)}) collective-permute-start(f32[48,128]{1,0:T(8,128)S(1)} %get-tuple-element.113), channel_id=1, source_target_pairs={{0,1},{1,2},{2,3},{3,0},{4,5},{5,6},{6,7},{7,4},{8,9},{9,10},{10,1... | collective-permute-start | bytes 73736 | tf_op jit(solution)/shard_map/ppermute | solution.py:773
  19.1 3.8 %collective-permute-start.11 = (f32[32,128]{1,0:T(8,128)S(1)}, f32[32,128]{1,0:T(8,128)S(1)}, u32[]{:S(2)}, u32[]{:S(2)}) collective-permute-start(f32[32,128]{1,0:T(8,128)S(1)} %get-tuple-element.110), channel_id=1, source_target_pairs={{0,4},{1,5},{2,6},{3,7},{4,0},{5,1},{6,2},{7,3},{8,12},{9,13},{10,... | collective-permute-start | bytes 49160 | tf_op jit(solution)/shard_map/ppermute | solution.py:771
  20.3 2.6 %collective-permute-start.12 = (f32[32,128]{1,0:T(8,128)S(1)}, f32[32,128]{1,0:T(8,128)S(1)}, u32[]{:S(2)}, u32[]{:S(2)}) collective-permute-start(f32[32,128]{1,0:T(8,128)S(1)} %get-tuple-element.111), channel_id=1, source_target_pairs={{0,1},{1,0},{2,3},{3,2},{4,8},{5,9},{6,10},{7,11},{8,4},{9,5},{10,... | collective-permute-start | bytes 49160 | tf_op jit(solution)/shard_map/ppermute | solution.py:772
  (3 other events, 2.3 us)
